TPU v7x, 32 devices: a whole 2x2x4 slice. The times are simulated.
32 devices in a mesh: dp: 8 (over z, x), mp: 4 (over y, core).
Axes of the slice: x: 2, y: 2, z: 4, core: 2. Of those that a mesh axis runs over, the one named last changes fastest.
Arguments:
- layer_in: float32 [4096, 768], P(('dp', 'mp')), may hold values from -6 to 6
- node_counts: int32 [32], P('dp'), may hold values from 32 to 127, as said below
- spatial_ids: int32 [32, 128, 128], P('dp'), may hold values from 0 to 20
- path_ids: int32 [32, 5, 128, 128], P('dp'), may hold values from 0 to 1535
- ln1_gain: float32 [768], replicated, may hold values from 0.25 to 1.75
- ln1_bias: float32 [768], replicated, may hold values from -3 to 3
- w_q: bfloat16 [768, 768], P('dp', 'mp'), may hold values from -0.21875 to 0.21875
- w_k: bfloat16 [768, 768], P('dp', 'mp'), may hold values from -0.21875 to 0.21875
- w_v: bfloat16 [768, 768], P('dp', 'mp'), may hold values from -0.21875 to 0.21875
- q_bias: float32 [768], P('mp'), may hold values from -3 to 3
- v_bias: float32 [768], P('mp'), may hold values from -3 to 3
- spatial_table: bfloat16 [22, 32], replicated, may hold values from -4 to 4
- edge_table: bfloat16 [1536, 32], P('dp'), may hold values from -4 to 4
- w_o: bfloat16 [768, 768], P('dp', 'mp'), may hold values from -0.875 to 0.875
- o_bias: float32 [768], replicated, may hold values from -3 to 3
- ln2_gain: float32 [768], replicated, may hold values from 0.25 to 1.75
- ln2_bias: float32 [768], replicated, may hold values from -3 to 3
- w_in: bfloat16 [768, 768], P('dp', 'mp'), may hold values from -0.21875 to 0.21875
- in_bias: float32 [768], P('mp'), may hold values from -3 to 3
- w_out: bfloat16 [768, 768], P('dp', 'mp'), may hold values from -0.3125 to 0.3125
- out_bias: float32 [768], replicated, may hold values from -3 to 3
- cotangent: float32 [4096, 768], P(('dp', 'mp')), may hold values from -6 to 6
Outputs:
- layer_out: float32 [4096, 768], P(('dp', 'mp'))
- grad_layer_in: float32 [4096, 768], P(('dp', 'mp'))
- grad_ln1_gain: float32 [768], replicated
- grad_ln1_bias: float32 [768], replicated
- grad_w_q: float32 [768, 768], P('dp', 'mp')
- grad_w_k: float32 [768, 768], P('dp', 'mp')
- grad_w_v: float32 [768, 768], P('dp', 'mp')
- grad_q_bias: float32 [768], P('mp')
- grad_v_bias: float32 [768], P('mp')
- grad_spatial_table: float32 [22, 32], P(None, 'mp')
- grad_edge_table: float32 [1536, 32], P('dp', 'mp')
- grad_w_o: float32 [768, 768], P('dp', 'mp')
- grad_o_bias: float32 [768], replicated
- grad_ln2_gain: float32 [768], replicated
- grad_ln2_bias: float32 [768], replicated
- grad_w_in: float32 [768, 768], P('dp', 'mp')
- grad_in_bias: float32 [768], P('mp')
- grad_w_out: float32 [768, 768], P('dp', 'mp')
- grad_out_bias: float32 [768], replicated
Inputs may be any that keep to these rules, and one draw needn't show every extreme that they name: Graph g holds its virtual node in slot 0 and its nodes in slots 1 to node_counts[g]; later slots are padding. `spatial_ids`: bucket 22 - 2 stands for unreachable pairs; bucket 22 - 1 is never given.
All inputs are finite; a program needn't handle non-finite values.
Results may differ from a plain program's by a relative error of at most 0.012.
Values may be sent and summed in bfloat16 or wider, within the bound.
No kernel may reach another device: no remote copies, remote signals or barrier semaphores. Data moves between devices by JAX's collectives and lax.ppermute only.
A program may use at most 64 MiB of HBM per device.

v0:
```python
import jax
import jax.numpy as jnp
from jax import lax
from jax.sharding import PartitionSpec as P

epsilon = 1e-05
masked_score = -1e30
pair_block = 2048


def normalize(values):
    centred = values - jnp.mean(values, axis=-1, keepdims=True)
    scale = lax.rsqrt(jnp.mean(centred * centred, axis=-1, keepdims=True) + epsilon)
    return (centred * scale, scale)


def normalize_back(grad_normed, normed, scale):
    inner = grad_normed - jnp.mean(grad_normed, axis=-1, keepdims=True)
    inner = inner - normed * jnp.mean(grad_normed * normed, axis=-1, keepdims=True)
    return inner * scale


def contract_first(left, right):
    return lax.dot_general(
        left, right, (((0,), (0,)), ((), ())), preferred_element_type=jnp.float32
    )


def contract_last(left, right):
    return lax.dot_general(
        left, right, (((1,), (1,)), ((), ())), preferred_element_type=jnp.float32
    )


def bucket_flat(spatial_g, buckets):
    slots = spatial_g.shape[0]
    rows = lax.broadcasted_iota(jnp.int32, (slots, slots), 0)
    columns = lax.broadcasted_iota(jnp.int32, (slots, slots), 1)
    chosen = jnp.where((rows == 0) | (columns == 0), buckets - 1, spatial_g)
    return chosen.reshape(1, slots * slots)


def bucket_onehot(flat_ids, count, buckets):
    kinds = lax.broadcasted_iota(jnp.int32, (buckets, count), 0)
    return (flat_ids == kinds).astype(jnp.bfloat16)


def edge_counts(path_flat, start, width, edges):
    labels = lax.dynamic_slice_in_dim(path_flat, start, width, 1)
    kinds = lax.broadcasted_iota(jnp.int32, (edges, width), 0)
    total = jnp.zeros((edges, width), jnp.bfloat16)
    for hop in range(labels.shape[0]):
        total = total + (labels[hop][None, :] == kinds).astype(jnp.bfloat16)
    return total


def pair_bias(spatial_g, path_g, spatial_tab, edge_tab, start, count):
    slots = spatial_g.shape[0]
    pairs = slots * slots
    flat_ids = bucket_flat(spatial_g, spatial_tab.shape[0])
    bias = contract_first(spatial_tab, bucket_onehot(flat_ids, count, spatial_tab.shape[0]))
    path_flat = path_g.reshape(path_g.shape[0], pairs)
    width = min(count, pair_block)

    def block_terms(offset):
        return contract_first(
            edge_tab, edge_counts(path_flat, start + offset, width, edge_tab.shape[0])
        )

    terms = lax.map(block_terms, jnp.arange(count // width, dtype=jnp.int32) * width)
    terms = jnp.transpose(terms, (1, 0, 2)).reshape(bias.shape)
    return bias + terms / path_g.shape[0]


def graph_scores(query, keys, bias, count):
    slots, heads, depth = query.shape
    scores = jnp.einsum(
        "qhd,khd->hqk", query, keys, preferred_element_type=jnp.float32
    ) * depth ** (-0.5)
    scores = scores + bias.reshape(heads, slots, slots)
    places = lax.broadcasted_iota(jnp.int32, (1, 1, slots), 2)
    return jnp.where(places <= count, scores, masked_score)


def attend_graph(query, keys, values, bias, count):
    scores = graph_scores(query, keys, bias, count)
    top = jnp.max(scores, axis=-1, keepdims=True)
    weights = jnp.exp(scores - top)
    total = jnp.sum(weights, axis=-1, keepdims=True)
    probs = (weights / total).astype(jnp.bfloat16)
    attended = jnp.einsum("hqk,khd->qhd", probs, values, preferred_element_type=jnp.float32)
    return (attended.astype(jnp.bfloat16), top + jnp.log(total))


def attend_graph_back(query, keys, values, bias, count, log_total, grad_attended):
    depth = query.shape[-1]
    scores = graph_scores(query, keys, bias, count)
    probs = jnp.exp(scores - log_total)
    grad_probs = jnp.einsum(
        "qhd,khd->hqk", grad_attended, values, preferred_element_type=jnp.float32
    )
    grad_values = jnp.einsum(
        "hqk,qhd->khd",
        probs.astype(jnp.bfloat16),
        grad_attended,
        preferred_element_type=jnp.float32,
    )
    grad_scores = probs * (grad_probs - jnp.sum(probs * grad_probs, axis=-1, keepdims=True))
    grad_scores = grad_scores.astype(jnp.bfloat16)
    grad_query = jnp.einsum(
        "hqk,khd->qhd", grad_scores, keys, preferred_element_type=jnp.float32
    ) * depth ** (-0.5)
    grad_keys = jnp.einsum(
        "hqk,qhd->khd", grad_scores, query, preferred_element_type=jnp.float32
    ) * depth ** (-0.5)
    return (
        grad_query.astype(jnp.bfloat16),
        grad_keys.astype(jnp.bfloat16),
        grad_values.astype(jnp.bfloat16),
        grad_scores,
    )


def table_grads(spatial_g, path_g, piece, start, spatial_grad, edge_grad):
    count = piece.shape[1]
    pairs = spatial_g.shape[0] * spatial_g.shape[1]
    flat_ids = bucket_flat(spatial_g, spatial_grad.shape[0])
    spatial_grad = spatial_grad + contract_last(
        bucket_onehot(flat_ids, count, spatial_grad.shape[0]), piece
    )
    path_flat = path_g.reshape(path_g.shape[0], pairs)
    width = min(count, pair_block)

    def add_block(index, total):
        offset = index * width
        counts = edge_counts(path_flat, start + offset, width, edge_grad.shape[0])
        block = lax.dynamic_slice_in_dim(piece, offset, width, 1)
        return total + contract_last(counts, block)

    edge_grad = lax.fori_loop(0, count // width, add_block, edge_grad)
    return (spatial_grad, edge_grad)


def local(
    layer_in,
    node_counts,
    spatial_ids,
    path_ids,
    ln1_gain,
    ln1_bias,
    w_q,
    w_k,
    w_v,
    q_bias,
    v_bias,
    spatial_table,
    edge_table,
    w_o,
    o_bias,
    ln2_gain,
    ln2_bias,
    w_in,
    in_bias,
    w_out,
    out_bias,
    cotangent,
):
    graphs, slots = (spatial_ids.shape[0], spatial_ids.shape[1])
    pairs = slots * slots
    all_heads = spatial_table.shape[1]
    heads = all_heads // lax.axis_size("mp")
    head_width = w_q.shape[1]
    ff_width = w_in.shape[1]
    depth = head_width // heads
    split_shape = (graphs, slots, heads, depth)
    row_count = graphs * slots
    head_start = lax.axis_index("mp") * heads
    gathered = (
        lax.all_gather(w_q, "dp", axis=0, tiled=True),
        lax.all_gather(w_k, "dp", axis=0, tiled=True),
        lax.all_gather(w_v, "dp", axis=0, tiled=True),
        lax.all_gather(w_o, "dp", axis=0, tiled=True),
        lax.all_gather(w_in, "dp", axis=0, tiled=True),
        lax.all_gather(w_out, "dp", axis=0, tiled=True),
        lax.all_gather(edge_table, "dp", axis=0, tiled=True),
    )
    full_q, full_k, full_v, full_o, full_in, full_out, full_edge = gathered
    first_normed, first_scale = normalize(layer_in)
    h1 = lax.all_gather(
        (first_normed * ln1_gain + ln1_bias).astype(jnp.bfloat16), "mp", axis=0, tiled=True
    )
    query = (jnp.dot(h1, full_q, preferred_element_type=jnp.float32) + q_bias).astype(jnp.bfloat16)
    keys = jnp.dot(h1, full_k, preferred_element_type=jnp.float32).astype(jnp.bfloat16)
    values = (jnp.dot(h1, full_v, preferred_element_type=jnp.float32) + v_bias).astype(jnp.bfloat16)
    query_split = query.reshape(split_shape)
    keys_split = keys.reshape(split_shape)
    values_split = values.reshape(split_shape)
    local_spatial = lax.dynamic_slice_in_dim(spatial_table, head_start, heads, 1)
    local_edge = lax.dynamic_slice_in_dim(full_edge, head_start, heads, 1)

    def head_bias(item):
        return pair_bias(item[0], item[1], local_spatial, local_edge, 0, pairs)

    biases = lax.map(head_bias, (spatial_ids, path_ids))

    def forward_graph(item):
        query_g, keys_g, values_g, bias, count = item
        return attend_graph(query_g, keys_g, values_g, bias, count)

    attended, log_total = lax.map(
        forward_graph, (query_split, keys_split, values_split, biases, node_counts)
    )
    attended = attended.reshape(row_count, head_width)
    branch = lax.psum_scatter(
        contract_last(attended, full_o), "mp", scatter_dimension=0, tiled=True
    )
    mid = layer_in + branch + o_bias
    second_normed, second_scale = normalize(mid)
    h2 = lax.all_gather(
        (second_normed * ln2_gain + ln2_bias).astype(jnp.bfloat16), "mp", axis=0, tiled=True
    )
    pre = jnp.dot(h2, full_in, preferred_element_type=jnp.float32) + in_bias
    hidden = jax.nn.gelu(pre, approximate=False).astype(jnp.bfloat16)
    feed = lax.psum_scatter(
        contract_last(hidden, full_out).astype(jnp.bfloat16), "mp", scatter_dimension=0, tiled=True
    ).astype(jnp.float32)
    layer_out = mid + feed + out_bias
    grad_ffn = lax.all_gather(cotangent.astype(jnp.bfloat16), "mp", axis=0, tiled=True)
    grad_w_out = contract_first(grad_ffn, hidden)
    grad_hidden = jnp.dot(grad_ffn, full_out, preferred_element_type=jnp.float32)
    unused, gelu_back = jax.vjp(lambda inner: jax.nn.gelu(inner, approximate=False), pre)
    grad_pre = gelu_back(grad_hidden)[0].astype(jnp.bfloat16)
    grad_w_in = contract_first(h2, grad_pre)
    grad_h2 = lax.psum_scatter(
        contract_last(grad_pre, full_in), "mp", scatter_dimension=0, tiled=True
    )
    grad_mid = cotangent + normalize_back(grad_h2 * ln2_gain, second_normed, second_scale)
    grad_branch = lax.all_gather(grad_mid.astype(jnp.bfloat16), "mp", axis=0, tiled=True)
    grad_w_o = contract_first(grad_branch, attended)
    grad_attended = jnp.dot(grad_branch, full_o, preferred_element_type=jnp.float32).astype(
        jnp.bfloat16
    )

    def backward_graph(item):
        query_g, keys_g, values_g, bias, count, log_g, grad_g = item
        return attend_graph_back(query_g, keys_g, values_g, bias, count, log_g, grad_g)

    grad_query, grad_keys, grad_values, grad_scores = lax.map(
        backward_graph,
        (
            query_split,
            keys_split,
            values_split,
            biases,
            node_counts,
            log_total,
            grad_attended.reshape(split_shape),
        ),
    )
    score_rows = grad_scores.reshape(graphs, heads, pairs)

    def table_step(carry, item):
        spatial_g, path_g, piece = item
        return (table_grads(spatial_g, path_g, piece, table_start, carry[0], carry[1]), 0)

    table_start = 0
    start_grads = (
        jnp.zeros((spatial_table.shape[0], heads), jnp.float32),
        jnp.zeros((full_edge.shape[0], heads), jnp.float32),
    )
    table_sums, unused_steps = lax.scan(
        table_step, start_grads, (spatial_ids, path_ids, score_rows)
    )
    spatial_full = lax.dynamic_update_slice_in_dim(
        jnp.zeros((spatial_table.shape[0], all_heads), jnp.float32), table_sums[0], head_start, 1
    )
    grad_edge = table_sums[1]
    grad_edge = grad_edge / path_ids.shape[1]
    grad_query = grad_query.reshape(row_count, head_width)
    grad_keys = grad_keys.reshape(row_count, head_width)
    grad_values = grad_values.reshape(row_count, head_width)
    grad_w_q = contract_first(h1, grad_query)
    grad_w_k = contract_first(h1, grad_keys)
    grad_w_v = contract_first(h1, grad_values)
    input_terms = contract_last(grad_query, full_q) + contract_last(grad_keys, full_k)
    input_terms = input_terms + contract_last(grad_values, full_v)
    grad_h1 = lax.psum_scatter(input_terms, "mp", scatter_dimension=0, tiled=True)
    grad_layer_in = grad_mid + normalize_back(grad_h1 * ln1_gain, first_normed, first_scale)
    summed = (
        lax.psum_scatter(grad_w_q, "dp", scatter_dimension=0, tiled=True),
        lax.psum_scatter(grad_w_k, "dp", scatter_dimension=0, tiled=True),
        lax.psum_scatter(grad_w_v, "dp", scatter_dimension=0, tiled=True),
        lax.psum_scatter(grad_w_o, "dp", scatter_dimension=0, tiled=True),
        lax.psum_scatter(grad_w_in, "dp", scatter_dimension=0, tiled=True),
        lax.psum_scatter(grad_w_out, "dp", scatter_dimension=0, tiled=True),
        lax.psum_scatter(grad_edge, "dp", scatter_dimension=0, tiled=True),
    )
    model_width = layer_in.shape[1]
    feature_start = lax.axis_index("mp") * head_width
    hidden_start = lax.axis_index("mp") * ff_width
    query_full = lax.dynamic_update_slice_in_dim(
        jnp.zeros((model_width,), jnp.float32),
        jnp.sum(grad_query.astype(jnp.float32), axis=0),
        feature_start,
        0,
    )
    value_full = lax.dynamic_update_slice_in_dim(
        jnp.zeros((model_width,), jnp.float32),
        jnp.sum(grad_values.astype(jnp.float32), axis=0),
        feature_start,
        0,
    )
    hidden_full = lax.dynamic_update_slice_in_dim(
        jnp.zeros((ff_width * lax.axis_size("mp"),), jnp.float32),
        jnp.sum(grad_pre.astype(jnp.float32), axis=0),
        hidden_start,
        0,
    )
    norm_totals = lax.psum(
        (
            jnp.sum(grad_h1 * first_normed, axis=0),
            jnp.sum(grad_h1, axis=0),
            jnp.sum(grad_h2 * second_normed, axis=0),
            jnp.sum(grad_h2, axis=0),
            jnp.sum(grad_mid, axis=0),
            jnp.sum(cotangent, axis=0),
            query_full,
            value_full,
            hidden_full,
            spatial_full,
        ),
        ("dp", "mp"),
    )
    grad_q_bias = lax.dynamic_slice_in_dim(norm_totals[6], feature_start, head_width, 0)
    grad_v_bias = lax.dynamic_slice_in_dim(norm_totals[7], feature_start, head_width, 0)
    grad_in_bias = lax.dynamic_slice_in_dim(norm_totals[8], hidden_start, ff_width, 0)
    grad_spatial = lax.dynamic_slice_in_dim(norm_totals[9], head_start, heads, 1)
    return (
        layer_out,
        grad_layer_in,
        norm_totals[0],
        norm_totals[1],
        summed[0],
        summed[1],
        summed[2],
        grad_q_bias,
        grad_v_bias,
        grad_spatial,
        summed[6],
        summed[3],
        norm_totals[4],
        norm_totals[2],
        norm_totals[3],
        summed[4],
        grad_in_bias,
        summed[5],
        norm_totals[5],
    )


def solution(mesh):
    return jax.shard_map(
        local,
        mesh=mesh,
        in_specs=(
            P(("dp", "mp"), None),
            P("dp"),
            P("dp", None, None),
            P("dp", None, None, None),
            P(),
            P(),
            P("dp", "mp"),
            P("dp", "mp"),
            P("dp", "mp"),
            P("mp"),
            P("mp"),
            P(),
            P("dp", None),
            P("dp", "mp"),
            P(),
            P(),
            P(),
            P("dp", "mp"),
            P("mp"),
            P("dp", "mp"),
            P(),
            P(("dp", "mp"), None),
        ),
        out_specs=(
            P(("dp", "mp"), None),
            P(("dp", "mp"), None),
            P(),
            P(),
            P("dp", "mp"),
            P("dp", "mp"),
            P("dp", "mp"),
            P("mp"),
            P("mp"),
            P(None, "mp"),
            P("dp", "mp"),
            P("dp", "mp"),
            P(),
            P(),
            P(),
            P("dp", "mp"),
            P("mp"),
            P("dp", "mp"),
            P(),
        ),
        check_vma=False,
    )
```

profile of v0, /device:TPU:0, one launch (start us, length us, event | category | flops | bytes accessed | tf_op | source)
XLA Modules:
  0.0 1440.9 jit_solution(12586913065994715846)
XLA Ops:
  7.3 32.5 %all-gather = bf16[8,192,32]{1,2,0:T(8,128)(2,1)S(1)} all-gather(bf16[1,192,32]{1,2,0:T(8,128)(2,1)} %bitcast.346), channel_id=1, replica_groups=mesh['dp'=8,'mp'=4] {'dp'}, dimensions={0}, use_global_device_ids=true | all-gather | bytes 110592 | tf_op jit(solution)/shard_map/all_gather | solution.py:185
  40.2 307.6 %while.76 = (s32[]{:T(128)}, f32[4,8,16384]{2,1,0:T(8,128)}, s32[4,128,128]{2,1,0:T(8,128)}, bf16[22,8]{0,1:T(8,128)(2,1)S(1)}, s32[4,5,128,128]{3,2,1,0:T(8,128...) while((s32[]{:T(128)}, f32[4,8,16384]{2,1,0:T(8,128)}, ...), condition=%wide.region_5.6_spmd, body=%wide.region_2.5_spmd.sunk | while | flops 119668880 | bytes 3820008 | solution.py:204
  41.5 73.4 %while.81 = (s32[]{:T(128)}, f32[8,8,2048]{2,1,0:T(8,128)S(1)}, s32[8]{0:T(128)S(1)}, s32[5,16384]{1,0:T(8,128)S(1)}, bf16[1536,8]{0,1:T(8,128)(2,1)S(1)}, /*ind...) while((s32[]{:T(128)}, f32[8,8,2048]{2,1,0:T(8,128)S(1)}, s32[8]{0:T(128)S(1)}, ...), condition=%wide.region_4.4_spmd, body=%wide.region_3.3_spmd.sunk | while | flops 113246216 | bytes 213227 | solution.py:70
  118.4 73.4 %while.81 = (s32[]{:T(128)}, f32[8,8,2048]{2,1,0:T(8,128)S(1)}, s32[8]{0:T(128)S(1)}, s32[5,16384]{1,0:T(8,128)S(1)}, bf16[1536,8]{0,1:T(8,128)(2,1)S(1)}, /*ind...) while((s32[]{:T(128)}, f32[8,8,2048]{2,1,0:T(8,128)S(1)}, s32[8]{0:T(128)S(1)}, ...), condition=%wide.region_4.4_spmd, body=%wide.region_3.3_spmd.sunk | while | flops 113246216 | bytes 213227 | solution.py:70
  195.3 73.4 %while.81 = (s32[]{:T(128)}, f32[8,8,2048]{2,1,0:T(8,128)S(1)}, s32[8]{0:T(128)S(1)}, s32[5,16384]{1,0:T(8,128)S(1)}, bf16[1536,8]{0,1:T(8,128)(2,1)S(1)}, /*ind...) while((s32[]{:T(128)}, f32[8,8,2048]{2,1,0:T(8,128)S(1)}, s32[8]{0:T(128)S(1)}, ...), condition=%wide.region_4.4_spmd, body=%wide.region_3.3_spmd.sunk | while | flops 113246216 | bytes 213227 | solution.py:70
  272.2 73.4 %while.81 = (s32[]{:T(128)}, f32[8,8,2048]{2,1,0:T(8,128)S(1)}, s32[8]{0:T(128)S(1)}, s32[5,16384]{1,0:T(8,128)S(1)}, bf16[1536,8]{0,1:T(8,128)(2,1)S(1)}, /*ind...) while((s32[]{:T(128)}, f32[8,8,2048]{2,1,0:T(8,128)S(1)}, s32[8]{0:T(128)S(1)}, ...), condition=%wide.region_4.4_spmd, body=%wide.region_3.3_spmd.sunk | while | flops 113246216 | bytes 213227 | solution.py:70
  348.7 8.7 all_gather.33
  357.4 31.2 %all_gather.34 = bf16[768,192]{1,0:T(8,128)(2,1)S(1)} all-gather(bf16[96,192]{1,0:T(8,128)(2,1)S(1)} %copy-done.34), channel_id=1, replica_groups=mesh['dp'=8,'mp'=4] {'dp'}, dimensions={0}, use_global_device_ids=true | all-gather | bytes 331776 | tf_op jit(solution)/shard_map/all_gather | solution.py:181
  389.9 31.0 %all_gather.35 = bf16[768,192]{1,0:T(8,128)(2,1)S(1)} all-gather(bf16[96,192]{1,0:T(8,128)(2,1)S(1)} %copy-done.35), channel_id=1, replica_groups=mesh['dp'=8,'mp'=4] {'dp'}, dimensions={0}, use_global_device_ids=true | all-gather | bytes 331776 | tf_op jit(solution)/shard_map/all_gather | solution.py:179
  421.4 31.1 %all_gather.36 = bf16[768,192]{1,0:T(8,128)(2,1)S(1)} all-gather(bf16[96,192]{1,0:T(8,128)(2,1)S(1)} %copy-done.36), channel_id=1, replica_groups=mesh['dp'=8,'mp'=4] {'dp'}, dimensions={0}, use_global_device_ids=true | all-gather | bytes 331776 | tf_op jit(solution)/shard_map/all_gather | solution.py:180
  453.1 15.5 %while.77 = (s32[]{:T(128)}, bf16[4,128,8,24]{1,3,2,0:T(8,128)(2,1)S(1)}, f32[4,8,128,1]{2,1,3,0:T(8,128)}, bf16[4,128,8,24]{1,3,2,0:T(8,128)(2,1)S(1)}, s32[4]{...) while((s32[]{:T(128)}, ...), condition=%wide.region_9.10_spmd, body=%wide.region_6.9_spmd.sunk | while | flops 13786242 | bytes 5475569 | solution.py:210
  468.8 31.5 %all_gather.38 = bf16[768,192]{1,0:T(8,128)(2,1)S(1)} all-gather(bf16[96,192]{1,0:T(8,128)(2,1)S(1)} %copy-done.37), channel_id=1, replica_groups=mesh['dp'=8,'mp'=4] {'dp'}, dimensions={0}, use_global_device_ids=true | all-gather | bytes 331776 | tf_op jit(solution)/shard_map/all_gather | solution.py:182
  502.0 31.3 %all_gather.40 = bf16[768,192]{1,0:T(8,128)(2,1)S(1)} all-gather(bf16[96,192]{1,0:T(8,128)(2,1)S(1)} %copy-done.38), channel_id=1, replica_groups=mesh['dp'=8,'mp'=4] {'dp'}, dimensions={0}, use_global_device_ids=true | all-gather | bytes 331776 | tf_op jit(solution)/shard_map/all_gather | solution.py:183
  533.2 31.2 %all_gather.41 = bf16[768,192]{1,0:T(8,128)(2,1)S(1)} all-gather(bf16[96,192]{1,0:T(8,128)(2,1)} %param.53), channel_id=1, replica_groups=mesh['dp'=8,'mp'=4] {'dp'}, dimensions={0}, use_global_device_ids=true | all-gather | bytes 331776 | tf_op jit(solution)/shard_map/all_gather | solution.py:184
  575.1 8.9 all_gather.39
  592.7 26.6 %reduce-scatter.20.cloned.1.call-done = f32[128,768]{1,0:T(8,128)} async-done(((f32[512,768]{1,0:T(8,128)}), f32[128,768]{1,0:T(8,128)}) %reduce-scatter.20.cloned.1.call-update) | async-done | bytes 393232 | tf_op jit(solution)/shard_map/reduce_scatter | solution.py:234
  621.1 24.0 %reduce-scatter.18.cloned.1.call-done = bf16[128,768]{1,0:T(8,128)(2,1)} async-done(((bf16[512,768]{1,0:T(8,128)(2,1)}), bf16[128,768]{1,0:T(8,128)(2,1)}) %reduce-scatter.18.cloned.1.call-update) | async-done | bytes 196624 | tf_op jit(solution)/shard_map/reduce_scatter | solution.py:224
  657.7 26.1 %while.78 = (s32[]{:T(128)}, bf16[4,128,8,24]{1,3,2,0:T(8,128)(2,1)S(1)}, bf16[4,128,8,24]{1,3,2,0:T(8,128)(2,1)S(1)}, bf16[4,128,8,24]{1,3,2,0:T(8,128)(2,1)S(1...) while((s32[]{:T(128)}, ...), condition=%wide.region_19.20_spmd, body=%wide.region_17.19_spmd.sunk | while | flops 32889984 | bytes 9169173 | solution.py:248
  688.2 258.5 %while.80 = (s32[]{:T(128)}, f32[22,8]{0,1:T(8,128)S(1)}, f32[1536,8]{0,1:T(8,128)S(1)}, s32[4,128,128]{2,1,0:T(8,128)}, bf16[4,8,16384]{2,1,0:T(8,128)(2,1)}, /...) while((s32[]{:T(128)}, f32[22,8]{0,1:T(8,128)S(1)}, ...), condition=%wide.region_37.38_spmd.clone, body=%wide.region_34.37_spmd.clone.sunk | while | flops 119419368 | bytes 2550782 | solution.py:271
  691.8 61.1 %while.82 = (s32[]{:T(128)}, f32[1536,8]{0,1:T(8,128)S(1)}, s32[5,16384]{1,0:T(8,128)S(1)}, bf16[8,16384]{1,0:T(8,128)(2,1)S(1)}, s32[]{:T(128)}, /*index=5*/s32...) while((s32[]{:T(128)}, f32[1536,8]{0,1:T(8,128)S(1)}, s32[5,16384]{1,0:T(8,128)S(1)}, ...), condition=%wide.region_36.36_spmd, body=%wide.region_35.35_spmd.sunk | while | flops 113258504 | bytes 254187 | solution.py:140
  756.4 61.1 %while.82 = (s32[]{:T(128)}, f32[1536,8]{0,1:T(8,128)S(1)}, s32[5,16384]{1,0:T(8,128)S(1)}, bf16[8,16384]{1,0:T(8,128)(2,1)S(1)}, s32[]{:T(128)}, /*index=5*/s32...) while((s32[]{:T(128)}, f32[1536,8]{0,1:T(8,128)S(1)}, s32[5,16384]{1,0:T(8,128)S(1)}, ...), condition=%wide.region_36.36_spmd, body=%wide.region_35.35_spmd.sunk | while | flops 113258504 | bytes 254187 | solution.py:140
  821.0 61.1 %while.82 = (s32[]{:T(128)}, f32[1536,8]{0,1:T(8,128)S(1)}, s32[5,16384]{1,0:T(8,128)S(1)}, bf16[8,16384]{1,0:T(8,128)(2,1)S(1)}, s32[]{:T(128)}, /*index=5*/s32...) while((s32[]{:T(128)}, f32[1536,8]{0,1:T(8,128)S(1)}, s32[5,16384]{1,0:T(8,128)S(1)}, ...), condition=%wide.region_36.36_spmd, body=%wide.region_35.35_spmd.sunk | while | flops 113258504 | bytes 254187 | solution.py:140
  885.6 61.1 %while.82 = (s32[]{:T(128)}, f32[1536,8]{0,1:T(8,128)S(1)}, s32[5,16384]{1,0:T(8,128)S(1)}, bf16[8,16384]{1,0:T(8,128)(2,1)S(1)}, s32[]{:T(128)}, /*index=5*/s32...) while((s32[]{:T(128)}, f32[1536,8]{0,1:T(8,128)S(1)}, s32[5,16384]{1,0:T(8,128)S(1)}, ...), condition=%wide.region_36.36_spmd, body=%wide.region_35.35_spmd.sunk | while | flops 113258504 | bytes 254187 | solution.py:140
  962.5 48.5 %reduce-scatter.34.cloned.1.call-done = f32[192,8]{1,0:T(8,128)} async-done(((f32[1536,8]{1,0:T(8,128)}), f32[192,8]{1,0:T(8,128)}) %reduce-scatter.34.cloned.1.call-update) | async-done | bytes 6160
  1012.5 28.0 %reduce-scatter.22.cloned.1.call-done = f32[128,768]{1,0:T(8,128)} async-done(((f32[512,768]{1,0:T(8,128)}), f32[128,768]{1,0:T(8,128)}) %reduce-scatter.22.cloned.1.call-update) | async-done | bytes 393232 | tf_op jit(solution)/shard_map/reduce_scatter | solution.py:287
  1041.8 40.8 %all-reduce = (f32[768]{0:T(1024)}, f32[768]{0:T(1024)}, f32[768]{0:T(1024)S(1)}, f32[768]{0:T(1024)S(1)}, f32[22,32]{0,1:T(8,128)S(1)}, /*index=5*/f32[768]{0:T...) all-reduce(f32[768]{0:T(1024)S(1)} %get-tuple-element.487, ...), channel_id=1, replica_groups=mesh['dp'=8,'mp'=4] {'dp','mp'}, use_global_device_ids=true, to_apply=%region_24.25 | all-reduce | flops 7616 | bytes 60928 | tf_op jit(solution)/shard_map/psum | solution.py:319
  1087.0 20.0 %reduce-scatter.32.cloned.1.call-done = f32[96,192]{1,0:T(8,128)} async-done(((f32[768,192]{1,0:T(8,128)}), f32[96,192]{1,0:T(8,128)}) %reduce-scatter.32.cloned.1.call-update) | async-done | bytes 73744 | tf_op jit(solution)/shard_map/reduce_scatter | solution.py:294
  1107.1 65.4 %reduce-scatter.36.cloned.1.call-done = f32[96,192]{1,0:T(8,128)} async-done(((f32[768,192]{1,0:T(8,128)}), f32[96,192]{1,0:T(8,128)}) %reduce-scatter.36.cloned.1.call-update) | async-done | bytes 73744
  1172.4 65.7 %reduce-scatter.30.cloned.1.call-done = f32[96,192]{1,0:T(8,128)} async-done(((f32[768,192]{1,0:T(8,128)}), f32[96,192]{1,0:T(8,128)}) %reduce-scatter.30.cloned.1.call-update) | async-done | bytes 73744 | tf_op jit(solution)/shard_map/reduce_scatter | solution.py:293
  1238.1 65.3 %reduce-scatter.24.cloned.1.call-done = f32[96,192]{1,0:T(8,128)} async-done(((f32[768,192]{1,0:T(8,128)}), f32[96,192]{1,0:T(8,128)}) %reduce-scatter.24.cloned.1.call-update) | async-done | bytes 73744 | tf_op jit(solution)/shard_map/reduce_scatter | solution.py:290
  1303.4 65.5 %reduce-scatter.26.cloned.1.call-done = f32[96,192]{1,0:T(8,128)} async-done(((f32[768,192]{1,0:T(8,128)}), f32[96,192]{1,0:T(8,128)}) %reduce-scatter.26.cloned.1.call-update) | async-done | bytes 73744 | tf_op jit(solution)/shard_map/reduce_scatter | solution.py:291
  1368.9 65.4 %reduce-scatter.28.cloned.1.call-done = f32[96,192]{1,0:T(8,128)} async-done(((f32[768,192]{1,0:T(8,128)}), f32[96,192]{1,0:T(8,128)}) %reduce-scatter.28.cloned.1.call-update) | async-done | bytes 73744 | tf_op jit(solution)/shard_map/reduce_scatter | solution.py:292
  (539 shorter events, 610.1 us)
Async XLA Ops:
  7.2 565.6 %reduce-scatter.16.cloned.1.call-start = ((), (), s32[]{:S(2)}) async-start(), calls=%async_computation.11 | async-start | bytes 1966080 | tf_op jit(solution)/shard_map/reduce_scatter | solution.py:214
  40.2 307.6 %copy-start.3 = (f32[128,768]{1,0:T(8,128)S(1)}, f32[128,768]{1,0:T(8,128)}, u32[]{:S(2)}) copy-start(f32[128,768]{1,0:T(8,128)} %param.34) | copy-start | bytes 1179652
  40.2 307.9 %copy-start.40 = (f32[768]{0:T(1024)S(1)}, f32[768]{0:T(1024)}, u32[]{:S(2)}) copy-start(f32[768]{0:T(1024)} %param.38) | copy-start | bytes 9220
  40.2 307.9 %copy-start.52 = (f32[768]{0:T(1024)S(1)}, f32[768]{0:T(1024)}, u32[]{:S(2)}) copy-start(f32[768]{0:T(1024)} %param.39) | copy-start | bytes 9220
  348.7 72.2 %copy-start.57 = (f32[192]{0:T(256)S(1)}, f32[192]{0:T(256)}, u32[]{:S(2)}) copy-start(f32[192]{0:T(256)} %param.43) | copy-start | bytes 2308
  357.4 95.1 %copy-start.1 = (bf16[512,768]{1,0:T(8,128)(2,1)}, bf16[512,768]{1,0:T(8,128)(2,1)S(1)}, u32[]{:S(2)}) copy-start(bf16[512,768]{1,0:T(8,128)(2,1)S(1)} %all_gather.33) | copy-start | bytes 2359300
  468.8 64.4 %copy-start.16 = (bf16[4,128,8,24]{1,0,3,2:T(4,128)(2,1)}, bf16[4,128,8,24]{1,0,3,2:T(4,128)(2,1)S(1)}, u32[]{:S(2)}) copy-start(bf16[4,128,8,24]{1,0,3,2:T(4,128)(2,1)S(1)} %copy.108) | copy-start | bytes 589828
  500.3 64.1 %copy-start.29 = (f32[128,768]{1,0:T(8,128)S(1)}, f32[128,768]{1,0:T(8,128)}, u32[]{:S(2)}) copy-start(f32[128,768]{1,0:T(8,128)} %param.55) | copy-start | bytes 1179652
  501.9 71.0 %copy-start.53 = (f32[768]{0:T(1024)S(1)}, f32[768]{0:T(1024)}, u32[]{:S(2)}) copy-start(f32[768]{0:T(1024)} %param.48) | copy-start | bytes 9220
  501.9 72.4 %copy-start.39 = (f32[768]{0:T(1024)S(1)}, f32[768]{0:T(1024)}, u32[]{:S(2)}) copy-start(f32[768]{0:T(1024)} %param.49) | copy-start | bytes 9220
  501.9 117.4 %reduce-scatter.20.cloned.1.call-start = ((), (), s32[]{:S(2)}) async-start(), calls=%async_computation.13 | async-start | bytes 1966080 | tf_op jit(solution)/shard_map/reduce_scatter | solution.py:234
  590.0 55.1 %copy-start.54 = (f32[768]{0:T(1024)S(1)}, f32[768]{0:T(1024)}, u32[]{:S(2)}) copy-start(f32[768]{0:T(1024)} %param.54) | copy-start | bytes 9220
  590.0 55.1 %reduce-scatter.18.cloned.1.call-start = ((), (), s32[]{:S(2)}) async-start(), calls=%async_computation.12 | async-start | bytes 983040 | tf_op jit(solution)/shard_map/reduce_scatter | solution.py:224
  592.6 418.3 %reduce-scatter.34.cloned.1.call-start = ((), (), s32[]{:S(2)}) async-start(), calls=%async_computation.20 | async-start | bytes 884736
  688.2 260.0 %copy-start.13 = (bf16[768,192]{1,0:T(8,128)(2,1)S(1)}, bf16[768,192]{1,0:T(8,128)(2,1)}, u32[]{:S(2)}) copy-start(bf16[768,192]{1,0:T(8,128)(2,1)} %copy-done.12) | copy-start | bytes 884740
  688.2 260.0 %copy-start.28 = (bf16[4,128,8,24]{1,0,3,2:T(4,128)(2,1)S(1)}, bf16[4,128,8,24]{1,0,3,2:T(4,128)(2,1)}, u32[]{:S(2)}) copy-start(bf16[4,128,8,24]{1,0,3,2:T(4,128)(2,1)} %copy.115) | copy-start | bytes 589828
  947.9 92.6 %reduce-scatter.22.cloned.1.call-start = ((), (), s32[]{:S(2)}) async-start(), calls=%async_computation.14 | async-start | bytes 1966080 | tf_op jit(solution)/shard_map/reduce_scatter | solution.py:287
  951.6 155.5 %reduce-scatter.32.cloned.1.call-start = ((), (), s32[]{:S(2)}) async-start(), calls=%async_computation.19 | async-start | bytes 884736 | tf_op jit(solution)/shard_map/reduce_scatter | solution.py:294
  954.0 218.4 %reduce-scatter.36.cloned.1.call-start = ((), (), s32[]{:S(2)}) async-start(), calls=%async_computation.21 | async-start | bytes 884736
  955.6 282.5 %reduce-scatter.30.cloned.1.call-start = ((), (), s32[]{:S(2)}) async-start(), calls=%async_computation.18 | async-start | bytes 884736 | tf_op jit(solution)/shard_map/reduce_scatter | solution.py:293
  957.1 346.3 %reduce-scatter.24.cloned.1.call-start = ((), (), s32[]{:S(2)}) async-start(), calls=%async_computation.15 | async-start | bytes 884736 | tf_op jit(solution)/shard_map/reduce_scatter | solution.py:290
  958.5 410.5 %reduce-scatter.26.cloned.1.call-start = ((), (), s32[]{:S(2)}) async-start(), calls=%async_computation.16 | async-start | bytes 884736 | tf_op jit(solution)/shard_map/reduce_scatter | solution.py:291
  959.8 80.7 %copy-start.4 = (f32[128,768]{1,0:T(8,128)S(1)}, f32[128,768]{1,0:T(8,128)}, u32[]{:S(2)}) copy-start(f32[128,768]{1,0:T(8,128)} %param.34) | copy-start | bytes 1179652
  959.8 80.7 %copy-start.41 = (f32[768]{0:T(1024)S(1)}, f32[768]{0:T(1024)}, u32[]{:S(2)}) copy-start(f32[768]{0:T(1024)} %param.38) | copy-start | bytes 9220
  959.8 80.7 %copy-start.47 = (f32[128]{0:T(128)S(1)}, f32[128]{0:T(128)}, u32[]{:S(2)}) copy-start(f32[128]{0:T(128)} %copy-done.46) | copy-start | bytes 1540
  959.8 80.7 %copy-start.49 = (f32[128]{0:T(128)S(1)}, f32[128]{0:T(128)}, u32[]{:S(2)}) copy-start(f32[128]{0:T(128)} %copy-done.48) | copy-start | bytes 1540
  959.9 81.9 %copy-start.42 = (f32[768]{0:T(1024)S(1)}, f32[768]{0:T(1024)}, u32[]{:S(2)}) copy-start(f32[768]{0:T(1024)} %get-tuple-element.606) | copy-start | bytes 9220
  959.9 81.9 %copy-start.43 = (f32[768]{0:T(1024)S(1)}, f32[768]{0:T(1024)}, u32[]{:S(2)}) copy-start(f32[768]{0:T(1024)} %get-tuple-element.485) | copy-start | bytes 9220
  959.9 81.9 %copy-start.44 = (f32[768]{0:T(1024)S(1)}, f32[768]{0:T(1024)}, u32[]{:S(2)}) copy-start(f32[768]{0:T(1024)} %get-tuple-element.491) | copy-start | bytes 9220
  959.9 81.9 %copy-start.45 = (f32[768]{0:T(1024)S(1)}, f32[768]{0:T(1024)}, u32[]{:S(2)}) copy-start(f32[768]{0:T(1024)} %get-tuple-element.588) | copy-start | bytes 9220
  959.9 125.2 %copy-start.11 = (f32[128,768]{1,0:T(8,128)S(1)}, f32[128,768]{1,0:T(8,128)}, u32[]{:S(2)}) copy-start(f32[128,768]{1,0:T(8,128)} %copy-done.10) | copy-start | bytes 1179652
  959.9 474.4 %reduce-scatter.28.cloned.1.call-start = ((), (), s32[]{:S(2)}) async-start(), calls=%async_computation.17 | async-start | bytes 884736 | tf_op jit(solution)/shard_map/reduce_scatter | solution.py:292
  (40 other events, 441.8 us)
Sparse Core Ops, SparseCore 0:
  502.0 27.9 reduce-scatter.15
  590.2 29.0 reduce-scatter.19
  621.8 23.2 reduce-scatter.17
  948.0 62.8 reduce-scatter.33
  1013.3 27.1 reduce-scatter.21
  1044.6 62.3 reduce-scatter.31
  1110.9 61.4 reduce-scatter.35
  1176.6 61.4 reduce-scatter.29
  1242.0 61.3 reduce-scatter.23
  1307.5 61.4 reduce-scatter.25
  1372.8 61.4 reduce-scatter.27
where the time goes:
time: 1440 us
  matrix products  487 us (34%)
  waiting for transfers between devices  475 us (33%)
  blocking collectives  294 us (20%)
  local copies, waits for them, and re-layouts  77.8 us (5%)
  loops' own time  63.7 us (4%)
  other arithmetic  28.2 us (2%)
  between operations  14.7 us (1%)
    dot_general x42, matrix products, contract_last(): lax.dot_general(left, right, (((1,), (1,)), ((), ())), preferred_element_...  252 us
    dot_general x42, matrix products, contract_first(): lax.dot_general(left, right, (((0,), (0,)), ((), ())), preferred_element_...  219 us
    unnamed x13, waiting for transfers between devices  114 us
    reduce_scatter x1, waiting for transfers between devices, local(): lax.psum_scatter(grad_w_o, 'dp', scatter_dimension=0, tiled=True)  65.7 us
    reduce_scatter x1, waiting for transfers between devices, local(): lax.psum_scatter(grad_w_k, 'dp', scatter_dimension=0, tiled=True)  65.5 us
    reduce_scatter x1, waiting for transfers between devices, local(): lax.psum_scatter(grad_w_v, 'dp', scatter_dimension=0, tiled=True)  65.4 us
    reduce_scatter x1, waiting for transfers between devices, local(): lax.psum_scatter(grad_w_q, 'dp', scatter_dimension=0, tiled=True)  65.3 us
    another operation x4, loops' own time, pair_bias(): lax.map(block_terms, jnp.arange(count // width, dtype=jnp.int32) * width)  62.5 us
  transfers between devices with their start and end apart: 11, of which 10 were waited for; matrix products, arithmetic and copies ran while one was open for 2% of the time, Pallas kernels for 0%

commit v1 on v0

v1 whole, which is shorter than its diff:
```python
import functools

import jax
import jax.numpy as jnp
from jax import lax
from jax.experimental import pallas as pl
from jax.experimental.pallas import tpu as pltpu
from jax.sharding import PartitionSpec as P

epsilon = 1e-05
masked_score = -1e30
edge_unit = 1638.0
spatial_unit = 4096.0
bf16 = jnp.bfloat16
f32 = jnp.float32
i32 = jnp.int32
vmem = pl.BlockSpec(memory_space=pltpu.VMEM)
smem = pl.BlockSpec(memory_space=pltpu.SMEM)
params = pltpu.CompilerParams(vmem_limit_bytes=48 << 20)


def normalize(values):
    centred = values - jnp.mean(values, axis=-1, keepdims=True)
    scale = lax.rsqrt(jnp.mean(centred * centred, axis=-1, keepdims=True) + epsilon)
    return (centred * scale, scale)


def normalize_back(grad_normed, normed, scale):
    inner = grad_normed - jnp.mean(grad_normed, axis=-1, keepdims=True)
    inner = inner - normed * jnp.mean(grad_normed * normed, axis=-1, keepdims=True)
    return inner * scale


def dot_nn(left, right):
    return lax.dot_general(
        left, right, (((1,), (0,)), ((), ())), preferred_element_type=f32
    )


def dot_nt(left, right):
    return lax.dot_general(
        left, right, (((1,), (1,)), ((), ())), preferred_element_type=f32
    )


def column_sum(values):
    return jnp.sum(values, axis=0, keepdims=True)


def shape(dims, kind):
    return jax.ShapeDtypeStruct(dims, kind)


def relative(place, side, which, step):
    z, x, y = place[0], place[1], place[2]
    flip_x = (0, 1 - side, side, 1)[which]
    flip_y = (0, side, 1 - side, 1)[which]
    row = (z ^ step) * 2 + (x ^ flip_x)
    column = (y ^ flip_y) * 2 + side
    return row, column


def pack_kernel(wq, wk, wv, wo, wi, wu, edge, first, second, table):
    first[...] = jnp.concatenate([wq[...], wk[...], wv[...], wo[...]], 1)
    second[...] = jnp.concatenate([wi[...], wu[...]], 1)
    table[...] = edge[...].astype(f32).T.astype(bf16)


def pack(wq, wk, wv, wo, wi, wu, edge):
    rows, width = wq.shape
    return pl.pallas_call(
        pack_kernel,
        out_shape=(
            shape((rows, 4 * width), bf16),
            shape((rows, 2 * width), bf16),
            shape((edge.shape[1], edge.shape[0]), bf16),
        ),
        in_specs=[vmem] * 7,
        out_specs=[vmem] * 3,
        compiler_params=params,
        name="pack",
    )(wq, wk, wv, wo, wi, wu, edge)


def prepare_kernel(virtual, place, spatial, path, layer_in, gain, bias, ids, buckets, h1, h1_t):
    slots = spatial.shape[1]
    for hop in range(path.shape[1]):
        ids[hop] = path[0, hop].T
    rows = lax.broadcasted_iota(i32, (slots, slots), 0)
    columns = lax.broadcasted_iota(i32, (slots, slots), 1)
    buckets[...] = jnp.where((rows == 0) | (columns == 0), virtual, spatial[0].T)
    normed, scale = normalize(layer_in[...])
    out = normed * gain[...] + bias[...]
    h1[...] = out.astype(bf16)
    h1_t[...] = out.T.astype(bf16)


def prepare(place, spatial, path, layer_in, gain, bias, virtual):
    hops, slots = path.shape[1], path.shape[2]
    rows, width = layer_in.shape
    whole = lambda dims: pl.BlockSpec(dims, lambda i, s: (0,) * len(dims))
    return pl.pallas_call(
        functools.partial(prepare_kernel, virtual),
        grid_spec=pltpu.PrefetchScalarGridSpec(
            num_scalar_prefetch=1,
            grid=(1,),
            in_specs=[
                pl.BlockSpec((1, slots, slots), lambda i, s: (s[4], 0, 0)),
                pl.BlockSpec((1, hops, slots, slots), lambda i, s: (s[4], 0, 0, 0)),
                whole((rows, width)),
                whole((1, width)),
                whole((1, width)),
            ],
            out_specs=[
                whole((hops, slots, slots)),
                whole((slots, slots)),
                whole((rows, width)),
                whole((width, rows)),
            ],
        ),
        out_shape=(
            shape((hops, slots, slots), i32),
            shape((slots, slots), i32),
            shape((rows, width), bf16),
            shape((width, rows), bf16),
        ),
        compiler_params=params,
        name="prepare",
    )(place, spatial, path, layer_in, gain, bias)


def quantize(table, unit):
    held = jnp.round(table.astype(f32) * unit).astype(i32)
    partner = jnp.concatenate([held[4:], held[:4]], 0)
    return held + partner * 65536


def lanes_gather(table, places):
    return jnp.take_along_axis(table, places, axis=1, mode="promise_in_bounds")


def lookup_kernel(first, step, share, place, chunk, ids, *refs):
    if first:
        total, table = refs
        previous = None
    else:
        previous, total, table = refs
    hops, slots = ids.shape[0], ids.shape[1]
    pairs = total.shape[0]
    heads = 2 * pairs
    rows = chunk.shape[1]
    packed = jnp.concatenate(
        [quantize(chunk[i * heads : (i + 1) * heads, :], edge_unit) for i in range(share // rows)], 1
    )
    blocks = share // 128
    for pair in range(pairs):
        head = (pair // 4) * 8 + pair % 4
        for block in range(blocks):
            table[pair, block] = jnp.broadcast_to(
                packed[head : head + 1, block * 128 : (block + 1) * 128], (8, 128)
            )
    base = (place[0] ^ step) * share

    def body(i, carry):
        offset = pl.multiple_of(i * 8, 8)
        sums = [None] * pairs
        if not first:
            sums = [previous[pair, pl.ds(offset, 8), :] for pair in range(pairs)]
        for hop in range(hops):
            relative_id = ids[hop, pl.ds(offset, 8), :] - base
            low = relative_id & 127
            high = relative_id >> 7
            masks = [high == block for block in range(blocks)]
            for pair in range(pairs):
                value = jnp.zeros((8, 128), i32)
                for block in range(blocks):
                    value = jnp.where(masks[block], lanes_gather(table[pair, block], low), value)
                sums[pair] = value if sums[pair] is None else sums[pair] + value
        for pair in range(pairs):
            total[pair, pl.ds(offset, 8), :] = sums[pair]
        return carry

    lax.fori_loop(0, slots // 8, body, 0)


def lookup(place, chunk, ids, previous, step, share):
    heads = chunk.shape[0] // (share // chunk.shape[1])
    pairs = heads // 2
    slots = ids.shape[1]
    first = previous is None
    out = shape((pairs, slots, slots), i32)
    return pl.pallas_call(
        functools.partial(lookup_kernel, first, step, share),
        out_shape=out,
        in_specs=[smem] + [vmem] * (2 if first else 3),
        out_specs=vmem,
        scratch_shapes=[pltpu.VMEM((pairs, share // 128, 8, 128), i32)],
        input_output_aliases={} if first else {3: 0},
        compiler_params=params,
        name="lookup",
    )(place, chunk, ids, *(() if first else (previous,)))


def assemble(place, parts, whole):
    if len(parts) == 1:
        whole[...] = parts[0][...]
        return
    core = place[3]
    rows = parts[0].shape[1]
    for other in range(2):
        for which in range(4):
            for step in range(4):
                row, column = relative(place, core ^ other, which, step)
                start = pl.multiple_of(row * rows, rows)
                whole[column, pl.ds(start, rows), :] = parts[other * 4 + which][step]


def head_masks(width, offset, depth):
    lanes = lax.broadcasted_iota(i32, (1, width), 1)
    out = []
    for head in range(8):
        start = offset + head * depth
        out.append(((lanes >= start) & (lanes < start + depth)).astype(f32).astype(bf16))
    return out


def attend_kernel(
    n_parts, place, counts, h1, biases, edge_sums, buckets, spatial_table, layer_in, o_bias, gain, bias, *refs
):
    parts = refs[:n_parts]
    weights, transposed, value_win, probs_out, att_low, att_high, mid, h2 = refs[n_parts:]
    assemble(place, parts, weights)
    slots = h1.shape[0]
    width = biases.shape[2]
    depth = width // 8
    pad = 256 - width
    hops = 5
    count = counts[place[4]]
    packed = quantize(spatial_table[...].astype(f32).T, spatial_unit)
    packed = jnp.concatenate([packed, jnp.zeros((packed.shape[0], 128 - packed.shape[1]), i32)], 1)
    rows_of = lax.broadcasted_iota(i32, (slots, slots), 0)
    hidden_key = rows_of > count
    bucket = buckets[...]
    key_masks = head_masks(256, pad, depth)
    mid[...] = layer_in[...] + o_bias[...]
    groups = biases.shape[0]
    for group in range(groups):
        natural = dot_nn(h1[...], weights[group, :, : 3 * width + pad])
        row_bias = jnp.concatenate(
            [
                biases[group, 0:1, :],
                jnp.zeros((1, width), f32),
                biases[group, 1:2, :],
                jnp.zeros((1, pad), f32),
            ],
            1,
        )
        natural = natural + row_bias
        natural_t = natural.T
        transposed[group] = natural_t[: 3 * width].astype(bf16)
        natural = natural.astype(bf16)
        value_win[group] = natural[:, 2 * width : 2 * width + 256]
        keys = natural[:, width - pad : 2 * width]
        stack = jnp.concatenate([keys * mask for mask in key_masks], 0)
        query = jnp.concatenate([jnp.zeros((pad, slots), f32), natural_t[:width]], 0).astype(bf16)
        scores = dot_nn(stack, query) * depth ** (-0.5)
        out = []
        for pair in range(4):
            word = edge_sums[group * 4 + pair]
            head = group * 8 + pair
            spatial_word = lanes_gather(
                jnp.broadcast_to(packed[head : head + 1], (slots, 128)), bucket
            )
            low = (word << 16) >> 16
            spatial_low = (spatial_word << 16) >> 16
            high = (word - low) >> 16
            spatial_high = (spatial_word - spatial_low) >> 16
            for part, spatial_part, place_in in ((low, spatial_low, pair), (high, spatial_high, pair + 4)):
                pair_bias = part.astype(f32) * (1.0 / (edge_unit * hops))
                pair_bias = pair_bias + spatial_part.astype(f32) * (1.0 / spatial_unit)
                score = scores[place_in * slots : (place_in + 1) * slots] + pair_bias
                score = jnp.where(hidden_key, masked_score, score)
                weight = jnp.exp(score - jnp.max(score, axis=0, keepdims=True))
                probs = weight * (1.0 / column_sum(weight))
                probs_out[group * 8 + place_in] = probs
                values = natural_t[2 * width + place_in * depth : 2 * width + (place_in + 1) * depth]
                out.append((place_in, dot_nn(values.astype(bf16), probs.astype(bf16))))
        out = [item[1] for item in sorted(out, key=lambda item: item[0])]
        gap = jnp.zeros((pad, slots), f32)
        att_low[group] = jnp.concatenate(out + [gap], 0).T.astype(bf16)
        high_form = jnp.concatenate([gap] + out, 0).T.astype(bf16)
        att_high[group] = high_form
        mid[...] += dot_nt(high_form, weights[group, :, 3 * width - pad : 4 * width])
    normed, scale = normalize(mid[...])
    h2[...] = (normed * gain[...] + bias[...]).astype(bf16)


def attend(place, counts, h1, biases, edge_sums, buckets, spatial_table, layer_in, o_bias, gain, bias, parts):
    slots, features = h1.shape
    groups, width = biases.shape[0], biases.shape[2]
    heads = groups * 8
    return pl.pallas_call(
        functools.partial(attend_kernel, len(parts)),
        out_shape=(
            shape((groups, features, 4 * width), bf16),
            shape((groups, 3 * width, slots), bf16),
            shape((groups, slots, 256), bf16),
            shape((heads, slots, slots), f32),
            shape((groups, slots, 256), bf16),
            shape((groups, slots, 256), bf16),
            shape((slots, features), f32),
            shape((slots, features), bf16),
        ),
        in_specs=[smem, smem] + [vmem] * (9 + len(parts)),
        out_specs=[vmem] * 8,
        compiler_params=params,
        name="attend",
    )(place, counts, h1, biases, edge_sums, buckets, spatial_table, layer_in, o_bias, gain, bias, *parts)


def feed_kernel(
    n_parts, place, mid, h2, weights_a, biases, out_bias, gain, cotangent, att_low, *refs
):
    parts = refs[:n_parts]
    layer_out, grad_mid, grad_att_t, columns, rows_t, sums, weights = refs[n_parts:]
    assemble(place, parts, weights)
    slots, features = mid.shape
    groups, width = biases.shape[0], biases.shape[2]
    pad = 256 - width
    lanes = lax.broadcasted_iota(i32, (1, 256), 1)
    cot = cotangent[...]
    grad_ffn = cot.astype(bf16)
    h2_value = h2[...]
    layer_out[...] = mid[...] + out_bias[...]
    grad_h2 = jnp.zeros((slots, features), f32)
    sums[...] = jnp.zeros_like(sums)
    for group in range(groups):
        in_bias = jnp.concatenate([biases[group, 2:3, :], jnp.zeros((1, pad), f32)], 1)
        pre = dot_nn(h2_value, weights[group, :, :256]) + in_bias
        cdf = 0.5 * (1.0 + lax.erf(pre * (0.5**0.5)))
        slope = cdf + pre * jnp.exp(-0.5 * pre * pre) * 0.3989422804014327
        hidden = pltpu.roll(pre * cdf, pad, 1)
        hidden = jnp.where(lanes >= pad, hidden, 0.0).astype(bf16)
        layer_out[...] += dot_nt(hidden, weights[group, :, width - pad : 2 * width])
        grad_hidden = dot_nn(grad_ffn, weights[group, :, width - pad : 2 * width])
        grad_hidden = pltpu.roll(grad_hidden, width, 1)
        grad_pre = jnp.where(lanes < width, grad_hidden * slope, 0.0).astype(bf16)
        grad_h2 = grad_h2 + dot_nt(grad_pre, weights[group, :, :256])
        columns[group, :, 0:256] = grad_pre
        columns[group, :, 256:512] = hidden
        columns[group, :, 512:768] = att_low[group]
        sums[12 + group : 13 + group, 0:256] = column_sum(grad_pre.astype(f32))
    normed, scale = normalize(mid[...])
    grad = cot + normalize_back(grad_h2 * gain[...], normed, scale)
    grad_mid[...] = grad
    branch = grad.astype(bf16)
    sums[2:3, :] = column_sum(grad)
    sums[3:4, :] = column_sum(grad_h2 * normed)
    sums[4:5, :] = column_sum(grad_h2)
    sums[5:6, :] = column_sum(cot)
    rows_t[0] = h2_value.astype(f32).T.astype(bf16)
    rows_t[1] = cot.T.astype(bf16)
    rows_t[2] = grad.T.astype(bf16)
    for group in range(groups):
        grad_att = dot_nn(branch, weights_a[group]).T
        grad_att = jnp.concatenate([grad_att[pad:], jnp.zeros((pad, slots), f32)], 0)
        grad_att_t[group] = grad_att.astype(bf16)


def feed(place, mid, h2, weights_a, biases, out_bias, gain, cotangent, att_low, parts):
    slots, features = mid.shape
    groups, width = biases.shape[0], biases.shape[2]
    whole = lambda dims: pl.BlockSpec(dims, lambda i: (0,) * len(dims))
    return pl.pallas_call(
        functools.partial(feed_kernel, len(parts)),
        grid=(1,),
        out_shape=(
            shape((slots, features), f32),
            shape((slots, features), f32),
            shape((groups, 256, slots), bf16),
            shape((groups, slots, 768), bf16),
            shape((3, features, slots), bf16),
            shape((16, features), f32),
        ),
        in_specs=[
            smem,
            whole(mid.shape),
            whole(h2.shape),
            pl.BlockSpec((groups, features, 256), lambda i: (0, 0, 2)),
            whole(biases.shape),
            whole(out_bias.shape),
            whole(gain.shape),
            whole(cotangent.shape),
            whole(att_low.shape),
        ]
        + [whole(part.shape) for part in parts],
        out_specs=[
            whole((slots, features)),
            whole((slots, features)),
            whole((groups, 256, slots)),
            whole((groups, slots, 768)),
            whole((3, features, slots)),
            whole((16, features)),
        ],
        scratch_shapes=[pltpu.VMEM((groups, features, 2 * width), bf16)],
        compiler_params=params,
        name="feed",
    )(place, mid, h2, weights_a, biases, out_bias, gain, cotangent, att_low, *parts)


def attend_back_kernel(
    probs_in, value_win, transposed, grad_att_t, weights, layer_in, gain, grad_mid, sums_in,
    score_grads, columns, grad_in, sums,
):
    slots, features = layer_in.shape
    groups = transposed.shape[0]
    width = transposed.shape[1] // 3
    depth = width // 8
    pad = 256 - width
    value_masks = head_masks(256, 0, depth)
    grad_h1 = jnp.zeros((slots, features), f32)
    sums[...] = sums_in[...]
    scale = depth ** (-0.5)
    for group in range(groups):
        values = value_win[group]
        stack = jnp.concatenate([values * mask for mask in value_masks], 0)
        grad_att = grad_att_t[group]
        grad_probs = dot_nn(stack, grad_att)
        grad_att = grad_att.astype(f32)
        held = transposed[group].astype(f32)
        query_out, key_out, value_out, score_out = [], [], [], []
        for head in range(8):
            probs = probs_in[group * 8 + head]
            part = probs * grad_probs[head * slots : (head + 1) * slots]
            grads = (part - probs * column_sum(part)).astype(bf16)
            score_out.append(grads)
            cut = slice(head * depth, (head + 1) * depth)
            value_out.append(dot_nt(grad_att[cut].astype(bf16), probs.astype(bf16)))
            key_rows = held[width + head * depth : width + (head + 1) * depth]
            query_out.append(dot_nn(key_rows.astype(bf16), grads) * scale)
            key_out.append(dot_nt(held[cut].astype(bf16), grads) * scale)
        score_grads[:, group * 8 : (group + 1) * 8, :] = jnp.swapaxes(
            jnp.stack([g.astype(f32) for g in score_out]), 0, 1
        ).astype(bf16)
        gap = jnp.zeros((pad, slots), f32)
        natural = jnp.concatenate(query_out + key_out + value_out + [gap], 0).T.astype(bf16)
        columns[group] = natural
        grad_h1 = grad_h1 + dot_nt(natural, weights[group, :, : 3 * width + pad])
        sums[8 + group : 9 + group, 0 : 3 * width + pad] = column_sum(natural.astype(f32))
    normed, inverse = normalize(layer_in[...])
    grad_in[...] = grad_mid[...] + normalize_back(grad_h1 * gain[...], normed, inverse)
    sums[0:1, :] = column_sum(grad_h1 * normed)
    sums[1:2, :] = column_sum(grad_h1)


def attend_back(probs, value_win, transposed, grad_att_t, weights, layer_in, gain, grad_mid, sums):
    slots, features = layer_in.shape
    groups = transposed.shape[0]
    width = transposed.shape[1] // 3
    return pl.pallas_call(
        attend_back_kernel,
        out_shape=(
            shape((slots, groups * 8, slots), bf16),
            shape((groups, slots, 2 * width + 256), bf16),
            shape((slots, features), f32),
            shape(sums.shape, f32),
        ),
        in_specs=[vmem] * 9,
        out_specs=[vmem] * 4,
        compiler_params=params,
        name="attend_back",
    )(probs, value_win, transposed, grad_att_t, weights, layer_in, gain, grad_mid, sums)


def weight_grads_kernel(plan, place, rows_own, rows_other, columns_own, columns_other, own, across, over, both, rows_t):
    kinds = rows_own.shape[0]
    slots = rows_own.shape[2]
    for kind in range(kinds):
        rows_t[kind, :, 0:slots] = rows_own[kind]
        rows_t[kind, :, slots : 2 * slots] = rows_other[kind]
    core = place[3]
    height = own.shape[1]
    for which, out in ((3, both), (2, over), (1, across), (0, own)):
        column = relative(place, core, which, 0)[1]
        right = jnp.concatenate([columns_own[column], columns_other[column]], 0)
        for step in range(4):
            row = relative(place, core, which, step)[0]
            start = pl.multiple_of(row * height, height)
            out[step] = plan(lambda kind: rows_t[kind, pl.ds(start, height), :], right).astype(bf16)


def plan_first(rows_of, right):
    return dot_nn(rows_of(0), right)


def plan_second(rows_of, right):
    grad_in = dot_nn(rows_of(0), right[:, 0:256])
    grad_out = dot_nn(rows_of(1), right[:, 256:512])
    grad_o = dot_nn(rows_of(2), right[:, 512:768])
    return jnp.concatenate(
        [grad_in[:, :128], grad_in[:, 128:] + grad_out[:, :128], grad_out[:, 128:], grad_o], 1
    )


def weight_grads(plan, place, rows_own, rows_other, columns_own, columns_other, height):
    kinds, features, slots = rows_own.shape
    out = shape((4, height, 640), bf16)
    return pl.pallas_call(
        functools.partial(weight_grads_kernel, plan),
        out_shape=(out,) * 4,
        in_specs=[smem] + [vmem] * 4,
        out_specs=[vmem] * 4,
        scratch_shapes=[pltpu.VMEM((kinds, features, 2 * slots), bf16)],
        compiler_params=params,
        name="weight_grads",
    )(place, rows_own, rows_other, columns_own, columns_other)


def table_kernel(digit, staged, span, place, grads, ids, buckets, *refs):
    if staged:
        mine, partner, spatial, total = refs
    else:
        total, spatial = refs
    hops = ids.shape[0]
    heads = grads.shape[1]
    high_count = total.shape[0] // heads
    total[...] = jnp.zeros_like(total)
    spatial[...] = jnp.zeros_like(spatial)
    digits = lax.broadcasted_iota(i32, (digit, 128), 0).astype(f32).astype(bf16)
    kinds = lax.broadcasted_iota(i32, (heads, 128), 0).astype(f32).astype(bf16)
    one = jnp.ones((), bf16)
    zero = jnp.zeros((), bf16)

    def body(i, carry):
        lefts, rights, plain, kind_rights = [], [], [], []
        for j in range(span):
            row = i * span + j
            piece = grads[row]
            bucket = buckets[pl.ds(row, 1), :].astype(f32).astype(bf16)
            plain.append(piece)
            kind_rights.append(jnp.where(jnp.broadcast_to(bucket, (heads, 128)) == kinds, one, zero))
            for hop in range(hops):
                value = ids[hop, pl.ds(row, 1), :].astype(f32)
                high = jnp.floor((value + 0.5) * (1.0 / digit))
                low = value - high * digit
                low = jnp.broadcast_to(low.astype(bf16), (digit, 128))
                high = jnp.broadcast_to(high.astype(bf16), (heads, 128))
                rights.append(jnp.where(low == digits, one, zero))
                lefts.append(
                    jnp.concatenate(
                        [jnp.where(high == jnp.full((), k, bf16), piece, zero) for k in range(high_count)], 0
                    )
                )
        total[...] += dot_nt(jnp.concatenate(lefts, 1), jnp.concatenate(rights, 1))
        spatial[...] += dot_nt(jnp.concatenate(plain, 1), jnp.concatenate(kind_rights, 1))
        return carry

    lax.fori_loop(0, grads.shape[0] // span, body, 0)
    if staged:
        core = place[3]
        for other, out in ((0, mine), (1, partner)):
            for which in range(4):
                for step in range(4):
                    row, column = relative(place, core ^ other, which, step)
                    start = pl.multiple_of(row * heads + column * 8, 8)
                    out[which, step] = total[pl.ds(start, 8), :] * (1.0 / hops)


def table_grads(place, grads, ids, buckets, digit, edges, staged):
    heads = grads.shape[1]
    high_count = edges // digit
    total = (high_count * heads, digit)
    block = shape((4, 4, 8, digit), f32)
    spatial = shape((heads, heads), f32)
    return pl.pallas_call(
        functools.partial(table_kernel, digit, staged, 8),
        out_shape=(block, block, spatial) if staged else (shape(total, f32), spatial),
        in_specs=[smem] + [vmem] * 3,
        out_specs=[vmem] * (3 if staged else 2),
        scratch_shapes=[pltpu.VMEM(total, f32)] if staged else [],
        compiler_params=params,
        name="table_grads",
    )(place, grads, ids, buckets)


class Links:
    def __init__(self):
        self.core = self.hop(lambda z, x, y, c: (z, x, y, 1 - c))
        self.first = self.hop(lambda z, x, y, c: (z, x, 1 - y, c) if c else (z, 1 - x, y, c))
        self.second = self.hop(lambda z, x, y, c: (z, 1 - x, y, c) if c else (z, x, 1 - y, c))
        self.along_x = self.hop(lambda z, x, y, c: (z, 1 - x, y, c))
        self.along_z = [self.hop(lambda z, x, y, c, k=k: (z ^ k, x, y, c)) for k in (1, 2, 3)]

    def hop(self, move):
        index = lambda z, x, y, c: (z * 2 + x) * 4 + y * 2 + c
        spots = [(z, x, y, c) for z in range(4) for x in range(2) for y in range(2) for c in range(2)]
        return [(index(*spot), index(*move(*spot))) for spot in spots]


def send(values, hop):
    return lax.ppermute(values, ("dp", "mp"), hop)


def gather_staged(links, own):
    stack = jnp.stack([own] + [send(own, hop) for hop in links.along_z])
    across = send(stack, links.first)
    over = send(stack, links.second)
    both = send(across, links.second)
    mine = (stack, across, over, both)
    return mine + tuple(send(part, links.core) for part in mine)


def add_rounded(*terms):
    total = terms[0].astype(f32)
    for term in terms[1:]:
        total = total + term.astype(f32)
    return total.astype(bf16)


def reduce_staged(links, own, across, over, both):
    across = add_rounded(across, send(both, links.second))
    own = add_rounded(own, send(over, links.second), send(across, links.first))
    total = own[0].astype(f32)
    for step, hop in enumerate(links.along_z):
        total = total + send(own[step + 1], hop).astype(f32)
    return total


def local(
    layer_in,
    node_counts,
    spatial_ids,
    path_ids,
    ln1_gain,
    ln1_bias,
    w_q,
    w_k,
    w_v,
    q_bias,
    v_bias,
    spatial_table,
    edge_table,
    w_o,
    o_bias,
    ln2_gain,
    ln2_bias,
    w_in,
    in_bias,
    w_out,
    out_bias,
    cotangent,
):
    dp_size, mp_size = lax.axis_size("dp"), lax.axis_size("mp")
    dp_index, mp_index = lax.axis_index("dp"), lax.axis_index("mp")
    staged = dp_size == 8 and mp_size == 4
    features = layer_in.shape[1]
    width = w_q.shape[1]
    height = w_q.shape[0]
    edges = edge_table.shape[0] * dp_size
    heads = spatial_table.shape[1]
    kinds = spatial_table.shape[0]
    hops = path_ids.shape[1]
    share = edges // 4
    digit = edges // 8
    place = jnp.stack([dp_index // 2, dp_index % 2, mp_index // 2, mp_index % 2, mp_index]).astype(i32)
    row = lambda v: v.reshape(1, features)

    biases = lax.all_gather(jnp.stack([q_bias, v_bias, in_bias]), "mp", axis=0, tiled=False)
    ids, buckets, h1, h1_t = prepare(
        place, spatial_ids, path_ids, layer_in, row(ln1_gain), row(ln1_bias), kinds - 1
    )
    if staged:
        links = Links()
        first, second, table_t = pack(w_q, w_k, w_v, w_o, w_in, w_out, edge_table)
        neighbour = send(table_t, links.along_x)
        even = dp_index % 2 == 0
        pair = jnp.concatenate(
            [jnp.where(even, table_t, neighbour), jnp.where(even, neighbour, table_t)], 0
        )
        chunks = [pair] + [send(pair, hop) for hop in links.along_z]
        parts_a = gather_staged(links, first)
        parts_b = gather_staged(links, second)
        lookup_place = place
    else:
        gathered = [
            lax.all_gather(lax.all_gather(w, "dp", axis=0, tiled=True), "mp", axis=0)
            for w in (w_q, w_k, w_v, w_o, w_in, w_out)
        ]
        parts_a = (jnp.concatenate(gathered[:4], 2),)
        parts_b = (jnp.concatenate(gathered[4:], 2),)
        table_t = lax.all_gather(edge_table, "dp", axis=0, tiled=True).T
        chunks = [table_t[:, i * share : (i + 1) * share] for i in range(4)]
        lookup_place = jnp.zeros((5,), i32)
    edge_sums = None
    for step in range(4):
        edge_sums = lookup(lookup_place, chunks[step], ids, edge_sums, step, share)

    weights, transposed, value_win, probs, att_low, att_high, mid, h2 = attend(
        place, node_counts, h1, biases, edge_sums, buckets, spatial_table,
        layer_in, row(o_bias), row(ln2_gain), row(ln2_bias), parts_a,
    )
    layer_out, grad_mid, grad_att_t, columns_b, rows_b, sums = feed(
        place, mid, h2, weights, biases, row(out_bias), row(ln2_gain), cotangent, att_low, parts_b
    )
    rows_a = h1_t.reshape(1, *h1_t.shape)
    if staged:
        other_rows_b = send(rows_b, links.core)
        other_columns_b = send(columns_b, links.core)
        other_rows_a = send(rows_a, links.core)
        pieces_b = weight_grads(
            plan_second, place, rows_b, other_rows_b, columns_b, other_columns_b, height
        )
        grads_b = reduce_staged(links, *pieces_b)
    score_grads, columns_a, grad_layer_in, sums = attend_back(
        probs, value_win, transposed, grad_att_t, weights, layer_in, row(ln1_gain), grad_mid, sums
    )
    if staged:
        other_columns_a = send(columns_a, links.core)
        pieces_a = weight_grads(
            plan_first, place, rows_a, other_rows_a, columns_a, other_columns_a, height
        )
        grads_a = reduce_staged(links, *pieces_a)
        mine, partner, spatial = table_grads(place, score_grads, ids, buckets, digit, edges, True)
        small = jnp.concatenate(
            [
                sums.reshape(-1, digit),
                jnp.pad(spatial, ((0, 0), (0, digit - heads))),
            ],
            0,
        )
        n_small = small.shape[0]
        flat = lambda a: a.reshape(-1, digit)
        got = send(jnp.concatenate([flat(partner), small], 0), links.core)
        table = mine + got[:-n_small].reshape(mine.shape)
        small = small + got[-n_small:]
        got = send(jnp.concatenate([flat(table[2:4]), small], 0), links.second)
        blocks = got[:-n_small].reshape(2, *mine.shape[1:])
        across = table[1] + blocks[1]
        small = small + got[-n_small:]
        got = send(jnp.concatenate([flat(across), small], 0), links.first)
        own = table[0] + blocks[0] + got[:-n_small].reshape(mine.shape[1:])
        small = small + got[-n_small:]
        grad_edge, total = own[0], small
        for step, hop in enumerate(links.along_z):
            got = send(jnp.concatenate([own[step + 1], small], 0), hop)
            grad_edge = grad_edge + got[: own.shape[1]]
            total = total + got[own.shape[1] :]
        grad_edge = grad_edge.T
        spatial = total[-heads:, :kinds]
        totals = total[:-heads].reshape(sums.shape)
        grad_w_q, grad_w_k, grad_w_v = (grads_a[:, i * width : (i + 1) * width] for i in range(3))
        grad_w_in, grad_w_out, grad_w_o = (grads_b[:, i * width : (i + 1) * width] for i in range(3))
    else:
        contract = lambda a, b: lax.dot_general(
            a, b, (((1,), (1,)), ((), ())), preferred_element_type=f32
        )

        def scatter(rows_t, columns):
            grads = contract(rows_t, columns)
            grads = jnp.transpose(grads, (1, 0, 2))
            grads = lax.psum_scatter(grads, "mp", scatter_dimension=0, tiled=False)
            return lax.psum_scatter(grads, "dp", scatter_dimension=0, tiled=True)

        grad_w_q, grad_w_k, grad_w_v = (
            scatter(h1_t, columns_a[:, :, i * width : (i + 1) * width]) for i in range(3)
        )
        grad_w_in = scatter(rows_b[0], columns_b[:, :, :width])
        grad_w_out = scatter(rows_b[1], columns_b[:, :, 512 - width : 512])
        grad_w_o = scatter(rows_b[2], columns_b[:, :, 512 : 512 + width])
        table, spatial = table_grads(place, score_grads, ids, buckets, digit, edges, False)
        table = table.reshape(-1, heads, digit).transpose(0, 2, 1).reshape(edges, heads) / hops
        table = lax.psum_scatter(table, "dp", scatter_dimension=0, tiled=True)
        table = lax.psum(table, "mp")
        grad_edge = lax.dynamic_slice_in_dim(table, mp_index * 8, 8, 1)
        totals, spatial = lax.psum((sums, spatial), ("dp", "mp"))
        spatial = spatial[:, :kinds]
    grad_spatial = lax.dynamic_slice_in_dim(spatial, mp_index * 8, 8, 0).T
    head_sums = lax.dynamic_slice_in_dim(totals, 8 + mp_index, 1, 0)[0]
    hidden_sums = lax.dynamic_slice_in_dim(totals, 12 + mp_index, 1, 0)[0]
    return (
        layer_out,
        grad_layer_in,
        totals[0],
        totals[1],
        grad_w_q,
        grad_w_k,
        grad_w_v,
        head_sums[:width],
        head_sums[2 * width : 3 * width],
        grad_spatial,
        grad_edge,
        grad_w_o,
        totals[2],
        totals[3],
        totals[4],
        grad_w_in,
        hidden_sums[:width],
        grad_w_out,
        totals[5],
    )


def solution(mesh):
    return jax.shard_map(
        local,
        mesh=mesh,
        in_specs=(
            P(("dp", "mp"), None),
            P("dp"),
            P("dp", None, None),
            P("dp", None, None, None),
            P(),
            P(),
            P("dp", "mp"),
            P("dp", "mp"),
            P("dp", "mp"),
            P("mp"),
            P("mp"),
            P(),
            P("dp", None),
            P("dp", "mp"),
            P(),
            P(),
            P(),
            P("dp", "mp"),
            P("mp"),
            P("dp", "mp"),
            P(),
            P(("dp", "mp"), None),
        ),
        out_specs=(
            P(("dp", "mp"), None),
            P(("dp", "mp"), None),
            P(),
            P(),
            P("dp", "mp"),
            P("dp", "mp"),
            P("dp", "mp"),
            P("mp"),
            P("mp"),
            P(None, "mp"),
            P("dp", "mp"),
            P("dp", "mp"),
            P(),
            P(),
            P(),
            P("dp", "mp"),
            P("mp"),
            P("dp", "mp"),
            P(),
        ),
        check_vma=False,
    )
```

time: 1440 us -> 222 us (0.15)
  matrix products: 487 us -> 0 us
  waiting for transfers between devices: 475 us -> 57.7 us
  blocking collectives: 294 us -> 5.37 us
  Pallas kernels: 0 us -> 66.6 us
  loops' own time: 63.7 us -> 0 us
  starting transfers between devices: 0.68 us -> 58.4 us
  local copies, waits for them, and re-layouts: 77.8 us -> 24.7 us
  other arithmetic: 28.2 us -> 6.85 us
    dot_general x118 -> x0, matrix products: 487 us -> none  [the longest x42 252 us: contract_last(): lax.dot_general(left, right, (((1,), (1,)), ((), ())), preferred_element_...]
    reduce_scatter x9 -> x0, waiting for transfers between devices: 361 us -> none  [the longest x1 65.7 us: local(): lax.psum_scatter(grad_w_o, 'dp', scatter_dimension=0, tiled=True)]
    all_gather x11 -> x1, blocking collectives: 253 us -> 5.37 us  [local(): lax.all_gather(jnp.stack([q_bias, v_bias, in_bias]), 'mp', axis=0, tiled=...]
    unnamed x13 -> x0, waiting for transfers between devices: 114 us -> none
    pallas_call x0 -> x12, Pallas kernels: none -> 66.6 us  [the longest x4 24.4 us: lookup(): pl.pallas_call(functools.partial(lookup_kernel, first, step, share), out_...]
    another operation x12 -> x0, loops' own time: 63.7 us -> none  [the longest x4 62.5 us: pair_bias(): lax.map(block_terms, jnp.arange(count // width, dtype=jnp.int32) * width)]
    ppermute x0 -> x46, starting transfers between devices: none -> 58.4 us  [send(): return lax.ppermute(values, ('dp', 'mp'), hop)]
    ppermute x0 -> x46, waiting for transfers between devices: none -> 57.7 us  [send(): return lax.ppermute(values, ('dp', 'mp'), hop)]
  transfers between devices with their start and end apart: 11 -> 46, of which waited for: 10 -> 23; matrix products, arithmetic and copies ran while one was open for 2% -> 7% of each run, Pallas kernels for 0% -> 17%
where the time goes in v1:
time: 222 us; the launch traced here: 221 us
  Pallas kernels  66.6 us (30%)
  starting transfers between devices  58.4 us (26%)
  waiting for transfers between devices  57.7 us (26%)
  local copies, waits for them, and re-layouts  24.7 us (11%)
  other arithmetic  6.85 us (3%)
  blocking collectives  5.37 us (2%)
    ppermute x46, starting transfers between devices, send(): return lax.ppermute(values, ('dp', 'mp'), hop)  58.4 us
    ppermute x46, waiting for transfers between devices, send(): return lax.ppermute(values, ('dp', 'mp'), hop)  57.7 us
    pallas_call x4, Pallas kernels, lookup(): pl.pallas_call(functools.partial(lookup_kernel, first, step, share), out_...  24.4 us
    pallas_call x1, Pallas kernels, table_grads(): pl.pallas_call(functools.partial(table_kernel, digit, staged, 8), out_sha...  15.1 us
    unnamed x81, local copies, waits for them, and re-layouts  13.8 us
    pallas_call x1, Pallas kernels, attend(): pl.pallas_call(functools.partial(attend_kernel, len(parts)), out_shape=(s...  7.95 us
    pallas_call x1, Pallas kernels, attend_back(): pl.pallas_call(attend_back_kernel, out_shape=(shape((slots, groups * 8, s...  7.12 us
    pallas_call x1, Pallas kernels, feed(): pl.pallas_call(functools.partial(feed_kernel, len(parts)), grid=(1,), out...  5.87 us
  transfers between devices with their start and end apart: 46, of which 23 were waited for; matrix products, arithmetic and copies ran while one was open for 7% of the time, Pallas kernels for 17%

profile of v1, /device:TPU:0, one launch (start us, length us, event | category | flops | bytes accessed | tf_op | source)
XLA Modules:
  0.0 220.8 jit_solution(12274126208027557149)
XLA Ops:
  6.6 3.1 %collective-permute-start.4 = (bf16[96,768]{1,0:T(8,128)(2,1)S(1)}, bf16[96,768]{1,0:T(8,128)(2,1)S(1)}, u32[]{:S(2)}, u32[]{:S(2)}) collective-permute-start(bf16[96,768]{1,0:T(8,128)(2,1)S(1)} %get-tuple-element.58), channel_id=1, source_target_pairs={{0,8},{1,9},{2,10},{3,11},{4,12},{5,13},{6,14},{7,15},{8,0},{9,1},... | collective-permute-start | bytes 442376 | tf_op jit(solution)/shard_map/ppermute | solution.py:601
  9.6 2.6 %collective-permute-start.5 = (bf16[96,768]{1,0:T(8,128)(2,1)S(1)}, bf16[96,768]{1,0:T(8,128)(2,1)S(1)}, u32[]{:S(2)}, u32[]{:S(2)}) collective-permute-start(bf16[96,768]{1,0:T(8,128)(2,1)S(1)} %get-tuple-element.58), channel_id=1, source_target_pairs={{0,16},{1,17},{2,18},{3,19},{4,20},{5,21},{6,22},{7,23},{8,24},{9,... | collective-permute-start | bytes 442376 | tf_op jit(solution)/shard_map/ppermute | solution.py:601
  12.2 3.3 %collective-permute-done.4 = bf16[96,768]{1,0:T(8,128)(2,1)S(1)} collective-permute-done((bf16[96,768]{1,0:T(8,128)(2,1)S(1)}, bf16[96,768]{1,0:T(8,128)(2,1)S(1)}, u32[]{:S(2)}, u32[]{:S(2)}) %collective-permute-start.4) | collective-permute-done | bytes 147488 | tf_op jit(solution)/shard_map/ppermute | solution.py:601
  15.5 8.1 %collective-permute-done.5 = bf16[96,768]{1,0:T(8,128)(2,1)S(1)} collective-permute-done((bf16[96,768]{1,0:T(8,128)(2,1)S(1)}, bf16[96,768]{1,0:T(8,128)(2,1)S(1)}, u32[]{:S(2)}, u32[]{:S(2)}) %collective-permute-start.5) | collective-permute-done | bytes 147488 | tf_op jit(solution)/shard_map/ppermute | solution.py:601
  26.8 2.3 %collective-permute-start.14 = (bf16[96,384]{1,0:T(8,128)(2,1)S(1)}, bf16[96,384]{1,0:T(8,128)(2,1)S(1)}, u32[]{:S(2)}, u32[]{:S(2)}) collective-permute-start(bf16[96,384]{1,0:T(8,128)(2,1)S(1)} %get-tuple-element.63), channel_id=1, source_target_pairs={{0,8},{1,9},{2,10},{3,11},{4,12},{5,13},{6,14},{7,15},{8,0},{9,1},... | collective-permute-start | bytes 221192 | tf_op jit(solution)/shard_map/ppermute | solution.py:601
  32.6 2.6 %collective-permute-done.15 = bf16[96,384]{1,0:T(8,128)(2,1)S(1)} collective-permute-done((bf16[96,384]{1,0:T(8,128)(2,1)S(1)}, bf16[96,384]{1,0:T(8,128)(2,1)S(1)}, u32[]{:S(2)}, u32[]{:S(2)}) %collective-permute-start.15) | collective-permute-done | bytes 73760 | tf_op jit(solution)/shard_map/ppermute | solution.py:601
  37.0 2.1 collective-permute-done.7.refs_1_
  39.5 3.2 %collective-permute-start.3 = (bf16[64,192]{1,0:T(8,128)(2,1)S(1)}, bf16[64,192]{1,0:T(8,128)(2,1)S(1)}, u32[]{:S(2)}, u32[]{:S(2)}) collective-permute-start(bf16[64,192]{1,0:T(8,128)(2,1)S(1)} %pad_maximum_fusion.8.chunk), channel_id=1, source_target_pairs={{0,8},{1,9},{2,10},{3,11},{4,12},{5,13},{6,14},{7,15},{8,0},{9,1},... | collective-permute-start | bytes 73736 | tf_op jit(solution)/shard_map/ppermute | solution.py:601
  44.8 2.3 %collective-permute-start.1 = (bf16[64,192]{1,0:T(8,128)(2,1)S(1)}, bf16[64,192]{1,0:T(8,128)(2,1)S(1)}, u32[]{:S(2)}, u32[]{:S(2)}) collective-permute-start(bf16[64,192]{1,0:T(8,128)(2,1)S(1)} %pad_maximum_fusion.8.chunk), channel_id=1, source_target_pairs={{0,24},{1,25},{2,26},{3,27},{4,28},{5,29},{6,30},{7,31},{8,16},{9,... | collective-permute-start | bytes 73736 | tf_op jit(solution)/shard_map/ppermute | solution.py:601
  52.1 3.2 %collective-permute-done.18.refs_2_ = bf16[4,96,384]{2,1,0:T(8,128)(2,1)} collective-permute-done((bf16[4,96,384]{2,1,0:T(8,128)(2,1)S(1)}, bf16[4,96,384]{2,1,0:T(8,128)(2,1)}, u32[]{:S(2)}, u32[]{:S(2)}) %collective-permute-start.18) | collective-permute-done | bytes 294944 | tf_op jit(solution)/shard_map/ppermute | solution.py:601
  56.9 5.3 %collective-permute-done.19.refs_3_ = bf16[4,96,384]{2,1,0:T(8,128)(2,1)} collective-permute-done((bf16[4,96,384]{2,1,0:T(8,128)(2,1)S(1)}, bf16[4,96,384]{2,1,0:T(8,128)(2,1)}, u32[]{:S(2)}, u32[]{:S(2)}) %collective-permute-start.19) | collective-permute-done | bytes 294944 | tf_op jit(solution)/shard_map/ppermute | solution.py:601
  72.2 5.4 %all-gather.1.biases = f32[4,3,192]{2,1,0:T(4,128)S(1)} all-gather(f32[1,3,192]{2,1,0:T(4,128)S(1)} %maximum_bitcast_fusion), channel_id=2, replica_groups=mesh['dp'=8,'mp'=4] {'mp'}, dimensions={0}, use_global_device_ids=true | all-gather | bytes 11520 | tf_op jit(solution)/shard_map/all_gather | solution.py:668
  77.5 6.1 %lookup.4.refs_0_ = s32[16,128,128]{2,1,0:T(8,128)S(1)} custom-call(s32[5]{0:T(128)S(1)} %stack.65.place, bf16[64,192]{1,0:T(8,128)(2,1)S(1)} %pad_maximum_fusion.8.chunk, s32[5,128,128]{2,1,0:T(8,128)S(1)} %get-tuple-element.56.ids), custom_call_target="tpu_custom_call" | custom-call | tf_op jit(solution)/shard_map/lookup/pallas_call | solution.py:192
  83.6 6.1 %lookup.5.refs_0_ = s32[16,128,128]{2,1,0:T(8,128)S(1)} custom-call(s32[5]{0:T(128)S(1)} %stack.65.place, bf16[64,192]{1,0:T(8,128)(2,1)S(1)} %collective-permute-done.3.chunk, s32[5,128,128]{2,1,0:T(8,128)S(1)} %get-tuple-element.56.ids, s32[16,128,128]{2,1,0:T(8,128)S(1)} %lookup.4.refs_0_), custom_call_target="tpu_custom_call", output_to_operand_aliasing={{}: (3, {})} | custom-call | tf_op jit(solution)/shard_map/lookup/pallas_call | solution.py:192
  89.8 6.1 %lookup.6.refs_0_ = s32[16,128,128]{2,1,0:T(8,128)S(1)} custom-call(s32[5]{0:T(128)S(1)} %stack.65.place, bf16[64,192]{1,0:T(8,128)(2,1)S(1)} %copy-done.26, s32[5,128,128]{2,1,0:T(8,128)S(1)} %get-tuple-element.56.ids, s32[16,128,128]{2,1,0:T(8,128)S(1)} %lookup.5.refs_0_), custom_call_target="tpu_custom_call", output_to_operand_aliasing={{}: (3, {})} | custom-call | tf_op jit(solution)/shard_map/lookup/pallas_call | solution.py:192
  95.9 6.1 %lookup.7.edge_sums = s32[16,128,128]{2,1,0:T(8,128)S(1)} custom-call(s32[5]{0:T(128)S(1)} %stack.65.place, bf16[64,192]{1,0:T(8,128)(2,1)S(1)} %copy-done.28, s32[5,128,128]{2,1,0:T(8,128)S(1)} %get-tuple-element.56.ids, s32[16,128,128]{2,1,0:T(8,128)S(1)} %lookup.6.refs_0_), custom_call_target="tpu_custom_call", output_to_operand_aliasing={{}: (3, {})} | custom-call | tf_op jit(solution)/shard_map/lookup/pallas_call | solution.py:192
  103.1 7.9 %attend.1 = (bf16[4,768,768]{2,1,0:T(8,128)(2,1)}, bf16[4,576,128]{2,1,0:T(8,128)(2,1)S(1)}, bf16[4,128,256]{2,1,0:T(8,128)(2,1)S(1)}, f32[32,128,128]{2,1,0:T(8...) custom-call(s32[5]{0:T(128)S(1)} %stack.65.place, ...), custom_call_target="tpu_custom_call" | custom-call | tf_op jit(solution)/shard_map/attend/pallas_call | solution.py:302
  111.1 5.9 %feed.1 = (f32[128,768]{1,0:T(8,128)}, f32[128,768]{1,0:T(8,128)S(1)}, bf16[4,256,128]{2,1,0:T(8,128)(2,1)S(1)}, bf16[4,128,768]{2,1,0:T(8,128)(2,1)S(1)}, bf16[...) custom-call(s32[5]{0:T(128)S(1)} %stack.65.place, f32[128,768]{1,0:T(8,128)S(1)} %get-tuple-element.59.mid, ...), custom_call_target="tpu_custom_call" | custom-call | tf_op jit(solution)/shard_map/feed/pallas_call | solution.py:374
  117.0 7.1 %attend_back.1 = (bf16[128,32,128]{2,1,0:T(8,128)(2,1)S(1)}, bf16[4,128,640]{2,1,0:T(8,128)(2,1)S(1)}, f32[128,768]{1,0:T(8,128)}, f32[16,768]{1,0:T(8,128)S(1)}) custom-call(f32[32,128,128]{2,1,0:T(8,128)S(1)} %copy-done.2, bf16[4,128,256]{2,1,0:T(8,128)(2,1)S(1)} %get-tuple-element.66.value_win, bf16[4,576,128]{2,1,0:T(8,128)(2,1)S(1)} %get-tuple-element.67.transposed, ...), custom_call_target="tpu_custom_call" | custom-call | tf_op jit(solution)/shard_map/attend_back/pallas_call | solution.py:460
  124.1 15.1 %table_grads.1 = (f32[4,4,8,192]{3,2,1,0:T(8,128)S(1)}, f32[4,4,8,192]{3,2,1,0:T(8,128)S(1)}, f32[32,32]{1,0:T(8,128)S(1)}) custom-call(s32[5]{0:T(128)S(1)} %stack.65.place, bf16[128,32,128]{2,1,0:T(8,128)(2,1)S(1)} %get-tuple-element.73.grads, s32[5,128,128]{2,1,0:T(8,128)S(1)} %get-tuple-element.56.ids, s32[128,128]{1,0:T(8,128)S(1)} %get-tuple-element.57.buckets), custom_call_target="tpu_custom_call" | custom-call | tf_op jit(solution)/shard_map/table_grads/pallas_call | solution.py:575
  142.6 3.8 %collective-permute-done.25 = f32[160,192]{1,0:T(8,128)S(1)} collective-permute-done((f32[160,192]{1,0:T(8,128)S(1)}, f32[160,192]{1,0:T(8,128)S(1)}, u32[]{:S(2)}, u32[]{:S(2)}) %collective-permute-start.25) | collective-permute-done | bytes 122912 | tf_op jit(solution)/shard_map/ppermute | solution.py:601
  149.0 2.5 %collective-permute-done.26 = f32[128,192]{1,0:T(8,128)S(1)} collective-permute-done((f32[128,192]{1,0:T(8,128)S(1)}, f32[128,192]{1,0:T(8,128)S(1)}, u32[]{:S(2)}, u32[]{:S(2)}) %collective-permute-start.26) | collective-permute-done | bytes 98336 | tf_op jit(solution)/shard_map/ppermute | solution.py:601
  152.3 2.3 %weight_grads.2 = (bf16[4,96,640]{2,1,0:T(8,128)(2,1)S(1)}, bf16[4,96,640]{2,1,0:T(8,128)(2,1)S(1)}, bf16[4,96,640]{2,1,0:T(8,128)(2,1)S(1)}, bf16[4,96,640]{2,1,0:T(8,128)(2,1)}) custom-call(s32[5]{0:T(128)S(1)} %stack.65.place, bf16[1,768,128]{2,1,0:T(8,128)(2,1)S(1)} %bitcast.80, bf16[1,768,128]{2,1,0:T(8,128)(2,1)S(1)} %collective-permute-done.30.rows_other, ...), custom_call_target="tpu_custom_call" | custom-call | tf_op jit(solution)/shard_map/weight_grads/pallas_call | solution.py:508
  159.0 2.4 %collective-permute-start.28 = (f32[104,192]{1,0:T(8,128)S(1)}, f32[104,192]{1,0:T(8,128)S(1)}, u32[]{:S(2)}, u32[]{:S(2)}) collective-permute-start(f32[104,192]{1,0:T(8,128)S(1)} %get-tuple-element.108), channel_id=1, source_target_pairs={{0,16},{1,17},{2,18},{3,19},{4,20},{5,21},{6,22},{7,23},{8,24},{9,... | collective-permute-start | bytes 239624 | tf_op jit(solution)/shard_map/ppermute | solution.py:601
  161.4 2.2 %collective-permute-done.27 = f32[104,192]{1,0:T(8,128)S(1)} collective-permute-done((f32[104,192]{1,0:T(8,128)S(1)}, f32[104,192]{1,0:T(8,128)S(1)}, u32[]{:S(2)}, u32[]{:S(2)}) %collective-permute-start.27) | collective-permute-done | bytes 79904 | tf_op jit(solution)/shard_map/ppermute | solution.py:601
  163.6 2.7 %collective-permute-start.29 = (f32[104,192]{1,0:T(8,128)S(1)}, f32[104,192]{1,0:T(8,128)S(1)}, u32[]{:S(2)}, u32[]{:S(2)}) collective-permute-start(f32[104,192]{1,0:T(8,128)S(1)} %get-tuple-element.109), channel_id=1, source_target_pairs={{0,24},{1,25},{2,26},{3,27},{4,28},{5,29},{6,30},{7,31},{8,16},{9,... | collective-permute-start | bytes 239624 | tf_op jit(solution)/shard_map/ppermute | solution.py:601
  172.2 3.0 %weight_grads.3 = (bf16[4,96,640]{2,1,0:T(8,128)(2,1)S(1)}, bf16[4,96,640]{2,1,0:T(8,128)(2,1)S(1)}, bf16[4,96,640]{2,1,0:T(8,128)(2,1)S(1)}, bf16[4,96,640]{2,1,0:T(8,128)(2,1)}) custom-call(s32[5]{0:T(128)S(1)} %stack.65.place, bf16[3,768,128]{2,1,0:T(8,128)(2,1)S(1)} %get-tuple-element.83.rows_own, ...), custom_call_target="tpu_custom_call" | custom-call | tf_op jit(solution)/shard_map/weight_grads/pallas_call | solution.py:508
  181.8 8.1 %collective-permute-done.41 = bf16[4,96,640]{2,1,0:T(8,128)(2,1)S(1)} collective-permute-done((bf16[4,96,640]{2,1,0:T(8,128)(2,1)}, bf16[4,96,640]{2,1,0:T(8,128)(2,1)S(1)}, u32[]{:S(2)}, u32[]{:S(2)}) %collective-permute-start.41) | collective-permute-done | bytes 491552 | tf_op jit(solution)/shard_map/ppermute | solution.py:601
  191.1 2.3 %collective-permute-start.42 = (bf16[4,96,640]{2,1,0:T(8,128)(2,1)S(1)}, bf16[4,96,640]{2,1,0:T(8,128)(2,1)S(1)}, u32[]{:S(2)}, u32[]{:S(2)}) collective-permute-start(bf16[4,96,640]{2,1,0:T(8,128)(2,1)S(1)} %add_convert_fusion.1), channel_id=1, source_target_pairs={{0,4},{1,3},{2,6},{3,1},{4,0},{5,7},{6,2},{7,5},{8,12},{9,11},{10,... | collective-permute-start | bytes 1474568 | tf_op jit(solution)/shard_map/ppermute | solution.py:601
  195.5 2.2 %collective-permute-start.36 = (bf16[96,640]{1,0:T(8,128)(2,1)S(1)}, bf16[96,640]{1,0:T(8,128)(2,1)S(1)}, u32[]{:S(2)}, u32[]{:S(2)}) collective-permute-start(bf16[96,640]{1,0:T(8,128)(2,1)S(1)} %get-tuple-element.94), channel_id=1, source_target_pairs={{0,16},{1,17},{2,18},{3,19},{4,20},{5,21},{6,22},{7,23},{8,24},{9,... | collective-permute-start | bytes 368648 | tf_op jit(solution)/shard_map/ppermute | solution.py:601
  206.2 4.8 %collective-permute-start.43 = (bf16[96,640]{1,0:T(8,128)(2,1)S(1)}, bf16[96,640]{1,0:T(8,128)(2,1)S(1)}, u32[]{:S(2)}, u32[]{:S(2)}) collective-permute-start(bf16[96,640]{1,0:T(8,128)(2,1)S(1)} %get-tuple-element.89), channel_id=1, source_target_pairs={{0,8},{1,9},{2,10},{3,11},{4,12},{5,13},{6,14},{7,15},{8,0},{9,1},... | collective-permute-start | bytes 368648 | tf_op jit(solution)/shard_map/ppermute | solution.py:601
  216.8 3.2 %collective-permute-done.45 = bf16[96,640]{1,0:T(8,128)(2,1)S(1)} collective-permute-done((bf16[96,640]{1,0:T(8,128)(2,1)S(1)}, bf16[96,640]{1,0:T(8,128)(2,1)S(1)}, u32[]{:S(2)}, u32[]{:S(2)}) %collective-permute-start.45) | collective-permute-done | bytes 122912 | tf_op jit(solution)/shard_map/ppermute | solution.py:601
  (205 shorter events, 76.4 us)
Async XLA Ops:
  6.6 8.9 %collective-permute-start.4 = (bf16[96,768]{1,0:T(8,128)(2,1)S(1)}, bf16[96,768]{1,0:T(8,128)(2,1)S(1)}, u32[]{:S(2)}, u32[]{:S(2)}) collective-permute-start(bf16[96,768]{1,0:T(8,128)(2,1)S(1)} %get-tuple-element.58), channel_id=1, source_target_pairs={{0,8},{1,9},{2,10},{3,11},{4,12},{5,13},{6,14},{7,15},{8,0},{9,1},... | collective-permute-start | bytes 442376 | tf_op jit(solution)/shard_map/ppermute | solution.py:601
  9.6 14.0 %collective-permute-start.5 = (bf16[96,768]{1,0:T(8,128)(2,1)S(1)}, bf16[96,768]{1,0:T(8,128)(2,1)S(1)}, u32[]{:S(2)}, u32[]{:S(2)}) collective-permute-start(bf16[96,768]{1,0:T(8,128)(2,1)S(1)} %get-tuple-element.58), channel_id=1, source_target_pairs={{0,16},{1,17},{2,18},{3,19},{4,20},{5,21},{6,22},{7,23},{8,24},{9,... | collective-permute-start | bytes 442376 | tf_op jit(solution)/shard_map/ppermute | solution.py:601
  12.2 11.4 %collective-permute-start.6 = (bf16[96,768]{1,0:T(8,128)(2,1)S(1)}, bf16[96,768]{1,0:T(8,128)(2,1)S(1)}, u32[]{:S(2)}, u32[]{:S(2)}) collective-permute-start(bf16[96,768]{1,0:T(8,128)(2,1)S(1)} %get-tuple-element.58), channel_id=1, source_target_pairs={{0,24},{1,25},{2,26},{3,27},{4,28},{5,29},{6,30},{7,31},{8,16},{9,... | collective-permute-start | bytes 442376 | tf_op jit(solution)/shard_map/ppermute | solution.py:601
  23.7 15.4 %collective-permute-start.7 = (bf16[4,96,768]{2,1,0:T(8,128)(2,1)S(1)}, bf16[4,96,768]{2,1,0:T(8,128)(2,1)S(1)}, u32[]{:S(2)}, u32[]{:S(2)}) collective-permute-start(bf16[4,96,768]{2,1,0:T(8,128)(2,1)S(1)} %pad_maximum_fusion.refs_0_), channel_id=1, source_target_pairs={{0,4},{1,3},{2,6},{3,1},{4,0},{5,7},{6,2},{7,5},{8,12},{9,11},{10,... | collective-permute-start | bytes 1769480 | tf_op jit(solution)/shard_map/ppermute | solution.py:601
  25.3 26.3 %collective-permute-start.8 = (bf16[4,96,768]{2,1,0:T(8,128)(2,1)S(1)}, bf16[4,96,768]{2,1,0:T(8,128)(2,1)}, u32[]{:S(2)}, u32[]{:S(2)}) collective-permute-start(bf16[4,96,768]{2,1,0:T(8,128)(2,1)S(1)} %pad_maximum_fusion.refs_0_), channel_id=1, source_target_pairs={{0,2},{1,5},{2,0},{3,7},{4,6},{5,1},{6,4},{7,3},{8,10},{9,13},{10,... | collective-permute-start | bytes 1769480 | tf_op jit(solution)/shard_map/ppermute | solution.py:601
  32.0 7.5 %collective-permute-start = (bf16[32,192]{1,0:T(8,128)(2,1)S(1)}, bf16[32,192]{1,0:T(8,128)(2,1)S(1)}, u32[]{:S(2)}, u32[]{:S(2)}) collective-permute-start(bf16[32,192]{1,0:T(8,128)(2,1)S(1)} %get-tuple-element.55), channel_id=1, source_target_pairs={{0,4},{1,5},{2,6},{3,7},{4,0},{5,1},{6,2},{7,3},{8,12},{9,13},{10,... | collective-permute-start | bytes 36872 | tf_op jit(solution)/shard_map/ppermute | solution.py:601
  36.4 14.7 %collective-permute-start.17 = (bf16[4,96,384]{2,1,0:T(8,128)(2,1)S(1)}, bf16[4,96,384]{2,1,0:T(8,128)(2,1)S(1)}, u32[]{:S(2)}, u32[]{:S(2)}) collective-permute-start(bf16[4,96,384]{2,1,0:T(8,128)(2,1)S(1)} %pad_maximum_fusion.1.refs_0_), channel_id=1, source_target_pairs={{0,4},{1,3},{2,6},{3,1},{4,0},{5,7},{6,2},{7,5},{8,12},{9,11},{10,... | collective-permute-start | bytes 884744 | tf_op jit(solution)/shard_map/ppermute | solution.py:601
  39.2 12.5 %collective-permute-start.9 = (bf16[4,96,768]{2,1,0:T(8,128)(2,1)S(1)}, bf16[4,96,768]{2,1,0:T(8,128)(2,1)}, u32[]{:S(2)}, u32[]{:S(2)}) collective-permute-start(bf16[4,96,768]{2,1,0:T(8,128)(2,1)S(1)} %collective-permute-done.7.refs_1_), channel_id=1, source_target_pairs={{0,2},{1,5},{2,0},{3,7},{4,6},{5,1},{6,4},{7,3},{8,10},{9,13},{10,... | collective-permute-start | bytes 1769480 | tf_op jit(solution)/shard_map/ppermute | solution.py:601
  48.5 6.8 %collective-permute-start.18 = (bf16[4,96,384]{2,1,0:T(8,128)(2,1)S(1)}, bf16[4,96,384]{2,1,0:T(8,128)(2,1)}, u32[]{:S(2)}, u32[]{:S(2)}) collective-permute-start(bf16[4,96,384]{2,1,0:T(8,128)(2,1)S(1)} %pad_maximum_fusion.1.refs_0_), channel_id=1, source_target_pairs={{0,2},{1,5},{2,0},{3,7},{4,6},{5,1},{6,4},{7,3},{8,10},{9,13},{10,... | collective-permute-start | bytes 884744 | tf_op jit(solution)/shard_map/ppermute | solution.py:601
  51.1 11.1 %collective-permute-start.10 = (bf16[4,96,768]{2,1,0:T(8,128)(2,1)S(1)}, bf16[4,96,768]{2,1,0:T(8,128)(2,1)S(1)}, u32[]{:S(2)}, u32[]{:S(2)}) collective-permute-start(bf16[4,96,768]{2,1,0:T(8,128)(2,1)S(1)} %pad_maximum_fusion.refs_0_), channel_id=1, source_target_pairs={{0,1},{1,0},{2,3},{3,2},{4,5},{5,4},{6,7},{7,6},{8,9},{9,8},{10,11... | collective-permute-start | bytes 1769480 | tf_op jit(solution)/shard_map/ppermute | solution.py:601
  51.1 12.4 %collective-permute-start.11 = (bf16[4,96,768]{2,1,0:T(8,128)(2,1)S(1)}, bf16[4,96,768]{2,1,0:T(8,128)(2,1)S(1)}, u32[]{:S(2)}, u32[]{:S(2)}) collective-permute-start(bf16[4,96,768]{2,1,0:T(8,128)(2,1)S(1)} %collective-permute-done.7.refs_1_), channel_id=1, source_target_pairs={{0,1},{1,0},{2,3},{3,2},{4,5},{5,4},{6,7},{7,6},{8,9},{9,8},{10,11... | collective-permute-start | bytes 1769480 | tf_op jit(solution)/shard_map/ppermute | solution.py:601
  51.6 12.7 %collective-permute-start.12 = (bf16[4,96,768]{2,1,0:T(8,128)(2,1)}, bf16[4,96,768]{2,1,0:T(8,128)(2,1)}, u32[]{:S(2)}, u32[]{:S(2)}) collective-permute-start(bf16[4,96,768]{2,1,0:T(8,128)(2,1)} %collective-permute-done.8.refs_2_), channel_id=1, source_target_pairs={{0,1},{1,0},{2,3},{3,2},{4,5},{5,4},{6,7},{7,6},{8,9},{9,8},{10,11... | collective-permute-start | bytes 1769480 | tf_op jit(solution)/shard_map/ppermute | solution.py:601
  51.7 51.4 %collective-permute-start.13 = (bf16[4,96,768]{2,1,0:T(8,128)(2,1)}, bf16[4,96,768]{2,1,0:T(8,128)(2,1)}, u32[]{:S(2)}, u32[]{:S(2)}) collective-permute-start(bf16[4,96,768]{2,1,0:T(8,128)(2,1)} %collective-permute-done.9.refs_3_), channel_id=1, source_target_pairs={{0,1},{1,0},{2,3},{3,2},{4,5},{5,4},{6,7},{7,6},{8,9},{9,8},{10,11... | collective-permute-start | bytes 1769480 | tf_op jit(solution)/shard_map/ppermute | solution.py:601
  55.3 6.8 %collective-permute-start.19 = (bf16[4,96,384]{2,1,0:T(8,128)(2,1)S(1)}, bf16[4,96,384]{2,1,0:T(8,128)(2,1)}, u32[]{:S(2)}, u32[]{:S(2)}) collective-permute-start(bf16[4,96,384]{2,1,0:T(8,128)(2,1)S(1)} %collective-permute-done.17.refs_1_), channel_id=1, source_target_pairs={{0,2},{1,5},{2,0},{3,7},{4,6},{5,1},{6,4},{7,3},{8,10},{9,13},{10,... | collective-permute-start | bytes 884744 | tf_op jit(solution)/shard_map/ppermute | solution.py:601
  62.2 48.9 %collective-permute-start.20 = (bf16[4,96,384]{2,1,0:T(8,128)(2,1)S(1)}, bf16[4,96,384]{2,1,0:T(8,128)(2,1)}, u32[]{:S(2)}, u32[]{:S(2)}) collective-permute-start(bf16[4,96,384]{2,1,0:T(8,128)(2,1)S(1)} %pad_maximum_fusion.1.refs_0_), channel_id=1, source_target_pairs={{0,1},{1,0},{2,3},{3,2},{4,5},{5,4},{6,7},{7,6},{8,9},{9,8},{10,11... | collective-permute-start | bytes 884744 | tf_op jit(solution)/shard_map/ppermute | solution.py:601
  63.0 48.1 %collective-permute-start.21 = (bf16[4,96,384]{2,1,0:T(8,128)(2,1)S(1)}, bf16[4,96,384]{2,1,0:T(8,128)(2,1)}, u32[]{:S(2)}, u32[]{:S(2)}) collective-permute-start(bf16[4,96,384]{2,1,0:T(8,128)(2,1)S(1)} %collective-permute-done.17.refs_1_), channel_id=1, source_target_pairs={{0,1},{1,0},{2,3},{3,2},{4,5},{5,4},{6,7},{7,6},{8,9},{9,8},{10,11... | collective-permute-start | bytes 884744 | tf_op jit(solution)/shard_map/ppermute | solution.py:601
  64.3 46.8 %collective-permute-start.22 = (bf16[4,96,384]{2,1,0:T(8,128)(2,1)}, bf16[4,96,384]{2,1,0:T(8,128)(2,1)}, u32[]{:S(2)}, u32[]{:S(2)}) collective-permute-start(bf16[4,96,384]{2,1,0:T(8,128)(2,1)} %collective-permute-done.18.refs_2_), channel_id=1, source_target_pairs={{0,1},{1,0},{2,3},{3,2},{4,5},{5,4},{6,7},{7,6},{8,9},{9,8},{10,11... | collective-permute-start | bytes 884744 | tf_op jit(solution)/shard_map/ppermute | solution.py:601
  64.3 46.8 %collective-permute-start.23 = (bf16[4,96,384]{2,1,0:T(8,128)(2,1)}, bf16[4,96,384]{2,1,0:T(8,128)(2,1)}, u32[]{:S(2)}, u32[]{:S(2)}) collective-permute-start(bf16[4,96,384]{2,1,0:T(8,128)(2,1)} %collective-permute-done.19.refs_3_), channel_id=1, source_target_pairs={{0,1},{1,0},{2,3},{3,2},{4,5},{5,4},{6,7},{7,6},{8,9},{9,8},{10,11... | collective-permute-start | bytes 884744 | tf_op jit(solution)/shard_map/ppermute | solution.py:601
  148.0 24.3 %collective-permute-start.39 = (bf16[4,128,768]{2,1,0:T(8,128)(2,1)S(1)}, bf16[4,128,768]{2,1,0:T(8,128)(2,1)S(1)}, u32[]{:S(2)}, u32[]{:S(2)}) collective-permute-start(bf16[4,128,768]{2,1,0:T(8,128)(2,1)S(1)} %get-tuple-element.84.columns_own), channel_id=1, source_target_pairs={{0,1},{1,0},{2,3},{3,2},{4,5},{5,4},{6,7},{7,6},{8,9},{9,8},{10,11... | collective-permute-start | bytes 2359304 | tf_op jit(solution)/shard_map/ppermute | solution.py:601
  148.5 23.8 %collective-permute-start.38 = (bf16[3,768,128]{2,1,0:T(8,128)(2,1)S(1)}, bf16[3,768,128]{2,1,0:T(8,128)(2,1)}, u32[]{:S(2)}, u32[]{:S(2)}) collective-permute-start(bf16[3,768,128]{2,1,0:T(8,128)(2,1)S(1)} %get-tuple-element.83.rows_own), channel_id=1, source_target_pairs={{0,1},{1,0},{2,3},{3,2},{4,5},{5,4},{6,7},{7,6},{8,9},{9,8},{10,11... | collective-permute-start | bytes 1769480 | tf_op jit(solution)/shard_map/ppermute | solution.py:601
  156.9 18.5 %collective-permute-start.33 = (bf16[4,96,640]{2,1,0:T(8,128)(2,1)}, bf16[4,96,640]{2,1,0:T(8,128)(2,1)}, u32[]{:S(2)}, u32[]{:S(2)}) collective-permute-start(bf16[4,96,640]{2,1,0:T(8,128)(2,1)} %get-tuple-element.82), channel_id=1, source_target_pairs={{0,2},{1,5},{2,0},{3,7},{4,6},{5,1},{6,4},{7,3},{8,10},{9,13},{10,... | collective-permute-start | bytes 1474568 | tf_op jit(solution)/shard_map/ppermute | solution.py:601
  159.0 9.2 %collective-permute-start.28 = (f32[104,192]{1,0:T(8,128)S(1)}, f32[104,192]{1,0:T(8,128)S(1)}, u32[]{:S(2)}, u32[]{:S(2)}) collective-permute-start(f32[104,192]{1,0:T(8,128)S(1)} %get-tuple-element.108), channel_id=1, source_target_pairs={{0,16},{1,17},{2,18},{3,19},{4,20},{5,21},{6,22},{7,23},{8,24},{9,... | collective-permute-start | bytes 239624 | tf_op jit(solution)/shard_map/ppermute | solution.py:601
  170.3 23.1 %collective-permute-start.32 = (bf16[4,96,640]{2,1,0:T(8,128)(2,1)}, bf16[4,96,640]{2,1,0:T(8,128)(2,1)}, u32[]{:S(2)}, u32[]{:S(2)}) collective-permute-start(bf16[4,96,640]{2,1,0:T(8,128)(2,1)} %copy-done.34), channel_id=1, source_target_pairs={{0,2},{1,5},{2,0},{3,7},{4,6},{5,1},{6,4},{7,3},{8,10},{9,13},{10,... | collective-permute-start | bytes 1474568 | tf_op jit(solution)/shard_map/ppermute | solution.py:601
  175.2 14.7 %collective-permute-start.41 = (bf16[4,96,640]{2,1,0:T(8,128)(2,1)}, bf16[4,96,640]{2,1,0:T(8,128)(2,1)S(1)}, u32[]{:S(2)}, u32[]{:S(2)}) collective-permute-start(bf16[4,96,640]{2,1,0:T(8,128)(2,1)} %get-tuple-element.88), channel_id=1, source_target_pairs={{0,2},{1,5},{2,0},{3,7},{4,6},{5,1},{6,4},{7,3},{8,10},{9,13},{10,... | collective-permute-start | bytes 1474568 | tf_op jit(solution)/shard_map/ppermute | solution.py:601
  177.0 16.3 %collective-permute-start.34 = (bf16[4,96,640]{2,1,0:T(8,128)(2,1)S(1)}, bf16[4,96,640]{2,1,0:T(8,128)(2,1)}, u32[]{:S(2)}, u32[]{:S(2)}) collective-permute-start(bf16[4,96,640]{2,1,0:T(8,128)(2,1)S(1)} %add_convert_fusion.3), channel_id=1, source_target_pairs={{0,4},{1,3},{2,6},{3,1},{4,0},{5,7},{6,2},{7,5},{8,12},{9,11},{10,... | collective-permute-start | bytes 1474568 | tf_op jit(solution)/shard_map/ppermute | solution.py:601
  180.3 25.6 %collective-permute-start.40 = (bf16[4,96,640]{2,1,0:T(8,128)(2,1)}, bf16[4,96,640]{2,1,0:T(8,128)(2,1)S(1)}, u32[]{:S(2)}, u32[]{:S(2)}) collective-permute-start(bf16[4,96,640]{2,1,0:T(8,128)(2,1)} %copy-done.35), channel_id=1, source_target_pairs={{0,2},{1,5},{2,0},{3,7},{4,6},{5,1},{6,4},{7,3},{8,10},{9,13},{10,... | collective-permute-start | bytes 1474568 | tf_op jit(solution)/shard_map/ppermute | solution.py:601
  191.1 14.9 %collective-permute-start.42 = (bf16[4,96,640]{2,1,0:T(8,128)(2,1)S(1)}, bf16[4,96,640]{2,1,0:T(8,128)(2,1)S(1)}, u32[]{:S(2)}, u32[]{:S(2)}) collective-permute-start(bf16[4,96,640]{2,1,0:T(8,128)(2,1)S(1)} %add_convert_fusion.1), channel_id=1, source_target_pairs={{0,4},{1,3},{2,6},{3,1},{4,0},{5,7},{6,2},{7,5},{8,12},{9,11},{10,... | collective-permute-start | bytes 1474568 | tf_op jit(solution)/shard_map/ppermute | solution.py:601
  194.8 9.7 %collective-permute-start.35 = (bf16[96,640]{1,0:T(8,128)(2,1)S(1)}, bf16[96,640]{1,0:T(8,128)(2,1)S(1)}, u32[]{:S(2)}, u32[]{:S(2)}) collective-permute-start(bf16[96,640]{1,0:T(8,128)(2,1)S(1)} %get-tuple-element.92), channel_id=1, source_target_pairs={{0,8},{1,9},{2,10},{3,11},{4,12},{5,13},{6,14},{7,15},{8,0},{9,1},... | collective-permute-start | bytes 368648 | tf_op jit(solution)/shard_map/ppermute | solution.py:601
  195.5 8.9 %collective-permute-start.36 = (bf16[96,640]{1,0:T(8,128)(2,1)S(1)}, bf16[96,640]{1,0:T(8,128)(2,1)S(1)}, u32[]{:S(2)}, u32[]{:S(2)}) collective-permute-start(bf16[96,640]{1,0:T(8,128)(2,1)S(1)} %get-tuple-element.94), channel_id=1, source_target_pairs={{0,16},{1,17},{2,18},{3,19},{4,20},{5,21},{6,22},{7,23},{8,24},{9,... | collective-permute-start | bytes 368648 | tf_op jit(solution)/shard_map/ppermute | solution.py:601
  197.8 8.1 %collective-permute-start.37 = (bf16[96,640]{1,0:T(8,128)(2,1)S(1)}, bf16[96,640]{1,0:T(8,128)(2,1)S(1)}, u32[]{:S(2)}, u32[]{:S(2)}) collective-permute-start(bf16[96,640]{1,0:T(8,128)(2,1)S(1)} %get-tuple-element.93), channel_id=1, source_target_pairs={{0,24},{1,25},{2,26},{3,27},{4,28},{5,29},{6,30},{7,31},{8,16},{9,... | collective-permute-start | bytes 368648 | tf_op jit(solution)/shard_map/ppermute | solution.py:601
  206.2 8.9 %collective-permute-start.43 = (bf16[96,640]{1,0:T(8,128)(2,1)S(1)}, bf16[96,640]{1,0:T(8,128)(2,1)S(1)}, u32[]{:S(2)}, u32[]{:S(2)}) collective-permute-start(bf16[96,640]{1,0:T(8,128)(2,1)S(1)} %get-tuple-element.89), channel_id=1, source_target_pairs={{0,8},{1,9},{2,10},{3,11},{4,12},{5,13},{6,14},{7,15},{8,0},{9,1},... | collective-permute-start | bytes 368648 | tf_op jit(solution)/shard_map/ppermute | solution.py:601
  213.0 7.0 %collective-permute-start.45 = (bf16[96,640]{1,0:T(8,128)(2,1)S(1)}, bf16[96,640]{1,0:T(8,128)(2,1)S(1)}, u32[]{:S(2)}, u32[]{:S(2)}) collective-permute-start(bf16[96,640]{1,0:T(8,128)(2,1)S(1)} %get-tuple-element.90), channel_id=1, source_target_pairs={{0,24},{1,25},{2,26},{3,27},{4,28},{5,29},{6,30},{7,31},{8,16},{9,... | collective-permute-start | bytes 368648 | tf_op jit(solution)/shard_map/ppermute | solution.py:601
  (54 other events, 637.8 us)

commit v2 on v1

v2 whole, which is shorter than its diff:
```python
import functools

import jax
import jax.numpy as jnp
from jax import lax
from jax.experimental import pallas as pl
from jax.experimental.pallas import tpu as pltpu
from jax.sharding import PartitionSpec as P

epsilon = 1e-05
masked_score = -1e30
edge_unit = 1638.0
spatial_unit = 4096.0
bf16 = jnp.bfloat16
f32 = jnp.float32
i32 = jnp.int32
vmem = pl.BlockSpec(memory_space=pltpu.VMEM)
smem = pl.BlockSpec(memory_space=pltpu.SMEM)
hbm = pl.BlockSpec(memory_space=pltpu.HBM)
untouched = pl.BlockSpec(memory_space=pl.ANY)


def params(mebibytes):
    return pltpu.CompilerParams(vmem_limit_bytes=mebibytes << 20)


def normalize(values):
    centred = values - jnp.mean(values, axis=-1, keepdims=True)
    scale = lax.rsqrt(jnp.mean(centred * centred, axis=-1, keepdims=True) + epsilon)
    return (centred * scale, scale)


def normalize_back(grad_normed, normed, scale):
    inner = grad_normed - jnp.mean(grad_normed, axis=-1, keepdims=True)
    inner = inner - normed * jnp.mean(grad_normed * normed, axis=-1, keepdims=True)
    return inner * scale


def dot_nn(left, right):
    return lax.dot_general(
        left, right, (((1,), (0,)), ((), ())), preferred_element_type=f32
    )


def dot_nt(left, right):
    return lax.dot_general(
        left, right, (((1,), (1,)), ((), ())), preferred_element_type=f32
    )


def column_sum(values):
    return jnp.sum(values, axis=0, keepdims=True)


def cost(microseconds):
    return pl.CostEstimate(flops=int(microseconds * 1.15e9), bytes_accessed=1024, transcendentals=0)


def as_row(ref):
    return ref[...].reshape(1, -1)


def shape(dims, kind):
    return jax.ShapeDtypeStruct(dims, kind)


def relative(place, side, which, step):
    z, x, y = place[0], place[1], place[2]
    flip_x = (0, 1 - side, side, 1)[which]
    flip_y = (0, side, 1 - side, 1)[which]
    row = (z ^ step) * 2 + (x ^ flip_x)
    column = (y ^ flip_y) * 2 + side
    return row, column


def pack_kernel(wq, wk, wv, wo, wi, wu, bq, bv, bi, first, second, biases, held, sems):
    copies = [
        pltpu.make_async_copy(source, held.at[i], sems.at[i])
        for i, source in enumerate((wq, wk, wv, wo, wi, wu))
    ]
    for copy in copies:
        copy.start()
    for i, bias in enumerate((bq, bv, bi)):
        biases[i : i + 1, :] = as_row(bias)
    for copy in copies:
        copy.wait()
    first[...] = jnp.concatenate([held[i] for i in range(4)], 1)
    second[...] = jnp.concatenate([held[4], held[5]], 1)


def pack(wq, wk, wv, wo, wi, wu, bq, bv, bi):
    rows, width = wq.shape
    return pl.pallas_call(
        pack_kernel,
        out_shape=(
            shape((rows, 4 * width), bf16),
            shape((rows, 2 * width), bf16),
            shape((3, width), f32),
        ),
        in_specs=[hbm] * 6 + [vmem] * 3,
        out_specs=[vmem] * 3,
        scratch_shapes=[pltpu.VMEM((6, rows, width), bf16), pltpu.SemaphoreType.DMA((6,))],
        compiler_params=params(4),
        cost_estimate=cost(1),
        name="pack",
    )(wq, wk, wv, wo, wi, wu, bq, bv, bi)


def prepare_kernel(virtual, place, spatial, path, layer_in, gain, bias, cotangent, ids, buckets, h1, rows_t):
    slots = spatial.shape[1]
    for hop in range(path.shape[1]):
        ids[hop] = path[0, hop].T
    rows = lax.broadcasted_iota(i32, (slots, slots), 0)
    columns = lax.broadcasted_iota(i32, (slots, slots), 1)
    buckets[...] = jnp.where((rows == 0) | (columns == 0), virtual, spatial[0].T)
    normed, scale = normalize(layer_in[...])
    out = normed * as_row(gain) + as_row(bias)
    h1[...] = out.astype(bf16)
    rows_t[0] = out.T.astype(bf16)
    rows_t[1] = cotangent[...].T.astype(bf16)


def prepare(place, spatial, path, layer_in, gain, bias, cotangent, virtual):
    hops, slots = path.shape[1], path.shape[2]
    rows, width = layer_in.shape
    whole = lambda dims: pl.BlockSpec(dims, lambda i, s: (0,) * len(dims))
    return pl.pallas_call(
        functools.partial(prepare_kernel, virtual),
        grid_spec=pltpu.PrefetchScalarGridSpec(
            num_scalar_prefetch=1,
            grid=(1,),
            in_specs=[
                pl.BlockSpec((1, slots, slots), lambda i, s: (s[4], 0, 0)),
                pl.BlockSpec((1, hops, slots, slots), lambda i, s: (s[4], 0, 0, 0)),
                whole((rows, width)),
                whole((width,)),
                whole((width,)),
                whole((rows, width)),
            ],
            out_specs=[
                whole((hops, slots, slots)),
                whole((slots, slots)),
                whole((rows, width)),
                whole((2, width, rows)),
            ],
        ),
        out_shape=(
            shape((hops, slots, slots), i32),
            shape((slots, slots), i32),
            shape((rows, width), bf16),
            shape((2, width, rows), bf16),
        ),
        compiler_params=params(8),
        cost_estimate=cost(1),
        name="prepare",
    )(place, spatial, path, layer_in, gain, bias, cotangent)


def quantize(table, unit):
    held = jnp.round(table.astype(f32) * unit).astype(i32)
    partner = jnp.concatenate([held[4:], held[:4]], 0)
    return held + partner * 65536


def lanes_gather(table, places):
    return jnp.take_along_axis(table, places, axis=1, mode="promise_in_bounds")


def lookup_kernel(first, step, share, place, chunk, ids, *refs):
    if first:
        total, table = refs
        previous = None
    else:
        previous, total, table = refs
    hops, slots = ids.shape[0], ids.shape[1]
    pairs = total.shape[0]
    heads = 2 * pairs
    rows = chunk.shape[1]
    packed = jnp.concatenate(
        [quantize(chunk[i * heads : (i + 1) * heads, :], edge_unit) for i in range(share // rows)], 1
    )
    blocks = share // 128
    for pair in range(pairs):
        head = (pair // 4) * 8 + pair % 4
        for block in range(blocks):
            table[pair, block] = jnp.broadcast_to(
                packed[head : head + 1, block * 128 : (block + 1) * 128], (8, 128)
            )
    base = (place[0] ^ step) * share

    def body(i, carry):
        offset = pl.multiple_of(i * 8, 8)
        sums = [None] * pairs
        if not first:
            sums = [previous[pair, pl.ds(offset, 8), :] for pair in range(pairs)]
        for hop in range(hops):
            relative_id = ids[hop, pl.ds(offset, 8), :] - base
            low = relative_id & 127
            high = relative_id >> 7
            masks = [high == block for block in range(blocks)]
            for pair in range(pairs):
                value = jnp.zeros((8, 128), i32)
                for block in range(blocks):
                    value = jnp.where(masks[block], lanes_gather(table[pair, block], low), value)
                sums[pair] = value if sums[pair] is None else sums[pair] + value
        for pair in range(pairs):
            total[pair, pl.ds(offset, 8), :] = sums[pair]
        return carry

    lax.fori_loop(0, slots // 8, body, 0)


def lookup(place, chunk, ids, previous, step, share):
    heads = chunk.shape[0] // (share // chunk.shape[1])
    pairs = heads // 2
    slots = ids.shape[1]
    first = previous is None
    out = shape((pairs, slots, slots), i32)
    return pl.pallas_call(
        functools.partial(lookup_kernel, first, step, share),
        out_shape=out,
        in_specs=[smem] + [vmem] * (2 if first else 3),
        out_specs=vmem,
        scratch_shapes=[pltpu.VMEM((pairs, share // 128, 8, 128), i32)],
        input_output_aliases={} if first else {3: 0},
        compiler_params=params(8),
        cost_estimate=cost(6),
        name="lookup",
    )(place, chunk, ids, *(() if first else (previous,)))


def assemble(place, parts, whole):
    if len(parts) == 1:
        whole[...] = parts[0][...]
        return
    core = place[3]
    rows = parts[0].shape[1]
    for other in range(2):
        for which in range(4):
            for step in range(4):
                row, column = relative(place, core ^ other, which, step)
                start = pl.multiple_of(row * rows, rows)
                whole[column, pl.ds(start, rows), :] = parts[other * 4 + which][step]


def collect_biases(place, parts, whole):
    if len(parts) == 1:
        whole[...] = parts[0][...]
        return
    for i, part in enumerate(parts):
        whole[(place[2] ^ (i % 2)) * 2 + (place[3] ^ (i // 2))] = part[...]


def head_masks(width, offset, depth):
    lanes = lax.broadcasted_iota(i32, (1, width), 1)
    out = []
    for head in range(8):
        start = offset + head * depth
        out.append(((lanes >= start) & (lanes < start + depth)).astype(f32).astype(bf16))
    return out


def attend_kernel(
    n_parts, n_biases, place, counts, h1, edge_sums, buckets, spatial_table, layer_in, o_bias, gain, bias, *refs
):
    parts, bias_parts, refs = refs[:n_parts], refs[n_parts : n_parts + n_biases], refs[n_parts + n_biases :]
    weights, biases, transposed, value_win, probs_out, att_low, mid, h2 = refs
    assemble(place, parts, weights)
    collect_biases(place, bias_parts, biases)
    slots = h1.shape[0]
    groups, width = biases.shape[0], biases.shape[2]
    depth = width // 8
    pad = 256 - width
    hops = 5
    count = counts[place[4]]
    packed = quantize(spatial_table[...].astype(f32).T, spatial_unit)
    packed = jnp.concatenate([packed, jnp.zeros((packed.shape[0], 128 - packed.shape[1]), i32)], 1)
    hidden_key = lax.broadcasted_iota(i32, (slots, slots), 0) > count
    bucket = buckets[...]
    key_masks = head_masks(256, pad, depth)
    mid[...] = layer_in[...] + as_row(o_bias)
    for group in range(groups):
        natural = dot_nn(h1[...], weights[group, :, : 3 * width + pad])
        row_bias = jnp.concatenate(
            [
                biases[group, 0:1, :],
                jnp.zeros((1, width), f32),
                biases[group, 1:2, :],
                jnp.zeros((1, pad), f32),
            ],
            1,
        )
        natural = natural + row_bias
        natural_t = natural.T
        transposed[group] = natural_t[: 2 * width].astype(bf16)
        natural = natural.astype(bf16)
        value_win[group] = natural[:, 2 * width : 2 * width + 256]
        keys = natural[:, width - pad : 2 * width]
        stack = jnp.concatenate([keys * mask for mask in key_masks], 0)
        query = jnp.concatenate([jnp.zeros((pad, slots), f32), natural_t[:width]], 0).astype(bf16)
        scores = dot_nn(stack, query) * depth ** (-0.5)
        out = [None] * 8
        for pair in range(4):
            word = edge_sums[group * 4 + pair]
            head = group * 8 + pair
            spatial_word = lanes_gather(
                jnp.broadcast_to(packed[head : head + 1], (slots, 128)), bucket
            )
            low = (word << 16) >> 16
            spatial_low = (spatial_word << 16) >> 16
            high = (word - low) >> 16
            spatial_high = (spatial_word - spatial_low) >> 16
            for part, spatial_part, spot in ((low, spatial_low, pair), (high, spatial_high, pair + 4)):
                pair_bias = part.astype(f32) * (1.0 / (edge_unit * hops))
                pair_bias = pair_bias + spatial_part.astype(f32) * (1.0 / spatial_unit)
                score = scores[spot * slots : (spot + 1) * slots] + pair_bias
                score = jnp.where(hidden_key, masked_score, score)
                weight = jnp.exp(score - jnp.max(score, axis=0, keepdims=True))
                probs = weight * (1.0 / column_sum(weight))
                probs_out[group * 8 + spot] = probs
                values = natural_t[2 * width + spot * depth : 2 * width + (spot + 1) * depth]
                out[spot] = dot_nn(values.astype(bf16), probs.astype(bf16))
        gap = jnp.zeros((pad, slots), f32)
        att_low[group] = jnp.concatenate(out + [gap], 0).T.astype(bf16)
        high_form = jnp.concatenate([gap] + out, 0).T.astype(bf16)
        mid[...] += dot_nt(high_form, weights[group, :, 3 * width - pad : 4 * width])
    normed, scale = normalize(mid[...])
    h2[...] = (normed * as_row(gain) + as_row(bias)).astype(bf16)


def attend(place, counts, h1, edge_sums, buckets, spatial_table, layer_in, o_bias, gain, bias, parts, bias_parts):
    slots, features = h1.shape
    width = bias_parts[0].shape[-1]
    heads = spatial_table.shape[1]
    groups = heads // 8
    return pl.pallas_call(
        functools.partial(attend_kernel, len(parts), len(bias_parts)),
        out_shape=(
            shape((groups, features, 4 * width), bf16),
            shape((groups, 3, width), f32),
            shape((groups, 2 * width, slots), bf16),
            shape((groups, slots, 256), bf16),
            shape((heads, slots, slots), f32),
            shape((groups, slots, 256), bf16),
            shape((slots, features), f32),
            shape((slots, features), bf16),
        ),
        in_specs=[smem, smem] + [vmem] * (8 + len(parts) + len(bias_parts)),
        out_specs=[vmem] * 8,
        cost_estimate=cost(7),
        compiler_params=params(28),
        name="attend",
    )(
        place, counts, h1, edge_sums, buckets, spatial_table, layer_in, o_bias, gain, bias,
        *parts, *bias_parts,
    )


def group_order(place):
    return [
        (theirs, y, y * 2 + (place[3] ^ theirs)) for theirs in (1, 0) for y in (0, 1)
    ]


def feed_kernel(
    n_parts, place, mid, h2, weights_a, biases, out_bias, gain, cotangent, att_low, probs_in, *refs
):
    parts = refs[:n_parts]
    layer_out, grad_mid, grad_att_t, grad_values, mine, theirs, rows_t, sums, weights = refs[n_parts:]
    assemble(place, parts, weights)
    slots, features = mid.shape
    width = biases.shape[2]
    depth = width // 8
    pad = 256 - width
    lanes = lax.broadcasted_iota(i32, (1, 256), 1)
    cot = cotangent[...]
    grad_ffn = cot.astype(bf16)
    h2_value = h2[...]
    layer_out[...] = mid[...] + as_row(out_bias)
    grad_h2 = jnp.zeros((slots, features), f32)
    sums[...] = jnp.zeros_like(sums)
    order = group_order(place)
    for side, y, group in order:
        columns = theirs if side else mine
        in_bias = jnp.concatenate([biases[group, 2:3, :], jnp.zeros((1, pad), f32)], 1)
        pre = dot_nn(h2_value, weights[group, :, :256]) + in_bias
        cdf = 0.5 * (1.0 + lax.erf(pre * (0.5**0.5)))
        slope = cdf + pre * jnp.exp(-0.5 * pre * pre) * 0.3989422804014327
        hidden = pltpu.roll(pre * cdf, pad, 1)
        hidden = jnp.where(lanes >= pad, hidden, 0.0).astype(bf16)
        layer_out[...] += dot_nt(hidden, weights[group, :, width - pad : 2 * width])
        grad_hidden = dot_nn(grad_ffn, weights[group, :, width - pad : 2 * width])
        grad_hidden = pltpu.roll(grad_hidden, width, 1)
        grad_pre = jnp.where(lanes < width, grad_hidden * slope, 0.0).astype(bf16)
        grad_h2 = grad_h2 + dot_nt(grad_pre, weights[group, :, :256])
        columns[y, :, 0:256] = grad_pre
        columns[y, :, 256:512] = hidden
        columns[y, :, 512:768] = att_low[group]
        sums[pl.ds(12 + group, 1), 0:256] = column_sum(grad_pre.astype(f32))
    normed, scale = normalize(mid[...])
    grad = cot + normalize_back(grad_h2 * as_row(gain), normed, scale)
    grad_mid[...] = grad
    branch = grad.astype(bf16)
    sums[2:3, :] = column_sum(grad)
    sums[3:4, :] = column_sum(grad_h2 * normed)
    sums[4:5, :] = column_sum(grad_h2)
    sums[5:6, :] = column_sum(cot)
    rows_t[0] = h2_value.astype(f32).T.astype(bf16)
    rows_t[1] = grad.T.astype(bf16)
    gap = jnp.zeros((pad, slots), f32)
    for side, y, group in order:
        columns = theirs if side else mine
        grad_att = dot_nn(branch, weights_a[group]).T[pad:]
        grad_att_t[group] = jnp.concatenate([grad_att, gap], 0).astype(bf16)
        out = []
        for head in range(8):
            out.append(
                dot_nt(
                    grad_att[head * depth : (head + 1) * depth].astype(bf16),
                    probs_in[group * 8 + head].astype(bf16),
                )
            )
        low_form = jnp.concatenate(out + [gap], 0).T.astype(bf16)
        grad_values[group] = low_form
        columns[y, :, 768:1024] = jnp.concatenate([gap] + out, 0).T.astype(bf16)
        sums[pl.ds(8 + group, 1), 512:768] = column_sum(low_form.astype(f32))


def feed(place, mid, h2, weights_a, biases, out_bias, gain, cotangent, att_low, probs, parts):
    slots, features = mid.shape
    groups, width = biases.shape[0], biases.shape[2]
    whole = lambda array: pl.BlockSpec(array.shape, lambda i: (0,) * len(array.shape))
    outs = (
        shape((slots, features), f32),
        shape((slots, features), f32),
        shape((groups, 256, slots), bf16),
        shape((groups, slots, 256), bf16),
        shape((2, slots, 1024), bf16),
        shape((2, slots, 1024), bf16),
        shape((2, features, slots), bf16),
        shape((16, features), f32),
    )
    rest = (biases, out_bias, gain, cotangent, att_low, probs)
    return pl.pallas_call(
        functools.partial(feed_kernel, len(parts)),
        grid=(1,),
        out_shape=outs,
        in_specs=[
            smem,
            whole(mid),
            whole(h2),
            pl.BlockSpec((groups, features, 256), lambda i: (0, 0, 2)),
        ]
        + [whole(a) for a in rest + tuple(parts)],
        out_specs=[whole(out) for out in outs],
        scratch_shapes=[pltpu.VMEM((groups, features, 2 * width), bf16)],
        cost_estimate=cost(7),
        compiler_params=params(32),
        name="feed",
    )(place, mid, h2, weights_a, *rest, *parts)


def attend_back_kernel(
    place, probs_in, value_win, transposed, grad_att_t, grad_values, weights, layer_in, gain, grad_mid,
    sums_in, after, score_grads, mine, theirs, grad_in, sums,
):
    slots, features = layer_in.shape
    width = transposed.shape[1] // 2
    depth = width // 8
    value_masks = head_masks(256, 0, depth)
    grad_h1 = jnp.zeros((slots, features), f32)
    sums[...] = sums_in[...]
    scale = depth ** (-0.5)
    for side, y, group in group_order(place):
        columns = theirs if side else mine
        values = value_win[group]
        stack = jnp.concatenate([values * mask for mask in value_masks], 0)
        grad_probs = dot_nn(stack, grad_att_t[group])
        held = transposed[group].astype(f32)
        query_out, key_out, score_out = [], [], []
        for head in range(8):
            probs = probs_in[group * 8 + head]
            part = probs * grad_probs[head * slots : (head + 1) * slots]
            exact = part - probs * column_sum(part)
            grads = exact.astype(bf16)
            score_out.append(exact)
            key_rows = held[width + head * depth : width + (head + 1) * depth]
            query_out.append(dot_nn(key_rows.astype(bf16), grads) * scale)
            query_rows = held[head * depth : (head + 1) * depth]
            key_out.append(dot_nt(query_rows.astype(bf16), grads) * scale)
        score_grads[group] = jnp.swapaxes(jnp.stack(score_out), 0, 1)
        natural = jnp.concatenate(query_out + key_out, 0).T.astype(bf16)
        columns[y] = natural
        grad_h1 = grad_h1 + dot_nt(natural, weights[group, :, : 2 * width])
        grad_h1 = grad_h1 + dot_nt(grad_values[group], weights[group, :, 2 * width : 2 * width + 256])
        sums[pl.ds(8 + group, 1), 0 : 2 * width] = column_sum(natural.astype(f32))
    normed, inverse = normalize(layer_in[...])
    grad_in[...] = grad_mid[...] + normalize_back(grad_h1 * as_row(gain), normed, inverse)
    sums[0:1, :] = column_sum(grad_h1 * normed)
    sums[1:2, :] = column_sum(grad_h1)


def attend_back(
    place, probs, value_win, transposed, grad_att_t, grad_values, weights, layer_in, gain, grad_mid, sums, after
):
    slots, features = layer_in.shape
    groups = transposed.shape[0]
    width = transposed.shape[1] // 2
    return pl.pallas_call(
        attend_back_kernel,
        out_shape=(
            shape((groups, slots, 8, slots), f32),
            shape((2, slots, 2 * width), bf16),
            shape((2, slots, 2 * width), bf16),
            shape((slots, features), f32),
            shape(sums.shape, f32),
        ),
        in_specs=[smem] + [vmem] * 10 + [untouched],
        out_specs=[vmem] * 5,
        cost_estimate=cost(7),
        compiler_params=params(24),
        name="attend_back",
    )(
        place, probs, value_win, transposed, grad_att_t, grad_values, weights, layer_in, gain, grad_mid,
        sums, after,
    )


def weight_grads_kernel(plan, n_rows, place, columns_own, columns_other, *refs):
    own_rows, other_rows = refs[:n_rows], refs[n_rows : 2 * n_rows]
    own, across, over, both, rows_t = refs[2 * n_rows :]
    kind = 0
    for mine, other in zip(own_rows, other_rows):
        slots = mine.shape[2]
        for i in range(mine.shape[0]):
            rows_t[kind, :, 0:slots] = mine[i]
            rows_t[kind, :, slots : 2 * slots] = other[i]
            kind += 1
    core = place[3]
    height = own.shape[1]
    for which, out in ((3, both), (2, over), (1, across), (0, own)):
        y = relative(place, core, which, 0)[1] >> 1
        right = jnp.concatenate([columns_own[y], columns_other[y]], 0)
        for step in range(4):
            row = relative(place, core, which, step)[0]
            start = pl.multiple_of(row * height, height)
            out[step] = plan(lambda kind: rows_t[kind, pl.ds(start, height), :], right).astype(bf16)


def plan_first(rows_of, right):
    return dot_nn(rows_of(0), right)


def plan_second(rows_of, right):
    grad_in = dot_nn(rows_of(2), right[:, 0:256])
    grad_out = dot_nn(rows_of(1), right[:, 256:512])
    grad_o = dot_nn(rows_of(3), right[:, 512:768])
    grad_v = dot_nn(rows_of(0), right[:, 768:1024])
    return jnp.concatenate(
        [
            grad_in[:, :128],
            grad_in[:, 128:] + grad_out[:, :128],
            grad_out[:, 128:],
            grad_o[:, :128],
            grad_o[:, 128:] + grad_v[:, :128],
            grad_v[:, 128:],
        ],
        1,
    )


def weight_grads(plan, place, columns_own, columns_other, own_rows, other_rows, height, lanes, microseconds):
    features, slots = own_rows[0].shape[1:]
    kinds = sum(rows.shape[0] for rows in own_rows)
    out = shape((4, height, lanes), bf16)
    return pl.pallas_call(
        functools.partial(weight_grads_kernel, plan, len(own_rows)),
        out_shape=(out,) * 4,
        in_specs=[smem] + [vmem] * (2 + 2 * len(own_rows)),
        out_specs=[vmem] * 4,
        scratch_shapes=[pltpu.VMEM((kinds, features, 2 * slots), bf16)],
        cost_estimate=cost(microseconds),
        compiler_params=params(20),
        name="weight_grads",
    )(place, columns_own, columns_other, *own_rows, *other_rows)


def table_kernel(digit, staged, span, place, grads, ids, buckets, sums, after, *refs):
    if staged:
        mine, theirs, small, total, spatial = refs
    else:
        total, spatial = refs
    hops = ids.shape[0]
    groups = grads.shape[0]
    heads = groups * 8
    high_count = total.shape[0] // heads
    total[...] = jnp.zeros_like(total)
    spatial[...] = jnp.zeros_like(spatial)
    digits = lax.broadcasted_iota(i32, (digit, 128), 0).astype(f32).astype(bf16)
    kinds = lax.broadcasted_iota(i32, (heads, 128), 0).astype(f32).astype(bf16)
    one = jnp.ones((), bf16)
    zero = jnp.zeros((), bf16)

    def body(i, carry):
        lefts, rights, plain, kind_rights = [], [], [], []
        for j in range(span):
            row = i * span + j
            piece = jnp.concatenate([grads[group, row] for group in range(groups)], 0).astype(bf16)
            bucket = buckets[pl.ds(row, 1), :].astype(f32).astype(bf16)
            plain.append(piece)
            kind_rights.append(jnp.where(jnp.broadcast_to(bucket, (heads, 128)) == kinds, one, zero))
            for hop in range(hops):
                value = ids[hop, pl.ds(row, 1), :].astype(f32)
                high = jnp.floor((value + 0.5) * (1.0 / digit))
                low = value - high * digit
                low = jnp.broadcast_to(low.astype(bf16), (digit, 128))
                high = jnp.broadcast_to(high.astype(bf16), (heads, 128))
                rights.append(jnp.where(low == digits, one, zero))
                lefts.append(
                    jnp.concatenate(
                        [jnp.where(high == jnp.full((), k, bf16), piece, zero) for k in range(high_count)], 0
                    )
                )
        total[...] += dot_nt(jnp.concatenate(lefts, 1), jnp.concatenate(rights, 1))
        spatial[...] += dot_nt(jnp.concatenate(plain, 1), jnp.concatenate(kind_rights, 1))
        return carry

    lax.fori_loop(0, grads.shape[1] // span, body, 0)
    if staged:
        core = place[3]
        for other, out in ((0, mine), (1, theirs)):
            for which in range(4):
                pieces = []
                for step in range(4):
                    row, column = relative(place, core ^ other, which, step)
                    start = pl.multiple_of(row * heads + column * 8, 8)
                    pieces.append(total[pl.ds(start, 8), :] * (1.0 / hops))
                out[which * 8 : (which + 1) * 8, :] = jnp.concatenate(pieces, 1)
        spread = []
        for group in range(4):
            spread += [spatial[group * 8 : (group + 1) * 8, :], jnp.zeros((8, 128 - heads), f32)]
        lanes = sums.shape[1]
        spread.append(jnp.zeros((8, lanes - 512), f32))
        spread = jnp.concatenate(spread, 1)
        small[0:16, :] = sums[...]
        small[16:24, :] = spread
        theirs[32:48, :] = sums[...]
        theirs[48:56, :] = spread


def table_grads(place, grads, ids, buckets, sums, after, digit, edges, staged):
    heads = grads.shape[0] * 8
    total = (edges // digit * heads, digit)
    lanes = sums.shape[1]
    outs = (shape((32, lanes), f32), shape((56, lanes), f32), shape((24, lanes), f32))
    inner = (shape(total, f32), shape((heads, heads), f32))
    return pl.pallas_call(
        functools.partial(table_kernel, digit, staged, 8),
        out_shape=outs if staged else inner,
        in_specs=[smem] + [vmem] * 4 + [untouched],
        out_specs=[vmem] * (3 if staged else 2),
        scratch_shapes=[pltpu.VMEM(a.shape, f32) for a in inner] if staged else [],
        cost_estimate=cost(15),
        compiler_params=params(12),
        name="table_grads",
    )(place, grads, ids, buckets, sums, after)


def meet_core_kernel(mine, small, got, out, keep):
    keep[...] = mine[0:16, :] + got[0:16, :]
    out[0:8, :] = mine[24:32, :] + got[24:32, :]
    out[8:16, :] = mine[16:24, :] + got[16:24, :]
    out[16:40, :] = small[...] + got[32:56, :]


def meet_second_kernel(keep, sent, got, out, kept):
    out[0:8, :] = keep[8:16, :] + got[0:8, :]
    out[8:32, :] = sent[16:40, :] + got[16:40, :]
    kept[...] = keep[0:8, :] + got[8:16, :]


def meet_first_kernel(kept, sent, got, *outs):
    own = kept[...] + got[0:8, :]
    small = sent[8:32, :] + got[8:32, :]
    digit = own.shape[1] // 4
    for step, out in enumerate(outs):
        out[0:8, 0:digit] = own[:, step * digit : (step + 1) * digit]
        out[0:8, digit:] = jnp.zeros((8, 3 * digit), f32)
        out[8:32, :] = small


def finish_kernel(place, own, first, second, third, edge, spatial, *outs):
    total = own[...] + first[...] + second[...] + third[...]
    digit = edge.shape[1]
    edge[...] = total[0:8, 0:digit]
    group = place[4]
    for i, out in enumerate(outs[:6]):
        out[...] = total[8 + i : 9 + i, :].reshape(out.shape)
    width = outs[6].shape[0]
    heads = total[16:17]
    hidden = total[20:21]
    kinds = total[24:32, 0:128]
    for other in range(1, 4):
        heads = jnp.where(group == other, total[16 + other : 17 + other], heads)
        hidden = jnp.where(group == other, total[20 + other : 21 + other], hidden)
        kinds = jnp.where(group == other, total[24:32, other * 128 : (other + 1) * 128], kinds)
    outs[6][...] = heads[:, :width].reshape(outs[6].shape)
    outs[7][...] = heads[:, 512 : 512 + width].reshape(outs[7].shape)
    outs[8][...] = hidden[:, :width].reshape(outs[8].shape)
    spatial[...] = kinds[:, : spatial.shape[1]]


def small_call(kernel, name, outs, *args):
    return pl.pallas_call(
        kernel,
        out_shape=outs,
        in_specs=[smem if args[i].ndim == 1 else vmem for i in range(len(args))],
        out_specs=[vmem] * len(outs),
        cost_estimate=cost(0.7),
        compiler_params=params(4),
        name=name,
    )(*args)


class Links:
    def __init__(self):
        self.core = self.hop(lambda z, x, y, c: (z, x, y, 1 - c))
        self.first = self.hop(lambda z, x, y, c: (z, x, 1 - y, c) if c else (z, 1 - x, y, c))
        self.second = self.hop(lambda z, x, y, c: (z, 1 - x, y, c) if c else (z, x, 1 - y, c))
        self.along_x = self.hop(lambda z, x, y, c: (z, 1 - x, y, c))
        self.along_y = self.hop(lambda z, x, y, c: (z, x, 1 - y, c))
        self.along_z = [self.hop(lambda z, x, y, c, k=k: (z ^ k, x, y, c)) for k in (1, 2, 3)]

    def hop(self, move):
        index = lambda z, x, y, c: (z * 2 + x) * 4 + y * 2 + c
        spots = [(z, x, y, c) for z in range(4) for x in range(2) for y in range(2) for c in range(2)]
        return [(index(*spot), index(*move(*spot))) for spot in spots]


def send(values, hop):
    return lax.ppermute(values, ("dp", "mp"), hop)


def gather_staged(links, own):
    stack = jnp.stack([own] + [send(own, hop) for hop in links.along_z])
    across = send(stack, links.first)
    over = send(stack, links.second)
    both = send(across, links.second)
    mine = (stack, across, over, both)
    return mine + tuple(send(part, links.core) for part in mine)


def add_rounded(*terms):
    total = terms[0].astype(f32)
    for term in terms[1:]:
        total = total + term.astype(f32)
    return total.astype(bf16)


def reduce_staged(links, own, across, over, both):
    across = add_rounded(across, send(both, links.second))
    own = add_rounded(own, send(over, links.second), send(across, links.first))
    total = own[0].astype(f32)
    for step, hop in enumerate(links.along_z):
        total = total + send(own[step + 1], hop).astype(f32)
    return total


def local(
    layer_in,
    node_counts,
    spatial_ids,
    path_ids,
    ln1_gain,
    ln1_bias,
    w_q,
    w_k,
    w_v,
    q_bias,
    v_bias,
    spatial_table,
    edge_table,
    w_o,
    o_bias,
    ln2_gain,
    ln2_bias,
    w_in,
    in_bias,
    w_out,
    out_bias,
    cotangent,
):
    dp_size, mp_size = lax.axis_size("dp"), lax.axis_size("mp")
    dp_index, mp_index = lax.axis_index("dp"), lax.axis_index("mp")
    staged = dp_size == 8 and mp_size == 4
    height, width = w_q.shape
    features = layer_in.shape[1]
    edges = edge_table.shape[0] * dp_size
    heads = spatial_table.shape[1]
    kinds = spatial_table.shape[0]
    hops = path_ids.shape[1]
    share = edges // 4
    digit = edges // 8
    place = jnp.stack([dp_index // 2, dp_index % 2, mp_index // 2, mp_index % 2, mp_index]).astype(i32)
    ids, buckets, h1, rows_early = prepare(
        place, spatial_ids, path_ids, layer_in, ln1_gain, ln1_bias, cotangent, kinds - 1
    )
    if staged:
        links = Links()
        first, second, own_biases = pack(w_q, w_k, w_v, w_o, w_in, w_out, q_bias, v_bias, in_bias)
        table_t = edge_table.T
        neighbour = send(table_t, links.along_x)
        even = dp_index % 2 == 0
        pair = jnp.concatenate(
            [jnp.where(even, table_t, neighbour), jnp.where(even, neighbour, table_t)], 0
        )
        chunks = [pair] + [send(pair, hop) for hop in links.along_z]
        parts_a = gather_staged(links, first)
        parts_b = gather_staged(links, second)
        y_biases = send(own_biases, links.along_y)
        bias_parts = (own_biases, y_biases, send(own_biases, links.core), send(y_biases, links.core))
        lookup_place = place
    else:
        gathered = [
            lax.all_gather(lax.all_gather(w, "dp", axis=0, tiled=True), "mp", axis=0)
            for w in (w_q, w_k, w_v, w_o, w_in, w_out)
        ]
        parts_a = (jnp.concatenate(gathered[:4], 2),)
        parts_b = (jnp.concatenate(gathered[4:], 2),)
        bias_parts = (lax.all_gather(jnp.stack([q_bias, v_bias, in_bias]), "mp", axis=0, tiled=False),)
        table_t = lax.all_gather(edge_table, "dp", axis=0, tiled=True).T
        chunks = [table_t[:, i * share : (i + 1) * share] for i in range(4)]
        lookup_place = jnp.zeros((5,), i32)
    edge_sums = None
    for step in range(4):
        edge_sums = lookup(lookup_place, chunks[step], ids, edge_sums, step, share)

    weights, biases, transposed, value_win, probs, att_low, mid, h2 = attend(
        place, node_counts, h1, edge_sums, buckets, spatial_table,
        layer_in, o_bias, ln2_gain, ln2_bias, parts_a, bias_parts,
    )
    layer_out, grad_mid, grad_att_t, grad_values, mine_b, theirs_b, rows_late, sums = feed(
        place, mid, h2, weights, biases, out_bias, ln2_gain, cotangent, att_low, probs, parts_b
    )
    after = sums
    if staged:
        rows_b = (rows_early, rows_late)
        other_rows_b = tuple(send(rows, links.core) for rows in rows_b)
        pieces_b = weight_grads(
            plan_second, place, mine_b, send(theirs_b, links.core), rows_b, other_rows_b, height, 4 * width, 4
        )
        grads_b = reduce_staged(links, *pieces_b)
        after = pieces_b[0]
    score_grads, mine_a, theirs_a, grad_layer_in, sums = attend_back(
        place, probs, value_win, transposed, grad_att_t, grad_values, weights,
        layer_in, ln1_gain, grad_mid, sums, after,
    )
    if staged:
        pieces_a = weight_grads(
            plan_first, place, mine_a, send(theirs_a, links.core),
            (rows_early[0:1],), (other_rows_b[0][0:1],), height, 2 * width, 2,
        )
        grads_a = reduce_staged(links, *pieces_a)
        mine, theirs, small = table_grads(
            place, score_grads, ids, buckets, sums, pieces_a[0], digit, edges, True
        )
        sent, keep = small_call(
            meet_core_kernel, "meet_core", (shape((40, features), f32), shape((16, features), f32)),
            mine, small, send(theirs, links.core),
        )
        sent, keep = small_call(
            meet_second_kernel, "meet_second", (shape((32, features), f32), shape((8, features), f32)),
            keep, sent, send(sent, links.second),
        )
        outs = small_call(
            meet_first_kernel, "meet_first", (shape((32, features), f32),) * 4,
            keep, sent, send(sent, links.first),
        )
        got = [send(out, hop) for out, hop in zip(outs[1:], links.along_z)]
        grad_edge, grad_spatial, *rows = small_call(
            finish_kernel, "finish",
            (shape((8, digit), f32), shape((8, kinds), f32))
            + (shape((features,), f32),) * 6
            + (shape((width,), f32),) * 3,
            place, outs[0], *got,
        )
        grad_edge = grad_edge.T
        grad_spatial = grad_spatial.T
        grad_w_q, grad_w_k = (grads_a[:, i * width : (i + 1) * width] for i in range(2))
        grad_w_in, grad_w_out, grad_w_o, grad_w_v = (
            grads_b[:, i * width : (i + 1) * width] for i in range(4)
        )
    else:
        contract = lambda a, b: lax.dot_general(
            a, b, (((1,), (1,)), ((), ())), preferred_element_type=f32
        )

        def unmix(mine, theirs):
            even = mp_index % 2 == 0
            cores = jnp.where(even, jnp.stack([mine, theirs], 1), jnp.stack([theirs, mine], 1))
            return cores.reshape(4, *mine.shape[1:])

        def scatter(rows_t, columns):
            grads = contract(rows_t, columns)
            grads = jnp.transpose(grads, (1, 0, 2))
            grads = lax.psum_scatter(grads, "mp", scatter_dimension=0, tiled=False)
            return lax.psum_scatter(grads, "dp", scatter_dimension=0, tiled=True)

        columns_a, columns_b = unmix(mine_a, theirs_a), unmix(mine_b, theirs_b)
        grad_w_q, grad_w_k = (
            scatter(rows_early[0], columns_a[:, :, i * width : (i + 1) * width]) for i in range(2)
        )
        grad_w_v = scatter(rows_early[0], columns_b[:, :, 1024 - width :])
        grad_w_in = scatter(rows_late[0], columns_b[:, :, :width])
        grad_w_out = scatter(rows_early[1], columns_b[:, :, 512 - width : 512])
        grad_w_o = scatter(rows_late[1], columns_b[:, :, 512 : 512 + width])
        table, spatial = table_grads(place, score_grads, ids, buckets, sums, sums, digit, edges, False)
        table = table.reshape(-1, heads, digit).transpose(0, 2, 1).reshape(edges, heads) / hops
        table = lax.psum_scatter(table, "dp", scatter_dimension=0, tiled=True)
        table = lax.psum(table, "mp")
        grad_edge = lax.dynamic_slice_in_dim(table, mp_index * 8, 8, 1)
        totals, spatial = lax.psum((sums, spatial), ("dp", "mp"))
        grad_spatial = lax.dynamic_slice_in_dim(spatial[:, :kinds], mp_index * 8, 8, 0).T
        head_sums = lax.dynamic_slice_in_dim(totals, 8 + mp_index, 1, 0)[0]
        hidden_sums = lax.dynamic_slice_in_dim(totals, 12 + mp_index, 1, 0)[0]
        rows = [totals[i] for i in range(6)]
        rows += [head_sums[:width], head_sums[512 : 512 + width], hidden_sums[:width]]
    return (
        layer_out,
        grad_layer_in,
        rows[0],
        rows[1],
        grad_w_q,
        grad_w_k,
        grad_w_v,
        rows[6],
        rows[7],
        grad_spatial,
        grad_edge,
        grad_w_o,
        rows[2],
        rows[3],
        rows[4],
        grad_w_in,
        rows[8],
        grad_w_out,
        rows[5],
    )


def solution(mesh):
    return jax.shard_map(
        local,
        mesh=mesh,
        in_specs=(
            P(("dp", "mp"), None),
            P("dp"),
            P("dp", None, None),
            P("dp", None, None, None),
            P(),
            P(),
            P("dp", "mp"),
            P("dp", "mp"),
            P("dp", "mp"),
            P("mp"),
            P("mp"),
            P(),
            P("dp", None),
            P("dp", "mp"),
            P(),
            P(),
            P(),
            P("dp", "mp"),
            P("mp"),
            P("dp", "mp"),
            P(),
            P(("dp", "mp"), None),
        ),
        out_specs=(
            P(("dp", "mp"), None),
            P(("dp", "mp"), None),
            P(),
            P(),
            P("dp", "mp"),
            P("dp", "mp"),
            P("dp", "mp"),
            P("mp"),
            P("mp"),
            P(None, "mp"),
            P("dp", "mp"),
            P("dp", "mp"),
            P(),
            P(),
            P(),
            P("dp", "mp"),
            P("mp"),
            P("dp", "mp"),
            P(),
        ),
        check_vma=False,
    )
```

time: 222 us -> 173 us (0.78)
  local copies, waits for them, and re-layouts: 24.7 us -> 9.36 us
  waiting for transfers between devices: 57.7 us -> 44.4 us
  starting transfers between devices: 58.4 us -> 50.7 us
  blocking collectives: 5.37 us -> 0 us
  Pallas kernels: 66.6 us -> 62.1 us
  other arithmetic: 6.85 us -> 2.73 us
    ppermute x46 -> x49, waiting for transfers between devices: 57.7 us -> 44.4 us  [send(): return lax.ppermute(values, ('dp', 'mp'), hop)]
    ppermute x46 -> x49, starting transfers between devices: 58.4 us -> 50.7 us  [send(): return lax.ppermute(values, ('dp', 'mp'), hop)]
    unnamed x81 -> x48, local copies, waits for them, and re-layouts: 13.8 us -> 7.66 us
    all_gather x1 -> x0, blocking collectives: 5.37 us -> none  [local(): lax.all_gather(jnp.stack([q_bias, v_bias, in_bias]), 'mp', axis=0, tiled=...]
    pallas_call x4 -> x8, Pallas kernels: 20.3 us -> 15.4 us  [the longest x1 5.43 us: attend(): pl.pallas_call(functools.partial(attend_kernel, len(parts), len(bias_part...]
    squeeze x7 -> x0, local copies, waits for them, and re-layouts: 4.01 us -> none  [the longest x1 0.67 us: local(): totals[0]]
    reshape x8 -> x0, local copies, waits for them, and re-layouts: 3.98 us -> none  [the longest x6 3.81 us: local(): row = lambda v: v.reshape(1, features)]
    convert_element_type x4, other arithmetic: 4.32 us -> 0.55 us  [add_rounded(): return total.astype(bf16)]
  transfers between devices with their start and end apart: 46 -> 49, of which waited for: 23 -> 13; matrix products, arithmetic and copies ran while one was open for 7% -> 2% of each run, Pallas kernels for 17% -> 28%
where the time goes in v2:
time: 173 us; the launch traced here: 170 us
  Pallas kernels  62.1 us (36%)
  starting transfers between devices  50.7 us (29%)
  waiting for transfers between devices  44.4 us (26%)
  local copies, waits for them, and re-layouts  9.36 us (5%)
  other arithmetic  2.73 us (2%)
    ppermute x49, starting transfers between devices, send(): return lax.ppermute(values, ('dp', 'mp'), hop)  50.7 us
    ppermute x49, waiting for transfers between devices, send(): return lax.ppermute(values, ('dp', 'mp'), hop)  44.4 us
    pallas_call x4, Pallas kernels, lookup(): pl.pallas_call(functools.partial(lookup_kernel, first, step, share), out_...  24.5 us
    pallas_call x1, Pallas kernels, table_grads(): pl.pallas_call(functools.partial(table_kernel, digit, staged, 8), out_sha...  14.9 us
    unnamed x48, local copies, waits for them, and re-layouts  7.66 us
    pallas_call x1, Pallas kernels, feed(): pl.pallas_call(functools.partial(feed_kernel, len(parts)), grid=(1,), out...  5.71 us
    pallas_call x1, Pallas kernels, attend(): pl.pallas_call(functools.partial(attend_kernel, len(parts), len(bias_part...  5.43 us
    pallas_call x1, Pallas kernels, attend_back(): pl.pallas_call(attend_back_kernel, out_shape=(shape((groups, slots, 8, sl...  5.23 us
  transfers between devices with their start and end apart: 49, of which 13 were waited for; matrix products, arithmetic and copies ran while one was open for 2% of the time, Pallas kernels for 28%

profile of v2, /device:TPU:0, one launch (start us, length us, event | category | flops | bytes accessed | tf_op | source)
XLA Modules:
  0.0 170.5 jit_solution(9479265594266183812)
XLA Ops:
  8.2 3.1 %collective-permute-start.4 = (bf16[96,768]{1,0:T(8,128)(2,1)S(1)}, bf16[96,768]{1,0:T(8,128)(2,1)}, u32[]{:S(2)}, u32[]{:S(2)}) collective-permute-start(bf16[96,768]{1,0:T(8,128)(2,1)S(1)} %get-tuple-element.80), channel_id=1, source_target_pairs={{0,8},{1,9},{2,10},{3,11},{4,12},{5,13},{6,14},{7,15},{8,0},{9,1},... | collective-permute-start | bytes 442376 | tf_op jit(solution)/shard_map/ppermute | solution.py:741
  11.3 2.6 %collective-permute-start.5 = (bf16[96,768]{1,0:T(8,128)(2,1)S(1)}, bf16[96,768]{1,0:T(8,128)(2,1)}, u32[]{:S(2)}, u32[]{:S(2)}) collective-permute-start(bf16[96,768]{1,0:T(8,128)(2,1)S(1)} %get-tuple-element.80), channel_id=1, source_target_pairs={{0,16},{1,17},{2,18},{3,19},{4,20},{5,21},{6,22},{7,23},{8,24},{9,... | collective-permute-start | bytes 442376 | tf_op jit(solution)/shard_map/ppermute | solution.py:741
  13.9 1.7 %collective-permute-start = (bf16[32,192]{1,0:T(8,128)(2,1)S(1)}, bf16[32,192]{1,0:T(8,128)(2,1)S(1)}, u32[]{:S(2)}, u32[]{:S(2)}) collective-permute-start(bf16[32,192]{1,0:T(8,128)(2,1)S(1)} %bitcast.44), channel_id=1, source_target_pairs={{0,4},{1,5},{2,6},{3,7},{4,0},{5,1},{6,2},{7,3},{8,12},{9,13},{10,... | collective-permute-start | bytes 36872 | tf_op jit(solution)/shard_map/ppermute | solution.py:741
  18.1 3.5 %collective-permute-start.18 = (bf16[96,384]{1,0:T(8,128)(2,1)S(1)}, bf16[96,384]{1,0:T(8,128)(2,1)S(1)}, u32[]{:S(2)}, u32[]{:S(2)}) collective-permute-start(bf16[96,384]{1,0:T(8,128)(2,1)S(1)} %get-tuple-element.88), channel_id=1, source_target_pairs={{0,16},{1,17},{2,18},{3,19},{4,20},{5,21},{6,22},{7,23},{8,24},{9,... | collective-permute-start | bytes 221192 | tf_op jit(solution)/shard_map/ppermute | solution.py:741
  21.6 6.1 %lookup.4.refs_0_ = s32[16,128,128]{2,1,0:T(8,128)S(1)} custom-call(s32[5]{0:T(128)S(1)} %stack.53.place, bf16[64,192]{1,0:T(8,128)(2,1)S(1)} %pad_maximum_fusion.2.chunk, s32[5,128,128]{2,1,0:T(8,128)S(1)} %get-tuple-element.78.ids), custom_call_target="tpu_custom_call" | custom-call | flops 6899999744 | bytes 1024 | tf_op jit(solution)/shard_map/lookup/pallas_call | solution.py:219
  28.0 1.5 collective-permute-start.14
  31.9 2.3 %collective-permute-done.3.chunk = bf16[64,192]{1,0:T(8,128)(2,1)S(1)} collective-permute-done((bf16[64,192]{1,0:T(8,128)(2,1)S(1)}, bf16[64,192]{1,0:T(8,128)(2,1)S(1)}, u32[]{:S(2)}, u32[]{:S(2)}) %collective-permute-start.3) | collective-permute-done | bytes 24608 | tf_op jit(solution)/shard_map/ppermute | solution.py:741
  34.9 6.1 %lookup.5.refs_0_ = s32[16,128,128]{2,1,0:T(8,128)S(1)} custom-call(s32[5]{0:T(128)S(1)} %stack.53.place, bf16[64,192]{1,0:T(8,128)(2,1)S(1)} %collective-permute-done.3.chunk, s32[5,128,128]{2,1,0:T(8,128)S(1)} %get-tuple-element.78.ids, s32[16,128,128]{2,1,0:T(8,128)S(1)} %lookup.4.refs_0_), custom_call_target="tpu_custom_call", output_to_operand_aliasing={{}: (3, {})} | custom-call | flops 6899999744 | bytes 1024 | tf_op jit(solution)/shard_map/lookup/pallas_call | solution.py:219
  41.6 3.7 %collective-permute-start.2 = (bf16[64,192]{1,0:T(8,128)(2,1)S(1)}, bf16[64,192]{1,0:T(8,128)(2,1)S(1)}, u32[]{:S(2)}, u32[]{:S(2)}) collective-permute-start(bf16[64,192]{1,0:T(8,128)(2,1)S(1)} %pad_maximum_fusion.2.chunk), channel_id=1, source_target_pairs={{0,16},{1,17},{2,18},{3,19},{4,20},{5,21},{6,22},{7,23},{8,24},{9,... | collective-permute-start | bytes 73736 | tf_op jit(solution)/shard_map/ppermute | solution.py:741
  47.0 1.6 collective-permute-start.21
  49.1 1.5 collective-permute-start.9
  50.6 6.1 %lookup.6.refs_0_ = s32[16,128,128]{2,1,0:T(8,128)S(1)} custom-call(s32[5]{0:T(128)S(1)} %stack.53.place, bf16[64,192]{1,0:T(8,128)(2,1)S(1)} %collective-permute-done.2.chunk, s32[5,128,128]{2,1,0:T(8,128)S(1)} %get-tuple-element.78.ids, s32[16,128,128]{2,1,0:T(8,128)S(1)} %lookup.5.refs_0_), custom_call_target="tpu_custom_call", output_to_operand_aliasing={{}: (3, {})} | custom-call | flops 6899999744 | bytes 1024 | tf_op jit(solution)/shard_map/lookup/pallas_call | solution.py:219
  56.9 1.5 collective-permute-start.22
  59.1 2.7 %collective-permute-done.8.refs_2_ = bf16[4,96,768]{2,1,0:T(8,128)(2,1)S(1)} collective-permute-done((bf16[4,96,768]{2,1,0:T(8,128)(2,1)S(1)}, bf16[4,96,768]{2,1,0:T(8,128)(2,1)S(1)}, u32[]{:S(2)}, u32[]{:S(2)}) %collective-permute-start.8) | collective-permute-done | bytes 589856 | tf_op jit(solution)/shard_map/ppermute | solution.py:741
  63.1 5.0 %collective-permute-done.9.refs_3_ = bf16[4,96,768]{2,1,0:T(8,128)(2,1)S(1)} collective-permute-done((bf16[4,96,768]{2,1,0:T(8,128)(2,1)S(1)}, bf16[4,96,768]{2,1,0:T(8,128)(2,1)S(1)}, u32[]{:S(2)}, u32[]{:S(2)}) %collective-permute-start.9) | collective-permute-done | bytes 589856 | tf_op jit(solution)/shard_map/ppermute | solution.py:741
  69.4 6.3 %lookup.7.edge_sums = s32[16,128,128]{2,1,0:T(8,128)S(1)} custom-call(s32[5]{0:T(128)S(1)} %stack.53.place, bf16[64,192]{1,0:T(8,128)(2,1)S(1)} %collective-permute-done.1.chunk, s32[5,128,128]{2,1,0:T(8,128)S(1)} %get-tuple-element.78.ids, s32[16,128,128]{2,1,0:T(8,128)S(1)} %lookup.6.refs_0_), custom_call_target="tpu_custom_call", output_to_operand_aliasing={{}: (3, {})} | custom-call | flops 6899999744 | bytes 1024 | tf_op jit(solution)/shard_map/lookup/pallas_call | solution.py:219
  76.9 5.4 %attend.1 = (bf16[4,768,768]{2,1,0:T(8,128)(2,1)S(1)}, f32[4,3,192]{2,1,0:T(4,128)S(1)}, bf16[4,384,128]{2,1,0:T(8,128)(2,1)S(1)}, bf16[4,128,256]{2,1,0:T(8,128...) custom-call(s32[5]{0:T(128)S(1)} %stack.53.place, ...), custom_call_target="tpu_custom_call" | custom-call | flops 8049999872 | bytes 1024 | tf_op jit(solution)/shard_map/attend/pallas_call | solution.py:336
  82.4 5.7 %feed.1 = (f32[128,768]{1,0:T(8,128)}, f32[128,768]{1,0:T(8,128)S(1)}, bf16[4,256,128]{2,1,0:T(8,128)(2,1)S(1)}, bf16[4,128,256]{2,1,0:T(8,128)(2,1)S(1)}, bf16[...) custom-call(s32[5]{0:T(128)S(1)} %stack.53.place, ...), custom_call_target="tpu_custom_call" | custom-call | flops 8049999872 | bytes 1024 | tf_op jit(solution)/shard_map/feed/pallas_call | solution.py:444
  88.7 1.9 %collective-permute-done.28.refs_2_ = bf16[2,768,128]{2,1,0:T(8,128)(2,1)S(1)} collective-permute-done((bf16[2,768,128]{2,1,0:T(8,128)(2,1)S(1)}, bf16[2,768,128]{2,1,0:T(8,128)(2,1)S(1)}, u32[]{:S(2)}, u32[]{:S(2)}) %collective-permute-start.28) | collective-permute-done | bytes 393248 | tf_op jit(solution)/shard_map/ppermute | solution.py:741
  91.1 2.3 %weight_grads.2 = (bf16[4,96,768]{2,1,0:T(8,128)(2,1)S(1)}, bf16[4,96,768]{2,1,0:T(8,128)(2,1)S(1)}, bf16[4,96,768]{2,1,0:T(8,128)(2,1)S(1)}, bf16[4,96,768]{2,1,0:T(8,128)(2,1)S(1)}) custom-call(s32[5]{0:T(128)S(1)} %stack.53.place, bf16[2,128,1024]{2,1,0:T(8,128)(2,1)S(1)} %get-tuple-element.96.columns_own, ...), custom_call_target="tpu_custom_call" | custom-call | flops 4600000000 | bytes 1024 | tf_op jit(solution)/shard_map/weight_grads/pallas_call | solution.py:576
  93.4 5.2 %attend_back.1 = (f32[4,128,8,128]{3,2,1,0:T(8,128)S(1)}, bf16[2,128,384]{2,1,0:T(8,128)(2,1)S(1)}, bf16[2,128,384]{2,1,0:T(8,128)(2,1)S(1)}, f32[128,768]{1,0:T(8,128)}, f32[16,768]{1,0:T(8,128)S(1)}) custom-call(s32[5]{0:T(128)S(1)} %stack.53.place, f32[32,128,128]{2,1,0:T(8,128)S(1)} %get-tuple-element.87.probs_in, ...), custom_call_target="tpu_custom_call" | custom-call | flops 8049999872 | bytes 1024 | tf_op jit(solution)/shard_map/attend_back/pallas_call | solution.py:509
  102.2 14.9 %table_grads.1 = (f32[32,768]{1,0:T(8,128)S(1)}, f32[56,768]{1,0:T(8,128)S(1)}, f32[24,768]{1,0:T(8,128)S(1)}) custom-call(s32[5]{0:T(128)S(1)} %stack.53.place, f32[4,128,8,128]{3,2,1,0:T(8,128)S(1)} %get-tuple-element.102.grads, s32[5,128,128]{2,1,0:T(8,128)S(1)} %get-tuple-element.78.ids, s32[128,128]{1,0:T(8,128)S(1)} %copy-done.22, ...), custom_call_target="tpu_custom_call" | custom-call | flops 17250000896 | bytes 1024 | tf_op jit(solution)/shard_map/table_grads/pallas_call | solution.py:657
  121.0 13.8 %collective-permute-done.32.got = f32[40,768]{1,0:T(8,128)S(1)} collective-permute-done((f32[40,768]{1,0:T(8,128)S(1)}, f32[40,768]{1,0:T(8,128)S(1)}, u32[]{:S(2)}, u32[]{:S(2)}) %collective-permute-start.32) | collective-permute-done | bytes 122912 | tf_op jit(solution)/shard_map/ppermute | solution.py:741
  137.1 2.4 %collective-permute-done.33.got = f32[32,768]{1,0:T(8,128)S(1)} collective-permute-done((f32[32,768]{1,0:T(8,128)S(1)}, f32[32,768]{1,0:T(8,128)S(1)}, u32[]{:S(2)}, u32[]{:S(2)}) %collective-permute-start.33) | collective-permute-done | bytes 98336 | tf_op jit(solution)/shard_map/ppermute | solution.py:741
  139.7 3.6 %collective-permute-start.35 = (f32[32,768]{1,0:T(8,128)S(1)}, f32[32,768]{1,0:T(8,128)S(1)}, u32[]{:S(2)}, u32[]{:S(2)}) collective-permute-start(f32[32,768]{1,0:T(8,128)S(1)} %get-tuple-element.116), channel_id=1, source_target_pairs={{0,16},{1,17},{2,18},{3,19},{4,20},{5,21},{6,22},{7,23},{8,24},{9,... | collective-permute-start | bytes 294920 | tf_op jit(solution)/shard_map/ppermute | solution.py:741
  144.6 6.2 %collective-permute-done.35.second = f32[32,768]{1,0:T(8,128)S(1)} collective-permute-done((f32[32,768]{1,0:T(8,128)S(1)}, f32[32,768]{1,0:T(8,128)S(1)}, u32[]{:S(2)}, u32[]{:S(2)}) %collective-permute-start.35) | collective-permute-done | bytes 98336 | tf_op jit(solution)/shard_map/ppermute | solution.py:741
  150.9 3.2 %collective-permute-start.42 = (bf16[96,384]{1,0:T(8,128)(2,1)S(1)}, bf16[96,384]{1,0:T(8,128)(2,1)S(1)}, u32[]{:S(2)}, u32[]{:S(2)}) collective-permute-start(bf16[96,384]{1,0:T(8,128)(2,1)S(1)} %get-tuple-element.143), channel_id=1, source_target_pairs={{0,24},{1,25},{2,26},{3,27},{4,28},{5,29},{6,30},{7,31},{8,16},{9,... | collective-permute-start | bytes 221192 | tf_op jit(solution)/shard_map/ppermute | solution.py:741
  155.3 2.5 %collective-permute-done.41 = bf16[96,384]{1,0:T(8,128)(2,1)S(1)} collective-permute-done((bf16[96,384]{1,0:T(8,128)(2,1)S(1)}, bf16[96,384]{1,0:T(8,128)(2,1)S(1)}, u32[]{:S(2)}, u32[]{:S(2)}) %collective-permute-start.41) | collective-permute-done | bytes 73760 | tf_op jit(solution)/shard_map/ppermute | solution.py:741
  158.1 2.0 %collective-permute-start.46 = (bf16[96,768]{1,0:T(8,128)(2,1)S(1)}, bf16[96,768]{1,0:T(8,128)(2,1)S(1)}, u32[]{:S(2)}, u32[]{:S(2)}) collective-permute-start(bf16[96,768]{1,0:T(8,128)(2,1)S(1)} %get-tuple-element.135), channel_id=1, source_target_pairs={{0,8},{1,9},{2,10},{3,11},{4,12},{5,13},{6,14},{7,15},{8,0},{9,1},... | collective-permute-start | bytes 442376 | tf_op jit(solution)/shard_map/ppermute | solution.py:741
  160.2 1.7 %collective-permute-start.47 = (bf16[96,768]{1,0:T(8,128)(2,1)S(1)}, bf16[96,768]{1,0:T(8,128)(2,1)S(1)}, u32[]{:S(2)}, u32[]{:S(2)}) collective-permute-start(bf16[96,768]{1,0:T(8,128)(2,1)S(1)} %get-tuple-element.137), channel_id=1, source_target_pairs={{0,16},{1,17},{2,18},{3,19},{4,20},{5,21},{6,22},{7,23},{8,24},{9,... | collective-permute-start | bytes 442376 | tf_op jit(solution)/shard_map/ppermute | solution.py:741
  163.4 1.7 collective-permute-done.46
  165.0 4.6 %collective-permute-done.47 = bf16[96,768]{1,0:T(8,128)(2,1)S(1)} collective-permute-done((bf16[96,768]{1,0:T(8,128)(2,1)S(1)}, bf16[96,768]{1,0:T(8,128)(2,1)S(1)}, u32[]{:S(2)}, u32[]{:S(2)}) %collective-permute-start.47) | collective-permute-done | bytes 147488 | tf_op jit(solution)/shard_map/ppermute | solution.py:741
  (147 shorter events, 37.0 us)
Async XLA Ops:
  8.2 19.4 %collective-permute-start.4 = (bf16[96,768]{1,0:T(8,128)(2,1)S(1)}, bf16[96,768]{1,0:T(8,128)(2,1)}, u32[]{:S(2)}, u32[]{:S(2)}) collective-permute-start(bf16[96,768]{1,0:T(8,128)(2,1)S(1)} %get-tuple-element.80), channel_id=1, source_target_pairs={{0,8},{1,9},{2,10},{3,11},{4,12},{5,13},{6,14},{7,15},{8,0},{9,1},... | collective-permute-start | bytes 442376 | tf_op jit(solution)/shard_map/ppermute | solution.py:741
  11.3 16.6 %collective-permute-start.5 = (bf16[96,768]{1,0:T(8,128)(2,1)S(1)}, bf16[96,768]{1,0:T(8,128)(2,1)}, u32[]{:S(2)}, u32[]{:S(2)}) collective-permute-start(bf16[96,768]{1,0:T(8,128)(2,1)S(1)} %get-tuple-element.80), channel_id=1, source_target_pairs={{0,16},{1,17},{2,18},{3,19},{4,20},{5,21},{6,22},{7,23},{8,24},{9,... | collective-permute-start | bytes 442376 | tf_op jit(solution)/shard_map/ppermute | solution.py:741
  13.9 15.6 %collective-permute-start.6 = (bf16[96,768]{1,0:T(8,128)(2,1)S(1)}, bf16[96,768]{1,0:T(8,128)(2,1)}, u32[]{:S(2)}, u32[]{:S(2)}) collective-permute-start(bf16[96,768]{1,0:T(8,128)(2,1)S(1)} %get-tuple-element.80), channel_id=1, source_target_pairs={{0,24},{1,25},{2,26},{3,27},{4,28},{5,29},{6,30},{7,31},{8,16},{9,... | collective-permute-start | bytes 442376 | tf_op jit(solution)/shard_map/ppermute | solution.py:741
  15.6 25.5 %collective-permute-start.17 = (bf16[96,384]{1,0:T(8,128)(2,1)S(1)}, bf16[96,384]{1,0:T(8,128)(2,1)}, u32[]{:S(2)}, u32[]{:S(2)}) collective-permute-start(bf16[96,384]{1,0:T(8,128)(2,1)S(1)} %get-tuple-element.88), channel_id=1, source_target_pairs={{0,8},{1,9},{2,10},{3,11},{4,12},{5,13},{6,14},{7,15},{8,0},{9,1},... | collective-permute-start | bytes 221192 | tf_op jit(solution)/shard_map/ppermute | solution.py:741
  18.1 23.5 %collective-permute-start.18 = (bf16[96,384]{1,0:T(8,128)(2,1)S(1)}, bf16[96,384]{1,0:T(8,128)(2,1)S(1)}, u32[]{:S(2)}, u32[]{:S(2)}) collective-permute-start(bf16[96,384]{1,0:T(8,128)(2,1)S(1)} %get-tuple-element.88), channel_id=1, source_target_pairs={{0,16},{1,17},{2,18},{3,19},{4,20},{5,21},{6,22},{7,23},{8,24},{9,... | collective-permute-start | bytes 221192 | tf_op jit(solution)/shard_map/ppermute | solution.py:741
  27.7 17.6 %collective-permute-start.19 = (bf16[96,384]{1,0:T(8,128)(2,1)S(1)}, bf16[96,384]{1,0:T(8,128)(2,1)S(1)}, u32[]{:S(2)}, u32[]{:S(2)}) collective-permute-start(bf16[96,384]{1,0:T(8,128)(2,1)S(1)} %get-tuple-element.88), channel_id=1, source_target_pairs={{0,24},{1,25},{2,26},{3,27},{4,28},{5,29},{6,30},{7,31},{8,16},{9,... | collective-permute-start | bytes 221192 | tf_op jit(solution)/shard_map/ppermute | solution.py:741
  28.0 13.0 %collective-permute-start.14 = (f32[3,192]{1,0:T(4,128)S(1)}, f32[3,192]{1,0:T(4,128)S(1)}, u32[]{:S(2)}, u32[]{:S(2)}) collective-permute-start(f32[3,192]{1,0:T(4,128)S(1)} %get-tuple-element.81.refs_8_), channel_id=1, source_target_pairs={{0,2},{1,3},{2,0},{3,1},{4,6},{5,7},{6,4},{7,5},{8,10},{9,11},{10,... | collective-permute-start | bytes 6920 | tf_op jit(solution)/shard_map/ppermute | solution.py:741
  34.2 14.9 %collective-permute-start.7 = (bf16[4,96,768]{2,1,0:T(8,128)(2,1)S(1)}, bf16[4,96,768]{2,1,0:T(8,128)(2,1)S(1)}, u32[]{:S(2)}, u32[]{:S(2)}) collective-permute-start(bf16[4,96,768]{2,1,0:T(8,128)(2,1)S(1)} %pad_maximum_fusion.refs_0_), channel_id=1, source_target_pairs={{0,4},{1,3},{2,6},{3,1},{4,0},{5,7},{6,2},{7,5},{8,12},{9,11},{10,... | collective-permute-start | bytes 1769480 | tf_op jit(solution)/shard_map/ppermute | solution.py:741
  41.6 7.0 %collective-permute-start.2 = (bf16[64,192]{1,0:T(8,128)(2,1)S(1)}, bf16[64,192]{1,0:T(8,128)(2,1)S(1)}, u32[]{:S(2)}, u32[]{:S(2)}) collective-permute-start(bf16[64,192]{1,0:T(8,128)(2,1)S(1)} %pad_maximum_fusion.2.chunk), channel_id=1, source_target_pairs={{0,16},{1,17},{2,18},{3,19},{4,20},{5,21},{6,22},{7,23},{8,24},{9,... | collective-permute-start | bytes 73736 | tf_op jit(solution)/shard_map/ppermute | solution.py:741
  45.3 11.5 %collective-permute-start.1 = (bf16[64,192]{1,0:T(8,128)(2,1)S(1)}, bf16[64,192]{1,0:T(8,128)(2,1)S(1)}, u32[]{:S(2)}, u32[]{:S(2)}) collective-permute-start(bf16[64,192]{1,0:T(8,128)(2,1)S(1)} %pad_maximum_fusion.2.chunk), channel_id=1, source_target_pairs={{0,24},{1,25},{2,26},{3,27},{4,28},{5,29},{6,30},{7,31},{8,16},{9,... | collective-permute-start | bytes 73736 | tf_op jit(solution)/shard_map/ppermute | solution.py:741
  46.9 10.0 %collective-permute-start.20 = (bf16[4,96,384]{2,1,0:T(8,128)(2,1)S(1)}, bf16[4,96,384]{2,1,0:T(8,128)(2,1)S(1)}, u32[]{:S(2)}, u32[]{:S(2)}) collective-permute-start(bf16[4,96,384]{2,1,0:T(8,128)(2,1)S(1)} %pad_maximum_fusion.1.refs_0_), channel_id=1, source_target_pairs={{0,4},{1,3},{2,6},{3,1},{4,0},{5,7},{6,2},{7,5},{8,12},{9,11},{10,... | collective-permute-start | bytes 884744 | tf_op jit(solution)/shard_map/ppermute | solution.py:741
  47.0 11.4 %collective-permute-start.21 = (bf16[4,96,384]{2,1,0:T(8,128)(2,1)S(1)}, bf16[4,96,384]{2,1,0:T(8,128)(2,1)S(1)}, u32[]{:S(2)}, u32[]{:S(2)}) collective-permute-start(bf16[4,96,384]{2,1,0:T(8,128)(2,1)S(1)} %pad_maximum_fusion.1.refs_0_), channel_id=1, source_target_pairs={{0,2},{1,5},{2,0},{3,7},{4,6},{5,1},{6,4},{7,3},{8,10},{9,13},{10,... | collective-permute-start | bytes 884744 | tf_op jit(solution)/shard_map/ppermute | solution.py:741
  48.6 13.1 %collective-permute-start.8 = (bf16[4,96,768]{2,1,0:T(8,128)(2,1)S(1)}, bf16[4,96,768]{2,1,0:T(8,128)(2,1)S(1)}, u32[]{:S(2)}, u32[]{:S(2)}) collective-permute-start(bf16[4,96,768]{2,1,0:T(8,128)(2,1)S(1)} %pad_maximum_fusion.refs_0_), channel_id=1, source_target_pairs={{0,2},{1,5},{2,0},{3,7},{4,6},{5,1},{6,4},{7,3},{8,10},{9,13},{10,... | collective-permute-start | bytes 1769480 | tf_op jit(solution)/shard_map/ppermute | solution.py:741
  49.1 19.0 %collective-permute-start.9 = (bf16[4,96,768]{2,1,0:T(8,128)(2,1)S(1)}, bf16[4,96,768]{2,1,0:T(8,128)(2,1)S(1)}, u32[]{:S(2)}, u32[]{:S(2)}) collective-permute-start(bf16[4,96,768]{2,1,0:T(8,128)(2,1)S(1)} %collective-permute-done.7.refs_1_), channel_id=1, source_target_pairs={{0,2},{1,5},{2,0},{3,7},{4,6},{5,1},{6,4},{7,3},{8,10},{9,13},{10,... | collective-permute-start | bytes 1769480 | tf_op jit(solution)/shard_map/ppermute | solution.py:741
  56.8 19.0 %collective-permute-start.10 = (bf16[4,96,768]{2,1,0:T(8,128)(2,1)S(1)}, bf16[4,96,768]{2,1,0:T(8,128)(2,1)S(1)}, u32[]{:S(2)}, u32[]{:S(2)}) collective-permute-start(bf16[4,96,768]{2,1,0:T(8,128)(2,1)S(1)} %pad_maximum_fusion.refs_0_), channel_id=1, source_target_pairs={{0,1},{1,0},{2,3},{3,2},{4,5},{5,4},{6,7},{7,6},{8,9},{9,8},{10,11... | collective-permute-start | bytes 1769480 | tf_op jit(solution)/shard_map/ppermute | solution.py:741
  56.9 18.8 %collective-permute-start.22 = (bf16[4,96,384]{2,1,0:T(8,128)(2,1)S(1)}, bf16[4,96,384]{2,1,0:T(8,128)(2,1)S(1)}, u32[]{:S(2)}, u32[]{:S(2)}) collective-permute-start(bf16[4,96,384]{2,1,0:T(8,128)(2,1)S(1)} %collective-permute-done.20.refs_1_), channel_id=1, source_target_pairs={{0,2},{1,5},{2,0},{3,7},{4,6},{5,1},{6,4},{7,3},{8,10},{9,13},{10,... | collective-permute-start | bytes 884744 | tf_op jit(solution)/shard_map/ppermute | solution.py:741
  58.4 17.9 %collective-permute-start.11 = (bf16[4,96,768]{2,1,0:T(8,128)(2,1)S(1)}, bf16[4,96,768]{2,1,0:T(8,128)(2,1)S(1)}, u32[]{:S(2)}, u32[]{:S(2)}) collective-permute-start(bf16[4,96,768]{2,1,0:T(8,128)(2,1)S(1)} %collective-permute-done.7.refs_1_), channel_id=1, source_target_pairs={{0,1},{1,0},{2,3},{3,2},{4,5},{5,4},{6,7},{7,6},{8,9},{9,8},{10,11... | collective-permute-start | bytes 1769480 | tf_op jit(solution)/shard_map/ppermute | solution.py:741
  61.8 14.6 %collective-permute-start.12 = (bf16[4,96,768]{2,1,0:T(8,128)(2,1)S(1)}, bf16[4,96,768]{2,1,0:T(8,128)(2,1)S(1)}, u32[]{:S(2)}, u32[]{:S(2)}) collective-permute-start(bf16[4,96,768]{2,1,0:T(8,128)(2,1)S(1)} %collective-permute-done.8.refs_2_), channel_id=1, source_target_pairs={{0,1},{1,0},{2,3},{3,2},{4,5},{5,4},{6,7},{7,6},{8,9},{9,8},{10,11... | collective-permute-start | bytes 1769480 | tf_op jit(solution)/shard_map/ppermute | solution.py:741
  68.1 8.7 %collective-permute-start.13 = (bf16[4,96,768]{2,1,0:T(8,128)(2,1)S(1)}, bf16[4,96,768]{2,1,0:T(8,128)(2,1)S(1)}, u32[]{:S(2)}, u32[]{:S(2)}) collective-permute-start(bf16[4,96,768]{2,1,0:T(8,128)(2,1)S(1)} %collective-permute-done.9.refs_3_), channel_id=1, source_target_pairs={{0,1},{1,0},{2,3},{3,2},{4,5},{5,4},{6,7},{7,6},{8,9},{9,8},{10,11... | collective-permute-start | bytes 1769480 | tf_op jit(solution)/shard_map/ppermute | solution.py:741
  98.8 37.0 %collective-permute-start.44 = (bf16[4,96,768]{2,1,0:T(8,128)(2,1)S(1)}, bf16[4,96,768]{2,1,0:T(8,128)(2,1)S(1)}, u32[]{:S(2)}, u32[]{:S(2)}) collective-permute-start(bf16[4,96,768]{2,1,0:T(8,128)(2,1)S(1)} %get-tuple-element.125), channel_id=1, source_target_pairs={{0,2},{1,5},{2,0},{3,7},{4,6},{5,1},{6,4},{7,3},{8,10},{9,13},{10,... | collective-permute-start | bytes 1769480 | tf_op jit(solution)/shard_map/ppermute | solution.py:741
  101.3 19.3 %collective-permute-start.38 = (bf16[4,96,384]{2,1,0:T(8,128)(2,1)S(1)}, bf16[4,96,384]{2,1,0:T(8,128)(2,1)S(1)}, u32[]{:S(2)}, u32[]{:S(2)}) collective-permute-start(bf16[4,96,384]{2,1,0:T(8,128)(2,1)S(1)} %get-tuple-element.122), channel_id=1, source_target_pairs={{0,2},{1,5},{2,0},{3,7},{4,6},{5,1},{6,4},{7,3},{8,10},{9,13},{10,... | collective-permute-start | bytes 884744 | tf_op jit(solution)/shard_map/ppermute | solution.py:741
  117.2 40.7 %collective-permute-start.43 = (bf16[4,96,768]{2,1,0:T(8,128)(2,1)S(1)}, bf16[4,96,768]{2,1,0:T(8,128)(2,1)S(1)}, u32[]{:S(2)}, u32[]{:S(2)}) collective-permute-start(bf16[4,96,768]{2,1,0:T(8,128)(2,1)S(1)} %get-tuple-element.123), channel_id=1, source_target_pairs={{0,2},{1,5},{2,0},{3,7},{4,6},{5,1},{6,4},{7,3},{8,10},{9,13},{10,... | collective-permute-start | bytes 1769480 | tf_op jit(solution)/shard_map/ppermute | solution.py:741
  118.4 21.3 %collective-permute-start.37 = (bf16[4,96,384]{2,1,0:T(8,128)(2,1)S(1)}, bf16[4,96,384]{2,1,0:T(8,128)(2,1)S(1)}, u32[]{:S(2)}, u32[]{:S(2)}) collective-permute-start(bf16[4,96,384]{2,1,0:T(8,128)(2,1)S(1)} %get-tuple-element.120), channel_id=1, source_target_pairs={{0,2},{1,5},{2,0},{3,7},{4,6},{5,1},{6,4},{7,3},{8,10},{9,13},{10,... | collective-permute-start | bytes 884744 | tf_op jit(solution)/shard_map/ppermute | solution.py:741
  119.3 15.5 %collective-permute-start.32 = (f32[40,768]{1,0:T(8,128)S(1)}, f32[40,768]{1,0:T(8,128)S(1)}, u32[]{:S(2)}, u32[]{:S(2)}) collective-permute-start(f32[40,768]{1,0:T(8,128)S(1)} %get-tuple-element.111.sent), channel_id=1, source_target_pairs={{0,2},{1,5},{2,0},{3,7},{4,6},{5,1},{6,4},{7,3},{8,10},{9,13},{10,... | collective-permute-start | bytes 368648 | tf_op jit(solution)/shard_map/ppermute | solution.py:741
  120.6 22.6 %collective-permute-start.39 = (bf16[4,96,384]{2,1,0:T(8,128)(2,1)S(1)}, bf16[4,96,384]{2,1,0:T(8,128)(2,1)S(1)}, u32[]{:S(2)}, u32[]{:S(2)}) collective-permute-start(bf16[4,96,384]{2,1,0:T(8,128)(2,1)S(1)} %add_convert_fusion.3), channel_id=1, source_target_pairs={{0,4},{1,3},{2,6},{3,1},{4,0},{5,7},{6,2},{7,5},{8,12},{9,11},{10,... | collective-permute-start | bytes 884744 | tf_op jit(solution)/shard_map/ppermute | solution.py:741
  135.9 21.9 %collective-permute-start.45 = (bf16[4,96,768]{2,1,0:T(8,128)(2,1)S(1)}, bf16[4,96,768]{2,1,0:T(8,128)(2,1)S(1)}, u32[]{:S(2)}, u32[]{:S(2)}) collective-permute-start(bf16[4,96,768]{2,1,0:T(8,128)(2,1)S(1)} %add_convert_fusion.1), channel_id=1, source_target_pairs={{0,4},{1,3},{2,6},{3,1},{4,0},{5,7},{6,2},{7,5},{8,12},{9,11},{10,... | collective-permute-start | bytes 1769480 | tf_op jit(solution)/shard_map/ppermute | solution.py:741
  139.7 11.2 %collective-permute-start.35 = (f32[32,768]{1,0:T(8,128)S(1)}, f32[32,768]{1,0:T(8,128)S(1)}, u32[]{:S(2)}, u32[]{:S(2)}) collective-permute-start(f32[32,768]{1,0:T(8,128)S(1)} %get-tuple-element.116), channel_id=1, source_target_pairs={{0,16},{1,17},{2,18},{3,19},{4,20},{5,21},{6,22},{7,23},{8,24},{9,... | collective-permute-start | bytes 294920 | tf_op jit(solution)/shard_map/ppermute | solution.py:741
  143.2 7.7 %collective-permute-start.36 = (f32[32,768]{1,0:T(8,128)S(1)}, f32[32,768]{1,0:T(8,128)S(1)}, u32[]{:S(2)}, u32[]{:S(2)}) collective-permute-start(f32[32,768]{1,0:T(8,128)S(1)} %get-tuple-element.117), channel_id=1, source_target_pairs={{0,24},{1,25},{2,26},{3,27},{4,28},{5,29},{6,30},{7,31},{8,16},{9,... | collective-permute-start | bytes 294920 | tf_op jit(solution)/shard_map/ppermute | solution.py:741
  144.2 11.1 %collective-permute-start.40 = (bf16[96,384]{1,0:T(8,128)(2,1)S(1)}, bf16[96,384]{1,0:T(8,128)(2,1)S(1)}, u32[]{:S(2)}, u32[]{:S(2)}) collective-permute-start(bf16[96,384]{1,0:T(8,128)(2,1)S(1)} %get-tuple-element.142), channel_id=1, source_target_pairs={{0,8},{1,9},{2,10},{3,11},{4,12},{5,13},{6,14},{7,15},{8,0},{9,1},... | collective-permute-start | bytes 221192 | tf_op jit(solution)/shard_map/ppermute | solution.py:741
  150.9 6.9 %collective-permute-start.41 = (bf16[96,384]{1,0:T(8,128)(2,1)S(1)}, bf16[96,384]{1,0:T(8,128)(2,1)S(1)}, u32[]{:S(2)}, u32[]{:S(2)}) collective-permute-start(bf16[96,384]{1,0:T(8,128)(2,1)S(1)} %get-tuple-element.144), channel_id=1, source_target_pairs={{0,16},{1,17},{2,18},{3,19},{4,20},{5,21},{6,22},{7,23},{8,24},{9,... | collective-permute-start | bytes 221192 | tf_op jit(solution)/shard_map/ppermute | solution.py:741
  160.2 9.4 %collective-permute-start.47 = (bf16[96,768]{1,0:T(8,128)(2,1)S(1)}, bf16[96,768]{1,0:T(8,128)(2,1)S(1)}, u32[]{:S(2)}, u32[]{:S(2)}) collective-permute-start(bf16[96,768]{1,0:T(8,128)(2,1)S(1)} %get-tuple-element.137), channel_id=1, source_target_pairs={{0,16},{1,17},{2,18},{3,19},{4,20},{5,21},{6,22},{7,23},{8,24},{9,... | collective-permute-start | bytes 442376 | tf_op jit(solution)/shard_map/ppermute | solution.py:741
  161.9 7.7 %collective-permute-start.48 = (bf16[96,768]{1,0:T(8,128)(2,1)S(1)}, bf16[96,768]{1,0:T(8,128)(2,1)S(1)}, u32[]{:S(2)}, u32[]{:S(2)}) collective-permute-start(bf16[96,768]{1,0:T(8,128)(2,1)S(1)} %get-tuple-element.136), channel_id=1, source_target_pairs={{0,24},{1,25},{2,26},{3,27},{4,28},{5,29},{6,30},{7,31},{8,16},{9,... | collective-permute-start | bytes 442376 | tf_op jit(solution)/shard_map/ppermute | solution.py:741
  (41 other events, 300.6 us)

commit v3 on v2

--- a/solution.py
+++ b/solution.py
@@ -73,37 +73,65 @@
     return row, column
 
 
-def pack_kernel(wq, wk, wv, wo, wi, wu, bq, bv, bi, first, second, biases, held, sems):
+def three_terms(values):
+    terms = []
+    for _ in range(3):
+        term = values.astype(bf16)
+        terms.append(term)
+        values = values - term.astype(f32)
+    return terms
+
+
+def pack_first_kernel(wq, wk, wv, wo, bq, bv, bi, weights, biases, held, sems):
     copies = [
-        pltpu.make_async_copy(source, held.at[i], sems.at[i])
-        for i, source in enumerate((wq, wk, wv, wo, wi, wu))
+        pltpu.make_async_copy(source, held.at[i], sems.at[i]) for i, source in enumerate((wq, wk, wv, wo))
     ]
     for copy in copies:
         copy.start()
-    for i, bias in enumerate((bq, bv, bi)):
-        biases[i : i + 1, :] = as_row(bias)
+    row = jnp.concatenate([as_row(bq), as_row(bv), as_row(bi)], 1)
+    lanes = weights.shape[1]
+    row = jnp.concatenate([row, jnp.zeros((1, lanes - row.shape[1]), f32)], 1)
+    terms = [term.astype(f32) for term in three_terms(row)]
+    biases[...] = jnp.concatenate(terms + [jnp.zeros((13, lanes), f32)], 0).astype(bf16)
     for copy in copies:
         copy.wait()
-    first[...] = jnp.concatenate([held[i] for i in range(4)], 1)
-    second[...] = jnp.concatenate([held[4], held[5]], 1)
-
-
-def pack(wq, wk, wv, wo, wi, wu, bq, bv, bi):
+    weights[...] = jnp.concatenate([held[i] for i in range(4)], 1)
+
+
+def pack_first(wq, wk, wv, wo, bq, bv, bi):
     rows, width = wq.shape
     return pl.pallas_call(
-        pack_kernel,
-        out_shape=(
-            shape((rows, 4 * width), bf16),
-            shape((rows, 2 * width), bf16),
-            shape((3, width), f32),
-        ),
-        in_specs=[hbm] * 6 + [vmem] * 3,
-        out_specs=[vmem] * 3,
-        scratch_shapes=[pltpu.VMEM((6, rows, width), bf16), pltpu.SemaphoreType.DMA((6,))],
+        pack_first_kernel,
+        out_shape=(shape((rows, 4 * width), bf16), shape((16, 4 * width), bf16)),
+        in_specs=[hbm] * 4 + [vmem] * 3,
+        out_specs=[vmem] * 2,
+        scratch_shapes=[pltpu.VMEM((4, rows, width), bf16), pltpu.SemaphoreType.DMA((4,))],
+        cost_estimate=cost(1),
+        compiler_params=params(62),
+        name="pack_first",
+    )(wq, wk, wv, wo, bq, bv, bi)
+
+
+def pack_second_kernel(place, wi, wu, edge, neighbour, out):
+    rows = wi.shape[0]
+    out[0:rows, :] = jnp.concatenate([wi[...], wu[...]], 1)
+    even = place[1] == 0
+    mine, other = edge[...].astype(f32), neighbour[...].astype(f32)
+    low, high = jnp.where(even, mine, other), jnp.where(even, other, mine)
+    out[rows:, :] = jnp.concatenate([low, high], 1).astype(bf16)
+
+
+def pack_second(place, wi, wu, edge, neighbour):
+    rows, width = wi.shape
+    return pl.pallas_call(
+        pack_second_kernel,
+        out_shape=shape((rows + edge.shape[0], 2 * width), bf16),
+        in_specs=[smem] + [vmem] * 4,
+        out_specs=vmem,
+        cost_estimate=cost(1),
         compiler_params=params(4),
-        cost_estimate=cost(1),
-        name="pack",
-    )(wq, wk, wv, wo, wi, wu, bq, bv, bi)
+        name="pack_second",
+    )(place, wi, wu, edge, neighbour)
 
 
 def prepare_kernel(virtual, place, spatial, path, layer_in, gain, bias, cotangent, ids, buckets, h1, rows_t):
@@ -174,11 +202,7 @@
         previous, total, table = refs
     hops, slots = ids.shape[0], ids.shape[1]
     pairs = total.shape[0]
-    heads = 2 * pairs
-    rows = chunk.shape[1]
-    packed = jnp.concatenate(
-        [quantize(chunk[i * heads : (i + 1) * heads, :], edge_unit) for i in range(share // rows)], 1
-    )
+    packed = quantize(chunk[chunk.shape[0] - 2 * pairs :, :], edge_unit)
     blocks = share // 128
     for pair in range(pairs):
         head = (pair // 4) * 8 + pair % 4
@@ -210,8 +234,8 @@
     lax.fori_loop(0, slots // 8, body, 0)
 
 
-def lookup(place, chunk, ids, previous, step, share):
-    heads = chunk.shape[0] // (share // chunk.shape[1])
+def lookup(place, chunk, ids, previous, step, heads):
+    share = chunk.shape[1]
     pairs = heads // 2
     slots = ids.shape[1]
     first = previous is None
@@ -229,26 +253,22 @@
     )(place, chunk, ids, *(() if first else (previous,)))
 
 
-def assemble(place, parts, whole):
+def assemble(place, parts, whole, biases=None):
     if len(parts) == 1:
         whole[...] = parts[0][...]
         return
     core = place[3]
-    rows = parts[0].shape[1]
+    rows = whole.shape[1] // 8
     for other in range(2):
         for which in range(4):
+            part = parts[other * 4 + which]
             for step in range(4):
                 row, column = relative(place, core ^ other, which, step)
                 start = pl.multiple_of(row * rows, rows)
-                whole[column, pl.ds(start, rows), :] = parts[other * 4 + which][step]
-
-
-def collect_biases(place, parts, whole):
-    if len(parts) == 1:
-        whole[...] = parts[0][...]
-        return
-    for i, part in enumerate(parts):
-        whole[(place[2] ^ (i % 2)) * 2 + (place[3] ^ (i // 2))] = part[...]
+                whole[column, pl.ds(start, rows), :] = part[step * rows : (step + 1) * rows, :]
+            if biases is not None:
+                terms = part[4 * rows : 4 * rows + 16, :].astype(f32)
+                biases[column] = terms[0:1] + terms[1:2] + terms[2:3]
 
 
 def head_masks(width, offset, depth):
@@ -261,14 +281,17 @@
 
 
 def attend_kernel(
-    n_parts, n_biases, place, counts, h1, edge_sums, buckets, spatial_table, layer_in, o_bias, gain, bias, *refs
+    n_parts, place, counts, h1, edge_sums, buckets, spatial_table, layer_in, o_bias, gain, bias, *refs
 ):
-    parts, bias_parts, refs = refs[:n_parts], refs[n_parts : n_parts + n_biases], refs[n_parts + n_biases :]
+    parts, refs = refs[:n_parts], refs[n_parts:]
     weights, biases, transposed, value_win, probs_out, att_low, mid, h2 = refs
-    assemble(place, parts, weights)
-    collect_biases(place, bias_parts, biases)
+    if n_parts == 2:
+        assemble(place, parts[:1], weights)
+        biases[...] = parts[1][...]
+    else:
+        assemble(place, parts, weights, biases)
     slots = h1.shape[0]
-    groups, width = biases.shape[0], biases.shape[2]
+    groups, width = biases.shape[0], biases.shape[2] // 4
     depth = width // 8
     pad = 256 - width
     hops = 5
@@ -283,9 +306,9 @@
         natural = dot_nn(h1[...], weights[group, :, : 3 * width + pad])
         row_bias = jnp.concatenate(
             [
-                biases[group, 0:1, :],
+                biases[group, 0:1, :width],
                 jnp.zeros((1, width), f32),
-                biases[group, 1:2, :],
+                biases[group, 0:1, width : 2 * width],
                 jnp.zeros((1, pad), f32),
             ],
             1,
@@ -328,16 +351,16 @@
     h2[...] = (normed * as_row(gain) + as_row(bias)).astype(bf16)
 
 
-def attend(place, counts, h1, edge_sums, buckets, spatial_table, layer_in, o_bias, gain, bias, parts, bias_parts):
+def attend(place, counts, h1, edge_sums, buckets, spatial_table, layer_in, o_bias, gain, bias, parts):
     slots, features = h1.shape
-    width = bias_parts[0].shape[-1]
+    width = parts[0].shape[-1] // 4
     heads = spatial_table.shape[1]
     groups = heads // 8
     return pl.pallas_call(
-        functools.partial(attend_kernel, len(parts), len(bias_parts)),
+        functools.partial(attend_kernel, len(parts)),
         out_shape=(
             shape((groups, features, 4 * width), bf16),
-            shape((groups, 3, width), f32),
+            shape((groups, 1, 4 * width), f32),
             shape((groups, 2 * width, slots), bf16),
             shape((groups, slots, 256), bf16),
             shape((heads, slots, slots), f32),
@@ -345,14 +368,14 @@
             shape((slots, features), f32),
             shape((slots, features), bf16),
         ),
-        in_specs=[smem, smem] + [vmem] * (8 + len(parts) + len(bias_parts)),
+        in_specs=[smem, smem] + [vmem] * (8 + len(parts)),
         out_specs=[vmem] * 8,
         cost_estimate=cost(7),
         compiler_params=params(28),
         name="attend",
     )(
         place, counts, h1, edge_sums, buckets, spatial_table, layer_in, o_bias, gain, bias,
-        *parts, *bias_parts,
+        *parts,
     )
 
 
@@ -369,7 +392,7 @@
     layer_out, grad_mid, grad_att_t, grad_values, mine, theirs, rows_t, sums, weights = refs[n_parts:]
     assemble(place, parts, weights)
     slots, features = mid.shape
-    width = biases.shape[2]
+    width = biases.shape[2] // 4
     depth = width // 8
     pad = 256 - width
     lanes = lax.broadcasted_iota(i32, (1, 256), 1)
@@ -382,7 +405,9 @@
     order = group_order(place)
     for side, y, group in order:
         columns = theirs if side else mine
-        in_bias = jnp.concatenate([biases[group, 2:3, :], jnp.zeros((1, pad), f32)], 1)
+        in_bias = jnp.concatenate(
+            [biases[group, 0:1, 2 * width : 3 * width], jnp.zeros((1, pad), f32)], 1
+        )
         pre = dot_nn(h2_value, weights[group, :, :256]) + in_bias
         cdf = 0.5 * (1.0 + lax.erf(pre * (0.5**0.5)))
         slope = cdf + pre * jnp.exp(-0.5 * pre * pre) * 0.3989422804014327
@@ -428,7 +453,7 @@
 
 def feed(place, mid, h2, weights_a, biases, out_bias, gain, cotangent, att_low, probs, parts):
     slots, features = mid.shape
-    groups, width = biases.shape[0], biases.shape[2]
+    groups, width = biases.shape[0], biases.shape[2] // 4
     whole = lambda array: pl.BlockSpec(array.shape, lambda i: (0,) * len(array.shape))
     outs = (
         shape((slots, features), f32),
@@ -741,8 +766,11 @@
     return lax.ppermute(values, ("dp", "mp"), hop)
 
 
-def gather_staged(links, own):
-    stack = jnp.stack([own] + [send(own, hop) for hop in links.along_z])
+def around(links, own):
+    return [own] + [send(own, hop) for hop in links.along_z]
+
+
+def spread(links, stack):
     across = send(stack, links.first)
     over = send(stack, links.second)
     both = send(across, links.second)
@@ -807,37 +835,32 @@
     )
     if staged:
         links = Links()
-        first, second, own_biases = pack(w_q, w_k, w_v, w_o, w_in, w_out, q_bias, v_bias, in_bias)
+        first, own_biases = pack_first(w_q, w_k, w_v, w_o, q_bias, v_bias, in_bias)
         table_t = edge_table.T
-        neighbour = send(table_t, links.along_x)
-        even = dp_index % 2 == 0
-        pair = jnp.concatenate(
-            [jnp.where(even, table_t, neighbour), jnp.where(even, neighbour, table_t)], 0
-        )
-        chunks = [pair] + [send(pair, hop) for hop in links.along_z]
-        parts_a = gather_staged(links, first)
-        parts_b = gather_staged(links, second)
-        y_biases = send(own_biases, links.along_y)
-        bias_parts = (own_biases, y_biases, send(own_biases, links.core), send(y_biases, links.core))
+        second = pack_second(place, w_in, w_out, table_t, send(table_t, links.along_x))
+        parts_a = spread(links, jnp.concatenate(around(links, first) + [own_biases], 0))
+        chunks = around(links, second)
+        parts_b = spread(links, jnp.concatenate([chunk[:height] for chunk in chunks], 0))
         lookup_place = place
     else:
         gathered = [
             lax.all_gather(lax.all_gather(w, "dp", axis=0, tiled=True), "mp", axis=0)
             for w in (w_q, w_k, w_v, w_o, w_in, w_out)
         ]
-        parts_a = (jnp.concatenate(gathered[:4], 2),)
+        bias_row = jnp.concatenate([q_bias, v_bias, in_bias, jnp.zeros((width,), f32)])
+        bias_row = lax.all_gather(bias_row[None], "mp", axis=0)
+        parts_a = (jnp.concatenate(gathered[:4], 2), bias_row)
         parts_b = (jnp.concatenate(gathered[4:], 2),)
-        bias_parts = (lax.all_gather(jnp.stack([q_bias, v_bias, in_bias]), "mp", axis=0, tiled=False),)
         table_t = lax.all_gather(edge_table, "dp", axis=0, tiled=True).T
         chunks = [table_t[:, i * share : (i + 1) * share] for i in range(4)]
         lookup_place = jnp.zeros((5,), i32)
     edge_sums = None
     for step in range(4):
-        edge_sums = lookup(lookup_place, chunks[step], ids, edge_sums, step, share)
+        edge_sums = lookup(lookup_place, chunks[step], ids, edge_sums, step, heads)
 
     weights, biases, transposed, value_win, probs, att_low, mid, h2 = attend(
         place, node_counts, h1, edge_sums, buckets, spatial_table,
-        layer_in, o_bias, ln2_gain, ln2_bias, parts_a, bias_parts,
+        layer_in, o_bias, ln2_gain, ln2_bias, parts_a,
     )
     layer_out, grad_mid, grad_att_t, grad_values, mine_b, theirs_b, rows_late, sums = feed(
         place, mid, h2, weights, biases, out_bias, ln2_gain, cotangent, att_low, probs, parts_b

time: 173 us -> 159 us (0.919); the launches traced: 170 us -> 158 us
  starting transfers between devices: 50.7 us -> 41.8 us
  local copies, waits for them, and re-layouts: 9.36 us -> 5.59 us
  Pallas kernels: 62.1 us -> 64.3 us
  other arithmetic: 2.73 us -> 0.69 us
    ppermute x49 -> x43, starting transfers between devices: 50.7 us -> 41.8 us  [send(): return lax.ppermute(values, ('dp', 'mp'), hop)]
    unnamed x48 -> x40, local copies, waits for them, and re-layouts: 7.66 us -> 3.85 us
    pallas_call x2 -> x3, Pallas kernels: 5.97 us -> 8.5 us  [the longest x1 5.37 us: attend(): pl.pallas_call(functools.partial(attend_kernel, len(parts)), out_shape=(s...]
    another operation x2 -> x0, other arithmetic: 2.06 us -> none  [gather_staged(): stack = jnp.stack([own] + [send(own, hop) for hop in links.along_z])]
    ppermute x49 -> x43, waiting for transfers between devices: 44.4 us -> 44.7 us  [send(): return lax.ppermute(values, ('dp', 'mp'), hop)]
  transfers between devices with their start and end apart: 49 -> 43, of which waited for: 13 -> 13; matrix products, arithmetic and copies ran while one was open for 2% -> 3% of each run, Pallas kernels for 28% -> 31%
where the time goes in v3:
time: 159 us; the launch traced here: 158 us
  Pallas kernels  64.3 us (40%)
  waiting for transfers between devices  44.7 us (28%)
  starting transfers between devices  41.8 us (26%)
  local copies, waits for them, and re-layouts  5.59 us (4%)
    ppermute x43, waiting for transfers between devices, send(): return lax.ppermute(values, ('dp', 'mp'), hop)  44.7 us
    ppermute x43, starting transfers between devices, send(): return lax.ppermute(values, ('dp', 'mp'), hop)  41.8 us
    pallas_call x4, Pallas kernels, lookup(): pl.pallas_call(functools.partial(lookup_kernel, first, step, share), out_...  24.3 us
    pallas_call x1, Pallas kernels, table_grads(): pl.pallas_call(functools.partial(table_kernel, digit, staged, 8), out_sha...  14.9 us
    pallas_call x1, Pallas kernels, feed(): pl.pallas_call(functools.partial(feed_kernel, len(parts)), grid=(1,), out...  5.69 us
    pallas_call x1, Pallas kernels, attend(): pl.pallas_call(functools.partial(attend_kernel, len(parts)), out_shape=(s...  5.37 us
    pallas_call x1, Pallas kernels, attend_back(): pl.pallas_call(attend_back_kernel, out_shape=(shape((groups, slots, 8, sl...  5.2 us
    unnamed x40, local copies, waits for them, and re-layouts  3.85 us
  transfers between devices with their start and end apart: 43, of which 13 were waited for; matrix products, arithmetic and copies ran while one was open for 3% of the time, Pallas kernels for 31%

profile of v3, /device:TPU:0, one launch (start us, length us, event | category | flops | bytes accessed | tf_op | source)
XLA Modules:
  0.0 158.4 jit_solution(11898453845517685618)
XLA Ops:
  0.7 2.5 %pack_first.1 = (bf16[96,768]{1,0:T(8,128)(2,1)}, bf16[16,768]{1,0:T(8,128)(2,1)}) custom-call(bf16[96,192]{1,0:T(8,128)(2,1)} %wq.1, bf16[96,192]{1,0:T(8,128)(2,1)} %wk.1, bf16[96,192]{1,0:T(8,128)(2,1)} %wv.1, bf16[96,192]{1,0:T(8,128)(2,1)} %wo.1, f32[192]{0:T(256)} %bq.1, f32[192]{0:T(256)} %bv.1, f32[192]{0:T(256)} %bi.1), custom_call_target="tpu_custom_call" | custom-call | flops 1150000000 | bytes 1024 | tf_op jit(solution)/shard_map/pack_first/pallas_call | solution.py:103
  3.2 3.1 %collective-permute-start.4 = (bf16[96,768]{1,0:T(8,128)(2,1)}, bf16[96,768]{1,0:T(8,128)(2,1)}, u32[]{:S(2)}, u32[]{:S(2)}) collective-permute-start(bf16[96,768]{1,0:T(8,128)(2,1)} %get-tuple-element.79), channel_id=1, source_target_pairs={{0,8},{1,9},{2,10},{3,11},{4,12},{5,13},{6,14},{7,15},{8,0},{9,1},... | collective-permute-start | bytes 442376 | tf_op jit(solution)/shard_map/ppermute | solution.py:766
  6.3 2.6 %collective-permute-start.5 = (bf16[96,768]{1,0:T(8,128)(2,1)}, bf16[96,768]{1,0:T(8,128)(2,1)}, u32[]{:S(2)}, u32[]{:S(2)}) collective-permute-start(bf16[96,768]{1,0:T(8,128)(2,1)} %get-tuple-element.79), channel_id=1, source_target_pairs={{0,16},{1,17},{2,18},{3,19},{4,20},{5,21},{6,22},{7,23},{8,24},{9,... | collective-permute-start | bytes 442376 | tf_op jit(solution)/shard_map/ppermute | solution.py:766
  8.9 1.5 collective-permute-start
  15.0 3.6 %collective-permute-start.1 = (bf16[128,384]{1,0:T(8,128)(2,1)S(1)}, bf16[128,384]{1,0:T(8,128)(2,1)S(1)}, u32[]{:S(2)}, u32[]{:S(2)}) collective-permute-start(bf16[128,384]{1,0:T(8,128)(2,1)S(1)} %pack_second.1.chunk), channel_id=1, source_target_pairs={{0,24},{1,25},{2,26},{3,27},{4,28},{5,29},{6,30},{7,31},{8,16},{9,... | collective-permute-start | bytes 294920 | tf_op jit(solution)/shard_map/ppermute | solution.py:766
  18.6 6.0 %lookup.4.refs_0_ = s32[16,128,128]{2,1,0:T(8,128)S(1)} custom-call(s32[5]{0:T(128)S(1)} %stack.23.place, bf16[128,384]{1,0:T(8,128)(2,1)S(1)} %pack_second.1.chunk, s32[5,128,128]{2,1,0:T(8,128)S(1)} %get-tuple-element.77.ids), custom_call_target="tpu_custom_call" | custom-call | flops 6899999744 | bytes 1024 | tf_op jit(solution)/shard_map/lookup/pallas_call | solution.py:243
  25.8 1.5 collective-permute-start.15
  29.2 2.6 %collective-permute-done.6 = bf16[96,768]{1,0:T(8,128)(2,1)S(1)} collective-permute-done((bf16[96,768]{1,0:T(8,128)(2,1)S(1)}, bf16[96,768]{1,0:T(8,128)(2,1)S(1)}, u32[]{:S(2)}, u32[]{:S(2)}) %collective-permute-start.6) | collective-permute-done | bytes 147488 | tf_op jit(solution)/shard_map/ppermute | solution.py:766
  32.5 6.0 %lookup.5.refs_0_ = s32[16,128,128]{2,1,0:T(8,128)S(1)} custom-call(s32[5]{0:T(128)S(1)} %stack.23.place, bf16[128,384]{1,0:T(8,128)(2,1)S(1)} %collective-permute-done.3.chunk, s32[5,128,128]{2,1,0:T(8,128)S(1)} %get-tuple-element.77.ids, s32[16,128,128]{2,1,0:T(8,128)S(1)} %lookup.4.refs_0_), custom_call_target="tpu_custom_call", output_to_operand_aliasing={{}: (3, {})} | custom-call | flops 6899999744 | bytes 1024 | tf_op jit(solution)/shard_map/lookup/pallas_call | solution.py:243
  38.6 1.6 %collective-permute-start.8 = (bf16[400,768]{1,0:T(8,128)(2,1)S(1)}, bf16[400,768]{1,0:T(8,128)(2,1)S(1)}, u32[]{:S(2)}, u32[]{:S(2)}) collective-permute-start(bf16[400,768]{1,0:T(8,128)(2,1)S(1)} %constant_dynamic-update-slice_fusion.refs_0_), channel_id=1, source_target_pairs={{0,2},{1,5},{2,0},{3,7},{4,6},{5,1},{6,4},{7,3},{8,10},{9,13},{10,... | collective-permute-start | bytes 1843208 | tf_op jit(solution)/shard_map/ppermute | solution.py:766
  40.1 5.0 %collective-permute-done.7.refs_1_ = bf16[400,768]{1,0:T(8,128)(2,1)S(1)} collective-permute-done((bf16[400,768]{1,0:T(8,128)(2,1)S(1)}, bf16[400,768]{1,0:T(8,128)(2,1)S(1)}, u32[]{:S(2)}, u32[]{:S(2)}) %collective-permute-start.7) | collective-permute-done | bytes 614432 | tf_op jit(solution)/shard_map/ppermute | solution.py:766
  45.2 2.5 %collective-permute-start.9 = (bf16[400,768]{1,0:T(8,128)(2,1)S(1)}, bf16[400,768]{1,0:T(8,128)(2,1)S(1)}, u32[]{:S(2)}, u32[]{:S(2)}) collective-permute-start(bf16[400,768]{1,0:T(8,128)(2,1)S(1)} %collective-permute-done.7.refs_1_), channel_id=1, source_target_pairs={{0,2},{1,5},{2,0},{3,7},{4,6},{5,1},{6,4},{7,3},{8,10},{9,13},{10,... | collective-permute-start | bytes 1843208 | tf_op jit(solution)/shard_map/ppermute | solution.py:766
  47.7 6.0 %lookup.6.refs_0_ = s32[16,128,128]{2,1,0:T(8,128)S(1)} custom-call(s32[5]{0:T(128)S(1)} %stack.23.place, bf16[128,384]{1,0:T(8,128)(2,1)S(1)} %collective-permute-done.2.chunk, s32[5,128,128]{2,1,0:T(8,128)S(1)} %get-tuple-element.77.ids, s32[16,128,128]{2,1,0:T(8,128)S(1)} %lookup.5.refs_0_), custom_call_target="tpu_custom_call", output_to_operand_aliasing={{}: (3, {})} | custom-call | flops 6899999744 | bytes 1024 | tf_op jit(solution)/shard_map/lookup/pallas_call | solution.py:243
  55.8 6.2 %lookup.7.edge_sums = s32[16,128,128]{2,1,0:T(8,128)S(1)} custom-call(s32[5]{0:T(128)S(1)} %stack.23.place, bf16[128,384]{1,0:T(8,128)(2,1)S(1)} %collective-permute-done.1.chunk, s32[5,128,128]{2,1,0:T(8,128)S(1)} %get-tuple-element.77.ids, s32[16,128,128]{2,1,0:T(8,128)S(1)} %lookup.6.refs_0_), custom_call_target="tpu_custom_call", output_to_operand_aliasing={{}: (3, {})} | custom-call | flops 6899999744 | bytes 1024 | tf_op jit(solution)/shard_map/lookup/pallas_call | solution.py:243
  63.3 5.4 %attend.1 = (bf16[4,768,768]{2,1,0:T(8,128)(2,1)S(1)}, f32[4,1,768]{2,1,0:T(1,128)S(1)}, bf16[4,384,128]{2,1,0:T(8,128)(2,1)S(1)}, bf16[4,128,256]{2,1,0:T(8,128...) custom-call(s32[5]{0:T(128)S(1)} %stack.23.place, ...), custom_call_target="tpu_custom_call" | custom-call | flops 8049999872 | bytes 1024 | tf_op jit(solution)/shard_map/attend/pallas_call | solution.py:359
  68.7 5.7 %feed.1 = (f32[128,768]{1,0:T(8,128)}, f32[128,768]{1,0:T(8,128)S(1)}, bf16[4,256,128]{2,1,0:T(8,128)(2,1)S(1)}, bf16[4,128,256]{2,1,0:T(8,128)(2,1)S(1)}, bf16[...) custom-call(s32[5]{0:T(128)S(1)} %stack.23.place, ...), custom_call_target="tpu_custom_call" | custom-call | flops 8049999872 | bytes 1024 | tf_op jit(solution)/shard_map/feed/pallas_call | solution.py:469
  75.4 1.6 %collective-permute-done.22.refs_2_ = bf16[2,768,128]{2,1,0:T(8,128)(2,1)S(1)} collective-permute-done((bf16[2,768,128]{2,1,0:T(8,128)(2,1)S(1)}, bf16[2,768,128]{2,1,0:T(8,128)(2,1)S(1)}, u32[]{:S(2)}, u32[]{:S(2)}) %collective-permute-start.22) | collective-permute-done | bytes 393248 | tf_op jit(solution)/shard_map/ppermute | solution.py:766
  77.5 2.3 %weight_grads.2 = (bf16[4,96,768]{2,1,0:T(8,128)(2,1)S(1)}, bf16[4,96,768]{2,1,0:T(8,128)(2,1)S(1)}, bf16[4,96,768]{2,1,0:T(8,128)(2,1)S(1)}, bf16[4,96,768]{2,1,0:T(8,128)(2,1)S(1)}) custom-call(s32[5]{0:T(128)S(1)} %stack.23.place, bf16[2,128,1024]{2,1,0:T(8,128)(2,1)S(1)} %get-tuple-element.94.columns_own, ...), custom_call_target="tpu_custom_call" | custom-call | flops 4600000000 | bytes 1024 | tf_op jit(solution)/shard_map/weight_grads/pallas_call | solution.py:601
  79.8 5.2 %attend_back.1 = (f32[4,128,8,128]{3,2,1,0:T(8,128)S(1)}, bf16[2,128,384]{2,1,0:T(8,128)(2,1)S(1)}, bf16[2,128,384]{2,1,0:T(8,128)(2,1)S(1)}, f32[128,768]{1,0:T(8,128)}, f32[16,768]{1,0:T(8,128)S(1)}) custom-call(s32[5]{0:T(128)S(1)} %stack.23.place, f32[32,128,128]{2,1,0:T(8,128)S(1)} %get-tuple-element.86.probs_in, ...), custom_call_target="tpu_custom_call" | custom-call | flops 8049999872 | bytes 1024 | tf_op jit(solution)/shard_map/attend_back/pallas_call | solution.py:534
  85.4 2.1 %collective-permute-start.38 = (bf16[4,96,768]{2,1,0:T(8,128)(2,1)S(1)}, bf16[4,96,768]{2,1,0:T(8,128)(2,1)S(1)}, u32[]{:S(2)}, u32[]{:S(2)}) collective-permute-start(bf16[4,96,768]{2,1,0:T(8,128)(2,1)S(1)} %get-tuple-element.123), channel_id=1, source_target_pairs={{0,2},{1,5},{2,0},{3,7},{4,6},{5,1},{6,4},{7,3},{8,10},{9,13},{10,... | collective-permute-start | bytes 1769480 | tf_op jit(solution)/shard_map/ppermute | solution.py:766
  89.7 14.9 %table_grads.1 = (f32[32,768]{1,0:T(8,128)S(1)}, f32[56,768]{1,0:T(8,128)S(1)}, f32[24,768]{1,0:T(8,128)S(1)}) custom-call(s32[5]{0:T(128)S(1)} %stack.23.place, f32[4,128,8,128]{3,2,1,0:T(8,128)S(1)} %get-tuple-element.100.grads, s32[5,128,128]{2,1,0:T(8,128)S(1)} %get-tuple-element.77.ids, s32[128,128]{1,0:T(8,128)S(1)} %get-tuple-element.78.buckets, ...), custom_call_target="tpu_custom_call" | custom-call | flops 17250000896 | bytes 1024 | tf_op jit(solution)/shard_map/table_grads/pallas_call | solution.py:682
  109.1 13.2 %collective-permute-done.26.got = f32[40,768]{1,0:T(8,128)S(1)} collective-permute-done((f32[40,768]{1,0:T(8,128)S(1)}, f32[40,768]{1,0:T(8,128)S(1)}, u32[]{:S(2)}, u32[]{:S(2)}) %collective-permute-start.26) | collective-permute-done | bytes 122912 | tf_op jit(solution)/shard_map/ppermute | solution.py:766
  123.2 1.4 collective-permute-start.39
  124.6 2.4 %collective-permute-done.27.got = f32[32,768]{1,0:T(8,128)S(1)} collective-permute-done((f32[32,768]{1,0:T(8,128)S(1)}, f32[32,768]{1,0:T(8,128)S(1)}, u32[]{:S(2)}, u32[]{:S(2)}) %collective-permute-start.27) | collective-permute-done | bytes 98336 | tf_op jit(solution)/shard_map/ppermute | solution.py:766
  128.5 3.0 %collective-permute-start.30 = (f32[32,768]{1,0:T(8,128)S(1)}, f32[32,768]{1,0:T(8,128)S(1)}, u32[]{:S(2)}, u32[]{:S(2)}) collective-permute-start(f32[32,768]{1,0:T(8,128)S(1)} %get-tuple-element.115), channel_id=1, source_target_pairs={{0,24},{1,25},{2,26},{3,27},{4,28},{5,29},{6,30},{7,31},{8,16},{9,... | collective-permute-start | bytes 294920 | tf_op jit(solution)/shard_map/ppermute | solution.py:766
  131.6 2.1 %collective-permute-done.28.first = f32[32,768]{1,0:T(8,128)S(1)} collective-permute-done((f32[32,768]{1,0:T(8,128)S(1)}, f32[32,768]{1,0:T(8,128)S(1)}, u32[]{:S(2)}, u32[]{:S(2)}) %collective-permute-start.28) | collective-permute-done | bytes 98336 | tf_op jit(solution)/shard_map/ppermute | solution.py:766
  133.9 5.3 %collective-permute-done.29.second = f32[32,768]{1,0:T(8,128)S(1)} collective-permute-done((f32[32,768]{1,0:T(8,128)S(1)}, f32[32,768]{1,0:T(8,128)S(1)}, u32[]{:S(2)}, u32[]{:S(2)}) %collective-permute-start.29) | collective-permute-done | bytes 98336 | tf_op jit(solution)/shard_map/ppermute | solution.py:766
  141.0 3.4 %collective-permute-done.35 = bf16[96,384]{1,0:T(8,128)(2,1)S(1)} collective-permute-done((bf16[96,384]{1,0:T(8,128)(2,1)S(1)}, bf16[96,384]{1,0:T(8,128)(2,1)S(1)}, u32[]{:S(2)}, u32[]{:S(2)}) %collective-permute-start.35) | collective-permute-done | bytes 73760 | tf_op jit(solution)/shard_map/ppermute | solution.py:766
  144.5 1.6 %collective-permute-done.36 = bf16[96,384]{1,0:T(8,128)(2,1)S(1)} collective-permute-done((bf16[96,384]{1,0:T(8,128)(2,1)S(1)}, bf16[96,384]{1,0:T(8,128)(2,1)S(1)}, u32[]{:S(2)}, u32[]{:S(2)}) %collective-permute-start.36) | collective-permute-done | bytes 73760 | tf_op jit(solution)/shard_map/ppermute | solution.py:766
  147.8 3.0 %collective-permute-start.42 = (bf16[96,768]{1,0:T(8,128)(2,1)S(1)}, bf16[96,768]{1,0:T(8,128)(2,1)S(1)}, u32[]{:S(2)}, u32[]{:S(2)}) collective-permute-start(bf16[96,768]{1,0:T(8,128)(2,1)S(1)} %get-tuple-element.134), channel_id=1, source_target_pairs={{0,24},{1,25},{2,26},{3,27},{4,28},{5,29},{6,30},{7,31},{8,16},{9,... | collective-permute-start | bytes 442376 | tf_op jit(solution)/shard_map/ppermute | solution.py:766
  151.6 1.7 %collective-permute-done.40 = bf16[96,768]{1,0:T(8,128)(2,1)S(1)} collective-permute-done((bf16[96,768]{1,0:T(8,128)(2,1)S(1)}, bf16[96,768]{1,0:T(8,128)(2,1)S(1)}, u32[]{:S(2)}, u32[]{:S(2)}) %collective-permute-start.40) | collective-permute-done | bytes 147488 | tf_op jit(solution)/shard_map/ppermute | solution.py:766
  153.3 4.2 %collective-permute-done.41 = bf16[96,768]{1,0:T(8,128)(2,1)S(1)} collective-permute-done((bf16[96,768]{1,0:T(8,128)(2,1)S(1)}, bf16[96,768]{1,0:T(8,128)(2,1)S(1)}, u32[]{:S(2)}, u32[]{:S(2)}) %collective-permute-start.41) | collective-permute-done | bytes 147488 | tf_op jit(solution)/shard_map/ppermute | solution.py:766
  (130 shorter events, 27.9 us)
Async XLA Ops:
  3.2 24.1 %collective-permute-start.4 = (bf16[96,768]{1,0:T(8,128)(2,1)}, bf16[96,768]{1,0:T(8,128)(2,1)}, u32[]{:S(2)}, u32[]{:S(2)}) collective-permute-start(bf16[96,768]{1,0:T(8,128)(2,1)} %get-tuple-element.79), channel_id=1, source_target_pairs={{0,8},{1,9},{2,10},{3,11},{4,12},{5,13},{6,14},{7,15},{8,0},{9,1},... | collective-permute-start | bytes 442376 | tf_op jit(solution)/shard_map/ppermute | solution.py:766
  6.3 21.9 %collective-permute-start.5 = (bf16[96,768]{1,0:T(8,128)(2,1)}, bf16[96,768]{1,0:T(8,128)(2,1)}, u32[]{:S(2)}, u32[]{:S(2)}) collective-permute-start(bf16[96,768]{1,0:T(8,128)(2,1)} %get-tuple-element.79), channel_id=1, source_target_pairs={{0,16},{1,17},{2,18},{3,19},{4,20},{5,21},{6,22},{7,23},{8,24},{9,... | collective-permute-start | bytes 442376 | tf_op jit(solution)/shard_map/ppermute | solution.py:766
  14.1 10.5 %collective-permute-start.3 = (bf16[128,384]{1,0:T(8,128)(2,1)S(1)}, bf16[128,384]{1,0:T(8,128)(2,1)S(1)}, u32[]{:S(2)}, u32[]{:S(2)}) collective-permute-start(bf16[128,384]{1,0:T(8,128)(2,1)S(1)} %pack_second.1.chunk), channel_id=1, source_target_pairs={{0,8},{1,9},{2,10},{3,11},{4,12},{5,13},{6,14},{7,15},{8,0},{9,1},... | collective-permute-start | bytes 294920 | tf_op jit(solution)/shard_map/ppermute | solution.py:766
  14.7 10.3 %collective-permute-start.2 = (bf16[128,384]{1,0:T(8,128)(2,1)S(1)}, bf16[128,384]{1,0:T(8,128)(2,1)S(1)}, u32[]{:S(2)}, u32[]{:S(2)}) collective-permute-start(bf16[128,384]{1,0:T(8,128)(2,1)S(1)} %pack_second.1.chunk), channel_id=1, source_target_pairs={{0,16},{1,17},{2,18},{3,19},{4,20},{5,21},{6,22},{7,23},{8,24},{9,... | collective-permute-start | bytes 294920 | tf_op jit(solution)/shard_map/ppermute | solution.py:766
  15.0 10.0 %collective-permute-start.1 = (bf16[128,384]{1,0:T(8,128)(2,1)S(1)}, bf16[128,384]{1,0:T(8,128)(2,1)S(1)}, u32[]{:S(2)}, u32[]{:S(2)}) collective-permute-start(bf16[128,384]{1,0:T(8,128)(2,1)S(1)} %pack_second.1.chunk), channel_id=1, source_target_pairs={{0,24},{1,25},{2,26},{3,27},{4,28},{5,29},{6,30},{7,31},{8,16},{9,... | collective-permute-start | bytes 294920 | tf_op jit(solution)/shard_map/ppermute | solution.py:766
  24.7 7.1 %collective-permute-start.6 = (bf16[96,768]{1,0:T(8,128)(2,1)S(1)}, bf16[96,768]{1,0:T(8,128)(2,1)S(1)}, u32[]{:S(2)}, u32[]{:S(2)}) collective-permute-start(bf16[96,768]{1,0:T(8,128)(2,1)S(1)} %copy-done.16), channel_id=1, source_target_pairs={{0,24},{1,25},{2,26},{3,27},{4,28},{5,29},{6,30},{7,31},{8,16},{9,... | collective-permute-start | bytes 442376 | tf_op jit(solution)/shard_map/ppermute | solution.py:766
  25.1 28.8 %collective-permute-start.14 = (bf16[384,384]{1,0:T(8,128)(2,1)S(1)}, bf16[384,384]{1,0:T(8,128)(2,1)S(1)}, u32[]{:S(2)}, u32[]{:S(2)}) collective-permute-start(bf16[384,384]{1,0:T(8,128)(2,1)S(1)} %pad_maximum_fusion.refs_0_), channel_id=1, source_target_pairs={{0,4},{1,3},{2,6},{3,1},{4,0},{5,7},{6,2},{7,5},{8,12},{9,11},{10,... | collective-permute-start | bytes 884744 | tf_op jit(solution)/shard_map/ppermute | solution.py:766
  25.8 28.2 %collective-permute-start.15 = (bf16[384,384]{1,0:T(8,128)(2,1)S(1)}, bf16[384,384]{1,0:T(8,128)(2,1)S(1)}, u32[]{:S(2)}, u32[]{:S(2)}) collective-permute-start(bf16[384,384]{1,0:T(8,128)(2,1)S(1)} %pad_maximum_fusion.refs_0_), channel_id=1, source_target_pairs={{0,2},{1,5},{2,0},{3,7},{4,6},{5,1},{6,4},{7,3},{8,10},{9,13},{10,... | collective-permute-start | bytes 884744 | tf_op jit(solution)/shard_map/ppermute | solution.py:766
  31.8 13.4 %collective-permute-start.7 = (bf16[400,768]{1,0:T(8,128)(2,1)S(1)}, bf16[400,768]{1,0:T(8,128)(2,1)S(1)}, u32[]{:S(2)}, u32[]{:S(2)}) collective-permute-start(bf16[400,768]{1,0:T(8,128)(2,1)S(1)} %constant_dynamic-update-slice_fusion.refs_0_), channel_id=1, source_target_pairs={{0,4},{1,3},{2,6},{3,1},{4,0},{5,7},{6,2},{7,5},{8,12},{9,11},{10,... | collective-permute-start | bytes 1843208 | tf_op jit(solution)/shard_map/ppermute | solution.py:766
  38.6 16.3 %collective-permute-start.8 = (bf16[400,768]{1,0:T(8,128)(2,1)S(1)}, bf16[400,768]{1,0:T(8,128)(2,1)S(1)}, u32[]{:S(2)}, u32[]{:S(2)}) collective-permute-start(bf16[400,768]{1,0:T(8,128)(2,1)S(1)} %constant_dynamic-update-slice_fusion.refs_0_), channel_id=1, source_target_pairs={{0,2},{1,5},{2,0},{3,7},{4,6},{5,1},{6,4},{7,3},{8,10},{9,13},{10,... | collective-permute-start | bytes 1843208 | tf_op jit(solution)/shard_map/ppermute | solution.py:766
  45.2 10.7 %collective-permute-start.9 = (bf16[400,768]{1,0:T(8,128)(2,1)S(1)}, bf16[400,768]{1,0:T(8,128)(2,1)S(1)}, u32[]{:S(2)}, u32[]{:S(2)}) collective-permute-start(bf16[400,768]{1,0:T(8,128)(2,1)S(1)} %collective-permute-done.7.refs_1_), channel_id=1, source_target_pairs={{0,2},{1,5},{2,0},{3,7},{4,6},{5,1},{6,4},{7,3},{8,10},{9,13},{10,... | collective-permute-start | bytes 1843208 | tf_op jit(solution)/shard_map/ppermute | solution.py:766
  53.8 8.8 %collective-permute-start.10 = (bf16[400,768]{1,0:T(8,128)(2,1)S(1)}, bf16[400,768]{1,0:T(8,128)(2,1)S(1)}, u32[]{:S(2)}, u32[]{:S(2)}) collective-permute-start(bf16[400,768]{1,0:T(8,128)(2,1)S(1)} %constant_dynamic-update-slice_fusion.refs_0_), channel_id=1, source_target_pairs={{0,1},{1,0},{2,3},{3,2},{4,5},{5,4},{6,7},{7,6},{8,9},{9,8},{10,11... | collective-permute-start | bytes 1843208 | tf_op jit(solution)/shard_map/ppermute | solution.py:766
  53.9 8.1 %collective-permute-start.16 = (bf16[384,384]{1,0:T(8,128)(2,1)S(1)}, bf16[384,384]{1,0:T(8,128)(2,1)S(1)}, u32[]{:S(2)}, u32[]{:S(2)}) collective-permute-start(bf16[384,384]{1,0:T(8,128)(2,1)S(1)} %collective-permute-done.14.refs_1_), channel_id=1, source_target_pairs={{0,2},{1,5},{2,0},{3,7},{4,6},{5,1},{6,4},{7,3},{8,10},{9,13},{10,... | collective-permute-start | bytes 884744 | tf_op jit(solution)/shard_map/ppermute | solution.py:766
  54.0 8.7 %collective-permute-start.11 = (bf16[400,768]{1,0:T(8,128)(2,1)S(1)}, bf16[400,768]{1,0:T(8,128)(2,1)S(1)}, u32[]{:S(2)}, u32[]{:S(2)}) collective-permute-start(bf16[400,768]{1,0:T(8,128)(2,1)S(1)} %collective-permute-done.7.refs_1_), channel_id=1, source_target_pairs={{0,1},{1,0},{2,3},{3,2},{4,5},{5,4},{6,7},{7,6},{8,9},{9,8},{10,11... | collective-permute-start | bytes 1843208 | tf_op jit(solution)/shard_map/ppermute | solution.py:766
  54.9 8.3 %collective-permute-start.12 = (bf16[400,768]{1,0:T(8,128)(2,1)S(1)}, bf16[400,768]{1,0:T(8,128)(2,1)S(1)}, u32[]{:S(2)}, u32[]{:S(2)}) collective-permute-start(bf16[400,768]{1,0:T(8,128)(2,1)S(1)} %collective-permute-done.8.refs_2_), channel_id=1, source_target_pairs={{0,1},{1,0},{2,3},{3,2},{4,5},{5,4},{6,7},{7,6},{8,9},{9,8},{10,11... | collective-permute-start | bytes 1843208 | tf_op jit(solution)/shard_map/ppermute | solution.py:766
  55.8 7.4 %collective-permute-start.13 = (bf16[400,768]{1,0:T(8,128)(2,1)S(1)}, bf16[400,768]{1,0:T(8,128)(2,1)S(1)}, u32[]{:S(2)}, u32[]{:S(2)}) collective-permute-start(bf16[400,768]{1,0:T(8,128)(2,1)S(1)} %collective-permute-done.9.refs_3_), channel_id=1, source_target_pairs={{0,1},{1,0},{2,3},{3,2},{4,5},{5,4},{6,7},{7,6},{8,9},{9,8},{10,11... | collective-permute-start | bytes 1843208 | tf_op jit(solution)/shard_map/ppermute | solution.py:766
  62.1 6.6 %collective-permute-start.17 = (bf16[384,384]{1,0:T(8,128)(2,1)S(1)}, bf16[384,384]{1,0:T(8,128)(2,1)S(1)}, u32[]{:S(2)}, u32[]{:S(2)}) collective-permute-start(bf16[384,384]{1,0:T(8,128)(2,1)S(1)} %pad_maximum_fusion.refs_0_), channel_id=1, source_target_pairs={{0,1},{1,0},{2,3},{3,2},{4,5},{5,4},{6,7},{7,6},{8,9},{9,8},{10,11... | collective-permute-start | bytes 884744 | tf_op jit(solution)/shard_map/ppermute | solution.py:766
  85.4 37.7 %collective-permute-start.38 = (bf16[4,96,768]{2,1,0:T(8,128)(2,1)S(1)}, bf16[4,96,768]{2,1,0:T(8,128)(2,1)S(1)}, u32[]{:S(2)}, u32[]{:S(2)}) collective-permute-start(bf16[4,96,768]{2,1,0:T(8,128)(2,1)S(1)} %get-tuple-element.123), channel_id=1, source_target_pairs={{0,2},{1,5},{2,0},{3,7},{4,6},{5,1},{6,4},{7,3},{8,10},{9,13},{10,... | collective-permute-start | bytes 1769480 | tf_op jit(solution)/shard_map/ppermute | solution.py:766
  88.7 19.2 %collective-permute-start.32 = (bf16[4,96,384]{2,1,0:T(8,128)(2,1)S(1)}, bf16[4,96,384]{2,1,0:T(8,128)(2,1)S(1)}, u32[]{:S(2)}, u32[]{:S(2)}) collective-permute-start(bf16[4,96,384]{2,1,0:T(8,128)(2,1)S(1)} %get-tuple-element.120), channel_id=1, source_target_pairs={{0,2},{1,5},{2,0},{3,7},{4,6},{5,1},{6,4},{7,3},{8,10},{9,13},{10,... | collective-permute-start | bytes 884744 | tf_op jit(solution)/shard_map/ppermute | solution.py:766
  104.7 41.4 %collective-permute-start.37 = (bf16[4,96,768]{2,1,0:T(8,128)(2,1)S(1)}, bf16[4,96,768]{2,1,0:T(8,128)(2,1)S(1)}, u32[]{:S(2)}, u32[]{:S(2)}) collective-permute-start(bf16[4,96,768]{2,1,0:T(8,128)(2,1)S(1)} %get-tuple-element.121), channel_id=1, source_target_pairs={{0,2},{1,5},{2,0},{3,7},{4,6},{5,1},{6,4},{7,3},{8,10},{9,13},{10,... | collective-permute-start | bytes 1769480 | tf_op jit(solution)/shard_map/ppermute | solution.py:766
  105.8 22.5 %collective-permute-start.31 = (bf16[4,96,384]{2,1,0:T(8,128)(2,1)S(1)}, bf16[4,96,384]{2,1,0:T(8,128)(2,1)S(1)}, u32[]{:S(2)}, u32[]{:S(2)}) collective-permute-start(bf16[4,96,384]{2,1,0:T(8,128)(2,1)S(1)} %get-tuple-element.118), channel_id=1, source_target_pairs={{0,2},{1,5},{2,0},{3,7},{4,6},{5,1},{6,4},{7,3},{8,10},{9,13},{10,... | collective-permute-start | bytes 884744 | tf_op jit(solution)/shard_map/ppermute | solution.py:766
  106.8 15.5 %collective-permute-start.26 = (f32[40,768]{1,0:T(8,128)S(1)}, f32[40,768]{1,0:T(8,128)S(1)}, u32[]{:S(2)}, u32[]{:S(2)}) collective-permute-start(f32[40,768]{1,0:T(8,128)S(1)} %get-tuple-element.109.sent), channel_id=1, source_target_pairs={{0,2},{1,5},{2,0},{3,7},{4,6},{5,1},{6,4},{7,3},{8,10},{9,13},{10,... | collective-permute-start | bytes 368648 | tf_op jit(solution)/shard_map/ppermute | solution.py:766
  108.0 20.5 %collective-permute-start.33 = (bf16[4,96,384]{2,1,0:T(8,128)(2,1)S(1)}, bf16[4,96,384]{2,1,0:T(8,128)(2,1)S(1)}, u32[]{:S(2)}, u32[]{:S(2)}) collective-permute-start(bf16[4,96,384]{2,1,0:T(8,128)(2,1)S(1)} %add_convert_fusion.3), channel_id=1, source_target_pairs={{0,4},{1,3},{2,6},{3,1},{4,0},{5,7},{6,2},{7,5},{8,12},{9,11},{10,... | collective-permute-start | bytes 884744 | tf_op jit(solution)/shard_map/ppermute | solution.py:766
  123.2 22.9 %collective-permute-start.39 = (bf16[4,96,768]{2,1,0:T(8,128)(2,1)S(1)}, bf16[4,96,768]{2,1,0:T(8,128)(2,1)S(1)}, u32[]{:S(2)}, u32[]{:S(2)}) collective-permute-start(bf16[4,96,768]{2,1,0:T(8,128)(2,1)S(1)} %add_convert_fusion.1), channel_id=1, source_target_pairs={{0,4},{1,3},{2,6},{3,1},{4,0},{5,7},{6,2},{7,5},{8,12},{9,11},{10,... | collective-permute-start | bytes 1769480 | tf_op jit(solution)/shard_map/ppermute | solution.py:766
  127.1 6.7 %collective-permute-start.28 = (f32[32,768]{1,0:T(8,128)S(1)}, f32[32,768]{1,0:T(8,128)S(1)}, u32[]{:S(2)}, u32[]{:S(2)}) collective-permute-start(f32[32,768]{1,0:T(8,128)S(1)} %get-tuple-element.113), channel_id=1, source_target_pairs={{0,8},{1,9},{2,10},{3,11},{4,12},{5,13},{6,14},{7,15},{8,0},{9,1},... | collective-permute-start | bytes 294920 | tf_op jit(solution)/shard_map/ppermute | solution.py:766
  128.3 10.9 %collective-permute-start.29 = (f32[32,768]{1,0:T(8,128)S(1)}, f32[32,768]{1,0:T(8,128)S(1)}, u32[]{:S(2)}, u32[]{:S(2)}) collective-permute-start(f32[32,768]{1,0:T(8,128)S(1)} %get-tuple-element.114), channel_id=1, source_target_pairs={{0,16},{1,17},{2,18},{3,19},{4,20},{5,21},{6,22},{7,23},{8,24},{9,... | collective-permute-start | bytes 294920 | tf_op jit(solution)/shard_map/ppermute | solution.py:766
  128.5 10.7 %collective-permute-start.30 = (f32[32,768]{1,0:T(8,128)S(1)}, f32[32,768]{1,0:T(8,128)S(1)}, u32[]{:S(2)}, u32[]{:S(2)}) collective-permute-start(f32[32,768]{1,0:T(8,128)S(1)} %get-tuple-element.115), channel_id=1, source_target_pairs={{0,24},{1,25},{2,26},{3,27},{4,28},{5,29},{6,30},{7,31},{8,16},{9,... | collective-permute-start | bytes 294920 | tf_op jit(solution)/shard_map/ppermute | solution.py:766
  133.7 7.3 %collective-permute-start.34 = (bf16[96,384]{1,0:T(8,128)(2,1)S(1)}, bf16[96,384]{1,0:T(8,128)(2,1)S(1)}, u32[]{:S(2)}, u32[]{:S(2)}) collective-permute-start(bf16[96,384]{1,0:T(8,128)(2,1)S(1)} %get-tuple-element.140), channel_id=1, source_target_pairs={{0,8},{1,9},{2,10},{3,11},{4,12},{5,13},{6,14},{7,15},{8,0},{9,1},... | collective-permute-start | bytes 221192 | tf_op jit(solution)/shard_map/ppermute | solution.py:766
  139.2 6.9 %collective-permute-start.36 = (bf16[96,384]{1,0:T(8,128)(2,1)S(1)}, bf16[96,384]{1,0:T(8,128)(2,1)S(1)}, u32[]{:S(2)}, u32[]{:S(2)}) collective-permute-start(bf16[96,384]{1,0:T(8,128)(2,1)S(1)} %get-tuple-element.141), channel_id=1, source_target_pairs={{0,24},{1,25},{2,26},{3,27},{4,28},{5,29},{6,30},{7,31},{8,16},{9,... | collective-permute-start | bytes 221192 | tf_op jit(solution)/shard_map/ppermute | solution.py:766
  146.4 6.9 %collective-permute-start.40 = (bf16[96,768]{1,0:T(8,128)(2,1)S(1)}, bf16[96,768]{1,0:T(8,128)(2,1)S(1)}, u32[]{:S(2)}, u32[]{:S(2)}) collective-permute-start(bf16[96,768]{1,0:T(8,128)(2,1)S(1)} %get-tuple-element.133), channel_id=1, source_target_pairs={{0,8},{1,9},{2,10},{3,11},{4,12},{5,13},{6,14},{7,15},{8,0},{9,1},... | collective-permute-start | bytes 442376 | tf_op jit(solution)/shard_map/ppermute | solution.py:766
  146.9 10.6 %collective-permute-start.41 = (bf16[96,768]{1,0:T(8,128)(2,1)S(1)}, bf16[96,768]{1,0:T(8,128)(2,1)S(1)}, u32[]{:S(2)}, u32[]{:S(2)}) collective-permute-start(bf16[96,768]{1,0:T(8,128)(2,1)S(1)} %get-tuple-element.135), channel_id=1, source_target_pairs={{0,16},{1,17},{2,18},{3,19},{4,20},{5,21},{6,22},{7,23},{8,24},{9,... | collective-permute-start | bytes 442376 | tf_op jit(solution)/shard_map/ppermute | solution.py:766
  147.8 9.7 %collective-permute-start.42 = (bf16[96,768]{1,0:T(8,128)(2,1)S(1)}, bf16[96,768]{1,0:T(8,128)(2,1)S(1)}, u32[]{:S(2)}, u32[]{:S(2)}) collective-permute-start(bf16[96,768]{1,0:T(8,128)(2,1)S(1)} %get-tuple-element.134), channel_id=1, source_target_pairs={{0,24},{1,25},{2,26},{3,27},{4,28},{5,29},{6,30},{7,31},{8,16},{9,... | collective-permute-start | bytes 442376 | tf_op jit(solution)/shard_map/ppermute | solution.py:766
  (29 other events, 185.4 us)

commit v4 on v3

--- a/solution.py
+++ b/solution.py
@@ -11,6 +11,7 @@
 masked_score = -1e30
 edge_unit = 1638.0
 spatial_unit = 4096.0
+hurry = 0.1
 bf16 = jnp.bfloat16
 f32 = jnp.float32
 i32 = jnp.int32
@@ -53,7 +54,7 @@
 
 
 def cost(microseconds):
-    return pl.CostEstimate(flops=int(microseconds * 1.15e9), bytes_accessed=1024, transcendentals=0)
+    return pl.CostEstimate(flops=int(microseconds * hurry * 1.15e9), bytes_accessed=1024, transcendentals=0)
 
 
 def as_row(ref):
@@ -82,7 +83,7 @@
     return terms
 
 
-def pack_first_kernel(wq, wk, wv, wo, bq, bv, bi, weights, biases, held, sems):
+def pack_first_kernel(place, wq, wk, wv, wo, bq, bv, bi, edge, neighbour, after, weights, biases, held, sems):
     copies = [
         pltpu.make_async_copy(source, held.at[i], sems.at[i]) for i, source in enumerate((wq, wk, wv, wo))
     ]
@@ -93,45 +94,46 @@
     row = jnp.concatenate([row, jnp.zeros((1, lanes - row.shape[1]), f32)], 1)
     terms = [term.astype(f32) for term in three_terms(row)]
     biases[...] = jnp.concatenate(terms + [jnp.zeros((13, lanes), f32)], 0).astype(bf16)
+    even = place[1] == 0
+    mine, other = edge[...].astype(f32), neighbour[...].astype(f32)
+    low, high = jnp.where(even, mine, other), jnp.where(even, other, mine)
+    rows = held.shape[1]
+    half = low.shape[0] // 2
+    weights[rows:, :] = jnp.concatenate([low[:half], low[half:], high[:half], high[half:]], 1).astype(bf16)
     for copy in copies:
         copy.wait()
-    weights[...] = jnp.concatenate([held[i] for i in range(4)], 1)
-
-
-def pack_first(wq, wk, wv, wo, bq, bv, bi):
+    weights[0:rows, :] = jnp.concatenate([held[i] for i in range(4)], 1)
+
+
+def pack_first(place, wq, wk, wv, wo, bq, bv, bi, edge, neighbour, after):
     rows, width = wq.shape
     return pl.pallas_call(
         pack_first_kernel,
-        out_shape=(shape((rows, 4 * width), bf16), shape((16, 4 * width), bf16)),
-        in_specs=[hbm] * 4 + [vmem] * 3,
+        out_shape=(shape((rows + 16, 4 * width), bf16), shape((16, 4 * width), bf16)),
+        in_specs=[smem] + [hbm] * 4 + [vmem] * 5 + [untouched],
         out_specs=[vmem] * 2,
         scratch_shapes=[pltpu.VMEM((4, rows, width), bf16), pltpu.SemaphoreType.DMA((4,))],
-        cost_estimate=cost(1),
-        compiler_params=params(62),
+        cost_estimate=cost(2),
+        compiler_params=params(60),
         name="pack_first",
-    )(wq, wk, wv, wo, bq, bv, bi)
-
-
-def pack_second_kernel(place, wi, wu, edge, neighbour, out):
-    rows = wi.shape[0]
-    out[0:rows, :] = jnp.concatenate([wi[...], wu[...]], 1)
-    even = place[1] == 0
-    mine, other = edge[...].astype(f32), neighbour[...].astype(f32)
-    low, high = jnp.where(even, mine, other), jnp.where(even, other, mine)
-    out[rows:, :] = jnp.concatenate([low, high], 1).astype(bf16)
-
-
-def pack_second(place, wi, wu, edge, neighbour):
+    )(place, wq, wk, wv, wo, bq, bv, bi, edge, neighbour, after)
+
+
+def pack_second_kernel(wi, wu, out):
+    out[...] = jnp.concatenate([wi[...], wu[...]], 1)
+
+
+def pack_second(wi, wu):
     rows, width = wi.shape
     return pl.pallas_call(
         pack_second_kernel,
-        out_shape=shape((rows + edge.shape[0], 2 * width), bf16),
-        in_specs=[smem] + [vmem] * 4,
+        out_shape=shape((rows, 2 * width), bf16),
+        in_specs=[vmem] * 2,
         out_specs=vmem,
         cost_estimate=cost(1),
-        compiler_params=params(4),
+        compiler_params=params(60),
         name="pack_second",
-    )(place, wi, wu, edge, neighbour)
+    )(wi, wu)
 
 
 def prepare_kernel(virtual, place, spatial, path, layer_in, gain, bias, cotangent, ids, buckets, h1, rows_t):
@@ -178,7 +180,7 @@
             shape((rows, width), bf16),
             shape((2, width, rows), bf16),
         ),
-        compiler_params=params(8),
+        compiler_params=params(62),
         cost_estimate=cost(1),
         name="prepare",
     )(place, spatial, path, layer_in, gain, bias, cotangent)
@@ -195,14 +197,19 @@
 
 
 def lookup_kernel(first, step, share, place, chunk, ids, *refs):
-    if first:
-        total, table = refs
-        previous = None
-    else:
-        previous, total, table = refs
+    total, table = refs[-2:]
+    previous = None if first else refs[0]
     hops, slots = ids.shape[0], ids.shape[1]
     pairs = total.shape[0]
-    packed = quantize(chunk[chunk.shape[0] - 2 * pairs :, :], edge_unit)
+    below = chunk[chunk.shape[0] - 16 :, :]
+    half = share // 2
+    below = [below[:, i * half : (i + 1) * half] for i in range(4)]
+    packed = quantize(
+        jnp.concatenate(
+            [jnp.concatenate([below[0], below[2]], 1), jnp.concatenate([below[1], below[3]], 1)], 0
+        ),
+        edge_unit,
+    )
     blocks = share // 128
     for pair in range(pairs):
         head = (pair // 4) * 8 + pair % 4
@@ -234,8 +241,8 @@
     lax.fori_loop(0, slots // 8, body, 0)
 
 
-def lookup(place, chunk, ids, previous, step, heads):
-    share = chunk.shape[1]
+def lookup(place, chunk, ids, previous, step, heads, after=()):
+    share = chunk.shape[1] // 2
     pairs = heads // 2
     slots = ids.shape[1]
     first = previous is None
@@ -243,31 +250,33 @@
     return pl.pallas_call(
         functools.partial(lookup_kernel, first, step, share),
         out_shape=out,
-        in_specs=[smem] + [vmem] * (2 if first else 3),
+        in_specs=[smem] + [vmem] * (2 if first else 3) + [untouched] * len(after),
         out_specs=vmem,
         scratch_shapes=[pltpu.VMEM((pairs, share // 128, 8, 128), i32)],
         input_output_aliases={} if first else {3: 0},
         compiler_params=params(8),
         cost_estimate=cost(6),
         name="lookup",
-    )(place, chunk, ids, *(() if first else (previous,)))
+    )(place, chunk, ids, *(() if first else (previous,)), *after)
 
 
 def assemble(place, parts, whole, biases=None):
-    if len(parts) == 1:
+    if len(parts) <= 2:
         whole[...] = parts[0][...]
         return
     core = place[3]
     rows = whole.shape[1] // 8
+    each = len(parts) // 2
     for other in range(2):
         for which in range(4):
-            part = parts[other * 4 + which]
             for step in range(4):
                 row, column = relative(place, core ^ other, which, step)
                 start = pl.multiple_of(row * rows, rows)
-                whole[column, pl.ds(start, rows), :] = part[step * rows : (step + 1) * rows, :]
+                part = parts[other * each + which // (4 // each)]
+                at = (step * (4 // each) + which % (4 // each)) * rows
+                whole[column, pl.ds(start, rows), :] = part[at : at + rows, :]
             if biases is not None:
-                terms = part[4 * rows : 4 * rows + 16, :].astype(f32)
+                terms = parts[other * each + which][4 * rows : 4 * rows + 16, :].astype(f32)
                 biases[column] = terms[0:1] + terms[1:2] + terms[2:3]
 
 
@@ -285,11 +294,9 @@
 ):
     parts, refs = refs[:n_parts], refs[n_parts:]
     weights, biases, transposed, value_win, probs_out, att_low, mid, h2 = refs
+    assemble(place, parts, weights, biases)
     if n_parts == 2:
-        assemble(place, parts[:1], weights)
         biases[...] = parts[1][...]
-    else:
-        assemble(place, parts, weights, biases)
     slots = h1.shape[0]
     groups, width = biases.shape[0], biases.shape[2] // 4
     depth = width // 8
@@ -389,7 +396,7 @@
     n_parts, place, mid, h2, weights_a, biases, out_bias, gain, cotangent, att_low, probs_in, *refs
 ):
     parts = refs[:n_parts]
-    layer_out, grad_mid, grad_att_t, grad_values, mine, theirs, rows_t, sums, weights = refs[n_parts:]
+    layer_out, grad_mid, grad_att_t, grad_values, mine, theirs, rows_t, sums, weights = refs[-9:]
     assemble(place, parts, weights)
     slots, features = mid.shape
     width = biases.shape[2] // 4
@@ -451,7 +458,7 @@
         sums[pl.ds(8 + group, 1), 512:768] = column_sum(low_form.astype(f32))
 
 
-def feed(place, mid, h2, weights_a, biases, out_bias, gain, cotangent, att_low, probs, parts):
+def feed(place, mid, h2, weights_a, biases, out_bias, gain, cotangent, att_low, probs, parts, after=()):
     slots, features = mid.shape
     groups, width = biases.shape[0], biases.shape[2] // 4
     whole = lambda array: pl.BlockSpec(array.shape, lambda i: (0,) * len(array.shape))
@@ -476,13 +483,14 @@
             whole(h2),
             pl.BlockSpec((groups, features, 256), lambda i: (0, 0, 2)),
         ]
-        + [whole(a) for a in rest + tuple(parts)],
+        + [whole(a) for a in rest + tuple(parts)]
+        + [untouched] * len(after),
         out_specs=[whole(out) for out in outs],
         scratch_shapes=[pltpu.VMEM((groups, features, 2 * width), bf16)],
         cost_estimate=cost(7),
         compiler_params=params(32),
         name="feed",
-    )(place, mid, h2, weights_a, *rest, *parts)
+    )(place, mid, h2, weights_a, *rest, *parts, *after)
 
 
 def attend_back_kernel(
@@ -553,7 +561,7 @@
 
 def weight_grads_kernel(plan, n_rows, place, columns_own, columns_other, *refs):
     own_rows, other_rows = refs[:n_rows], refs[n_rows : 2 * n_rows]
-    own, across, over, both, rows_t = refs[2 * n_rows :]
+    own, across, second, rows_t = refs[-4:]
     kind = 0
     for mine, other in zip(own_rows, other_rows):
         slots = mine.shape[2]
@@ -563,13 +571,13 @@
             kind += 1
     core = place[3]
     height = own.shape[1]
-    for which, out in ((3, both), (2, over), (1, across), (0, own)):
+    for which, out, at in ((3, second, 0), (2, second, 4), (1, across, 0), (0, own, 0)):
         y = relative(place, core, which, 0)[1] >> 1
         right = jnp.concatenate([columns_own[y], columns_other[y]], 0)
         for step in range(4):
             row = relative(place, core, which, step)[0]
             start = pl.multiple_of(row * height, height)
-            out[step] = plan(lambda kind: rows_t[kind, pl.ds(start, height), :], right).astype(bf16)
+            out[at + step] = plan(lambda kind: rows_t[kind, pl.ds(start, height), :], right).astype(bf16)
 
 
 def plan_first(rows_of, right):
@@ -594,33 +602,39 @@
     )
 
 
-def weight_grads(plan, place, columns_own, columns_other, own_rows, other_rows, height, lanes, microseconds):
+def weight_grads(
+    plan, place, columns_own, columns_other, own_rows, other_rows, height, lanes, microseconds, after=()
+):
     features, slots = own_rows[0].shape[1:]
     kinds = sum(rows.shape[0] for rows in own_rows)
     out = shape((4, height, lanes), bf16)
     return pl.pallas_call(
         functools.partial(weight_grads_kernel, plan, len(own_rows)),
-        out_shape=(out,) * 4,
-        in_specs=[smem] + [vmem] * (2 + 2 * len(own_rows)),
-        out_specs=[vmem] * 4,
+        out_shape=(out, out, shape((8, height, lanes), bf16)),
+        in_specs=[smem] + [vmem] * (2 + 2 * len(own_rows)) + [untouched] * len(after),
+        out_specs=[vmem] * 3,
         scratch_shapes=[pltpu.VMEM((kinds, features, 2 * slots), bf16)],
         cost_estimate=cost(microseconds),
         compiler_params=params(20),
         name="weight_grads",
-    )(place, columns_own, columns_other, *own_rows, *other_rows)
-
-
-def table_kernel(digit, staged, span, place, grads, ids, buckets, sums, after, *refs):
-    if staged:
-        mine, theirs, small, total, spatial = refs
-    else:
-        total, spatial = refs
+    )(place, columns_own, columns_other, *own_rows, *other_rows, *after)
+
+
+def table_kernel(digit, start, stop, previous, last, place, grads, ids, buckets, *refs):
     hops = ids.shape[0]
     groups = grads.shape[0]
     heads = groups * 8
+    span = 8
+    if previous:
+        total_in, spatial_in = refs[:2]
+    if last:
+        sums = refs[2]
+        mine, theirs, small, total, spatial = refs[-5:]
+    else:
+        total, spatial = refs[-2:]
+    total[...] = total_in[...] if previous else jnp.zeros_like(total)
+    spatial[...] = spatial_in[...] if previous else jnp.zeros_like(spatial)
     high_count = total.shape[0] // heads
-    total[...] = jnp.zeros_like(total)
-    spatial[...] = jnp.zeros_like(spatial)
     digits = lax.broadcasted_iota(i32, (digit, 128), 0).astype(f32).astype(bf16)
     kinds = lax.broadcasted_iota(i32, (heads, 128), 0).astype(f32).astype(bf16)
     one = jnp.ones((), bf16)
@@ -650,99 +664,125 @@
         spatial[...] += dot_nt(jnp.concatenate(plain, 1), jnp.concatenate(kind_rights, 1))
         return carry
 
-    lax.fori_loop(0, grads.shape[1] // span, body, 0)
-    if staged:
+    lax.fori_loop(start // span, stop // span, body, 0)
+    if last:
         core = place[3]
         for other, out in ((0, mine), (1, theirs)):
             for which in range(4):
                 pieces = []
                 for step in range(4):
                     row, column = relative(place, core ^ other, which, step)
-                    start = pl.multiple_of(row * heads + column * 8, 8)
-                    pieces.append(total[pl.ds(start, 8), :] * (1.0 / hops))
-                out[which * 8 : (which + 1) * 8, :] = jnp.concatenate(pieces, 1)
-        spread = []
-        for group in range(4):
-            spread += [spatial[group * 8 : (group + 1) * 8, :], jnp.zeros((8, 128 - heads), f32)]
-        lanes = sums.shape[1]
-        spread.append(jnp.zeros((8, lanes - 512), f32))
-        spread = jnp.concatenate(spread, 1)
-        small[0:16, :] = sums[...]
-        small[16:24, :] = spread
-        theirs[32:48, :] = sums[...]
-        theirs[48:56, :] = spread
-
-
-def table_grads(place, grads, ids, buckets, sums, after, digit, edges, staged):
+                    at = pl.multiple_of(row * heads + column * 8, 8)
+                    pieces.append(total[pl.ds(at, 8), :] * (1.0 / hops))
+                out[which * 16 : which * 16 + 8, :] = jnp.concatenate(pieces[:2], 1)
+                out[which * 16 + 8 : which * 16 + 16, :] = jnp.concatenate(pieces[2:], 1)
+        half = small.shape[1]
+        held = sums[...]
+        spread = [jnp.zeros((8, digit), f32)] + [spatial[group * 8 : (group + 1) * 8, :] for group in range(4)]
+        spread.append(jnp.zeros((8, half - digit - 4 * heads), f32))
+        packed = [jnp.concatenate(spread, 1), held[0:8, :half], held[0:8, half:]]
+        packed.append(
+            jnp.concatenate(
+                [
+                    jnp.concatenate([held[8:12, :digit], held[12:16, :digit]], 0),
+                    jnp.concatenate([held[8:12, 512 : 512 + digit], jnp.zeros((4, digit), f32)], 0),
+                ],
+                1,
+            )
+        )
+        packed = jnp.concatenate(packed, 0)
+        small[...] = packed
+        theirs[64:96, :] = packed
+
+
+def table_grads(place, grads, ids, buckets, digit, edges, start, stop, previous=(), sums=None, after=()):
     heads = grads.shape[0] * 8
-    total = (edges // digit * heads, digit)
-    lanes = sums.shape[1]
-    outs = (shape((32, lanes), f32), shape((56, lanes), f32), shape((24, lanes), f32))
-    inner = (shape(total, f32), shape((heads, heads), f32))
+    last = sums is not None
+    inner = (shape((edges // digit * heads, digit), f32), shape((heads, heads), f32))
+    outs = inner
+    if last:
+        lanes = sums.shape[1] // 2
+        outs = (shape((64, lanes), f32), shape((96, lanes), f32), shape((32, lanes), f32))
+    inputs = tuple(previous) + ((sums,) if last else ())
     return pl.pallas_call(
-        functools.partial(table_kernel, digit, staged, 8),
-        out_shape=outs if staged else inner,
-        in_specs=[smem] + [vmem] * 4 + [untouched],
-        out_specs=[vmem] * (3 if staged else 2),
-        scratch_shapes=[pltpu.VMEM(a.shape, f32) for a in inner] if staged else [],
-        cost_estimate=cost(15),
+        functools.partial(table_kernel, digit, start, stop, len(previous) > 0, last),
+        out_shape=outs,
+        in_specs=[smem] + [vmem] * (3 + len(inputs)) + [untouched] * len(after),
+        out_specs=[vmem] * len(outs),
+        scratch_shapes=[pltpu.VMEM(a.shape, f32) for a in inner] if last else [],
+        cost_estimate=cost(15 * (stop - start) / grads.shape[1]),
         compiler_params=params(12),
         name="table_grads",
-    )(place, grads, ids, buckets, sums, after)
-
-
-def meet_core_kernel(mine, small, got, out, keep):
-    keep[...] = mine[0:16, :] + got[0:16, :]
-    out[0:8, :] = mine[24:32, :] + got[24:32, :]
-    out[8:16, :] = mine[16:24, :] + got[16:24, :]
-    out[16:40, :] = small[...] + got[32:56, :]
-
-
-def meet_second_kernel(keep, sent, got, out, kept):
-    out[0:8, :] = keep[8:16, :] + got[0:8, :]
-    out[8:32, :] = sent[16:40, :] + got[16:40, :]
-    kept[...] = keep[0:8, :] + got[8:16, :]
-
-
-def meet_first_kernel(kept, sent, got, *outs):
-    own = kept[...] + got[0:8, :]
-    small = sent[8:32, :] + got[8:32, :]
-    digit = own.shape[1] // 4
+    )(place, grads, ids, buckets, *inputs, *after)
+
+
+def meet_core_kernel(mine, small, got, after, out, keep):
+    keep[0:16, :] = mine[0:16, :] + got[0:16, :]
+    keep[16:32, :] = mine[32:48, :] + got[32:48, :]
+    out[0:16, :] = mine[48:64, :] + got[48:64, :]
+    out[16:32, :] = mine[16:32, :] + got[16:32, :]
+    out[32:64, :] = small[...] + got[64:96, :]
+
+
+def meet_near_kernel(keep, sent, got, out, kept):
+    out[0:16, :] = keep[16:32, :] + got[0:16, :]
+    out[16:48, :] = sent[32:64, :] + got[32:64, :]
+    kept[...] = keep[0:16, :] + got[16:32, :]
+
+
+def meet_far_kernel(kept, sent, got, own, first_hop, second_hop, *outs):
+    table = kept[...] + got[0:16, :]
+    small = sent[16:48, :] + got[16:48, :]
+    digit = table.shape[1] // 2
+    rows = own.shape[1]
     for step, out in enumerate(outs):
-        out[0:8, 0:digit] = own[:, step * digit : (step + 1) * digit]
-        out[0:8, digit:] = jnp.zeros((8, 3 * digit), f32)
-        out[8:32, :] = small
-
-
-def finish_kernel(place, own, first, second, third, edge, spatial, *outs):
-    total = own[...] + first[...] + second[...] + third[...]
+        total = own[step].astype(f32) + first_hop[step].astype(f32) + second_hop[step + 4].astype(f32)
+        out[0:rows, :] = total.astype(bf16)
+        block = table[(step // 2) * 8 : (step // 2) * 8 + 8, (step % 2) * digit : (step % 2 + 1) * digit]
+        head = jnp.concatenate([block, small[0:8, digit:]], 1)
+        out[rows:, :] = jnp.concatenate([head, small[8:32]], 0).astype(bf16)
+
+
+def finish_kernel(place, own, first, second, third, after, *outs):
+    total = own[...].astype(f32)
+    for part in (first, second, third):
+        total = total + part[...].astype(f32)
+    query, key, edge, spatial = outs[:4]
+    outs = outs[4:]
+    rows, width = query.shape
     digit = edge.shape[1]
-    edge[...] = total[0:8, 0:digit]
+    query[...] = total[0:rows, 0:width]
+    key[...] = total[0:rows, width : 2 * width]
+    edge[...] = total[rows : rows + 8, 0:digit]
     group = place[4]
+    at = rows + 8
     for i, out in enumerate(outs[:6]):
-        out[...] = total[8 + i : 9 + i, :].reshape(out.shape)
-    width = outs[6].shape[0]
-    heads = total[16:17]
-    hidden = total[20:21]
-    kinds = total[24:32, 0:128]
+        row = jnp.concatenate([total[at + i : at + i + 1, :], total[at + 8 + i : at + 9 + i, :]], 1)
+        out[...] = row.reshape(out.shape)
+    at = rows + 24
+    heads = total[at : at + 1]
+    hidden = total[at + 4 : at + 5]
+    kinds = total[rows : rows + 8, digit : digit + 32]
     for other in range(1, 4):
-        heads = jnp.where(group == other, total[16 + other : 17 + other], heads)
-        hidden = jnp.where(group == other, total[20 + other : 21 + other], hidden)
-        kinds = jnp.where(group == other, total[24:32, other * 128 : (other + 1) * 128], kinds)
+        heads = jnp.where(group == other, total[at + other : at + other + 1], heads)
+        hidden = jnp.where(group == other, total[at + 4 + other : at + 5 + other], hidden)
+        start = digit + other * 32
+        kinds = jnp.where(group == other, total[rows : rows + 8, start : start + 32], kinds)
     outs[6][...] = heads[:, :width].reshape(outs[6].shape)
-    outs[7][...] = heads[:, 512 : 512 + width].reshape(outs[7].shape)
+    outs[7][...] = heads[:, width : 2 * width].reshape(outs[7].shape)
     outs[8][...] = hidden[:, :width].reshape(outs[8].shape)
     spatial[...] = kinds[:, : spatial.shape[1]]
 
 
-def small_call(kernel, name, outs, *args):
+def small_call(kernel, name, outs, *args, waits=0, mebibytes=8):
     return pl.pallas_call(
         kernel,
         out_shape=outs,
-        in_specs=[smem if args[i].ndim == 1 else vmem for i in range(len(args))],
+        in_specs=[smem if args[i].ndim == 1 else vmem for i in range(len(args) - waits)]
+        + [untouched] * waits,
         out_specs=[vmem] * len(outs),
-        cost_estimate=cost(0.7),
-        compiler_params=params(4),
+        cost_estimate=cost(1),
+        compiler_params=params(mebibytes),
         name=name,
     )(*args)
 
@@ -770,28 +810,102 @@
     return [own] + [send(own, hop) for hop in links.along_z]
 
 
-def spread(links, stack):
-    across = send(stack, links.first)
-    over = send(stack, links.second)
-    both = send(across, links.second)
-    mine = (stack, across, over, both)
-    return mine + tuple(send(part, links.core) for part in mine)
-
-
-def add_rounded(*terms):
-    total = terms[0].astype(f32)
-    for term in terms[1:]:
-        total = total + term.astype(f32)
+def join_kernel(rows, count, *refs):
+    out = refs[-1]
+    for i in range(count):
+        stop = min((i + 1) * rows, out.shape[0])
+        out[i * rows : stop, :] = refs[i][0 : stop - i * rows, :]
+
+
+def join(parts, rows, after=()):
+    total = rows * (len(parts) - 1) + parts[-1].shape[0] if len(parts) == 5 else rows * len(parts)
+    return small_call(
+        functools.partial(join_kernel, rows, len(parts)), "join",
+        (shape((total, parts[0].shape[1]), bf16),), *parts, *after, waits=len(after),
+    )[0]
+
+
+def join_pairs_kernel(rows, own, near, *refs):
+    out = refs[-1]
+    for i, (part, at) in enumerate(((own, 0), (near, 0), (own, rows), (near, rows))):
+        out[i * rows : (i + 1) * rows, :] = part[at : at + rows, :]
+
+
+def join_pairs(own, near, rows, after):
+    return small_call(
+        functools.partial(join_pairs_kernel, rows), "join_pairs",
+        (shape((4 * rows, own.shape[1]), bf16),), own, near, *after, waits=len(after),
+    )[0]
+
+
+def add_kernel(count, *refs):
+    for step in range(4):
+        total = refs[0][step].astype(f32)
+        for ref in refs[1:count]:
+            total = total + ref[step].astype(f32)
+        refs[-1][step] = total.astype(bf16)
+
+
+def add_rounded(terms, after):
+    return small_call(
+        functools.partial(add_kernel, len(terms)), "add",
+        (shape(terms[0].shape, bf16),), *terms, *after, waits=len(after),
+    )[0]
+
+
+def step_sum(refs, step):
+    total = refs[0][step].astype(f32)
+    for ref in refs[1:]:
+        total = total + ref[step + ref.shape[0] - 4].astype(f32)
     return total.astype(bf16)
 
 
-def reduce_staged(links, own, across, over, both):
-    across = add_rounded(across, send(both, links.second))
-    own = add_rounded(own, send(over, links.second), send(across, links.first))
-    total = own[0].astype(f32)
-    for step, hop in enumerate(links.along_z):
-        total = total + send(own[step + 1], hop).astype(f32)
-    return total
+def add_pair_kernel(count, *refs):
+    stay, go = refs[-2:]
+    for i in range(2):
+        stay[i] = step_sum(refs[:count], 2 * i)
+        go[i] = step_sum(refs[:count], 2 * i + 1)
+
+
+def add_pair(terms, after):
+    out = shape((2,) + terms[0].shape[1:], bf16)
+    return small_call(
+        functools.partial(add_pair_kernel, len(terms)), "add_pair",
+        (out,) * 2, *terms, *after, waits=len(after),
+    )
+
+
+def add_half_kernel(count, stay, got, *refs):
+    for i, out in enumerate(refs[-2:]):
+        out[...] = (stay[i].astype(f32) + got[i].astype(f32)).astype(bf16)
+
+
+def add_half(stay, got, after):
+    out = shape(stay.shape[1:], bf16)
+    return small_call(
+        functools.partial(add_half_kernel, 2), "add_half", (out,) * 2, stay, got, *after, waits=len(after)
+    )
+
+
+def settle_kernel(count, *refs):
+    total = refs[0][...].astype(f32) + refs[1][...].astype(f32)
+    outs = refs[len(refs) - count :]
+    width = outs[0].shape[1]
+    for i, out in enumerate(outs):
+        out[...] = total[:, i * width : (i + 1) * width]
+
+
+def settle(terms, width, after):
+    rows, lanes = terms[0].shape
+    count = lanes // width
+    return small_call(
+        functools.partial(settle_kernel, count), "settle",
+        (shape((rows, width), f32),) * count, *terms, *after, waits=len(after), mebibytes=60,
+    )
+
+
+def held_until(values, *others):
+    return lax.optimization_barrier((values, others))[0]
 
 
 def local(
@@ -835,12 +949,13 @@
     )
     if staged:
         links = Links()
-        first, own_biases = pack_first(w_q, w_k, w_v, w_o, q_bias, v_bias, in_bias)
         table_t = edge_table.T
-        second = pack_second(place, w_in, w_out, table_t, send(table_t, links.along_x))
-        parts_a = spread(links, jnp.concatenate(around(links, first) + [own_biases], 0))
-        chunks = around(links, second)
-        parts_b = spread(links, jnp.concatenate([chunk[:height] for chunk in chunks], 0))
+        second = pack_second(w_in, w_out)
+        first, own_biases = pack_first(
+            place, w_q, w_k, w_v, w_o, q_bias, v_bias, in_bias, table_t, send(table_t, links.along_x), second
+        )
+        chunks = around(links, first)
+        pair_b = join([second, send(second, links.first)], height)
         lookup_place = place
     else:
         gathered = [
@@ -852,67 +967,114 @@
         parts_a = (jnp.concatenate(gathered[:4], 2), bias_row)
         parts_b = (jnp.concatenate(gathered[4:], 2),)
         table_t = lax.all_gather(edge_table, "dp", axis=0, tiled=True).T
-        chunks = [table_t[:, i * share : (i + 1) * share] for i in range(4)]
+        half = share // 2
+        chunks = []
+        for i in range(4):
+            low, high = (table_t[:, i * share + n * half : i * share + (n + 1) * half] for n in range(2))
+            chunks.append(
+                jnp.concatenate([low[: heads // 2], low[heads // 2 :], high[: heads // 2], high[heads // 2 :]], 1)
+            )
         lookup_place = jnp.zeros((5,), i32)
     edge_sums = None
-    for step in range(4):
-        edge_sums = lookup(lookup_place, chunks[step], ids, edge_sums, step, heads)
+    look = lambda step, after: lookup(lookup_place, chunks[step], ids, edge_sums, step, heads, after)
+    if staged:
+        edge_sums = look(0, (pair_b,))
+        stack_a = join(chunks + [own_biases], height, (edge_sums,))
+        across_a, over_a = send(stack_a, links.first), send(stack_a, links.second)
+        pair_b = held_until(pair_b, stack_a)
+        far_b = send(pair_b, links.along_z[1])
+        edge_sums = look(1, (stack_a,))
+        four_b = join([pair_b, far_b], 2 * height, (edge_sums,))
+        near_b = send(four_b, links.along_z[0])
+        edge_sums = look(2, (four_b,))
+        across_a = held_until(across_a, edge_sums)
+        both_a = send(across_a, links.second)
+        eight_b = join_pairs(four_b, near_b, 2 * height, (edge_sums,))
+        over_b = send(eight_b, links.second)
+        edge_sums = look(3, (eight_b,))
+        mine = (stack_a, across_a, over_a)
+        theirs = tuple(send(held_until(part, eight_b), links.core) for part in mine)
+        parts_a = mine + (both_a,) + theirs + (send(both_a, links.core),)
+    else:
+        for step in range(4):
+            edge_sums = look(step, ())
 
     weights, biases, transposed, value_win, probs, att_low, mid, h2 = attend(
         place, node_counts, h1, edge_sums, buckets, spatial_table,
         layer_in, o_bias, ln2_gain, ln2_bias, parts_a,
     )
+    if staged:
+        parts_b = (
+            eight_b, over_b, send(held_until(eight_b, edge_sums), links.core),
+            send(held_until(over_b, mid), links.core),
+        )
+        other_rows_early = send(held_until(rows_early, mid), links.core)
+        feed_after = (other_rows_early,)
+    else:
+        feed_after = ()
     layer_out, grad_mid, grad_att_t, grad_values, mine_b, theirs_b, rows_late, sums = feed(
-        place, mid, h2, weights, biases, out_bias, ln2_gain, cotangent, att_low, probs, parts_b
+        place, mid, h2, weights, biases, out_bias, ln2_gain, cotangent, att_low, probs, parts_b, feed_after
     )
     after = sums
     if staged:
         rows_b = (rows_early, rows_late)
-        other_rows_b = tuple(send(rows, links.core) for rows in rows_b)
-        pieces_b = weight_grads(
+        other_rows_b = (other_rows_early, send(rows_late, links.core))
+        own_b, across_b, second_b = weight_grads(
             plan_second, place, mine_b, send(theirs_b, links.core), rows_b, other_rows_b, height, 4 * width, 4
         )
-        grads_b = reduce_staged(links, *pieces_b)
-        after = pieces_b[0]
+        got_second_b = send(second_b, links.second)
+        after = own_b
     score_grads, mine_a, theirs_a, grad_layer_in, sums = attend_back(
         place, probs, value_win, transposed, grad_att_t, grad_values, weights,
         layer_in, ln1_gain, grad_mid, sums, after,
     )
+    table = functools.partial(table_grads, place, score_grads, ids, buckets, digit, edges)
+    slots = ids.shape[1]
     if staged:
-        pieces_a = weight_grads(
-            plan_first, place, mine_a, send(theirs_a, links.core),
-            (rows_early[0:1],), (other_rows_b[0][0:1],), height, 2 * width, 2,
-        )
-        grads_a = reduce_staged(links, *pieces_a)
-        mine, theirs, small = table_grads(
-            place, score_grads, ids, buckets, sums, pieces_a[0], digit, edges, True
-        )
+        other_columns_a = send(theirs_a, links.core)
+        partial = table(0, 64)
+        across_b = add_rounded((across_b, got_second_b), (partial[0],))
+        got_across_b = send(across_b, links.first)
+        own_a, across_a, second_a = weight_grads(
+            plan_first, place, mine_a, other_columns_a,
+            (rows_early[0:1],), (other_rows_b[0][0:1],), height, 2 * width, 2, (partial[0],),
+        )
+        partial = table(64, 96, partial, after=(own_a, across_b))
+        mine, theirs, small = table(96, slots, partial, sums)
+        got_core = send(theirs, links.core)
+        got_second_a = send(held_until(second_a, small), links.second)
+        stay_b, go_b = add_pair((own_b, got_across_b, got_second_b), (small,))
+        got_pair_b = send(go_b, links.along_z[0])
+        half = features // 2
         sent, keep = small_call(
-            meet_core_kernel, "meet_core", (shape((40, features), f32), shape((16, features), f32)),
-            mine, small, send(theirs, links.core),
+            meet_core_kernel, "meet_core", (shape((64, half), f32), shape((32, half), f32)),
+            mine, small, got_core, stay_b, waits=1,
         )
         sent, keep = small_call(
-            meet_second_kernel, "meet_second", (shape((32, features), f32), shape((8, features), f32)),
-            keep, sent, send(sent, links.second),
-        )
-        outs = small_call(
-            meet_first_kernel, "meet_first", (shape((32, features), f32),) * 4,
+            meet_near_kernel, "meet_near", (shape((48, half), f32), shape((16, half), f32)),
             keep, sent, send(sent, links.first),
         )
-        got = [send(out, hop) for out, hop in zip(outs[1:], links.along_z)]
-        grad_edge, grad_spatial, *rows = small_call(
+        got_last = send(sent, links.second)
+        own_b, go_b = add_half(stay_b, got_pair_b, (sent,))
+        got_b = send(go_b, links.along_z[1])
+        across_a = add_rounded((across_a, got_second_a), (own_b,))
+        got_across_a = send(across_a, links.first)
+        own_a = small_call(
+            meet_far_kernel, "meet_far", (shape((height + 32, half), bf16),) * 4,
+            keep, sent, got_last, own_a, got_across_a, got_second_a,
+        )
+        got_a = [send(own_a[step + 1], hop) for step, hop in enumerate(links.along_z)]
+        grad_w_in, grad_w_out, grad_w_o, grad_w_v = settle([own_b, got_b], width, (own_a[0],))
+        grad_w_q, grad_w_k, grad_edge, grad_spatial, *rows = small_call(
             finish_kernel, "finish",
-            (shape((8, digit), f32), shape((8, kinds), f32))
+            (shape((height, width), f32),) * 2
+            + (shape((8, digit), f32), shape((8, kinds), f32))
             + (shape((features,), f32),) * 6
             + (shape((width,), f32),) * 3,
-            place, outs[0], *got,
+            place, own_a[0], *got_a, grad_w_in, waits=1, mebibytes=60,
         )
         grad_edge = grad_edge.T
         grad_spatial = grad_spatial.T
-        grad_w_q, grad_w_k = (grads_a[:, i * width : (i + 1) * width] for i in range(2))
-        grad_w_in, grad_w_out, grad_w_o, grad_w_v = (
-            grads_b[:, i * width : (i + 1) * width] for i in range(4)
-        )
     else:
         contract = lambda a, b: lax.dot_general(
             a, b, (((1,), (1,)), ((), ())), preferred_element_type=f32
@@ -937,7 +1099,7 @@
         grad_w_in = scatter(rows_late[0], columns_b[:, :, :width])
         grad_w_out = scatter(rows_early[1], columns_b[:, :, 512 - width : 512])
         grad_w_o = scatter(rows_late[1], columns_b[:, :, 512 : 512 + width])
-        table, spatial = table_grads(place, score_grads, ids, buckets, sums, sums, digit, edges, False)
+        table, spatial = table(0, slots)
         table = table.reshape(-1, heads, digit).transpose(0, 2, 1).reshape(edges, heads) / hops
         table = lax.psum_scatter(table, "dp", scatter_dimension=0, tiled=True)
         table = lax.psum(table, "mp")

time: 159 us -> 141 us (0.89)
  waiting for transfers between devices: 44.7 us -> 30.6 us
  starting transfers between devices: 41.8 us -> 32.3 us
  Pallas kernels: 64.3 us -> 72.2 us
    ppermute x43 -> x33, waiting for transfers between devices: 44.7 us -> 30.6 us  [send(): return lax.ppermute(values, ('dp', 'mp'), hop)]
    ppermute x43 -> x33, starting transfers between devices: 41.8 us -> 32.3 us  [send(): return lax.ppermute(values, ('dp', 'mp'), hop)]
    pallas_call x4 -> x13, Pallas kernels: 1.29 us -> 4.54 us  [small_call(): pl.pallas_call(kernel, out_shape=outs, in_specs=[smem if args[i].ndim ==...]
    pallas_call x3 -> x5, Pallas kernels: 18 us -> 20.3 us  [the longest x3 16.3 us: table_grads(): pl.pallas_call(functools.partial(table_kernel, digit, start, stop, len(pr...]
    pallas_call x1, Pallas kernels: 0.99 us -> 3.22 us  [prepare(): pl.pallas_call(functools.partial(prepare_kernel, virtual), grid_spec=pltp...]
    unnamed x40 -> x50, local copies, waits for them, and re-layouts: 3.85 us -> 3.65 us
  transfers between devices with their start and end apart: 43 -> 33, of which waited for: 13 -> 14; matrix products, arithmetic and copies ran while one was open for 3% -> 0% of each run, Pallas kernels for 31% -> 42%
where the time goes in v4:
time: 141 us
  Pallas kernels  72.2 us (51%)
  starting transfers between devices  32.3 us (23%)
  waiting for transfers between devices  30.6 us (22%)
  local copies, waits for them, and re-layouts  4.34 us (3%)
    ppermute x33, starting transfers between devices, send(): return lax.ppermute(values, ('dp', 'mp'), hop)  32.3 us
    ppermute x33, waiting for transfers between devices, send(): return lax.ppermute(values, ('dp', 'mp'), hop)  30.6 us
    pallas_call x4, Pallas kernels, lookup(): pl.pallas_call(functools.partial(lookup_kernel, first, step, share), out_...  24.5 us
    pallas_call x3, Pallas kernels, table_grads(): pl.pallas_call(functools.partial(table_kernel, digit, start, stop, len(pr...  16.3 us
    pallas_call x1, Pallas kernels, feed(): pl.pallas_call(functools.partial(feed_kernel, len(parts)), grid=(1,), out...  5.7 us
    pallas_call x1, Pallas kernels, attend(): pl.pallas_call(functools.partial(attend_kernel, len(parts)), out_shape=(s...  5.4 us
    pallas_call x1, Pallas kernels, attend_back(): pl.pallas_call(attend_back_kernel, out_shape=(shape((groups, slots, 8, sl...  5.01 us
    pallas_call x13, Pallas kernels, small_call(): pl.pallas_call(kernel, out_shape=outs, in_specs=[smem if args[i].ndim ==...  4.54 us
  transfers between devices with their start and end apart: 33, of which 14 were waited for; matrix products, arithmetic and copies ran while one was open for 0% of the time, Pallas kernels for 42%

profile of v4, /device:TPU:0, one launch (start us, length us, event | category | flops | bytes accessed | tf_op | source)
XLA Modules:
  0.0 140.7 jit_solution(7632988325179605919)
XLA Ops:
  0.7 3.0 %collective-permute-start = (bf16[32,192]{1,0:T(8,128)(2,1)}, bf16[32,192]{1,0:T(8,128)(2,1)S(1)}, u32[]{:S(2)}, u32[]{:S(2)}) collective-permute-start(bf16[32,192]{1,0:T(8,128)(2,1)} %bitcast.8), channel_id=1, source_target_pairs={{0,4},{1,5},{2,6},{3,7},{4,0},{5,1},{6,2},{7,3},{8,12},{9,13},{10,... | collective-permute-start | bytes 36872 | tf_op jit(solution)/shard_map/ppermute | solution.py:806
  4.3 1.5 %pack_second.1.after.refs_0_ = bf16[96,384]{1,0:T(8,128)(2,1)} custom-call(bf16[96,192]{1,0:T(8,128)(2,1)} %wi.1, bf16[96,192]{1,0:T(8,128)(2,1)} %wu.1), custom_call_target="tpu_custom_call" | custom-call | flops 115000000 | bytes 1024 | tf_op jit(solution)/shard_map/pack_second/pallas_call | solution.py:128
  6.5 2.5 %pack_first.1 = (bf16[112,768]{1,0:T(8,128)(2,1)}, bf16[16,768]{1,0:T(8,128)(2,1)}) custom-call(s32[5]{0:T(128)} %stack.23.place, bf16[96,192]{1,0:T(8,128)(2,1)} %wq.1, bf16[96,192]{1,0:T(8,128)(2,1)} %wk.1, bf16[96,192]{1,0:T(8,128)(2,1)} %wv.1, bf16[96,192]{1,0:T(8,128)(2,1)} %wo.1, f32[192]{0:T(256)} %bq.1, f32[192]{0:T(256)} %bv.1, f32[192]{0:T(256)} %bi.1, ...), custom_call_target="tpu_custom_call" | custom-call | flops 230000000 | bytes 1024 | tf_op jit(solution)/shard_map/pack_first/pallas_call | solution.py:110
  9.0 3.9 %collective-permute-start.1 = (bf16[112,768]{1,0:T(8,128)(2,1)}, bf16[112,768]{1,0:T(8,128)(2,1)S(1)}, u32[]{:S(2)}, u32[]{:S(2)}) collective-permute-start(bf16[112,768]{1,0:T(8,128)(2,1)} %get-tuple-element.98.chunk.refs_0_), channel_id=1, source_target_pairs={{0,24},{1,25},{2,26},{3,27},{4,28},{5,29},{6,30},{7,31},{8,16},{9,... | collective-permute-start | bytes 516104 | tf_op jit(solution)/shard_map/ppermute | solution.py:806
  13.5 1.6 %collective-permute-start.4 = (bf16[96,384]{1,0:T(8,128)(2,1)}, bf16[96,384]{1,0:T(8,128)(2,1)S(1)}, u32[]{:S(2)}, u32[]{:S(2)}) collective-permute-start(bf16[96,384]{1,0:T(8,128)(2,1)} %pack_second.1.after.refs_0_), channel_id=1, source_target_pairs={{0,4},{1,3},{2,6},{3,1},{4,0},{5,7},{6,2},{7,5},{8,12},{9,11},{10,... | collective-permute-start | bytes 221192 | tf_op jit(solution)/shard_map/ppermute | solution.py:806
  15.2 3.2 %prepare.1 = (s32[5,128,128]{2,1,0:T(8,128)}, s32[128,128]{1,0:T(8,128)}, bf16[128,768]{1,0:T(8,128)(2,1)}, bf16[2,768,128]{2,1,0:T(8,128)(2,1)}) custom-call(s32[5]{0:T(128)} %stack.23.place, s32[4,128,128]{2,1,0:T(8,128)} %spatial.1, s32[4,5,128,128]{3,2,1,0:T(8,128)} %path.1, f32[128,768]{1,0:T(8,128)} %layer_in.5, f32[768]{0:T(1024)} %gain.7, f32[768]{0:T(1024)} %bias.2, ...), custom_call_target="tpu_custom_call" | custom-call | flops 115000000 | bytes 1024 | tf_op jit(solution)/shard_map/prepare/pallas_call | solution.py:157
  19.4 6.1 %lookup.4.refs_5_.refs_0_ = s32[16,128,128]{2,1,0:T(8,128)S(1)} custom-call(s32[5]{0:T(128)S(1)} %copy-done.10, bf16[112,768]{1,0:T(8,128)(2,1)S(1)} %copy-done.7, s32[5,128,128]{2,1,0:T(8,128)S(1)} %copy-done, bf16[192,384]{1,0:T(8,128)(2,1)S(1)} %join.3.refs_0_), custom_call_target="tpu_custom_call" | custom-call | flops 690000000 | bytes 1024 | tf_op jit(solution)/shard_map/lookup/pallas_call | solution.py:250
  25.5 1.6 %collective-permute-done.2.refs_2_.chunk = bf16[112,768]{1,0:T(8,128)(2,1)S(1)} collective-permute-done((bf16[112,768]{1,0:T(8,128)(2,1)}, bf16[112,768]{1,0:T(8,128)(2,1)S(1)}, u32[]{:S(2)}, u32[]{:S(2)}) %collective-permute-start.2) | collective-permute-done | bytes 172064 | tf_op jit(solution)/shard_map/ppermute | solution.py:806
  30.7 6.1 %lookup.5.refs_2_.refs_0_ = s32[16,128,128]{2,1,0:T(8,128)S(1)} custom-call(s32[5]{0:T(128)S(1)} %copy-done.10, bf16[112,768]{1,0:T(8,128)(2,1)S(1)} %collective-permute-done.3.refs_1_.chunk, s32[5,128,128]{2,1,0:T(8,128)S(1)} %copy-done.1, s32[16,128,128]{2,1,0:T(8,128)S(1)} %lookup.4.refs_5_.refs_0_, ...), custom_call_target="tpu_custom_call", output_to_operand_aliasing={{}: (3, {})} | custom-call | flops 690000000 | bytes 1024 | tf_op jit(solution)/shard_map/lookup/pallas_call | solution.py:250
  36.8 6.1 %lookup.6.refs_0_ = s32[16,128,128]{2,1,0:T(8,128)S(1)} custom-call(s32[5]{0:T(128)S(1)} %copy-done.10, bf16[112,768]{1,0:T(8,128)(2,1)S(1)} %collective-permute-done.2.refs_2_.chunk, s32[5,128,128]{2,1,0:T(8,128)S(1)} %copy-done.1, s32[16,128,128]{2,1,0:T(8,128)S(1)} %lookup.5.refs_2_.refs_0_, ...), custom_call_target="tpu_custom_call", output_to_operand_aliasing={{}: (3, {})} | custom-call | flops 690000000 | bytes 1024 | tf_op jit(solution)/shard_map/lookup/pallas_call | solution.py:250
  43.9 1.7 %collective-permute-start.6 = (bf16[384,384]{1,0:T(8,128)(2,1)S(1)}, bf16[384,384]{1,0:T(8,128)(2,1)S(1)}, u32[]{:S(2)}, u32[]{:S(2)}) collective-permute-start(bf16[384,384]{1,0:T(8,128)(2,1)S(1)} %join.5.refs_1_.own), channel_id=1, source_target_pairs={{0,8},{1,9},{2,10},{3,11},{4,12},{5,13},{6,14},{7,15},{8,0},{9,1},... | collective-permute-start | bytes 884744 | tf_op jit(solution)/shard_map/ppermute | solution.py:806
  45.6 6.0 %collective-permute-done.6.near = bf16[384,384]{1,0:T(8,128)(2,1)S(1)} collective-permute-done((bf16[384,384]{1,0:T(8,128)(2,1)S(1)}, bf16[384,384]{1,0:T(8,128)(2,1)S(1)}, u32[]{:S(2)}, u32[]{:S(2)}) %collective-permute-start.6) | collective-permute-done | bytes 294944 | tf_op jit(solution)/shard_map/ppermute | solution.py:806
  54.0 6.3 %lookup.7.edge_sums = s32[16,128,128]{2,1,0:T(8,128)S(1)} custom-call(s32[5]{0:T(128)S(1)} %copy-done.10, bf16[112,768]{1,0:T(8,128)(2,1)S(1)} %collective-permute-done.1.refs_3_.chunk, s32[5,128,128]{2,1,0:T(8,128)S(1)} %copy-done.1, s32[16,128,128]{2,1,0:T(8,128)S(1)} %lookup.6.refs_0_, ...), custom_call_target="tpu_custom_call", output_to_operand_aliasing={{}: (3, {})} | custom-call | flops 690000000 | bytes 1024 | tf_op jit(solution)/shard_map/lookup/pallas_call | solution.py:250
  61.1 5.4 %attend.1 = (bf16[4,768,768]{2,1,0:T(8,128)(2,1)S(1)}, f32[4,1,768]{2,1,0:T(1,128)S(1)}, bf16[4,384,128]{2,1,0:T(8,128)(2,1)S(1)}, bf16[4,128,256]{2,1,0:T(8,128...) custom-call(s32[5]{0:T(128)S(1)} %copy-done.10, ...), custom_call_target="tpu_custom_call" | custom-call | flops 805000000 | bytes 1024 | tf_op jit(solution)/shard_map/attend/pallas_call | solution.py:366
  67.1 2.0 %collective-permute-done.17.refs_4_.refs_2_ = bf16[2,768,128]{2,1,0:T(8,128)(2,1)S(1)} collective-permute-done((bf16[2,768,128]{2,1,0:T(8,128)(2,1)S(1)}, bf16[2,768,128]{2,1,0:T(8,128)(2,1)S(1)}, u32[]{:S(2)}, u32[]{:S(2)}) %collective-permute-start.17) | collective-permute-done | bytes 393248 | tf_op jit(solution)/shard_map/ppermute | solution.py:806
  69.2 5.7 %feed.1 = (f32[128,768]{1,0:T(8,128)}, f32[128,768]{1,0:T(8,128)S(1)}, bf16[4,256,128]{2,1,0:T(8,128)(2,1)S(1)}, bf16[4,128,256]{2,1,0:T(8,128)(2,1)S(1)}, bf16[...) custom-call(s32[5]{0:T(128)S(1)} %copy-done.10, ...), custom_call_target="tpu_custom_call" | custom-call | flops 805000000 | bytes 1024 | tf_op jit(solution)/shard_map/feed/pallas_call | solution.py:476
  75.4 2.0 %collective-permute-done.19.refs_3_ = bf16[2,768,128]{2,1,0:T(8,128)(2,1)S(1)} collective-permute-done((bf16[2,768,128]{2,1,0:T(8,128)(2,1)S(1)}, bf16[2,768,128]{2,1,0:T(8,128)(2,1)S(1)}, u32[]{:S(2)}, u32[]{:S(2)}) %collective-permute-start.19) | collective-permute-done | bytes 393248 | tf_op jit(solution)/shard_map/ppermute | solution.py:806
  77.4 2.3 %weight_grads.2 = (bf16[4,96,768]{2,1,0:T(8,128)(2,1)S(1)}, bf16[4,96,768]{2,1,0:T(8,128)(2,1)S(1)}, bf16[8,96,768]{2,1,0:T(8,128)(2,1)S(1)}) custom-call(s32[5]{0:T(128)S(1)} %copy-done.10, bf16[2,128,1024]{2,1,0:T(8,128)(2,1)S(1)} %get-tuple-element.124.columns_own, bf16[2,128,1024]{2,1,0:T(8,128)(2,1)S(1)} %collective-permute-done.18.columns_other, ...), custom_call_target="tpu_custom_call" | custom-call | flops 460000000 | bytes 1024 | tf_op jit(solution)/shard_map/weight_grads/pallas_call | solution.py:611
  80.8 5.0 %attend_back.1 = (f32[4,128,8,128]{3,2,1,0:T(8,128)S(1)}, bf16[2,128,384]{2,1,0:T(8,128)(2,1)S(1)}, bf16[2,128,384]{2,1,0:T(8,128)(2,1)S(1)}, f32[128,768]{1,0:T(8,128)}, f32[16,768]{1,0:T(8,128)S(1)}) custom-call(s32[5]{0:T(128)S(1)} %copy-done.10, f32[32,128,128]{2,1,0:T(8,128)S(1)} %get-tuple-element.112.probs_in, ...), custom_call_target="tpu_custom_call" | custom-call | flops 805000000 | bytes 1024 | tf_op jit(solution)/shard_map/attend_back/pallas_call | solution.py:542
  85.8 7.9 %table_grads.3 = (f32[256,192]{1,0:T(8,128)S(1)}, f32[32,32]{1,0:T(8,128)S(1)}) custom-call(s32[5]{0:T(128)S(1)} %copy-done.10, f32[4,128,8,128]{3,2,1,0:T(8,128)S(1)} %get-tuple-element.129.grads, s32[5,128,128]{2,1,0:T(8,128)S(1)} %copy-done.1, s32[128,128]{1,0:T(8,128)S(1)} %copy-done.5), custom_call_target="tpu_custom_call" | custom-call | flops 862499968 | bytes 1024 | tf_op jit(solution)/shard_map/table_grads/pallas_call | solution.py:707
  93.7 2.2 %collective-permute-done.21.refs_1_.refs_2_ = bf16[8,96,768]{2,1,0:T(8,128)(2,1)S(1)} collective-permute-done((bf16[8,96,768]{2,1,0:T(8,128)(2,1)S(1)}, bf16[8,96,768]{2,1,0:T(8,128)(2,1)S(1)}, u32[]{:S(2)}, u32[]{:S(2)}) %collective-permute-start.21) | collective-permute-done | bytes 1179680 | tf_op jit(solution)/shard_map/ppermute | solution.py:806
  99.9 4.1 %table_grads.4 = (f32[256,192]{1,0:T(8,128)S(1)}, f32[32,32]{1,0:T(8,128)S(1)}) custom-call(s32[5]{0:T(128)S(1)} %copy-done.10, f32[4,128,8,128]{3,2,1,0:T(8,128)S(1)} %get-tuple-element.129.grads, s32[5,128,128]{2,1,0:T(8,128)S(1)} %copy-done.1, s32[128,128]{1,0:T(8,128)S(1)} %copy-done.5, f32[256,192]{1,0:T(8,128)S(1)} %get-tuple-element.130.refs_2_.refs_0_, ...), custom_call_target="tpu_custom_call" | custom-call | flops 431249984 | bytes 1024 | tf_op jit(solution)/shard_map/table_grads/pallas_call | solution.py:707
  104.1 4.2 %table_grads.5 = (f32[64,384]{1,0:T(8,128)S(1)}, f32[96,384]{1,0:T(8,128)S(1)}, f32[32,384]{1,0:T(8,128)S(1)}) custom-call(s32[5]{0:T(128)S(1)} %copy-done.10, f32[4,128,8,128]{3,2,1,0:T(8,128)S(1)} %get-tuple-element.129.grads, s32[5,128,128]{2,1,0:T(8,128)S(1)} %copy-done.1, s32[128,128]{1,0:T(8,128)S(1)} %copy-done.5, ...), custom_call_target="tpu_custom_call" | custom-call | flops 431249984 | bytes 1024 | tf_op jit(solution)/shard_map/table_grads/pallas_call | solution.py:707
  109.4 2.0 %collective-permute-start.27 = (bf16[2,96,768]{2,1,0:T(8,128)(2,1)S(1)}, bf16[2,96,768]{2,1,0:T(8,128)(2,1)S(1)}, u32[]{:S(2)}, u32[]{:S(2)}) collective-permute-start(bf16[2,96,768]{2,1,0:T(8,128)(2,1)S(1)} %get-tuple-element.151), channel_id=1, source_target_pairs={{0,8},{1,9},{2,10},{3,11},{4,12},{5,13},{6,14},{7,15},{8,0},{9,1},... | collective-permute-start | bytes 884744 | tf_op jit(solution)/shard_map/ppermute | solution.py:806
  113.7 4.8 %collective-permute-done.24.got = f32[64,384]{1,0:T(8,128)S(1)} collective-permute-done((f32[64,384]{1,0:T(8,128)S(1)}, f32[64,384]{1,0:T(8,128)S(1)}, u32[]{:S(2)}, u32[]{:S(2)}) %collective-permute-start.24) | collective-permute-done | bytes 98336 | tf_op jit(solution)/shard_map/ppermute | solution.py:806
  121.4 2.1 %collective-permute-start.32 = (bf16[96,768]{1,0:T(8,128)(2,1)S(1)}, bf16[96,768]{1,0:T(8,128)(2,1)S(1)}, u32[]{:S(2)}, u32[]{:S(2)}) collective-permute-start(bf16[96,768]{1,0:T(8,128)(2,1)S(1)} %get-tuple-element.157), channel_id=1, source_target_pairs={{0,16},{1,17},{2,18},{3,19},{4,20},{5,21},{6,22},{7,23},{8,24},{9,... | collective-permute-start | bytes 442376 | tf_op jit(solution)/shard_map/ppermute | solution.py:806
  123.5 1.7 %collective-permute-done.25.got = f32[48,384]{1,0:T(8,128)S(1)} collective-permute-done((f32[48,384]{1,0:T(8,128)S(1)}, f32[48,384]{1,0:T(8,128)S(1)}, u32[]{:S(2)}, u32[]{:S(2)}) %collective-permute-start.25) | collective-permute-done | bytes 73760 | tf_op jit(solution)/shard_map/ppermute | solution.py:806
  127.0 1.7 %collective-permute-start.29 = (bf16[128,384]{1,0:T(8,128)(2,1)S(1)}, bf16[128,384]{1,0:T(8,128)(2,1)S(1)}, u32[]{:S(2)}, u32[]{:S(2)}) collective-permute-start(bf16[128,384]{1,0:T(8,128)(2,1)S(1)} %get-tuple-element.154), channel_id=1, source_target_pairs={{0,8},{1,9},{2,10},{3,11},{4,12},{5,13},{6,14},{7,15},{8,0},{9,1},... | collective-permute-start | bytes 294920 | tf_op jit(solution)/shard_map/ppermute | solution.py:806
  129.4 1.9 %collective-permute-start.31 = (bf16[128,384]{1,0:T(8,128)(2,1)S(1)}, bf16[128,384]{1,0:T(8,128)(2,1)S(1)}, u32[]{:S(2)}, u32[]{:S(2)}) collective-permute-start(bf16[128,384]{1,0:T(8,128)(2,1)S(1)} %get-tuple-element.156), channel_id=1, source_target_pairs={{0,24},{1,25},{2,26},{3,27},{4,28},{5,29},{6,30},{7,31},{8,16},{9,... | collective-permute-start | bytes 294920 | tf_op jit(solution)/shard_map/ppermute | solution.py:806
  132.0 1.8 %settle.1 = (f32[96,192]{1,0:T(8,128)}, f32[96,192]{1,0:T(8,128)}, f32[96,192]{1,0:T(8,128)}, f32[96,192]{1,0:T(8,128)}) custom-call(bf16[96,768]{1,0:T(8,128)(2,1)} %copy-done.8, bf16[96,768]{1,0:T(8,128)(2,1)} %copy-done.23, bf16[128,384]{1,0:T(8,128)(2,1)} %copy-done.9), custom_call_target="tpu_custom_call" | custom-call | flops 115000000 | bytes 1024 | tf_op jit(solution)/shard_map/settle/pallas_call | solution.py:778
  133.8 4.1 %collective-permute-done.30.second = bf16[128,384]{1,0:T(8,128)(2,1)S(1)} collective-permute-done((bf16[128,384]{1,0:T(8,128)(2,1)S(1)}, bf16[128,384]{1,0:T(8,128)(2,1)S(1)}, u32[]{:S(2)}, u32[]{:S(2)}) %collective-permute-start.30) | collective-permute-done | bytes 98336 | tf_op jit(solution)/shard_map/ppermute | solution.py:806
  138.6 2.0 %finish.1 = (f32[96,192]{1,0:T(8,128)}, f32[96,192]{1,0:T(8,128)}, f32[8,192]{1,0:T(8,128)}, f32[8,22]{1,0:T(8,128)}, f32[768]{0:T(1024)}, /*index=5*/f32[768]{0...) custom-call(s32[5]{0:T(128)} %stack.23.place, ...), custom_call_target="tpu_custom_call" | custom-call | flops 115000000 | bytes 1024 | tf_op jit(solution)/shard_map/finish/pallas_call | solution.py:778
  (115 shorter events, 27.0 us)
Async XLA Ops:
  0.7 5.2 %collective-permute-start = (bf16[32,192]{1,0:T(8,128)(2,1)}, bf16[32,192]{1,0:T(8,128)(2,1)S(1)}, u32[]{:S(2)}, u32[]{:S(2)}) collective-permute-start(bf16[32,192]{1,0:T(8,128)(2,1)} %bitcast.8), channel_id=1, source_target_pairs={{0,4},{1,5},{2,6},{3,7},{4,0},{5,1},{6,2},{7,3},{8,12},{9,13},{10,... | collective-permute-start | bytes 36872 | tf_op jit(solution)/shard_map/ppermute | solution.py:806
  9.0 16.5 %collective-permute-start.1 = (bf16[112,768]{1,0:T(8,128)(2,1)}, bf16[112,768]{1,0:T(8,128)(2,1)S(1)}, u32[]{:S(2)}, u32[]{:S(2)}) collective-permute-start(bf16[112,768]{1,0:T(8,128)(2,1)} %get-tuple-element.98.chunk.refs_0_), channel_id=1, source_target_pairs={{0,24},{1,25},{2,26},{3,27},{4,28},{5,29},{6,30},{7,31},{8,16},{9,... | collective-permute-start | bytes 516104 | tf_op jit(solution)/shard_map/ppermute | solution.py:806
  12.9 14.3 %collective-permute-start.2 = (bf16[112,768]{1,0:T(8,128)(2,1)}, bf16[112,768]{1,0:T(8,128)(2,1)S(1)}, u32[]{:S(2)}, u32[]{:S(2)}) collective-permute-start(bf16[112,768]{1,0:T(8,128)(2,1)} %get-tuple-element.98.chunk.refs_0_), channel_id=1, source_target_pairs={{0,16},{1,17},{2,18},{3,19},{4,20},{5,21},{6,22},{7,23},{8,24},{9,... | collective-permute-start | bytes 516104 | tf_op jit(solution)/shard_map/ppermute | solution.py:806
  12.9 14.3 %collective-permute-start.3 = (bf16[112,768]{1,0:T(8,128)(2,1)}, bf16[112,768]{1,0:T(8,128)(2,1)S(1)}, u32[]{:S(2)}, u32[]{:S(2)}) collective-permute-start(bf16[112,768]{1,0:T(8,128)(2,1)} %get-tuple-element.98.chunk.refs_0_), channel_id=1, source_target_pairs={{0,8},{1,9},{2,10},{3,11},{4,12},{5,13},{6,14},{7,15},{8,0},{9,1},... | collective-permute-start | bytes 516104 | tf_op jit(solution)/shard_map/ppermute | solution.py:806
  13.5 4.9 %collective-permute-start.4 = (bf16[96,384]{1,0:T(8,128)(2,1)}, bf16[96,384]{1,0:T(8,128)(2,1)S(1)}, u32[]{:S(2)}, u32[]{:S(2)}) collective-permute-start(bf16[96,384]{1,0:T(8,128)(2,1)} %pack_second.1.after.refs_0_), channel_id=1, source_target_pairs={{0,4},{1,3},{2,6},{3,1},{4,0},{5,7},{6,2},{7,5},{8,12},{9,11},{10,... | collective-permute-start | bytes 221192 | tf_op jit(solution)/shard_map/ppermute | solution.py:806
  27.2 16.2 %collective-permute-start.7 = (bf16[400,768]{1,0:T(8,128)(2,1)S(1)}, bf16[400,768]{1,0:T(8,128)(2,1)S(1)}, u32[]{:S(2)}, u32[]{:S(2)}) collective-permute-start(bf16[400,768]{1,0:T(8,128)(2,1)S(1)} %join.4.refs_1_.refs_0_), channel_id=1, source_target_pairs={{0,4},{1,3},{2,6},{3,1},{4,0},{5,7},{6,2},{7,5},{8,12},{9,11},{10,... | collective-permute-start | bytes 1843208 | tf_op jit(solution)/shard_map/ppermute | solution.py:806
  28.2 8.6 %collective-permute-start.5 = (bf16[192,384]{1,0:T(8,128)(2,1)S(1)}, bf16[192,384]{1,0:T(8,128)(2,1)S(1)}, u32[]{:S(2)}, u32[]{:S(2)}) collective-permute-start(bf16[192,384]{1,0:T(8,128)(2,1)S(1)} %join.3.refs_0_), channel_id=1, source_target_pairs={{0,16},{1,17},{2,18},{3,19},{4,20},{5,21},{6,22},{7,23},{8,24},{9,... | collective-permute-start | bytes 442376 | tf_op jit(solution)/shard_map/ppermute | solution.py:806
  29.2 22.6 %collective-permute-start.8 = (bf16[400,768]{1,0:T(8,128)(2,1)S(1)}, bf16[400,768]{1,0:T(8,128)(2,1)S(1)}, u32[]{:S(2)}, u32[]{:S(2)}) collective-permute-start(bf16[400,768]{1,0:T(8,128)(2,1)S(1)} %join.4.refs_1_.refs_0_), channel_id=1, source_target_pairs={{0,2},{1,5},{2,0},{3,7},{4,6},{5,1},{6,4},{7,3},{8,10},{9,13},{10,... | collective-permute-start | bytes 1843208 | tf_op jit(solution)/shard_map/ppermute | solution.py:806
  43.4 10.1 %collective-permute-start.9 = (bf16[400,768]{1,0:T(8,128)(2,1)S(1)}, bf16[400,768]{1,0:T(8,128)(2,1)S(1)}, u32[]{:S(2)}, u32[]{:S(2)}) collective-permute-start(bf16[400,768]{1,0:T(8,128)(2,1)S(1)} %collective-permute-done.7.refs_1_), channel_id=1, source_target_pairs={{0,2},{1,5},{2,0},{3,7},{4,6},{5,1},{6,4},{7,3},{8,10},{9,13},{10,... | collective-permute-start | bytes 1843208 | tf_op jit(solution)/shard_map/ppermute | solution.py:806
  43.9 7.7 %collective-permute-start.6 = (bf16[384,384]{1,0:T(8,128)(2,1)S(1)}, bf16[384,384]{1,0:T(8,128)(2,1)S(1)}, u32[]{:S(2)}, u32[]{:S(2)}) collective-permute-start(bf16[384,384]{1,0:T(8,128)(2,1)S(1)} %join.5.refs_1_.own), channel_id=1, source_target_pairs={{0,8},{1,9},{2,10},{3,11},{4,12},{5,13},{6,14},{7,15},{8,0},{9,1},... | collective-permute-start | bytes 884744 | tf_op jit(solution)/shard_map/ppermute | solution.py:806
  51.7 8.6 %collective-permute-start.10 = (bf16[400,768]{1,0:T(8,128)(2,1)S(1)}, bf16[400,768]{1,0:T(8,128)(2,1)S(1)}, u32[]{:S(2)}, u32[]{:S(2)}) collective-permute-start(bf16[400,768]{1,0:T(8,128)(2,1)S(1)} %join.4.refs_1_.refs_0_), channel_id=1, source_target_pairs={{0,1},{1,0},{2,3},{3,2},{4,5},{5,4},{6,7},{7,6},{8,9},{9,8},{10,11... | collective-permute-start | bytes 1843208 | tf_op jit(solution)/shard_map/ppermute | solution.py:806
  51.8 9.2 %collective-permute-start.12 = (bf16[400,768]{1,0:T(8,128)(2,1)S(1)}, bf16[400,768]{1,0:T(8,128)(2,1)S(1)}, u32[]{:S(2)}, u32[]{:S(2)}) collective-permute-start(bf16[400,768]{1,0:T(8,128)(2,1)S(1)} %collective-permute-done.8.refs_2_), channel_id=1, source_target_pairs={{0,1},{1,0},{2,3},{3,2},{4,5},{5,4},{6,7},{7,6},{8,9},{9,8},{10,11... | collective-permute-start | bytes 1843208 | tf_op jit(solution)/shard_map/ppermute | solution.py:806
  52.3 8.7 %collective-permute-start.11 = (bf16[400,768]{1,0:T(8,128)(2,1)S(1)}, bf16[400,768]{1,0:T(8,128)(2,1)S(1)}, u32[]{:S(2)}, u32[]{:S(2)}) collective-permute-start(bf16[400,768]{1,0:T(8,128)(2,1)S(1)} %collective-permute-done.7.refs_1_), channel_id=1, source_target_pairs={{0,1},{1,0},{2,3},{3,2},{4,5},{5,4},{6,7},{7,6},{8,9},{9,8},{10,11... | collective-permute-start | bytes 1843208 | tf_op jit(solution)/shard_map/ppermute | solution.py:806
  53.5 7.5 %collective-permute-start.13 = (bf16[400,768]{1,0:T(8,128)(2,1)S(1)}, bf16[400,768]{1,0:T(8,128)(2,1)S(1)}, u32[]{:S(2)}, u32[]{:S(2)}) collective-permute-start(bf16[400,768]{1,0:T(8,128)(2,1)S(1)} %collective-permute-done.9.refs_3_), channel_id=1, source_target_pairs={{0,1},{1,0},{2,3},{3,2},{4,5},{5,4},{6,7},{7,6},{8,9},{9,8},{10,11... | collective-permute-start | bytes 1843208 | tf_op jit(solution)/shard_map/ppermute | solution.py:806
  53.5 13.0 %collective-permute-start.14 = (bf16[768,384]{1,0:T(8,128)(2,1)S(1)}, bf16[768,384]{1,0:T(8,128)(2,1)S(1)}, u32[]{:S(2)}, u32[]{:S(2)}) collective-permute-start(bf16[768,384]{1,0:T(8,128)(2,1)S(1)} %join_pairs.1.refs_1_.refs_0_), channel_id=1, source_target_pairs={{0,2},{1,5},{2,0},{3,7},{4,6},{5,1},{6,4},{7,3},{8,10},{9,13},{10,... | collective-permute-start | bytes 1769480 | tf_op jit(solution)/shard_map/ppermute | solution.py:806
  60.3 6.8 %collective-permute-start.15 = (bf16[768,384]{1,0:T(8,128)(2,1)S(1)}, bf16[768,384]{1,0:T(8,128)(2,1)S(1)}, u32[]{:S(2)}, u32[]{:S(2)}) collective-permute-start(bf16[768,384]{1,0:T(8,128)(2,1)S(1)} %join_pairs.1.refs_1_.refs_0_), channel_id=1, source_target_pairs={{0,1},{1,0},{2,3},{3,2},{4,5},{5,4},{6,7},{7,6},{8,9},{9,8},{10,11... | collective-permute-start | bytes 1769480 | tf_op jit(solution)/shard_map/ppermute | solution.py:806
  66.5 2.6 %collective-permute-start.16 = (bf16[768,384]{1,0:T(8,128)(2,1)S(1)}, bf16[768,384]{1,0:T(8,128)(2,1)S(1)}, u32[]{:S(2)}, u32[]{:S(2)}) collective-permute-start(bf16[768,384]{1,0:T(8,128)(2,1)S(1)} %collective-permute-done.14.refs_1_), channel_id=1, source_target_pairs={{0,1},{1,0},{2,3},{3,2},{4,5},{5,4},{6,7},{7,6},{8,9},{9,8},{10,11... | collective-permute-start | bytes 1769480 | tf_op jit(solution)/shard_map/ppermute | solution.py:806
  66.6 2.5 %collective-permute-start.17 = (bf16[2,768,128]{2,1,0:T(8,128)(2,1)S(1)}, bf16[2,768,128]{2,1,0:T(8,128)(2,1)S(1)}, u32[]{:S(2)}, u32[]{:S(2)}) collective-permute-start(bf16[2,768,128]{2,1,0:T(8,128)(2,1)S(1)} %copy-done.4), channel_id=1, source_target_pairs={{0,1},{1,0},{2,3},{3,2},{4,5},{5,4},{6,7},{7,6},{8,9},{9,8},{10,11... | collective-permute-start | bytes 1179656 | tf_op jit(solution)/shard_map/ppermute | solution.py:806
  74.9 2.5 %collective-permute-start.18 = (bf16[2,128,1024]{2,1,0:T(8,128)(2,1)S(1)}, bf16[2,128,1024]{2,1,0:T(8,128)(2,1)S(1)}, u32[]{:S(2)}, u32[]{:S(2)}) collective-permute-start(bf16[2,128,1024]{2,1,0:T(8,128)(2,1)S(1)} %get-tuple-element.125), channel_id=1, source_target_pairs={{0,1},{1,0},{2,3},{3,2},{4,5},{5,4},{6,7},{7,6},{8,9},{9,8},{10,11... | collective-permute-start | bytes 1572872 | tf_op jit(solution)/shard_map/ppermute | solution.py:806
  75.0 2.3 %collective-permute-start.19 = (bf16[2,768,128]{2,1,0:T(8,128)(2,1)S(1)}, bf16[2,768,128]{2,1,0:T(8,128)(2,1)S(1)}, u32[]{:S(2)}, u32[]{:S(2)}) collective-permute-start(bf16[2,768,128]{2,1,0:T(8,128)(2,1)S(1)} %get-tuple-element.126.refs_1_), channel_id=1, source_target_pairs={{0,1},{1,0},{2,3},{3,2},{4,5},{5,4},{6,7},{7,6},{8,9},{9,8},{10,11... | collective-permute-start | bytes 1179656 | tf_op jit(solution)/shard_map/ppermute | solution.py:806
  79.6 16.3 %collective-permute-start.21 = (bf16[8,96,768]{2,1,0:T(8,128)(2,1)S(1)}, bf16[8,96,768]{2,1,0:T(8,128)(2,1)S(1)}, u32[]{:S(2)}, u32[]{:S(2)}) collective-permute-start(bf16[8,96,768]{2,1,0:T(8,128)(2,1)S(1)} %get-tuple-element.136), channel_id=1, source_target_pairs={{0,2},{1,5},{2,0},{3,7},{4,6},{5,1},{6,4},{7,3},{8,10},{9,13},{10,... | collective-permute-start | bytes 3538952 | tf_op jit(solution)/shard_map/ppermute | solution.py:806
  96.0 13.2 %collective-permute-start.23 = (bf16[4,96,768]{2,1,0:T(8,128)(2,1)S(1)}, bf16[4,96,768]{2,1,0:T(8,128)(2,1)S(1)}, u32[]{:S(2)}, u32[]{:S(2)}) collective-permute-start(bf16[4,96,768]{2,1,0:T(8,128)(2,1)S(1)} %add.13.refs_3_), channel_id=1, source_target_pairs={{0,4},{1,3},{2,6},{3,1},{4,0},{5,7},{6,2},{7,5},{8,12},{9,11},{10,... | collective-permute-start | bytes 1769480 | tf_op jit(solution)/shard_map/ppermute | solution.py:806
  97.3 1.4 %collective-permute-start.20 = (bf16[2,128,384]{2,1,0:T(8,128)(2,1)S(1)}, bf16[2,128,384]{2,1,0:T(8,128)(2,1)S(1)}, u32[]{:S(2)}, u32[]{:S(2)}) collective-permute-start(bf16[2,128,384]{2,1,0:T(8,128)(2,1)S(1)} %get-tuple-element.133), channel_id=1, source_target_pairs={{0,1},{1,0},{2,3},{3,2},{4,5},{5,4},{6,7},{7,6},{8,9},{9,8},{10,11... | collective-permute-start | bytes 589832 | tf_op jit(solution)/shard_map/ppermute | solution.py:806
  108.3 11.0 %collective-permute-start.26 = (bf16[8,96,384]{2,1,0:T(8,128)(2,1)S(1)}, bf16[8,96,384]{2,1,0:T(8,128)(2,1)S(1)}, u32[]{:S(2)}, u32[]{:S(2)}) collective-permute-start(bf16[8,96,384]{2,1,0:T(8,128)(2,1)S(1)} %get-tuple-element.150), channel_id=1, source_target_pairs={{0,2},{1,5},{2,0},{3,7},{4,6},{5,1},{6,4},{7,3},{8,10},{9,13},{10,... | collective-permute-start | bytes 1769480 | tf_op jit(solution)/shard_map/ppermute | solution.py:806
  109.4 9.1 %collective-permute-start.27 = (bf16[2,96,768]{2,1,0:T(8,128)(2,1)S(1)}, bf16[2,96,768]{2,1,0:T(8,128)(2,1)S(1)}, u32[]{:S(2)}, u32[]{:S(2)}) collective-permute-start(bf16[2,96,768]{2,1,0:T(8,128)(2,1)S(1)} %get-tuple-element.151), channel_id=1, source_target_pairs={{0,8},{1,9},{2,10},{3,11},{4,12},{5,13},{6,14},{7,15},{8,0},{9,1},... | collective-permute-start | bytes 884744 | tf_op jit(solution)/shard_map/ppermute | solution.py:806
  112.8 5.7 %collective-permute-start.24 = (f32[64,384]{1,0:T(8,128)S(1)}, f32[64,384]{1,0:T(8,128)S(1)}, u32[]{:S(2)}, u32[]{:S(2)}) collective-permute-start(f32[64,384]{1,0:T(8,128)S(1)} %get-tuple-element.145.sent), channel_id=1, source_target_pairs={{0,4},{1,3},{2,6},{3,1},{4,0},{5,7},{6,2},{7,5},{8,12},{9,11},{10,... | collective-permute-start | bytes 294920 | tf_op jit(solution)/shard_map/ppermute | solution.py:806
  119.4 6.8 %collective-permute-start.28 = (bf16[4,96,384]{2,1,0:T(8,128)(2,1)S(1)}, bf16[4,96,384]{2,1,0:T(8,128)(2,1)S(1)}, u32[]{:S(2)}, u32[]{:S(2)}) collective-permute-start(bf16[4,96,384]{2,1,0:T(8,128)(2,1)S(1)} %add.14), channel_id=1, source_target_pairs={{0,4},{1,3},{2,6},{3,1},{4,0},{5,7},{6,2},{7,5},{8,12},{9,11},{10,... | collective-permute-start | bytes 884744 | tf_op jit(solution)/shard_map/ppermute | solution.py:806
  120.4 4.8 %collective-permute-start.25 = (f32[48,384]{1,0:T(8,128)S(1)}, f32[48,384]{1,0:T(8,128)S(1)}, u32[]{:S(2)}, u32[]{:S(2)}) collective-permute-start(f32[48,384]{1,0:T(8,128)S(1)} %get-tuple-element.147.refs_0_.sent), channel_id=1, source_target_pairs={{0,2},{1,5},{2,0},{3,7},{4,6},{5,1},{6,4},{7,3},{8,10},{9,13},{10,... | collective-permute-start | bytes 221192 | tf_op jit(solution)/shard_map/ppermute | solution.py:806
  121.4 10.0 %collective-permute-start.32 = (bf16[96,768]{1,0:T(8,128)(2,1)S(1)}, bf16[96,768]{1,0:T(8,128)(2,1)S(1)}, u32[]{:S(2)}, u32[]{:S(2)}) collective-permute-start(bf16[96,768]{1,0:T(8,128)(2,1)S(1)} %get-tuple-element.157), channel_id=1, source_target_pairs={{0,16},{1,17},{2,18},{3,19},{4,20},{5,21},{6,22},{7,23},{8,24},{9,... | collective-permute-start | bytes 442376 | tf_op jit(solution)/shard_map/ppermute | solution.py:806
  127.0 6.8 %collective-permute-start.29 = (bf16[128,384]{1,0:T(8,128)(2,1)S(1)}, bf16[128,384]{1,0:T(8,128)(2,1)S(1)}, u32[]{:S(2)}, u32[]{:S(2)}) collective-permute-start(bf16[128,384]{1,0:T(8,128)(2,1)S(1)} %get-tuple-element.154), channel_id=1, source_target_pairs={{0,8},{1,9},{2,10},{3,11},{4,12},{5,13},{6,14},{7,15},{8,0},{9,1},... | collective-permute-start | bytes 294920 | tf_op jit(solution)/shard_map/ppermute | solution.py:806
  128.7 9.3 %collective-permute-start.30 = (bf16[128,384]{1,0:T(8,128)(2,1)S(1)}, bf16[128,384]{1,0:T(8,128)(2,1)S(1)}, u32[]{:S(2)}, u32[]{:S(2)}) collective-permute-start(bf16[128,384]{1,0:T(8,128)(2,1)S(1)} %get-tuple-element.155), channel_id=1, source_target_pairs={{0,16},{1,17},{2,18},{3,19},{4,20},{5,21},{6,22},{7,23},{8,24},{9,... | collective-permute-start | bytes 294920 | tf_op jit(solution)/shard_map/ppermute | solution.py:806
  129.4 8.5 %collective-permute-start.31 = (bf16[128,384]{1,0:T(8,128)(2,1)S(1)}, bf16[128,384]{1,0:T(8,128)(2,1)S(1)}, u32[]{:S(2)}, u32[]{:S(2)}) collective-permute-start(bf16[128,384]{1,0:T(8,128)(2,1)S(1)} %get-tuple-element.156), channel_id=1, source_target_pairs={{0,24},{1,25},{2,26},{3,27},{4,28},{5,29},{6,30},{7,31},{8,16},{9,... | collective-permute-start | bytes 294920 | tf_op jit(solution)/shard_map/ppermute | solution.py:806
  (26 other events, 190.7 us)

commit v5 on v4

--- a/solution.py
+++ b/solution.py
@@ -11,7 +11,7 @@
 masked_score = -1e30
 edge_unit = 1638.0
 spatial_unit = 4096.0
-hurry = 0.1
+hurry = 0.02
 bf16 = jnp.bfloat16
 f32 = jnp.float32
 i32 = jnp.int32
@@ -136,7 +136,9 @@
     )(wi, wu)
 
 
-def prepare_kernel(virtual, place, spatial, path, layer_in, gain, bias, cotangent, ids, buckets, h1, rows_t):
+def prepare_kernel(
+    virtual, place, spatial, path, layer_in, gain, bias, cotangent, after, ids, buckets, h1, rows_t
+):
     slots = spatial.shape[1]
     for hop in range(path.shape[1]):
         ids[hop] = path[0, hop].T
@@ -150,7 +152,7 @@
     rows_t[1] = cotangent[...].T.astype(bf16)
 
 
-def prepare(place, spatial, path, layer_in, gain, bias, cotangent, virtual):
+def prepare(place, spatial, path, layer_in, gain, bias, cotangent, virtual, after):
     hops, slots = path.shape[1], path.shape[2]
     rows, width = layer_in.shape
     whole = lambda dims: pl.BlockSpec(dims, lambda i, s: (0,) * len(dims))
@@ -166,6 +168,7 @@
                 whole((width,)),
                 whole((width,)),
                 whole((rows, width)),
+                untouched,
             ],
             out_specs=[
                 whole((hops, slots, slots)),
@@ -183,7 +186,7 @@
         compiler_params=params(62),
         cost_estimate=cost(1),
         name="prepare",
-    )(place, spatial, path, layer_in, gain, bias, cotangent)
+    )(place, spatial, path, layer_in, gain, bias, cotangent, after)
 
 
 def quantize(table, unit):
@@ -578,6 +581,8 @@
             row = relative(place, core, which, step)[0]
             start = pl.multiple_of(row * height, height)
             out[at + step] = plan(lambda kind: rows_t[kind, pl.ds(start, height), :], right).astype(bf16)
+    for extra in range(8, second.shape[0]):
+        second[extra] = jnp.zeros(second.shape[1:], bf16)
 
 
 def plan_first(rows_of, right):
@@ -603,14 +608,14 @@
 
 
 def weight_grads(
-    plan, place, columns_own, columns_other, own_rows, other_rows, height, lanes, microseconds, after=()
+    plan, place, columns_own, columns_other, own_rows, other_rows, height, lanes, microseconds, after=(), blocks=8
 ):
     features, slots = own_rows[0].shape[1:]
     kinds = sum(rows.shape[0] for rows in own_rows)
     out = shape((4, height, lanes), bf16)
     return pl.pallas_call(
         functools.partial(weight_grads_kernel, plan, len(own_rows)),
-        out_shape=(out, out, shape((8, height, lanes), bf16)),
+        out_shape=(out, out, shape((blocks, height, lanes), bf16)),
         in_specs=[smem] + [vmem] * (2 + 2 * len(own_rows)) + [untouched] * len(after),
         out_specs=[vmem] * 3,
         scratch_shapes=[pltpu.VMEM((kinds, features, 2 * slots), bf16)],
@@ -624,7 +629,7 @@
     hops = ids.shape[0]
     groups = grads.shape[0]
     heads = groups * 8
-    span = 8
+    span = 16
     if previous:
         total_in, spatial_in = refs[:2]
     if last:
@@ -717,10 +722,9 @@
 
 
 def meet_core_kernel(mine, small, got, after, out, keep):
-    keep[0:16, :] = mine[0:16, :] + got[0:16, :]
-    keep[16:32, :] = mine[32:48, :] + got[32:48, :]
+    keep[...] = mine[0:32, :] + got[0:32, :]
     out[0:16, :] = mine[48:64, :] + got[48:64, :]
-    out[16:32, :] = mine[16:32, :] + got[16:32, :]
+    out[16:32, :] = mine[32:48, :] + got[32:48, :]
     out[32:64, :] = small[...] + got[64:96, :]
 
 
@@ -827,6 +831,7 @@
 
 def join_pairs_kernel(rows, own, near, *refs):
     out = refs[-1]
+    out[4 * rows :, :] = jnp.zeros((out.shape[0] - 4 * rows, out.shape[1]), bf16)
     for i, (part, at) in enumerate(((own, 0), (near, 0), (own, rows), (near, rows))):
         out[i * rows : (i + 1) * rows, :] = part[at : at + rows, :]
 
@@ -834,7 +839,7 @@
 def join_pairs(own, near, rows, after):
     return small_call(
         functools.partial(join_pairs_kernel, rows), "join_pairs",
-        (shape((4 * rows, own.shape[1]), bf16),), own, near, *after, waits=len(after),
+        (shape((4 * rows + 64, own.shape[1]), bf16),), own, near, *after, waits=len(after),
     )[0]
 
 
@@ -856,7 +861,7 @@
 def step_sum(refs, step):
     total = refs[0][step].astype(f32)
     for ref in refs[1:]:
-        total = total + ref[step + ref.shape[0] - 4].astype(f32)
+        total = total + ref[step + (4 if ref.shape[0] > 4 else 0)].astype(f32)
     return total.astype(bf16)
 
 
@@ -944,9 +949,6 @@
     share = edges // 4
     digit = edges // 8
     place = jnp.stack([dp_index // 2, dp_index % 2, mp_index // 2, mp_index % 2, mp_index]).astype(i32)
-    ids, buckets, h1, rows_early = prepare(
-        place, spatial_ids, path_ids, layer_in, ln1_gain, ln1_bias, cotangent, kinds - 1
-    )
     if staged:
         links = Links()
         table_t = edge_table.T
@@ -955,7 +957,10 @@
             place, w_q, w_k, w_v, w_o, q_bias, v_bias, in_bias, table_t, send(table_t, links.along_x), second
         )
         chunks = around(links, first)
-        pair_b = join([second, send(second, links.first)], height)
+        ids, buckets, h1, rows_early = prepare(
+            place, spatial_ids, path_ids, layer_in, ln1_gain, ln1_bias, cotangent, kinds - 1, own_biases
+        )
+        pair_b = join([second, send(second, links.first)], height, (h1,))
         lookup_place = place
     else:
         gathered = [
@@ -975,6 +980,9 @@
                 jnp.concatenate([low[: heads // 2], low[heads // 2 :], high[: heads // 2], high[heads // 2 :]], 1)
             )
         lookup_place = jnp.zeros((5,), i32)
+        ids, buckets, h1, rows_early = prepare(
+            place, spatial_ids, path_ids, layer_in, ln1_gain, ln1_bias, cotangent, kinds - 1, spatial_ids
+        )
     edge_sums = None
     look = lambda step, after: lookup(lookup_place, chunks[step], ids, edge_sums, step, heads, after)
     if staged:
@@ -983,18 +991,18 @@
         across_a, over_a = send(stack_a, links.first), send(stack_a, links.second)
         pair_b = held_until(pair_b, stack_a)
         far_b = send(pair_b, links.along_z[1])
+        other_rows_early = send(held_until(rows_early, edge_sums), links.core)
         edge_sums = look(1, (stack_a,))
         four_b = join([pair_b, far_b], 2 * height, (edge_sums,))
         near_b = send(four_b, links.along_z[0])
         edge_sums = look(2, (four_b,))
-        across_a = held_until(across_a, edge_sums)
-        both_a = send(across_a, links.second)
         eight_b = join_pairs(four_b, near_b, 2 * height, (edge_sums,))
+        both_a = send(held_until(across_a, eight_b), links.second)
         over_b = send(eight_b, links.second)
-        edge_sums = look(3, (eight_b,))
+        edge_sums = look(3, (eight_b, other_rows_early))
         mine = (stack_a, across_a, over_a)
         theirs = tuple(send(held_until(part, eight_b), links.core) for part in mine)
-        parts_a = mine + (both_a,) + theirs + (send(both_a, links.core),)
+        parts_a = mine + (both_a,) + theirs + (send(held_until(both_a, edge_sums), links.core),)
     else:
         for step in range(4):
             edge_sums = look(step, ())
@@ -1005,11 +1013,10 @@
     )
     if staged:
         parts_b = (
-            eight_b, over_b, send(held_until(eight_b, edge_sums), links.core),
+            eight_b, over_b, send(held_until(eight_b, mid), links.core),
             send(held_until(over_b, mid), links.core),
         )
-        other_rows_early = send(held_until(rows_early, mid), links.core)
-        feed_after = (other_rows_early,)
+        feed_after = ()
     else:
         feed_after = ()
     layer_out, grad_mid, grad_att_t, grad_values, mine_b, theirs_b, rows_late, sums = feed(
@@ -1032,33 +1039,34 @@
     slots = ids.shape[1]
     if staged:
         other_columns_a = send(theirs_a, links.core)
-        partial = table(0, 64)
+        partial = table(0, 16)
+        own_a, across_a, second_a = weight_grads(
+            plan_first, place, mine_a, other_columns_a,
+            (rows_early[0:1],), (other_rows_b[0][0:1],), height, 2 * width, 2, (partial[0],), 9,
+        )
+        got_second_a = send(second_a, links.second)
+        partial = table(16, 64, partial, after=(own_a,))
         across_b = add_rounded((across_b, got_second_b), (partial[0],))
         got_across_b = send(across_b, links.first)
-        own_a, across_a, second_a = weight_grads(
-            plan_first, place, mine_a, other_columns_a,
-            (rows_early[0:1],), (other_rows_b[0][0:1],), height, 2 * width, 2, (partial[0],),
-        )
-        partial = table(64, 96, partial, after=(own_a, across_b))
-        mine, theirs, small = table(96, slots, partial, sums)
+        partial = table(64, 112, partial, after=(across_b,))
+        mine, theirs, small = table(112, slots, partial, sums)
         got_core = send(theirs, links.core)
-        got_second_a = send(held_until(second_a, small), links.second)
         stay_b, go_b = add_pair((own_b, got_across_b, got_second_b), (small,))
         got_pair_b = send(go_b, links.along_z[0])
+        across_a = add_rounded((across_a, got_second_a), (stay_b,))
+        got_across_a = send(across_a, links.first)
         half = features // 2
         sent, keep = small_call(
             meet_core_kernel, "meet_core", (shape((64, half), f32), shape((32, half), f32)),
-            mine, small, got_core, stay_b, waits=1,
+            mine, small, got_core, across_a, waits=1,
         )
         sent, keep = small_call(
             meet_near_kernel, "meet_near", (shape((48, half), f32), shape((16, half), f32)),
-            keep, sent, send(sent, links.first),
-        )
-        got_last = send(sent, links.second)
+            keep, sent, send(sent, links.second),
+        )
+        got_last = send(sent, links.first)
         own_b, go_b = add_half(stay_b, got_pair_b, (sent,))
         got_b = send(go_b, links.along_z[1])
-        across_a = add_rounded((across_a, got_second_a), (own_b,))
-        got_across_a = send(across_a, links.first)
         own_a = small_call(
             meet_far_kernel, "meet_far", (shape((height + 32, half), bf16),) * 4,
             keep, sent, got_last, own_a, got_across_a, got_second_a,

time: 141 us -> 136 us (0.965)
  waiting for transfers between devices: 30.6 us -> 25.9 us
    ppermute x33, waiting for transfers between devices: 30.6 us -> 25.9 us  [send(): return lax.ppermute(values, ('dp', 'mp'), hop)]
    pallas_call x3 -> x4, Pallas kernels: 16.3 us -> 15 us  [table_grads(): pl.pallas_call(functools.partial(table_kernel, digit, start, stop, len(pr...]
    unnamed x50 -> x52, local copies, waits for them, and re-layouts: 3.65 us -> 4.57 us
  transfers between devices with their start and end apart: 33 -> 33, of which waited for: 14 -> 15; matrix products, arithmetic and copies ran while one was open for 0% -> 1% of each run, Pallas kernels for 42% -> 43%
where the time goes in v5:
time: 136 us
  Pallas kernels  71.2 us (52%)
  starting transfers between devices  32 us (24%)
  waiting for transfers between devices  25.9 us (19%)
  local copies, waits for them, and re-layouts  5.28 us (4%)
    ppermute x33, starting transfers between devices, send(): return lax.ppermute(values, ('dp', 'mp'), hop)  32 us
    ppermute x33, waiting for transfers between devices, send(): return lax.ppermute(values, ('dp', 'mp'), hop)  25.9 us
    pallas_call x4, Pallas kernels, lookup(): pl.pallas_call(functools.partial(lookup_kernel, first, step, share), out_...  24.5 us
    pallas_call x4, Pallas kernels, table_grads(): pl.pallas_call(functools.partial(table_kernel, digit, start, stop, len(pr...  15 us
    pallas_call x1, Pallas kernels, feed(): pl.pallas_call(functools.partial(feed_kernel, len(parts)), grid=(1,), out...  5.68 us
    pallas_call x1, Pallas kernels, attend(): pl.pallas_call(functools.partial(attend_kernel, len(parts)), out_shape=(s...  5.41 us
    pallas_call x1, Pallas kernels, attend_back(): pl.pallas_call(attend_back_kernel, out_shape=(shape((groups, slots, 8, sl...  5.23 us
    unnamed x52, local copies, waits for them, and re-layouts  4.57 us
  transfers between devices with their start and end apart: 33, of which 15 were waited for; matrix products, arithmetic and copies ran while one was open for 1% of the time, Pallas kernels for 43%

profile of v5, /device:TPU:0, one launch (start us, length us, event | category | flops | bytes accessed | tf_op | source)
XLA Modules:
  0.0 135.7 jit_solution(660065018114145923)
XLA Ops:
  0.7 3.0 %collective-permute-start = (bf16[32,192]{1,0:T(8,128)(2,1)}, bf16[32,192]{1,0:T(8,128)(2,1)S(1)}, u32[]{:S(2)}, u32[]{:S(2)}) collective-permute-start(bf16[32,192]{1,0:T(8,128)(2,1)} %bitcast.8), channel_id=1, source_target_pairs={{0,4},{1,5},{2,6},{3,7},{4,0},{5,1},{6,2},{7,3},{8,12},{9,13},{10,... | collective-permute-start | bytes 36872 | tf_op jit(solution)/shard_map/ppermute | solution.py:810
  4.3 1.5 %pack_second.1.after.refs_0_ = bf16[96,384]{1,0:T(8,128)(2,1)} custom-call(bf16[96,192]{1,0:T(8,128)(2,1)} %wi.1, bf16[96,192]{1,0:T(8,128)(2,1)} %wu.1), custom_call_target="tpu_custom_call" | custom-call | flops 23000000 | bytes 1024 | tf_op jit(solution)/shard_map/pack_second/pallas_call | solution.py:128
  6.5 2.5 %pack_first.1 = (bf16[112,768]{1,0:T(8,128)(2,1)}, bf16[16,768]{1,0:T(8,128)(2,1)}) custom-call(s32[5]{0:T(128)} %stack.23.place, bf16[96,192]{1,0:T(8,128)(2,1)} %wq.1, bf16[96,192]{1,0:T(8,128)(2,1)} %wk.1, bf16[96,192]{1,0:T(8,128)(2,1)} %wv.1, bf16[96,192]{1,0:T(8,128)(2,1)} %wo.1, f32[192]{0:T(256)} %bq.1, f32[192]{0:T(256)} %bv.1, f32[192]{0:T(256)} %bi.1, ...), custom_call_target="tpu_custom_call" | custom-call | flops 46000000 | bytes 1024 | tf_op jit(solution)/shard_map/pack_first/pallas_call | solution.py:110
  9.0 3.9 %collective-permute-start.1 = (bf16[112,768]{1,0:T(8,128)(2,1)}, bf16[112,768]{1,0:T(8,128)(2,1)S(1)}, u32[]{:S(2)}, u32[]{:S(2)}) collective-permute-start(bf16[112,768]{1,0:T(8,128)(2,1)} %get-tuple-element.100.chunk.refs_0_), channel_id=1, source_target_pairs={{0,24},{1,25},{2,26},{3,27},{4,28},{5,29},{6,30},{7,31},{8,16},{9,... | collective-permute-start | bytes 516104 | tf_op jit(solution)/shard_map/ppermute | solution.py:810
  13.5 1.6 %collective-permute-start.4 = (bf16[96,384]{1,0:T(8,128)(2,1)}, bf16[96,384]{1,0:T(8,128)(2,1)S(1)}, u32[]{:S(2)}, u32[]{:S(2)}) collective-permute-start(bf16[96,384]{1,0:T(8,128)(2,1)} %pack_second.1.after.refs_0_), channel_id=1, source_target_pairs={{0,4},{1,3},{2,6},{3,1},{4,0},{5,7},{6,2},{7,5},{8,12},{9,11},{10,... | collective-permute-start | bytes 221192 | tf_op jit(solution)/shard_map/ppermute | solution.py:810
  15.2 3.3 %prepare.1 = (s32[5,128,128]{2,1,0:T(8,128)}, s32[128,128]{1,0:T(8,128)}, bf16[128,768]{1,0:T(8,128)(2,1)}, bf16[2,768,128]{2,1,0:T(8,128)(2,1)}) custom-call(s32[5]{0:T(128)} %stack.23.place, s32[4,128,128]{2,1,0:T(8,128)} %spatial.1, s32[4,5,128,128]{3,2,1,0:T(8,128)} %path.1, f32[128,768]{1,0:T(8,128)} %layer_in.5, f32[768]{0:T(1024)} %gain.7, f32[768]{0:T(1024)} %bias.2, ...), custom_call_target="tpu_custom_call" | custom-call | flops 23000000 | bytes 1024 | tf_op jit(solution)/shard_map/prepare/pallas_call | solution.py:159
  20.5 6.1 %lookup.4.refs_5_.refs_0_ = s32[16,128,128]{2,1,0:T(8,128)S(1)} custom-call(s32[5]{0:T(128)S(1)} %copy-done.11, bf16[112,768]{1,0:T(8,128)(2,1)S(1)} %copy-done.8, s32[5,128,128]{2,1,0:T(8,128)S(1)} %copy-done, bf16[192,384]{1,0:T(8,128)(2,1)S(1)} %join.3.refs_0_), custom_call_target="tpu_custom_call" | custom-call | flops 138000000 | bytes 1024 | tf_op jit(solution)/shard_map/lookup/pallas_call | solution.py:253
  28.1 1.9 %collective-permute-start.5 = (bf16[192,384]{1,0:T(8,128)(2,1)S(1)}, bf16[192,384]{1,0:T(8,128)(2,1)S(1)}, u32[]{:S(2)}, u32[]{:S(2)}) collective-permute-start(bf16[192,384]{1,0:T(8,128)(2,1)S(1)} %join.3.refs_0_), channel_id=1, source_target_pairs={{0,16},{1,17},{2,18},{3,19},{4,20},{5,21},{6,22},{7,23},{8,24},{9,... | collective-permute-start | bytes 442376 | tf_op jit(solution)/shard_map/ppermute | solution.py:810
  30.1 6.1 %lookup.5.refs_2_.refs_0_ = s32[16,128,128]{2,1,0:T(8,128)S(1)} custom-call(s32[5]{0:T(128)S(1)} %copy-done.11, bf16[112,768]{1,0:T(8,128)(2,1)S(1)} %collective-permute-done.3.refs_1_.chunk, s32[5,128,128]{2,1,0:T(8,128)S(1)} %copy-done.1, s32[16,128,128]{2,1,0:T(8,128)S(1)} %lookup.4.refs_5_.refs_0_, ...), custom_call_target="tpu_custom_call", output_to_operand_aliasing={{}: (3, {})} | custom-call | flops 138000000 | bytes 1024 | tf_op jit(solution)/shard_map/lookup/pallas_call | solution.py:253
  36.6 1.7 %collective-permute-start.6 = (bf16[384,384]{1,0:T(8,128)(2,1)S(1)}, bf16[384,384]{1,0:T(8,128)(2,1)S(1)}, u32[]{:S(2)}, u32[]{:S(2)}) collective-permute-start(bf16[384,384]{1,0:T(8,128)(2,1)S(1)} %join.5.refs_1_.own), channel_id=1, source_target_pairs={{0,8},{1,9},{2,10},{3,11},{4,12},{5,13},{6,14},{7,15},{8,0},{9,1},... | collective-permute-start | bytes 884744 | tf_op jit(solution)/shard_map/ppermute | solution.py:810
  39.8 6.1 %lookup.6.refs_0_ = s32[16,128,128]{2,1,0:T(8,128)S(1)} custom-call(s32[5]{0:T(128)S(1)} %copy-done.11, bf16[112,768]{1,0:T(8,128)(2,1)S(1)} %collective-permute-done.2.refs_2_.chunk, s32[5,128,128]{2,1,0:T(8,128)S(1)} %copy-done.1, s32[16,128,128]{2,1,0:T(8,128)S(1)} %lookup.5.refs_2_.refs_0_, ...), custom_call_target="tpu_custom_call", output_to_operand_aliasing={{}: (3, {})} | custom-call | flops 138000000 | bytes 1024 | tf_op jit(solution)/shard_map/lookup/pallas_call | solution.py:253
  46.7 1.5 %collective-permute-start.15 = (bf16[832,384]{1,0:T(8,128)(2,1)S(1)}, bf16[832,384]{1,0:T(8,128)(2,1)S(1)}, u32[]{:S(2)}, u32[]{:S(2)}) collective-permute-start(bf16[832,384]{1,0:T(8,128)(2,1)S(1)} %join_pairs.1.refs_1_.refs_0_), channel_id=1, source_target_pairs={{0,2},{1,5},{2,0},{3,7},{4,6},{5,1},{6,4},{7,3},{8,10},{9,13},{10,... | collective-permute-start | bytes 1916936 | tf_op jit(solution)/shard_map/ppermute | solution.py:810
  48.4 6.3 %lookup.7.edge_sums = s32[16,128,128]{2,1,0:T(8,128)S(1)} custom-call(s32[5]{0:T(128)S(1)} %copy-done.11, bf16[112,768]{1,0:T(8,128)(2,1)S(1)} %collective-permute-done.1.refs_3_.chunk, s32[5,128,128]{2,1,0:T(8,128)S(1)} %copy-done.1, s32[16,128,128]{2,1,0:T(8,128)S(1)} %lookup.6.refs_0_, ...), custom_call_target="tpu_custom_call", output_to_operand_aliasing={{}: (3, {})} | custom-call | flops 138000000 | bytes 1024 | tf_op jit(solution)/shard_map/lookup/pallas_call | solution.py:253
  58.6 5.4 %attend.1 = (bf16[4,768,768]{2,1,0:T(8,128)(2,1)S(1)}, f32[4,1,768]{2,1,0:T(1,128)S(1)}, bf16[4,384,128]{2,1,0:T(8,128)(2,1)S(1)}, bf16[4,128,256]{2,1,0:T(8,128...) custom-call(s32[5]{0:T(128)S(1)} %copy-done.11, ...), custom_call_target="tpu_custom_call" | custom-call | flops 161000000 | bytes 1024 | tf_op jit(solution)/shard_map/attend/pallas_call | solution.py:369
  64.6 1.6 %collective-permute-done.17.refs_3_ = bf16[832,384]{1,0:T(8,128)(2,1)S(1)} collective-permute-done((bf16[832,384]{1,0:T(8,128)(2,1)S(1)}, bf16[832,384]{1,0:T(8,128)(2,1)S(1)}, u32[]{:S(2)}, u32[]{:S(2)}) %collective-permute-start.17) | collective-permute-done | bytes 639008 | tf_op jit(solution)/shard_map/ppermute | solution.py:810
  67.1 5.7 %feed.1 = (f32[128,768]{1,0:T(8,128)}, f32[128,768]{1,0:T(8,128)S(1)}, bf16[4,256,128]{2,1,0:T(8,128)(2,1)S(1)}, bf16[4,128,256]{2,1,0:T(8,128)(2,1)S(1)}, bf16[...) custom-call(s32[5]{0:T(128)S(1)} %copy-done.11, ...), custom_call_target="tpu_custom_call" | custom-call | flops 161000000 | bytes 1024 | tf_op jit(solution)/shard_map/feed/pallas_call | solution.py:479
  73.3 2.0 %collective-permute-done.19.refs_3_ = bf16[2,768,128]{2,1,0:T(8,128)(2,1)S(1)} collective-permute-done((bf16[2,768,128]{2,1,0:T(8,128)(2,1)S(1)}, bf16[2,768,128]{2,1,0:T(8,128)(2,1)S(1)}, u32[]{:S(2)}, u32[]{:S(2)}) %collective-permute-start.19) | collective-permute-done | bytes 393248 | tf_op jit(solution)/shard_map/ppermute | solution.py:810
  75.3 2.3 %weight_grads.2 = (bf16[4,96,768]{2,1,0:T(8,128)(2,1)S(1)}, bf16[4,96,768]{2,1,0:T(8,128)(2,1)S(1)}, bf16[8,96,768]{2,1,0:T(8,128)(2,1)S(1)}) custom-call(s32[5]{0:T(128)S(1)} %copy-done.11, bf16[2,128,1024]{2,1,0:T(8,128)(2,1)S(1)} %get-tuple-element.125.columns_own, bf16[2,128,1024]{2,1,0:T(8,128)(2,1)S(1)} %collective-permute-done.18.columns_other, ...), custom_call_target="tpu_custom_call" | custom-call | flops 92000000 | bytes 1024 | tf_op jit(solution)/shard_map/weight_grads/pallas_call | solution.py:616
  77.6 1.6 %collective-permute-start.21 = (bf16[8,96,768]{2,1,0:T(8,128)(2,1)S(1)}, bf16[8,96,768]{2,1,0:T(8,128)(2,1)S(1)}, u32[]{:S(2)}, u32[]{:S(2)}) collective-permute-start(bf16[8,96,768]{2,1,0:T(8,128)(2,1)S(1)} %get-tuple-element.139), channel_id=1, source_target_pairs={{0,2},{1,5},{2,0},{3,7},{4,6},{5,1},{6,4},{7,3},{8,10},{9,13},{10,... | collective-permute-start | bytes 3538952 | tf_op jit(solution)/shard_map/ppermute | solution.py:810
  79.1 5.2 %attend_back.1 = (f32[4,128,8,128]{3,2,1,0:T(8,128)S(1)}, bf16[2,128,384]{2,1,0:T(8,128)(2,1)S(1)}, bf16[2,128,384]{2,1,0:T(8,128)(2,1)S(1)}, f32[128,768]{1,0:T(8,128)}, f32[16,768]{1,0:T(8,128)S(1)}) custom-call(s32[5]{0:T(128)S(1)} %copy-done.11, f32[32,128,128]{2,1,0:T(8,128)S(1)} %get-tuple-element.115.probs_in, ...), custom_call_target="tpu_custom_call" | custom-call | flops 161000000 | bytes 1024 | tf_op jit(solution)/shard_map/attend_back/pallas_call | solution.py:545
  84.4 2.1 %table_grads.4 = (f32[256,192]{1,0:T(8,128)S(1)}, f32[32,32]{1,0:T(8,128)S(1)}) custom-call(s32[5]{0:T(128)S(1)} %copy-done.11, f32[4,128,8,128]{3,2,1,0:T(8,128)S(1)} %get-tuple-element.130.grads, s32[5,128,128]{2,1,0:T(8,128)S(1)} %copy-done.1, s32[128,128]{1,0:T(8,128)S(1)} %copy-done.3), custom_call_target="tpu_custom_call" | custom-call | flops 43125000 | bytes 1024 | tf_op jit(solution)/shard_map/table_grads/pallas_call | solution.py:712
  88.5 5.3 %table_grads.5 = (f32[256,192]{1,0:T(8,128)S(1)}, f32[32,32]{1,0:T(8,128)S(1)}) custom-call(s32[5]{0:T(128)S(1)} %copy-done.11, f32[4,128,8,128]{3,2,1,0:T(8,128)S(1)} %get-tuple-element.130.grads, s32[5,128,128]{2,1,0:T(8,128)S(1)} %copy-done.1, s32[128,128]{1,0:T(8,128)S(1)} %copy-done.3, f32[256,192]{1,0:T(8,128)S(1)} %get-tuple-element.131.refs_2_.refs_0_, ...), custom_call_target="tpu_custom_call" | custom-call | flops 129375000 | bytes 1024 | tf_op jit(solution)/shard_map/table_grads/pallas_call | solution.py:712
  95.3 5.3 %table_grads.6 = (f32[256,192]{1,0:T(8,128)S(1)}, f32[32,32]{1,0:T(8,128)S(1)}) custom-call(s32[5]{0:T(128)S(1)} %copy-done.11, f32[4,128,8,128]{3,2,1,0:T(8,128)S(1)} %get-tuple-element.130.grads, s32[5,128,128]{2,1,0:T(8,128)S(1)} %copy-done.1, s32[128,128]{1,0:T(8,128)S(1)} %copy-done.3, f32[256,192]{1,0:T(8,128)S(1)} %get-tuple-element.136.refs_2_.refs_0_, ...), custom_call_target="tpu_custom_call" | custom-call | flops 129375000 | bytes 1024 | tf_op jit(solution)/shard_map/table_grads/pallas_call | solution.py:712
  100.6 2.2 %table_grads.7 = (f32[64,384]{1,0:T(8,128)S(1)}, f32[96,384]{1,0:T(8,128)S(1)}, f32[32,384]{1,0:T(8,128)S(1)}) custom-call(s32[5]{0:T(128)S(1)} %copy-done.11, f32[4,128,8,128]{3,2,1,0:T(8,128)S(1)} %get-tuple-element.130.grads, s32[5,128,128]{2,1,0:T(8,128)S(1)} %copy-done.1, s32[128,128]{1,0:T(8,128)S(1)} %copy-done.3, ...), custom_call_target="tpu_custom_call" | custom-call | flops 43125000 | bytes 1024 | tf_op jit(solution)/shard_map/table_grads/pallas_call | solution.py:712
  102.8 3.8 %collective-permute-done.24.refs_1_ = bf16[4,96,768]{2,1,0:T(8,128)(2,1)S(1)} collective-permute-done((bf16[4,96,768]{2,1,0:T(8,128)(2,1)S(1)}, bf16[4,96,768]{2,1,0:T(8,128)(2,1)S(1)}, u32[]{:S(2)}, u32[]{:S(2)}) %collective-permute-start.24) | collective-permute-done | bytes 589856 | tf_op jit(solution)/shard_map/ppermute | solution.py:810
  108.5 1.5 %collective-permute-start.25 = (f32[64,384]{1,0:T(8,128)S(1)}, f32[64,384]{1,0:T(8,128)S(1)}, u32[]{:S(2)}, u32[]{:S(2)}) collective-permute-start(f32[64,384]{1,0:T(8,128)S(1)} %get-tuple-element.150.sent), channel_id=1, source_target_pairs={{0,2},{1,5},{2,0},{3,7},{4,6},{5,1},{6,4},{7,3},{8,10},{9,13},{10,... | collective-permute-start | bytes 294920 | tf_op jit(solution)/shard_map/ppermute | solution.py:810
  110.0 4.3 %collective-permute-done.25.got = f32[64,384]{1,0:T(8,128)S(1)} collective-permute-done((f32[64,384]{1,0:T(8,128)S(1)}, f32[64,384]{1,0:T(8,128)S(1)}, u32[]{:S(2)}, u32[]{:S(2)}) %collective-permute-start.25) | collective-permute-done | bytes 98336 | tf_op jit(solution)/shard_map/ppermute | solution.py:810
  119.5 1.8 %collective-permute-start.28 = (bf16[128,384]{1,0:T(8,128)(2,1)S(1)}, bf16[128,384]{1,0:T(8,128)(2,1)S(1)}, u32[]{:S(2)}, u32[]{:S(2)}) collective-permute-start(bf16[128,384]{1,0:T(8,128)(2,1)S(1)} %get-tuple-element.154), channel_id=1, source_target_pairs={{0,8},{1,9},{2,10},{3,11},{4,12},{5,13},{6,14},{7,15},{8,0},{9,1},... | collective-permute-start | bytes 294920 | tf_op jit(solution)/shard_map/ppermute | solution.py:810
  122.3 1.6 %collective-permute-start.30 = (bf16[128,384]{1,0:T(8,128)(2,1)S(1)}, bf16[128,384]{1,0:T(8,128)(2,1)S(1)}, u32[]{:S(2)}, u32[]{:S(2)}) collective-permute-start(bf16[128,384]{1,0:T(8,128)(2,1)S(1)} %get-tuple-element.156), channel_id=1, source_target_pairs={{0,24},{1,25},{2,26},{3,27},{4,28},{5,29},{6,30},{7,31},{8,16},{9,... | collective-permute-start | bytes 294920 | tf_op jit(solution)/shard_map/ppermute | solution.py:810
  123.9 6.5 %collective-permute-done.32.refs_1_ = bf16[96,768]{1,0:T(8,128)(2,1)S(1)} collective-permute-done((bf16[96,768]{1,0:T(8,128)(2,1)S(1)}, bf16[96,768]{1,0:T(8,128)(2,1)S(1)}, u32[]{:S(2)}, u32[]{:S(2)}) %collective-permute-start.32) | collective-permute-done | bytes 147488 | tf_op jit(solution)/shard_map/ppermute | solution.py:810
  131.1 1.8 %settle.1 = (f32[96,192]{1,0:T(8,128)}, f32[96,192]{1,0:T(8,128)}, f32[96,192]{1,0:T(8,128)}, f32[96,192]{1,0:T(8,128)}) custom-call(bf16[96,768]{1,0:T(8,128)(2,1)} %copy-done.12, bf16[96,768]{1,0:T(8,128)(2,1)} %copy-done.21, bf16[128,384]{1,0:T(8,128)(2,1)} %copy-done.10), custom_call_target="tpu_custom_call" | custom-call | flops 23000000 | bytes 1024 | tf_op jit(solution)/shard_map/settle/pallas_call | solution.py:782
  133.6 2.0 %finish.1 = (f32[96,192]{1,0:T(8,128)}, f32[96,192]{1,0:T(8,128)}, f32[8,192]{1,0:T(8,128)}, f32[8,22]{1,0:T(8,128)}, f32[768]{0:T(1024)}, /*index=5*/f32[768]{0...) custom-call(s32[5]{0:T(128)} %stack.23.place, ...), custom_call_target="tpu_custom_call" | custom-call | flops 23000000 | bytes 1024 | tf_op jit(solution)/shard_map/finish/pallas_call | solution.py:782
  (118 shorter events, 27.1 us)
Async XLA Ops:
  0.7 5.2 %collective-permute-start = (bf16[32,192]{1,0:T(8,128)(2,1)}, bf16[32,192]{1,0:T(8,128)(2,1)S(1)}, u32[]{:S(2)}, u32[]{:S(2)}) collective-permute-start(bf16[32,192]{1,0:T(8,128)(2,1)} %bitcast.8), channel_id=1, source_target_pairs={{0,4},{1,5},{2,6},{3,7},{4,0},{5,1},{6,2},{7,3},{8,12},{9,13},{10,... | collective-permute-start | bytes 36872 | tf_op jit(solution)/shard_map/ppermute | solution.py:810
  9.0 17.6 %collective-permute-start.1 = (bf16[112,768]{1,0:T(8,128)(2,1)}, bf16[112,768]{1,0:T(8,128)(2,1)S(1)}, u32[]{:S(2)}, u32[]{:S(2)}) collective-permute-start(bf16[112,768]{1,0:T(8,128)(2,1)} %get-tuple-element.100.chunk.refs_0_), channel_id=1, source_target_pairs={{0,24},{1,25},{2,26},{3,27},{4,28},{5,29},{6,30},{7,31},{8,16},{9,... | collective-permute-start | bytes 516104 | tf_op jit(solution)/shard_map/ppermute | solution.py:810
  12.9 14.3 %collective-permute-start.2 = (bf16[112,768]{1,0:T(8,128)(2,1)}, bf16[112,768]{1,0:T(8,128)(2,1)S(1)}, u32[]{:S(2)}, u32[]{:S(2)}) collective-permute-start(bf16[112,768]{1,0:T(8,128)(2,1)} %get-tuple-element.100.chunk.refs_0_), channel_id=1, source_target_pairs={{0,16},{1,17},{2,18},{3,19},{4,20},{5,21},{6,22},{7,23},{8,24},{9,... | collective-permute-start | bytes 516104 | tf_op jit(solution)/shard_map/ppermute | solution.py:810
  12.9 14.3 %collective-permute-start.3 = (bf16[112,768]{1,0:T(8,128)(2,1)}, bf16[112,768]{1,0:T(8,128)(2,1)S(1)}, u32[]{:S(2)}, u32[]{:S(2)}) collective-permute-start(bf16[112,768]{1,0:T(8,128)(2,1)} %get-tuple-element.100.chunk.refs_0_), channel_id=1, source_target_pairs={{0,8},{1,9},{2,10},{3,11},{4,12},{5,13},{6,14},{7,15},{8,0},{9,1},... | collective-permute-start | bytes 516104 | tf_op jit(solution)/shard_map/ppermute | solution.py:810
  13.5 5.0 %collective-permute-start.4 = (bf16[96,384]{1,0:T(8,128)(2,1)}, bf16[96,384]{1,0:T(8,128)(2,1)S(1)}, u32[]{:S(2)}, u32[]{:S(2)}) collective-permute-start(bf16[96,384]{1,0:T(8,128)(2,1)} %pack_second.1.after.refs_0_), channel_id=1, source_target_pairs={{0,4},{1,3},{2,6},{3,1},{4,0},{5,7},{6,2},{7,5},{8,12},{9,11},{10,... | collective-permute-start | bytes 221192 | tf_op jit(solution)/shard_map/ppermute | solution.py:810
  27.2 18.9 %collective-permute-start.8 = (bf16[400,768]{1,0:T(8,128)(2,1)S(1)}, bf16[400,768]{1,0:T(8,128)(2,1)S(1)}, u32[]{:S(2)}, u32[]{:S(2)}) collective-permute-start(bf16[400,768]{1,0:T(8,128)(2,1)S(1)} %join.4.refs_1_.refs_0_), channel_id=1, source_target_pairs={{0,4},{1,3},{2,6},{3,1},{4,0},{5,7},{6,2},{7,5},{8,12},{9,11},{10,... | collective-permute-start | bytes 1843208 | tf_op jit(solution)/shard_map/ppermute | solution.py:810
  28.1 8.5 %collective-permute-start.5 = (bf16[192,384]{1,0:T(8,128)(2,1)S(1)}, bf16[192,384]{1,0:T(8,128)(2,1)S(1)}, u32[]{:S(2)}, u32[]{:S(2)}) collective-permute-start(bf16[192,384]{1,0:T(8,128)(2,1)S(1)} %join.3.refs_0_), channel_id=1, source_target_pairs={{0,16},{1,17},{2,18},{3,19},{4,20},{5,21},{6,22},{7,23},{8,24},{9,... | collective-permute-start | bytes 442376 | tf_op jit(solution)/shard_map/ppermute | solution.py:810
  36.6 9.3 %collective-permute-start.6 = (bf16[384,384]{1,0:T(8,128)(2,1)S(1)}, bf16[384,384]{1,0:T(8,128)(2,1)S(1)}, u32[]{:S(2)}, u32[]{:S(2)}) collective-permute-start(bf16[384,384]{1,0:T(8,128)(2,1)S(1)} %join.5.refs_1_.own), channel_id=1, source_target_pairs={{0,8},{1,9},{2,10},{3,11},{4,12},{5,13},{6,14},{7,15},{8,0},{9,1},... | collective-permute-start | bytes 884744 | tf_op jit(solution)/shard_map/ppermute | solution.py:810
  38.3 16.8 %collective-permute-start.9 = (bf16[400,768]{1,0:T(8,128)(2,1)S(1)}, bf16[400,768]{1,0:T(8,128)(2,1)S(1)}, u32[]{:S(2)}, u32[]{:S(2)}) collective-permute-start(bf16[400,768]{1,0:T(8,128)(2,1)S(1)} %join.4.refs_1_.refs_0_), channel_id=1, source_target_pairs={{0,2},{1,5},{2,0},{3,7},{4,6},{5,1},{6,4},{7,3},{8,10},{9,13},{10,... | collective-permute-start | bytes 1843208 | tf_op jit(solution)/shard_map/ppermute | solution.py:810
  46.1 10.2 %collective-permute-start.10 = (bf16[400,768]{1,0:T(8,128)(2,1)S(1)}, bf16[400,768]{1,0:T(8,128)(2,1)S(1)}, u32[]{:S(2)}, u32[]{:S(2)}) collective-permute-start(bf16[400,768]{1,0:T(8,128)(2,1)S(1)} %collective-permute-done.8.refs_1_), channel_id=1, source_target_pairs={{0,2},{1,5},{2,0},{3,7},{4,6},{5,1},{6,4},{7,3},{8,10},{9,13},{10,... | collective-permute-start | bytes 1843208 | tf_op jit(solution)/shard_map/ppermute | solution.py:810
  46.7 1.7 %collective-permute-start.7 = (bf16[2,768,128]{2,1,0:T(8,128)(2,1)S(1)}, bf16[2,768,128]{2,1,0:T(8,128)(2,1)S(1)}, u32[]{:S(2)}, u32[]{:S(2)}) collective-permute-start(bf16[2,768,128]{2,1,0:T(8,128)(2,1)S(1)} %copy-done.5), channel_id=1, source_target_pairs={{0,1},{1,0},{2,3},{3,2},{4,5},{5,4},{6,7},{7,6},{8,9},{9,8},{10,11... | collective-permute-start | bytes 1179656 | tf_op jit(solution)/shard_map/ppermute | solution.py:810
  46.7 17.4 %collective-permute-start.15 = (bf16[832,384]{1,0:T(8,128)(2,1)S(1)}, bf16[832,384]{1,0:T(8,128)(2,1)S(1)}, u32[]{:S(2)}, u32[]{:S(2)}) collective-permute-start(bf16[832,384]{1,0:T(8,128)(2,1)S(1)} %join_pairs.1.refs_1_.refs_0_), channel_id=1, source_target_pairs={{0,2},{1,5},{2,0},{3,7},{4,6},{5,1},{6,4},{7,3},{8,10},{9,13},{10,... | collective-permute-start | bytes 1916936 | tf_op jit(solution)/shard_map/ppermute | solution.py:810
  48.2 8.1 %collective-permute-start.11 = (bf16[400,768]{1,0:T(8,128)(2,1)S(1)}, bf16[400,768]{1,0:T(8,128)(2,1)S(1)}, u32[]{:S(2)}, u32[]{:S(2)}) collective-permute-start(bf16[400,768]{1,0:T(8,128)(2,1)S(1)} %join.4.refs_1_.refs_0_), channel_id=1, source_target_pairs={{0,1},{1,0},{2,3},{3,2},{4,5},{5,4},{6,7},{7,6},{8,9},{9,8},{10,11... | collective-permute-start | bytes 1843208 | tf_op jit(solution)/shard_map/ppermute | solution.py:810
  54.7 3.0 %collective-permute-start.12 = (bf16[400,768]{1,0:T(8,128)(2,1)S(1)}, bf16[400,768]{1,0:T(8,128)(2,1)S(1)}, u32[]{:S(2)}, u32[]{:S(2)}) collective-permute-start(bf16[400,768]{1,0:T(8,128)(2,1)S(1)} %collective-permute-done.8.refs_1_), channel_id=1, source_target_pairs={{0,1},{1,0},{2,3},{3,2},{4,5},{5,4},{6,7},{7,6},{8,9},{9,8},{10,11... | collective-permute-start | bytes 1843208 | tf_op jit(solution)/shard_map/ppermute | solution.py:810
  55.1 2.6 %collective-permute-start.13 = (bf16[400,768]{1,0:T(8,128)(2,1)S(1)}, bf16[400,768]{1,0:T(8,128)(2,1)S(1)}, u32[]{:S(2)}, u32[]{:S(2)}) collective-permute-start(bf16[400,768]{1,0:T(8,128)(2,1)S(1)} %collective-permute-done.9.refs_2_), channel_id=1, source_target_pairs={{0,1},{1,0},{2,3},{3,2},{4,5},{5,4},{6,7},{7,6},{8,9},{9,8},{10,11... | collective-permute-start | bytes 1843208 | tf_op jit(solution)/shard_map/ppermute | solution.py:810
  56.3 2.2 %collective-permute-start.14 = (bf16[400,768]{1,0:T(8,128)(2,1)S(1)}, bf16[400,768]{1,0:T(8,128)(2,1)S(1)}, u32[]{:S(2)}, u32[]{:S(2)}) collective-permute-start(bf16[400,768]{1,0:T(8,128)(2,1)S(1)} %collective-permute-done.10.refs_3_), channel_id=1, source_target_pairs={{0,1},{1,0},{2,3},{3,2},{4,5},{5,4},{6,7},{7,6},{8,9},{9,8},{10,11... | collective-permute-start | bytes 1843208 | tf_op jit(solution)/shard_map/ppermute | solution.py:810
  64.1 2.1 %collective-permute-start.17 = (bf16[832,384]{1,0:T(8,128)(2,1)S(1)}, bf16[832,384]{1,0:T(8,128)(2,1)S(1)}, u32[]{:S(2)}, u32[]{:S(2)}) collective-permute-start(bf16[832,384]{1,0:T(8,128)(2,1)S(1)} %collective-permute-done.15.refs_1_), channel_id=1, source_target_pairs={{0,1},{1,0},{2,3},{3,2},{4,5},{5,4},{6,7},{7,6},{8,9},{9,8},{10,11... | collective-permute-start | bytes 1916936 | tf_op jit(solution)/shard_map/ppermute | solution.py:810
  64.4 2.7 %collective-permute-start.16 = (bf16[832,384]{1,0:T(8,128)(2,1)S(1)}, bf16[832,384]{1,0:T(8,128)(2,1)S(1)}, u32[]{:S(2)}, u32[]{:S(2)}) collective-permute-start(bf16[832,384]{1,0:T(8,128)(2,1)S(1)} %join_pairs.1.refs_1_.refs_0_), channel_id=1, source_target_pairs={{0,1},{1,0},{2,3},{3,2},{4,5},{5,4},{6,7},{7,6},{8,9},{9,8},{10,11... | collective-permute-start | bytes 1916936 | tf_op jit(solution)/shard_map/ppermute | solution.py:810
  72.8 2.5 %collective-permute-start.18 = (bf16[2,128,1024]{2,1,0:T(8,128)(2,1)S(1)}, bf16[2,128,1024]{2,1,0:T(8,128)(2,1)S(1)}, u32[]{:S(2)}, u32[]{:S(2)}) collective-permute-start(bf16[2,128,1024]{2,1,0:T(8,128)(2,1)S(1)} %get-tuple-element.126), channel_id=1, source_target_pairs={{0,1},{1,0},{2,3},{3,2},{4,5},{5,4},{6,7},{7,6},{8,9},{9,8},{10,11... | collective-permute-start | bytes 1572872 | tf_op jit(solution)/shard_map/ppermute | solution.py:810
  73.1 2.2 %collective-permute-start.19 = (bf16[2,768,128]{2,1,0:T(8,128)(2,1)S(1)}, bf16[2,768,128]{2,1,0:T(8,128)(2,1)S(1)}, u32[]{:S(2)}, u32[]{:S(2)}) collective-permute-start(bf16[2,768,128]{2,1,0:T(8,128)(2,1)S(1)} %get-tuple-element.127.refs_1_), channel_id=1, source_target_pairs={{0,1},{1,0},{2,3},{3,2},{4,5},{5,4},{6,7},{7,6},{8,9},{9,8},{10,11... | collective-permute-start | bytes 1179656 | tf_op jit(solution)/shard_map/ppermute | solution.py:810
  77.6 16.3 %collective-permute-start.21 = (bf16[8,96,768]{2,1,0:T(8,128)(2,1)S(1)}, bf16[8,96,768]{2,1,0:T(8,128)(2,1)S(1)}, u32[]{:S(2)}, u32[]{:S(2)}) collective-permute-start(bf16[8,96,768]{2,1,0:T(8,128)(2,1)S(1)} %get-tuple-element.139), channel_id=1, source_target_pairs={{0,2},{1,5},{2,0},{3,7},{4,6},{5,1},{6,4},{7,3},{8,10},{9,13},{10,... | collective-permute-start | bytes 3538952 | tf_op jit(solution)/shard_map/ppermute | solution.py:810
  84.4 2.2 %collective-permute-start.20 = (bf16[2,128,384]{2,1,0:T(8,128)(2,1)S(1)}, bf16[2,128,384]{2,1,0:T(8,128)(2,1)S(1)}, u32[]{:S(2)}, u32[]{:S(2)}) collective-permute-start(bf16[2,128,384]{2,1,0:T(8,128)(2,1)S(1)} %get-tuple-element.134), channel_id=1, source_target_pairs={{0,1},{1,0},{2,3},{3,2},{4,5},{5,4},{6,7},{7,6},{8,9},{9,8},{10,11... | collective-permute-start | bytes 589832 | tf_op jit(solution)/shard_map/ppermute | solution.py:810
  87.8 19.7 %collective-permute-start.23 = (bf16[9,96,384]{2,1,0:T(8,128)(2,1)S(1)}, bf16[9,96,384]{2,1,0:T(8,128)(2,1)S(1)}, u32[]{:S(2)}, u32[]{:S(2)}) collective-permute-start(bf16[9,96,384]{2,1,0:T(8,128)(2,1)S(1)} %get-tuple-element.147), channel_id=1, source_target_pairs={{0,2},{1,5},{2,0},{3,7},{4,6},{5,1},{6,4},{7,3},{8,10},{9,13},{10,... | collective-permute-start | bytes 1990664 | tf_op jit(solution)/shard_map/ppermute | solution.py:810
  94.0 12.6 %collective-permute-start.24 = (bf16[4,96,768]{2,1,0:T(8,128)(2,1)S(1)}, bf16[4,96,768]{2,1,0:T(8,128)(2,1)S(1)}, u32[]{:S(2)}, u32[]{:S(2)}) collective-permute-start(bf16[4,96,768]{2,1,0:T(8,128)(2,1)S(1)} %add.13.refs_2_), channel_id=1, source_target_pairs={{0,4},{1,3},{2,6},{3,1},{4,0},{5,7},{6,2},{7,5},{8,12},{9,11},{10,... | collective-permute-start | bytes 1769480 | tf_op jit(solution)/shard_map/ppermute | solution.py:810
  106.8 9.5 %collective-permute-start.31 = (bf16[2,96,768]{2,1,0:T(8,128)(2,1)S(1)}, bf16[2,96,768]{2,1,0:T(8,128)(2,1)S(1)}, u32[]{:S(2)}, u32[]{:S(2)}) collective-permute-start(bf16[2,96,768]{2,1,0:T(8,128)(2,1)S(1)} %get-tuple-element.157), channel_id=1, source_target_pairs={{0,8},{1,9},{2,10},{3,11},{4,12},{5,13},{6,14},{7,15},{8,0},{9,1},... | collective-permute-start | bytes 884744 | tf_op jit(solution)/shard_map/ppermute | solution.py:810
  107.6 11.2 %collective-permute-start.27 = (bf16[4,96,384]{2,1,0:T(8,128)(2,1)S(1)}, bf16[4,96,384]{2,1,0:T(8,128)(2,1)S(1)}, u32[]{:S(2)}, u32[]{:S(2)}) collective-permute-start(bf16[4,96,384]{2,1,0:T(8,128)(2,1)S(1)} %add.14.after), channel_id=1, source_target_pairs={{0,4},{1,3},{2,6},{3,1},{4,0},{5,7},{6,2},{7,5},{8,12},{9,11},{10,... | collective-permute-start | bytes 884744 | tf_op jit(solution)/shard_map/ppermute | solution.py:810
  108.5 5.8 %collective-permute-start.25 = (f32[64,384]{1,0:T(8,128)S(1)}, f32[64,384]{1,0:T(8,128)S(1)}, u32[]{:S(2)}, u32[]{:S(2)}) collective-permute-start(f32[64,384]{1,0:T(8,128)S(1)} %get-tuple-element.150.sent), channel_id=1, source_target_pairs={{0,2},{1,5},{2,0},{3,7},{4,6},{5,1},{6,4},{7,3},{8,10},{9,13},{10,... | collective-permute-start | bytes 294920 | tf_op jit(solution)/shard_map/ppermute | solution.py:810
  114.3 4.4 %collective-permute-start.26 = (f32[48,384]{1,0:T(8,128)S(1)}, f32[48,384]{1,0:T(8,128)S(1)}, u32[]{:S(2)}, u32[]{:S(2)}) collective-permute-start(f32[48,384]{1,0:T(8,128)S(1)} %get-tuple-element.152.sent.refs_0_), channel_id=1, source_target_pairs={{0,4},{1,3},{2,6},{3,1},{4,0},{5,7},{6,2},{7,5},{8,12},{9,11},{10,... | collective-permute-start | bytes 221192 | tf_op jit(solution)/shard_map/ppermute | solution.py:810
  116.3 14.1 %collective-permute-start.32 = (bf16[96,768]{1,0:T(8,128)(2,1)S(1)}, bf16[96,768]{1,0:T(8,128)(2,1)S(1)}, u32[]{:S(2)}, u32[]{:S(2)}) collective-permute-start(bf16[96,768]{1,0:T(8,128)(2,1)S(1)} %get-tuple-element.159), channel_id=1, source_target_pairs={{0,16},{1,17},{2,18},{3,19},{4,20},{5,21},{6,22},{7,23},{8,24},{9,... | collective-permute-start | bytes 442376 | tf_op jit(solution)/shard_map/ppermute | solution.py:810
  119.5 13.3 %collective-permute-start.28 = (bf16[128,384]{1,0:T(8,128)(2,1)S(1)}, bf16[128,384]{1,0:T(8,128)(2,1)S(1)}, u32[]{:S(2)}, u32[]{:S(2)}) collective-permute-start(bf16[128,384]{1,0:T(8,128)(2,1)S(1)} %get-tuple-element.154), channel_id=1, source_target_pairs={{0,8},{1,9},{2,10},{3,11},{4,12},{5,13},{6,14},{7,15},{8,0},{9,1},... | collective-permute-start | bytes 294920 | tf_op jit(solution)/shard_map/ppermute | solution.py:810
  121.3 11.5 %collective-permute-start.29 = (bf16[128,384]{1,0:T(8,128)(2,1)S(1)}, bf16[128,384]{1,0:T(8,128)(2,1)S(1)}, u32[]{:S(2)}, u32[]{:S(2)}) collective-permute-start(bf16[128,384]{1,0:T(8,128)(2,1)S(1)} %get-tuple-element.155), channel_id=1, source_target_pairs={{0,16},{1,17},{2,18},{3,19},{4,20},{5,21},{6,22},{7,23},{8,24},{9,... | collective-permute-start | bytes 294920 | tf_op jit(solution)/shard_map/ppermute | solution.py:810
  122.3 10.5 %collective-permute-start.30 = (bf16[128,384]{1,0:T(8,128)(2,1)S(1)}, bf16[128,384]{1,0:T(8,128)(2,1)S(1)}, u32[]{:S(2)}, u32[]{:S(2)}) collective-permute-start(bf16[128,384]{1,0:T(8,128)(2,1)S(1)} %get-tuple-element.156), channel_id=1, source_target_pairs={{0,24},{1,25},{2,26},{3,27},{4,28},{5,29},{6,30},{7,31},{8,16},{9,... | collective-permute-start | bytes 294920 | tf_op jit(solution)/shard_map/ppermute | solution.py:810
  (27 other events, 203.2 us)

commit v6 on v5

--- a/solution.py
+++ b/solution.py
@@ -728,7 +728,7 @@
     out[32:64, :] = small[...] + got[64:96, :]
 
 
-def meet_near_kernel(keep, sent, got, out, kept):
+def meet_near_kernel(keep, sent, got, after, out, kept):
     out[0:16, :] = keep[16:32, :] + got[0:16, :]
     out[16:48, :] = sent[32:64, :] + got[32:64, :]
     kept[...] = keep[0:16, :] + got[16:32, :]
@@ -905,7 +905,7 @@
     count = lanes // width
     return small_call(
         functools.partial(settle_kernel, count), "settle",
-        (shape((rows, width), f32),) * count, *terms, *after, waits=len(after), mebibytes=60,
+        (shape((rows, width), f32),) * count, *terms, *after, waits=len(after), mebibytes=20,
     )
 
 
@@ -1013,7 +1013,7 @@
     )
     if staged:
         parts_b = (
-            eight_b, over_b, send(held_until(eight_b, mid), links.core),
+            eight_b, over_b, send(held_until(eight_b, edge_sums), links.core),
             send(held_until(over_b, mid), links.core),
         )
         feed_after = ()
@@ -1051,18 +1051,18 @@
         partial = table(64, 112, partial, after=(across_b,))
         mine, theirs, small = table(112, slots, partial, sums)
         got_core = send(theirs, links.core)
-        stay_b, go_b = add_pair((own_b, got_across_b, got_second_b), (small,))
+        half = features // 2
+        sent, keep = small_call(
+            meet_core_kernel, "meet_core", (shape((64, half), f32), shape((32, half), f32)),
+            mine, small, got_core, small, waits=1,
+        )
+        stay_b, go_b = add_pair((own_b, got_across_b, got_second_b), (sent,))
         got_pair_b = send(go_b, links.along_z[0])
         across_a = add_rounded((across_a, got_second_a), (stay_b,))
         got_across_a = send(across_a, links.first)
-        half = features // 2
-        sent, keep = small_call(
-            meet_core_kernel, "meet_core", (shape((64, half), f32), shape((32, half), f32)),
-            mine, small, got_core, across_a, waits=1,
-        )
         sent, keep = small_call(
             meet_near_kernel, "meet_near", (shape((48, half), f32), shape((16, half), f32)),
-            keep, sent, send(sent, links.second),
+            keep, sent, send(sent, links.second), across_a, waits=1,
         )
         got_last = send(sent, links.first)
         own_b, go_b = add_half(stay_b, got_pair_b, (sent,))
@@ -1079,7 +1079,7 @@
             + (shape((8, digit), f32), shape((8, kinds), f32))
             + (shape((features,), f32),) * 6
             + (shape((width,), f32),) * 3,
-            place, own_a[0], *got_a, grad_w_in, waits=1, mebibytes=60,
+            place, own_a[0], *got_a, grad_w_in, waits=1, mebibytes=30,
         )
         grad_edge = grad_edge.T
         grad_spatial = grad_spatial.T

time: 136 us -> 134 us (0.985)
  Pallas kernels: 71.2 us -> 69.8 us
    pallas_call x13, Pallas kernels: 4.54 us -> 3.06 us  [small_call(): pl.pallas_call(kernel, out_shape=outs, in_specs=[smem if args[i].ndim ==...]
    unnamed x52 -> x42, local copies, waits for them, and re-layouts: 4.57 us -> 3.47 us
  transfers between devices with their start and end apart: 33 -> 33, of which waited for: 15 -> 15; matrix products, arithmetic and copies ran while one was open for 1% -> 0% of each run, Pallas kernels for 43% -> 43%
where the time goes in v6:
time: 134 us
  Pallas kernels  69.8 us (52%)
  starting transfers between devices  32.5 us (24%)
  waiting for transfers between devices  26.2 us (20%)
  local copies, waits for them, and re-layouts  4.1 us (3%)
    ppermute x33, starting transfers between devices, send(): return lax.ppermute(values, ('dp', 'mp'), hop)  32.5 us
    ppermute x33, waiting for transfers between devices, send(): return lax.ppermute(values, ('dp', 'mp'), hop)  26.2 us
    pallas_call x4, Pallas kernels, lookup(): pl.pallas_call(functools.partial(lookup_kernel, first, step, share), out_...  24.5 us
    pallas_call x4, Pallas kernels, table_grads(): pl.pallas_call(functools.partial(table_kernel, digit, start, stop, len(pr...  15 us
    pallas_call x1, Pallas kernels, feed(): pl.pallas_call(functools.partial(feed_kernel, len(parts)), grid=(1,), out...  5.68 us
    pallas_call x1, Pallas kernels, attend(): pl.pallas_call(functools.partial(attend_kernel, len(parts)), out_shape=(s...  5.4 us
    pallas_call x1, Pallas kernels, attend_back(): pl.pallas_call(attend_back_kernel, out_shape=(shape((groups, slots, 8, sl...  5.22 us
    pallas_call x2, Pallas kernels, weight_grads(): pl.pallas_call(functools.partial(weight_grads_kernel, plan, len(own_rows)...  3.51 us
  transfers between devices with their start and end apart: 33, of which 15 were waited for; matrix products, arithmetic and copies ran while one was open for 0% of the time, Pallas kernels for 43%

profile of v6, /device:TPU:0, one launch (start us, length us, event | category | flops | bytes accessed | tf_op | source)
XLA Modules:
  0.0 133.8 jit_solution(3190950795965757817)
XLA Ops:
  0.7 3.0 %collective-permute-start = (bf16[32,192]{1,0:T(8,128)(2,1)}, bf16[32,192]{1,0:T(8,128)(2,1)S(1)}, u32[]{:S(2)}, u32[]{:S(2)}) collective-permute-start(bf16[32,192]{1,0:T(8,128)(2,1)} %bitcast.8), channel_id=1, source_target_pairs={{0,4},{1,5},{2,6},{3,7},{4,0},{5,1},{6,2},{7,3},{8,12},{9,13},{10,... | collective-permute-start | bytes 36872 | tf_op jit(solution)/shard_map/ppermute | solution.py:810
  4.3 1.5 %pack_second.1.after.refs_0_ = bf16[96,384]{1,0:T(8,128)(2,1)} custom-call(bf16[96,192]{1,0:T(8,128)(2,1)} %wi.1, bf16[96,192]{1,0:T(8,128)(2,1)} %wu.1), custom_call_target="tpu_custom_call" | custom-call | flops 23000000 | bytes 1024 | tf_op jit(solution)/shard_map/pack_second/pallas_call | solution.py:128
  6.4 2.5 %pack_first.1 = (bf16[112,768]{1,0:T(8,128)(2,1)}, bf16[16,768]{1,0:T(8,128)(2,1)}) custom-call(s32[5]{0:T(128)} %stack.23.place, bf16[96,192]{1,0:T(8,128)(2,1)} %wq.1, bf16[96,192]{1,0:T(8,128)(2,1)} %wk.1, bf16[96,192]{1,0:T(8,128)(2,1)} %wv.1, bf16[96,192]{1,0:T(8,128)(2,1)} %wo.1, f32[192]{0:T(256)} %bq.1, f32[192]{0:T(256)} %bv.1, f32[192]{0:T(256)} %bi.1, ...), custom_call_target="tpu_custom_call" | custom-call | flops 46000000 | bytes 1024 | tf_op jit(solution)/shard_map/pack_first/pallas_call | solution.py:110
  8.9 4.0 %collective-permute-start.1 = (bf16[112,768]{1,0:T(8,128)(2,1)}, bf16[112,768]{1,0:T(8,128)(2,1)S(1)}, u32[]{:S(2)}, u32[]{:S(2)}) collective-permute-start(bf16[112,768]{1,0:T(8,128)(2,1)} %get-tuple-element.100.chunk.refs_0_), channel_id=1, source_target_pairs={{0,24},{1,25},{2,26},{3,27},{4,28},{5,29},{6,30},{7,31},{8,16},{9,... | collective-permute-start | bytes 516104 | tf_op jit(solution)/shard_map/ppermute | solution.py:810
  13.5 1.6 %collective-permute-start.4 = (bf16[96,384]{1,0:T(8,128)(2,1)}, bf16[96,384]{1,0:T(8,128)(2,1)S(1)}, u32[]{:S(2)}, u32[]{:S(2)}) collective-permute-start(bf16[96,384]{1,0:T(8,128)(2,1)} %pack_second.1.after.refs_0_), channel_id=1, source_target_pairs={{0,4},{1,3},{2,6},{3,1},{4,0},{5,7},{6,2},{7,5},{8,12},{9,11},{10,... | collective-permute-start | bytes 221192 | tf_op jit(solution)/shard_map/ppermute | solution.py:810
  15.2 3.3 %prepare.1 = (s32[5,128,128]{2,1,0:T(8,128)}, s32[128,128]{1,0:T(8,128)}, bf16[128,768]{1,0:T(8,128)(2,1)}, bf16[2,768,128]{2,1,0:T(8,128)(2,1)}) custom-call(s32[5]{0:T(128)} %stack.23.place, s32[4,128,128]{2,1,0:T(8,128)} %spatial.1, s32[4,5,128,128]{3,2,1,0:T(8,128)} %path.1, f32[128,768]{1,0:T(8,128)} %layer_in.5, f32[768]{0:T(1024)} %gain.7, f32[768]{0:T(1024)} %bias.2, ...), custom_call_target="tpu_custom_call" | custom-call | flops 23000000 | bytes 1024 | tf_op jit(solution)/shard_map/prepare/pallas_call | solution.py:159
  20.5 6.1 %lookup.4.refs_5_.refs_0_ = s32[16,128,128]{2,1,0:T(8,128)S(1)} custom-call(s32[5]{0:T(128)S(1)} %copy-done.10, bf16[112,768]{1,0:T(8,128)(2,1)S(1)} %copy-done.8, s32[5,128,128]{2,1,0:T(8,128)S(1)} %copy-done, bf16[192,384]{1,0:T(8,128)(2,1)S(1)} %join.3.refs_0_), custom_call_target="tpu_custom_call" | custom-call | flops 138000000 | bytes 1024 | tf_op jit(solution)/shard_map/lookup/pallas_call | solution.py:253
  28.1 1.9 %collective-permute-start.5 = (bf16[192,384]{1,0:T(8,128)(2,1)S(1)}, bf16[192,384]{1,0:T(8,128)(2,1)S(1)}, u32[]{:S(2)}, u32[]{:S(2)}) collective-permute-start(bf16[192,384]{1,0:T(8,128)(2,1)S(1)} %join.3.refs_0_), channel_id=1, source_target_pairs={{0,16},{1,17},{2,18},{3,19},{4,20},{5,21},{6,22},{7,23},{8,24},{9,... | collective-permute-start | bytes 442376 | tf_op jit(solution)/shard_map/ppermute | solution.py:810
  30.1 6.1 %lookup.5.refs_2_.refs_0_ = s32[16,128,128]{2,1,0:T(8,128)S(1)} custom-call(s32[5]{0:T(128)S(1)} %copy-done.10, bf16[112,768]{1,0:T(8,128)(2,1)S(1)} %collective-permute-done.3.refs_1_.chunk, s32[5,128,128]{2,1,0:T(8,128)S(1)} %copy-done.1, s32[16,128,128]{2,1,0:T(8,128)S(1)} %lookup.4.refs_5_.refs_0_, ...), custom_call_target="tpu_custom_call", output_to_operand_aliasing={{}: (3, {})} | custom-call | flops 138000000 | bytes 1024 | tf_op jit(solution)/shard_map/lookup/pallas_call | solution.py:253
  36.5 1.8 %collective-permute-start.6 = (bf16[384,384]{1,0:T(8,128)(2,1)S(1)}, bf16[384,384]{1,0:T(8,128)(2,1)S(1)}, u32[]{:S(2)}, u32[]{:S(2)}) collective-permute-start(bf16[384,384]{1,0:T(8,128)(2,1)S(1)} %join.5.refs_1_.own), channel_id=1, source_target_pairs={{0,8},{1,9},{2,10},{3,11},{4,12},{5,13},{6,14},{7,15},{8,0},{9,1},... | collective-permute-start | bytes 884744 | tf_op jit(solution)/shard_map/ppermute | solution.py:810
  38.3 1.5 %collective-permute-start.9 = (bf16[400,768]{1,0:T(8,128)(2,1)S(1)}, bf16[400,768]{1,0:T(8,128)(2,1)S(1)}, u32[]{:S(2)}, u32[]{:S(2)}) collective-permute-start(bf16[400,768]{1,0:T(8,128)(2,1)S(1)} %join.4.refs_1_.refs_0_), channel_id=1, source_target_pairs={{0,2},{1,5},{2,0},{3,7},{4,6},{5,1},{6,4},{7,3},{8,10},{9,13},{10,... | collective-permute-start | bytes 1843208 | tf_op jit(solution)/shard_map/ppermute | solution.py:810
  39.8 6.1 %lookup.6.refs_0_ = s32[16,128,128]{2,1,0:T(8,128)S(1)} custom-call(s32[5]{0:T(128)S(1)} %copy-done.10, bf16[112,768]{1,0:T(8,128)(2,1)S(1)} %collective-permute-done.2.refs_2_.chunk, s32[5,128,128]{2,1,0:T(8,128)S(1)} %copy-done.1, s32[16,128,128]{2,1,0:T(8,128)S(1)} %lookup.5.refs_2_.refs_0_, ...), custom_call_target="tpu_custom_call", output_to_operand_aliasing={{}: (3, {})} | custom-call | flops 138000000 | bytes 1024 | tf_op jit(solution)/shard_map/lookup/pallas_call | solution.py:253
  46.7 1.5 %collective-permute-start.15 = (bf16[832,384]{1,0:T(8,128)(2,1)S(1)}, bf16[832,384]{1,0:T(8,128)(2,1)S(1)}, u32[]{:S(2)}, u32[]{:S(2)}) collective-permute-start(bf16[832,384]{1,0:T(8,128)(2,1)S(1)} %join_pairs.1.refs_1_.refs_0_), channel_id=1, source_target_pairs={{0,2},{1,5},{2,0},{3,7},{4,6},{5,1},{6,4},{7,3},{8,10},{9,13},{10,... | collective-permute-start | bytes 1916936 | tf_op jit(solution)/shard_map/ppermute | solution.py:810
  48.4 6.3 %lookup.7.edge_sums = s32[16,128,128]{2,1,0:T(8,128)S(1)} custom-call(s32[5]{0:T(128)S(1)} %copy-done.10, bf16[112,768]{1,0:T(8,128)(2,1)S(1)} %collective-permute-done.1.refs_3_.chunk, s32[5,128,128]{2,1,0:T(8,128)S(1)} %copy-done.1, s32[16,128,128]{2,1,0:T(8,128)S(1)} %lookup.6.refs_0_, ...), custom_call_target="tpu_custom_call", output_to_operand_aliasing={{}: (3, {})} | custom-call | flops 138000000 | bytes 1024 | tf_op jit(solution)/shard_map/lookup/pallas_call | solution.py:253
  58.6 5.4 %attend.1 = (bf16[4,768,768]{2,1,0:T(8,128)(2,1)S(1)}, f32[4,1,768]{2,1,0:T(1,128)S(1)}, bf16[4,384,128]{2,1,0:T(8,128)(2,1)S(1)}, bf16[4,128,256]{2,1,0:T(8,128...) custom-call(s32[5]{0:T(128)S(1)} %copy-done.10, ...), custom_call_target="tpu_custom_call" | custom-call | flops 161000000 | bytes 1024 | tf_op jit(solution)/shard_map/attend/pallas_call | solution.py:369
  64.4 1.8 %collective-permute-done.17.refs_3_ = bf16[832,384]{1,0:T(8,128)(2,1)S(1)} collective-permute-done((bf16[832,384]{1,0:T(8,128)(2,1)S(1)}, bf16[832,384]{1,0:T(8,128)(2,1)S(1)}, u32[]{:S(2)}, u32[]{:S(2)}) %collective-permute-start.17) | collective-permute-done | bytes 639008 | tf_op jit(solution)/shard_map/ppermute | solution.py:810
  66.2 5.7 %feed.1 = (f32[128,768]{1,0:T(8,128)}, f32[128,768]{1,0:T(8,128)S(1)}, bf16[4,256,128]{2,1,0:T(8,128)(2,1)S(1)}, bf16[4,128,256]{2,1,0:T(8,128)(2,1)S(1)}, bf16[...) custom-call(s32[5]{0:T(128)S(1)} %copy-done.10, ...), custom_call_target="tpu_custom_call" | custom-call | flops 161000000 | bytes 1024 | tf_op jit(solution)/shard_map/feed/pallas_call | solution.py:479
  72.4 2.0 %collective-permute-done.19.refs_3_ = bf16[2,768,128]{2,1,0:T(8,128)(2,1)S(1)} collective-permute-done((bf16[2,768,128]{2,1,0:T(8,128)(2,1)S(1)}, bf16[2,768,128]{2,1,0:T(8,128)(2,1)S(1)}, u32[]{:S(2)}, u32[]{:S(2)}) %collective-permute-start.19) | collective-permute-done | bytes 393248 | tf_op jit(solution)/shard_map/ppermute | solution.py:810
  74.4 2.3 %weight_grads.2 = (bf16[4,96,768]{2,1,0:T(8,128)(2,1)S(1)}, bf16[4,96,768]{2,1,0:T(8,128)(2,1)S(1)}, bf16[8,96,768]{2,1,0:T(8,128)(2,1)S(1)}) custom-call(s32[5]{0:T(128)S(1)} %copy-done.10, bf16[2,128,1024]{2,1,0:T(8,128)(2,1)S(1)} %get-tuple-element.125.columns_own, bf16[2,128,1024]{2,1,0:T(8,128)(2,1)S(1)} %collective-permute-done.18.columns_other, ...), custom_call_target="tpu_custom_call" | custom-call | flops 92000000 | bytes 1024 | tf_op jit(solution)/shard_map/weight_grads/pallas_call | solution.py:616
  76.6 1.6 %collective-permute-start.21 = (bf16[8,96,768]{2,1,0:T(8,128)(2,1)S(1)}, bf16[8,96,768]{2,1,0:T(8,128)(2,1)S(1)}, u32[]{:S(2)}, u32[]{:S(2)}) collective-permute-start(bf16[8,96,768]{2,1,0:T(8,128)(2,1)S(1)} %get-tuple-element.139), channel_id=1, source_target_pairs={{0,2},{1,5},{2,0},{3,7},{4,6},{5,1},{6,4},{7,3},{8,10},{9,13},{10,... | collective-permute-start | bytes 3538952 | tf_op jit(solution)/shard_map/ppermute | solution.py:810
  78.2 5.2 %attend_back.1 = (f32[4,128,8,128]{3,2,1,0:T(8,128)S(1)}, bf16[2,128,384]{2,1,0:T(8,128)(2,1)S(1)}, bf16[2,128,384]{2,1,0:T(8,128)(2,1)S(1)}, f32[128,768]{1,0:T(8,128)}, f32[16,768]{1,0:T(8,128)S(1)}) custom-call(s32[5]{0:T(128)S(1)} %copy-done.10, f32[32,128,128]{2,1,0:T(8,128)S(1)} %get-tuple-element.115.probs_in, ...), custom_call_target="tpu_custom_call" | custom-call | flops 161000000 | bytes 1024 | tf_op jit(solution)/shard_map/attend_back/pallas_call | solution.py:545
  83.5 2.1 %table_grads.4 = (f32[256,192]{1,0:T(8,128)S(1)}, f32[32,32]{1,0:T(8,128)S(1)}) custom-call(s32[5]{0:T(128)S(1)} %copy-done.10, f32[4,128,8,128]{3,2,1,0:T(8,128)S(1)} %get-tuple-element.130.grads, s32[5,128,128]{2,1,0:T(8,128)S(1)} %copy-done.1, s32[128,128]{1,0:T(8,128)S(1)} %copy-done.3), custom_call_target="tpu_custom_call" | custom-call | flops 43125000 | bytes 1024 | tf_op jit(solution)/shard_map/table_grads/pallas_call | solution.py:712
  87.6 5.3 %table_grads.5 = (f32[256,192]{1,0:T(8,128)S(1)}, f32[32,32]{1,0:T(8,128)S(1)}) custom-call(s32[5]{0:T(128)S(1)} %copy-done.10, f32[4,128,8,128]{3,2,1,0:T(8,128)S(1)} %get-tuple-element.130.grads, s32[5,128,128]{2,1,0:T(8,128)S(1)} %copy-done.1, s32[128,128]{1,0:T(8,128)S(1)} %copy-done.3, f32[256,192]{1,0:T(8,128)S(1)} %get-tuple-element.131.refs_2_.refs_0_, ...), custom_call_target="tpu_custom_call" | custom-call | flops 129375000 | bytes 1024 | tf_op jit(solution)/shard_map/table_grads/pallas_call | solution.py:712
  94.4 5.3 %table_grads.6 = (f32[256,192]{1,0:T(8,128)S(1)}, f32[32,32]{1,0:T(8,128)S(1)}) custom-call(s32[5]{0:T(128)S(1)} %copy-done.10, f32[4,128,8,128]{3,2,1,0:T(8,128)S(1)} %get-tuple-element.130.grads, s32[5,128,128]{2,1,0:T(8,128)S(1)} %copy-done.1, s32[128,128]{1,0:T(8,128)S(1)} %copy-done.3, f32[256,192]{1,0:T(8,128)S(1)} %get-tuple-element.136.refs_2_.refs_0_, ...), custom_call_target="tpu_custom_call" | custom-call | flops 129375000 | bytes 1024 | tf_op jit(solution)/shard_map/table_grads/pallas_call | solution.py:712
  99.7 2.2 %table_grads.7 = (f32[64,384]{1,0:T(8,128)S(1)}, f32[96,384]{1,0:T(8,128)S(1)}, f32[32,384]{1,0:T(8,128)S(1)}) custom-call(s32[5]{0:T(128)S(1)} %copy-done.10, f32[4,128,8,128]{3,2,1,0:T(8,128)S(1)} %get-tuple-element.130.grads, s32[5,128,128]{2,1,0:T(8,128)S(1)} %copy-done.1, s32[128,128]{1,0:T(8,128)S(1)} %copy-done.3, ...), custom_call_target="tpu_custom_call" | custom-call | flops 43125000 | bytes 1024 | tf_op jit(solution)/shard_map/table_grads/pallas_call | solution.py:712
  102.0 1.4 %collective-permute-done.22.got = f32[96,384]{1,0:T(8,128)S(1)} collective-permute-done((f32[96,384]{1,0:T(8,128)S(1)}, f32[96,384]{1,0:T(8,128)S(1)}, u32[]{:S(2)}, u32[]{:S(2)}) %collective-permute-start.22) | collective-permute-done | bytes 147488 | tf_op jit(solution)/shard_map/ppermute | solution.py:810
  103.4 2.3 %collective-permute-done.25.refs_1_ = bf16[4,96,768]{2,1,0:T(8,128)(2,1)S(1)} collective-permute-done((bf16[4,96,768]{2,1,0:T(8,128)(2,1)S(1)}, bf16[4,96,768]{2,1,0:T(8,128)(2,1)S(1)}, u32[]{:S(2)}, u32[]{:S(2)}) %collective-permute-start.25) | collective-permute-done | bytes 589856 | tf_op jit(solution)/shard_map/ppermute | solution.py:810
  108.4 4.4 %collective-permute-done.23.got = f32[64,384]{1,0:T(8,128)S(1)} collective-permute-done((f32[64,384]{1,0:T(8,128)S(1)}, f32[64,384]{1,0:T(8,128)S(1)}, u32[]{:S(2)}, u32[]{:S(2)}) %collective-permute-start.23) | collective-permute-done | bytes 98336 | tf_op jit(solution)/shard_map/ppermute | solution.py:810
  117.3 2.0 %collective-permute-start.28 = (bf16[128,384]{1,0:T(8,128)(2,1)S(1)}, bf16[128,384]{1,0:T(8,128)(2,1)S(1)}, u32[]{:S(2)}, u32[]{:S(2)}) collective-permute-start(bf16[128,384]{1,0:T(8,128)(2,1)S(1)} %get-tuple-element.154), channel_id=1, source_target_pairs={{0,8},{1,9},{2,10},{3,11},{4,12},{5,13},{6,14},{7,15},{8,0},{9,1},... | collective-permute-start | bytes 294920 | tf_op jit(solution)/shard_map/ppermute | solution.py:810
  120.4 1.4 %collective-permute-start.30 = (bf16[128,384]{1,0:T(8,128)(2,1)S(1)}, bf16[128,384]{1,0:T(8,128)(2,1)S(1)}, u32[]{:S(2)}, u32[]{:S(2)}) collective-permute-start(bf16[128,384]{1,0:T(8,128)(2,1)S(1)} %get-tuple-element.156), channel_id=1, source_target_pairs={{0,24},{1,25},{2,26},{3,27},{4,28},{5,29},{6,30},{7,31},{8,16},{9,... | collective-permute-start | bytes 294920 | tf_op jit(solution)/shard_map/ppermute | solution.py:810
  121.8 7.4 %collective-permute-done.32.refs_1_ = bf16[96,768]{1,0:T(8,128)(2,1)S(1)} collective-permute-done((bf16[96,768]{1,0:T(8,128)(2,1)S(1)}, bf16[96,768]{1,0:T(8,128)(2,1)S(1)}, u32[]{:S(2)}, u32[]{:S(2)}) %collective-permute-start.32) | collective-permute-done | bytes 147488 | tf_op jit(solution)/shard_map/ppermute | solution.py:810
  132.1 1.5 %finish.1 = (f32[96,192]{1,0:T(8,128)}, f32[96,192]{1,0:T(8,128)}, f32[8,192]{1,0:T(8,128)}, f32[8,22]{1,0:T(8,128)}, f32[768]{0:T(1024)}, /*index=5*/f32[768]{0...) custom-call(s32[5]{0:T(128)S(1)} %copy-done.10, ...), custom_call_target="tpu_custom_call" | custom-call | flops 23000000 | bytes 1024 | tf_op jit(solution)/shard_map/finish/pallas_call | solution.py:782
  (108 shorter events, 26.1 us)
Async XLA Ops:
  0.7 5.2 %collective-permute-start = (bf16[32,192]{1,0:T(8,128)(2,1)}, bf16[32,192]{1,0:T(8,128)(2,1)S(1)}, u32[]{:S(2)}, u32[]{:S(2)}) collective-permute-start(bf16[32,192]{1,0:T(8,128)(2,1)} %bitcast.8), channel_id=1, source_target_pairs={{0,4},{1,5},{2,6},{3,7},{4,0},{5,1},{6,2},{7,3},{8,12},{9,13},{10,... | collective-permute-start | bytes 36872 | tf_op jit(solution)/shard_map/ppermute | solution.py:810
  8.9 17.6 %collective-permute-start.1 = (bf16[112,768]{1,0:T(8,128)(2,1)}, bf16[112,768]{1,0:T(8,128)(2,1)S(1)}, u32[]{:S(2)}, u32[]{:S(2)}) collective-permute-start(bf16[112,768]{1,0:T(8,128)(2,1)} %get-tuple-element.100.chunk.refs_0_), channel_id=1, source_target_pairs={{0,24},{1,25},{2,26},{3,27},{4,28},{5,29},{6,30},{7,31},{8,16},{9,... | collective-permute-start | bytes 516104 | tf_op jit(solution)/shard_map/ppermute | solution.py:810
  12.9 14.2 %collective-permute-start.2 = (bf16[112,768]{1,0:T(8,128)(2,1)}, bf16[112,768]{1,0:T(8,128)(2,1)S(1)}, u32[]{:S(2)}, u32[]{:S(2)}) collective-permute-start(bf16[112,768]{1,0:T(8,128)(2,1)} %get-tuple-element.100.chunk.refs_0_), channel_id=1, source_target_pairs={{0,16},{1,17},{2,18},{3,19},{4,20},{5,21},{6,22},{7,23},{8,24},{9,... | collective-permute-start | bytes 516104 | tf_op jit(solution)/shard_map/ppermute | solution.py:810
  12.9 14.2 %collective-permute-start.3 = (bf16[112,768]{1,0:T(8,128)(2,1)}, bf16[112,768]{1,0:T(8,128)(2,1)S(1)}, u32[]{:S(2)}, u32[]{:S(2)}) collective-permute-start(bf16[112,768]{1,0:T(8,128)(2,1)} %get-tuple-element.100.chunk.refs_0_), channel_id=1, source_target_pairs={{0,8},{1,9},{2,10},{3,11},{4,12},{5,13},{6,14},{7,15},{8,0},{9,1},... | collective-permute-start | bytes 516104 | tf_op jit(solution)/shard_map/ppermute | solution.py:810
  13.5 5.0 %collective-permute-start.4 = (bf16[96,384]{1,0:T(8,128)(2,1)}, bf16[96,384]{1,0:T(8,128)(2,1)S(1)}, u32[]{:S(2)}, u32[]{:S(2)}) collective-permute-start(bf16[96,384]{1,0:T(8,128)(2,1)} %pack_second.1.after.refs_0_), channel_id=1, source_target_pairs={{0,4},{1,3},{2,6},{3,1},{4,0},{5,7},{6,2},{7,5},{8,12},{9,11},{10,... | collective-permute-start | bytes 221192 | tf_op jit(solution)/shard_map/ppermute | solution.py:810
  27.1 19.0 %collective-permute-start.8 = (bf16[400,768]{1,0:T(8,128)(2,1)S(1)}, bf16[400,768]{1,0:T(8,128)(2,1)S(1)}, u32[]{:S(2)}, u32[]{:S(2)}) collective-permute-start(bf16[400,768]{1,0:T(8,128)(2,1)S(1)} %join.4.refs_1_.refs_0_), channel_id=1, source_target_pairs={{0,4},{1,3},{2,6},{3,1},{4,0},{5,7},{6,2},{7,5},{8,12},{9,11},{10,... | collective-permute-start | bytes 1843208 | tf_op jit(solution)/shard_map/ppermute | solution.py:810
  28.1 8.3 %collective-permute-start.5 = (bf16[192,384]{1,0:T(8,128)(2,1)S(1)}, bf16[192,384]{1,0:T(8,128)(2,1)S(1)}, u32[]{:S(2)}, u32[]{:S(2)}) collective-permute-start(bf16[192,384]{1,0:T(8,128)(2,1)S(1)} %join.3.refs_0_), channel_id=1, source_target_pairs={{0,16},{1,17},{2,18},{3,19},{4,20},{5,21},{6,22},{7,23},{8,24},{9,... | collective-permute-start | bytes 442376 | tf_op jit(solution)/shard_map/ppermute | solution.py:810
  36.5 9.4 %collective-permute-start.6 = (bf16[384,384]{1,0:T(8,128)(2,1)S(1)}, bf16[384,384]{1,0:T(8,128)(2,1)S(1)}, u32[]{:S(2)}, u32[]{:S(2)}) collective-permute-start(bf16[384,384]{1,0:T(8,128)(2,1)S(1)} %join.5.refs_1_.own), channel_id=1, source_target_pairs={{0,8},{1,9},{2,10},{3,11},{4,12},{5,13},{6,14},{7,15},{8,0},{9,1},... | collective-permute-start | bytes 884744 | tf_op jit(solution)/shard_map/ppermute | solution.py:810
  38.3 16.8 %collective-permute-start.9 = (bf16[400,768]{1,0:T(8,128)(2,1)S(1)}, bf16[400,768]{1,0:T(8,128)(2,1)S(1)}, u32[]{:S(2)}, u32[]{:S(2)}) collective-permute-start(bf16[400,768]{1,0:T(8,128)(2,1)S(1)} %join.4.refs_1_.refs_0_), channel_id=1, source_target_pairs={{0,2},{1,5},{2,0},{3,7},{4,6},{5,1},{6,4},{7,3},{8,10},{9,13},{10,... | collective-permute-start | bytes 1843208 | tf_op jit(solution)/shard_map/ppermute | solution.py:810
  46.1 10.2 %collective-permute-start.10 = (bf16[400,768]{1,0:T(8,128)(2,1)S(1)}, bf16[400,768]{1,0:T(8,128)(2,1)S(1)}, u32[]{:S(2)}, u32[]{:S(2)}) collective-permute-start(bf16[400,768]{1,0:T(8,128)(2,1)S(1)} %collective-permute-done.8.refs_1_), channel_id=1, source_target_pairs={{0,2},{1,5},{2,0},{3,7},{4,6},{5,1},{6,4},{7,3},{8,10},{9,13},{10,... | collective-permute-start | bytes 1843208 | tf_op jit(solution)/shard_map/ppermute | solution.py:810
  46.7 1.7 %collective-permute-start.7 = (bf16[2,768,128]{2,1,0:T(8,128)(2,1)S(1)}, bf16[2,768,128]{2,1,0:T(8,128)(2,1)S(1)}, u32[]{:S(2)}, u32[]{:S(2)}) collective-permute-start(bf16[2,768,128]{2,1,0:T(8,128)(2,1)S(1)} %copy-done.5), channel_id=1, source_target_pairs={{0,1},{1,0},{2,3},{3,2},{4,5},{5,4},{6,7},{7,6},{8,9},{9,8},{10,11... | collective-permute-start | bytes 1179656 | tf_op jit(solution)/shard_map/ppermute | solution.py:810
  46.7 17.4 %collective-permute-start.15 = (bf16[832,384]{1,0:T(8,128)(2,1)S(1)}, bf16[832,384]{1,0:T(8,128)(2,1)S(1)}, u32[]{:S(2)}, u32[]{:S(2)}) collective-permute-start(bf16[832,384]{1,0:T(8,128)(2,1)S(1)} %join_pairs.1.refs_1_.refs_0_), channel_id=1, source_target_pairs={{0,2},{1,5},{2,0},{3,7},{4,6},{5,1},{6,4},{7,3},{8,10},{9,13},{10,... | collective-permute-start | bytes 1916936 | tf_op jit(solution)/shard_map/ppermute | solution.py:810
  48.2 8.1 %collective-permute-start.11 = (bf16[400,768]{1,0:T(8,128)(2,1)S(1)}, bf16[400,768]{1,0:T(8,128)(2,1)S(1)}, u32[]{:S(2)}, u32[]{:S(2)}) collective-permute-start(bf16[400,768]{1,0:T(8,128)(2,1)S(1)} %join.4.refs_1_.refs_0_), channel_id=1, source_target_pairs={{0,1},{1,0},{2,3},{3,2},{4,5},{5,4},{6,7},{7,6},{8,9},{9,8},{10,11... | collective-permute-start | bytes 1843208 | tf_op jit(solution)/shard_map/ppermute | solution.py:810
  54.7 3.0 %collective-permute-start.12 = (bf16[400,768]{1,0:T(8,128)(2,1)S(1)}, bf16[400,768]{1,0:T(8,128)(2,1)S(1)}, u32[]{:S(2)}, u32[]{:S(2)}) collective-permute-start(bf16[400,768]{1,0:T(8,128)(2,1)S(1)} %collective-permute-done.8.refs_1_), channel_id=1, source_target_pairs={{0,1},{1,0},{2,3},{3,2},{4,5},{5,4},{6,7},{7,6},{8,9},{9,8},{10,11... | collective-permute-start | bytes 1843208 | tf_op jit(solution)/shard_map/ppermute | solution.py:810
  55.1 2.6 %collective-permute-start.13 = (bf16[400,768]{1,0:T(8,128)(2,1)S(1)}, bf16[400,768]{1,0:T(8,128)(2,1)S(1)}, u32[]{:S(2)}, u32[]{:S(2)}) collective-permute-start(bf16[400,768]{1,0:T(8,128)(2,1)S(1)} %collective-permute-done.9.refs_2_), channel_id=1, source_target_pairs={{0,1},{1,0},{2,3},{3,2},{4,5},{5,4},{6,7},{7,6},{8,9},{9,8},{10,11... | collective-permute-start | bytes 1843208 | tf_op jit(solution)/shard_map/ppermute | solution.py:810
  56.3 2.2 %collective-permute-start.14 = (bf16[400,768]{1,0:T(8,128)(2,1)S(1)}, bf16[400,768]{1,0:T(8,128)(2,1)S(1)}, u32[]{:S(2)}, u32[]{:S(2)}) collective-permute-start(bf16[400,768]{1,0:T(8,128)(2,1)S(1)} %collective-permute-done.10.refs_3_), channel_id=1, source_target_pairs={{0,1},{1,0},{2,3},{3,2},{4,5},{5,4},{6,7},{7,6},{8,9},{9,8},{10,11... | collective-permute-start | bytes 1843208 | tf_op jit(solution)/shard_map/ppermute | solution.py:810
  56.3 8.1 %collective-permute-start.16 = (bf16[832,384]{1,0:T(8,128)(2,1)S(1)}, bf16[832,384]{1,0:T(8,128)(2,1)S(1)}, u32[]{:S(2)}, u32[]{:S(2)}) collective-permute-start(bf16[832,384]{1,0:T(8,128)(2,1)S(1)} %join_pairs.1.refs_1_.refs_0_), channel_id=1, source_target_pairs={{0,1},{1,0},{2,3},{3,2},{4,5},{5,4},{6,7},{7,6},{8,9},{9,8},{10,11... | collective-permute-start | bytes 1916936 | tf_op jit(solution)/shard_map/ppermute | solution.py:810
  64.1 2.1 %collective-permute-start.17 = (bf16[832,384]{1,0:T(8,128)(2,1)S(1)}, bf16[832,384]{1,0:T(8,128)(2,1)S(1)}, u32[]{:S(2)}, u32[]{:S(2)}) collective-permute-start(bf16[832,384]{1,0:T(8,128)(2,1)S(1)} %collective-permute-done.15.refs_1_), channel_id=1, source_target_pairs={{0,1},{1,0},{2,3},{3,2},{4,5},{5,4},{6,7},{7,6},{8,9},{9,8},{10,11... | collective-permute-start | bytes 1916936 | tf_op jit(solution)/shard_map/ppermute | solution.py:810
  71.9 2.5 %collective-permute-start.18 = (bf16[2,128,1024]{2,1,0:T(8,128)(2,1)S(1)}, bf16[2,128,1024]{2,1,0:T(8,128)(2,1)S(1)}, u32[]{:S(2)}, u32[]{:S(2)}) collective-permute-start(bf16[2,128,1024]{2,1,0:T(8,128)(2,1)S(1)} %get-tuple-element.126), channel_id=1, source_target_pairs={{0,1},{1,0},{2,3},{3,2},{4,5},{5,4},{6,7},{7,6},{8,9},{9,8},{10,11... | collective-permute-start | bytes 1572872 | tf_op jit(solution)/shard_map/ppermute | solution.py:810
  72.2 2.2 %collective-permute-start.19 = (bf16[2,768,128]{2,1,0:T(8,128)(2,1)S(1)}, bf16[2,768,128]{2,1,0:T(8,128)(2,1)S(1)}, u32[]{:S(2)}, u32[]{:S(2)}) collective-permute-start(bf16[2,768,128]{2,1,0:T(8,128)(2,1)S(1)} %get-tuple-element.127.refs_1_), channel_id=1, source_target_pairs={{0,1},{1,0},{2,3},{3,2},{4,5},{5,4},{6,7},{7,6},{8,9},{9,8},{10,11... | collective-permute-start | bytes 1179656 | tf_op jit(solution)/shard_map/ppermute | solution.py:810
  76.6 16.3 %collective-permute-start.21 = (bf16[8,96,768]{2,1,0:T(8,128)(2,1)S(1)}, bf16[8,96,768]{2,1,0:T(8,128)(2,1)S(1)}, u32[]{:S(2)}, u32[]{:S(2)}) collective-permute-start(bf16[8,96,768]{2,1,0:T(8,128)(2,1)S(1)} %get-tuple-element.139), channel_id=1, source_target_pairs={{0,2},{1,5},{2,0},{3,7},{4,6},{5,1},{6,4},{7,3},{8,10},{9,13},{10,... | collective-permute-start | bytes 3538952 | tf_op jit(solution)/shard_map/ppermute | solution.py:810
  83.5 2.2 %collective-permute-start.20 = (bf16[2,128,384]{2,1,0:T(8,128)(2,1)S(1)}, bf16[2,128,384]{2,1,0:T(8,128)(2,1)S(1)}, u32[]{:S(2)}, u32[]{:S(2)}) collective-permute-start(bf16[2,128,384]{2,1,0:T(8,128)(2,1)S(1)} %get-tuple-element.134), channel_id=1, source_target_pairs={{0,1},{1,0},{2,3},{3,2},{4,5},{5,4},{6,7},{7,6},{8,9},{9,8},{10,11... | collective-permute-start | bytes 589832 | tf_op jit(solution)/shard_map/ppermute | solution.py:810
  86.9 19.2 %collective-permute-start.24 = (bf16[9,96,384]{2,1,0:T(8,128)(2,1)S(1)}, bf16[9,96,384]{2,1,0:T(8,128)(2,1)S(1)}, u32[]{:S(2)}, u32[]{:S(2)}) collective-permute-start(bf16[9,96,384]{2,1,0:T(8,128)(2,1)S(1)} %get-tuple-element.149), channel_id=1, source_target_pairs={{0,2},{1,5},{2,0},{3,7},{4,6},{5,1},{6,4},{7,3},{8,10},{9,13},{10,... | collective-permute-start | bytes 1990664 | tf_op jit(solution)/shard_map/ppermute | solution.py:810
  93.1 12.6 %collective-permute-start.25 = (bf16[4,96,768]{2,1,0:T(8,128)(2,1)S(1)}, bf16[4,96,768]{2,1,0:T(8,128)(2,1)S(1)}, u32[]{:S(2)}, u32[]{:S(2)}) collective-permute-start(bf16[4,96,768]{2,1,0:T(8,128)(2,1)S(1)} %add.13.refs_2_), channel_id=1, source_target_pairs={{0,4},{1,3},{2,6},{3,1},{4,0},{5,7},{6,2},{7,5},{8,12},{9,11},{10,... | collective-permute-start | bytes 1769480 | tf_op jit(solution)/shard_map/ppermute | solution.py:810
  105.9 9.5 %collective-permute-start.31 = (bf16[2,96,768]{2,1,0:T(8,128)(2,1)S(1)}, bf16[2,96,768]{2,1,0:T(8,128)(2,1)S(1)}, u32[]{:S(2)}, u32[]{:S(2)}) collective-permute-start(bf16[2,96,768]{2,1,0:T(8,128)(2,1)S(1)} %get-tuple-element.157), channel_id=1, source_target_pairs={{0,8},{1,9},{2,10},{3,11},{4,12},{5,13},{6,14},{7,15},{8,0},{9,1},... | collective-permute-start | bytes 884744 | tf_op jit(solution)/shard_map/ppermute | solution.py:810
  106.1 11.0 %collective-permute-start.27 = (bf16[4,96,384]{2,1,0:T(8,128)(2,1)S(1)}, bf16[4,96,384]{2,1,0:T(8,128)(2,1)S(1)}, u32[]{:S(2)}, u32[]{:S(2)}) collective-permute-start(bf16[4,96,384]{2,1,0:T(8,128)(2,1)S(1)} %add.14.after), channel_id=1, source_target_pairs={{0,4},{1,3},{2,6},{3,1},{4,0},{5,7},{6,2},{7,5},{8,12},{9,11},{10,... | collective-permute-start | bytes 884744 | tf_op jit(solution)/shard_map/ppermute | solution.py:810
  107.0 5.7 %collective-permute-start.23 = (f32[64,384]{1,0:T(8,128)S(1)}, f32[64,384]{1,0:T(8,128)S(1)}, u32[]{:S(2)}, u32[]{:S(2)}) collective-permute-start(f32[64,384]{1,0:T(8,128)S(1)} %get-tuple-element.147.refs_3_.sent), channel_id=1, source_target_pairs={{0,2},{1,5},{2,0},{3,7},{4,6},{5,1},{6,4},{7,3},{8,10},{9,13},{10,... | collective-permute-start | bytes 294920 | tf_op jit(solution)/shard_map/ppermute | solution.py:810
  112.7 4.4 %collective-permute-start.26 = (f32[48,384]{1,0:T(8,128)S(1)}, f32[48,384]{1,0:T(8,128)S(1)}, u32[]{:S(2)}, u32[]{:S(2)}) collective-permute-start(f32[48,384]{1,0:T(8,128)S(1)} %get-tuple-element.152.sent.refs_0_), channel_id=1, source_target_pairs={{0,4},{1,3},{2,6},{3,1},{4,0},{5,7},{6,2},{7,5},{8,12},{9,11},{10,... | collective-permute-start | bytes 221192 | tf_op jit(solution)/shard_map/ppermute | solution.py:810
  115.4 13.7 %collective-permute-start.32 = (bf16[96,768]{1,0:T(8,128)(2,1)S(1)}, bf16[96,768]{1,0:T(8,128)(2,1)S(1)}, u32[]{:S(2)}, u32[]{:S(2)}) collective-permute-start(bf16[96,768]{1,0:T(8,128)(2,1)S(1)} %get-tuple-element.159), channel_id=1, source_target_pairs={{0,16},{1,17},{2,18},{3,19},{4,20},{5,21},{6,22},{7,23},{8,24},{9,... | collective-permute-start | bytes 442376 | tf_op jit(solution)/shard_map/ppermute | solution.py:810
  117.3 12.6 %collective-permute-start.28 = (bf16[128,384]{1,0:T(8,128)(2,1)S(1)}, bf16[128,384]{1,0:T(8,128)(2,1)S(1)}, u32[]{:S(2)}, u32[]{:S(2)}) collective-permute-start(bf16[128,384]{1,0:T(8,128)(2,1)S(1)} %get-tuple-element.154), channel_id=1, source_target_pairs={{0,8},{1,9},{2,10},{3,11},{4,12},{5,13},{6,14},{7,15},{8,0},{9,1},... | collective-permute-start | bytes 294920 | tf_op jit(solution)/shard_map/ppermute | solution.py:810
  119.3 11.9 %collective-permute-start.29 = (bf16[128,384]{1,0:T(8,128)(2,1)S(1)}, bf16[128,384]{1,0:T(8,128)(2,1)S(1)}, u32[]{:S(2)}, u32[]{:S(2)}) collective-permute-start(bf16[128,384]{1,0:T(8,128)(2,1)S(1)} %get-tuple-element.155), channel_id=1, source_target_pairs={{0,16},{1,17},{2,18},{3,19},{4,20},{5,21},{6,22},{7,23},{8,24},{9,... | collective-permute-start | bytes 294920 | tf_op jit(solution)/shard_map/ppermute | solution.py:810
  120.4 10.9 %collective-permute-start.30 = (bf16[128,384]{1,0:T(8,128)(2,1)S(1)}, bf16[128,384]{1,0:T(8,128)(2,1)S(1)}, u32[]{:S(2)}, u32[]{:S(2)}) collective-permute-start(bf16[128,384]{1,0:T(8,128)(2,1)S(1)} %get-tuple-element.156), channel_id=1, source_target_pairs={{0,24},{1,25},{2,26},{3,27},{4,28},{5,29},{6,30},{7,31},{8,16},{9,... | collective-permute-start | bytes 294920 | tf_op jit(solution)/shard_map/ppermute | solution.py:810
  (22 other events, 196.8 us)

commit v7 on v6

--- a/solution.py
+++ b/solution.py
@@ -83,11 +83,16 @@
     return terms
 
 
-def pack_first_kernel(place, wq, wk, wv, wo, bq, bv, bi, edge, neighbour, after, weights, biases, held, sems):
+def pack_first_kernel(
+    place, wq, wk, wv, wo, bq, bv, bi, edge, neighbour, after, weights, biases, held, sems, table, table_sems
+):
     copies = [
         pltpu.make_async_copy(source, held.at[i], sems.at[i]) for i, source in enumerate((wq, wk, wv, wo))
     ]
-    for copy in copies:
+    table_copies = [
+        pltpu.make_async_copy(source, table.at[i], table_sems.at[i]) for i, source in enumerate((edge, neighbour))
+    ]
+    for copy in copies + table_copies:
         copy.start()
     row = jnp.concatenate([as_row(bq), as_row(bv), as_row(bi)], 1)
     lanes = weights.shape[1]
@@ -95,7 +100,9 @@
     terms = [term.astype(f32) for term in three_terms(row)]
     biases[...] = jnp.concatenate(terms + [jnp.zeros((13, lanes), f32)], 0).astype(bf16)
     even = place[1] == 0
-    mine, other = edge[...].astype(f32), neighbour[...].astype(f32)
+    for copy in table_copies:
+        copy.wait()
+    mine, other = table[0].astype(f32), table[1].astype(f32)
     low, high = jnp.where(even, mine, other), jnp.where(even, other, mine)
     rows = held.shape[1]
     half = low.shape[0] // 2
@@ -110,9 +117,14 @@
     return pl.pallas_call(
         pack_first_kernel,
         out_shape=(shape((rows + 16, 4 * width), bf16), shape((16, 4 * width), bf16)),
-        in_specs=[smem] + [hbm] * 4 + [vmem] * 5 + [untouched],
+        in_specs=[smem] + [hbm] * 4 + [vmem] * 3 + [hbm] * 2 + [untouched],
         out_specs=[vmem] * 2,
-        scratch_shapes=[pltpu.VMEM((4, rows, width), bf16), pltpu.SemaphoreType.DMA((4,))],
+        scratch_shapes=[
+            pltpu.VMEM((4, rows, width), bf16),
+            pltpu.SemaphoreType.DMA((4,)),
+            pltpu.VMEM((2,) + edge.shape, bf16),
+            pltpu.SemaphoreType.DMA((2,)),
+        ],
         cost_estimate=cost(2),
         compiler_params=params(60),
         name="pack_first",
@@ -562,9 +574,20 @@
     )
 
 
-def weight_grads_kernel(plan, n_rows, place, columns_own, columns_other, *refs):
+def weight_grads_kernel(plan, n_rows, hops, place, columns_own, columns_other, *refs):
     own_rows, other_rows = refs[:n_rows], refs[n_rows : 2 * n_rows]
-    own, across, second, rows_t = refs[-4:]
+    rows_t = refs[-1]
+    if hops == 2:
+        second = refs[-2]
+    elif hops == 1:
+        own, across = refs[-3:-1]
+    else:
+        own, across, second = refs[-4:-1]
+    targets = []
+    if hops != 1:
+        targets += [(3, second, 0), (2, second, 4)]
+    if hops != 2:
+        targets += [(1, across, 0), (0, own, 0)]
     kind = 0
     for mine, other in zip(own_rows, other_rows):
         slots = mine.shape[2]
@@ -573,15 +596,15 @@
             rows_t[kind, :, slots : 2 * slots] = other[i]
             kind += 1
     core = place[3]
-    height = own.shape[1]
-    for which, out, at in ((3, second, 0), (2, second, 4), (1, across, 0), (0, own, 0)):
+    height = targets[0][1].shape[1]
+    for which, out, at in targets:
         y = relative(place, core, which, 0)[1] >> 1
         right = jnp.concatenate([columns_own[y], columns_other[y]], 0)
         for step in range(4):
             row = relative(place, core, which, step)[0]
             start = pl.multiple_of(row * height, height)
             out[at + step] = plan(lambda kind: rows_t[kind, pl.ds(start, height), :], right).astype(bf16)
-    for extra in range(8, second.shape[0]):
+    for extra in range(8, targets[0][1].shape[0]):
         second[extra] = jnp.zeros(second.shape[1:], bf16)
 
 
@@ -608,16 +631,18 @@
 
 
 def weight_grads(
-    plan, place, columns_own, columns_other, own_rows, other_rows, height, lanes, microseconds, after=(), blocks=8
+    plan, place, columns_own, columns_other, own_rows, other_rows, height, lanes, microseconds, after=(), blocks=8, hops=0
 ):
     features, slots = own_rows[0].shape[1:]
     kinds = sum(rows.shape[0] for rows in own_rows)
     out = shape((4, height, lanes), bf16)
+    far = shape((blocks, height, lanes), bf16)
+    outs = ((out, out, far), (out, out), (far,))[hops]
     return pl.pallas_call(
-        functools.partial(weight_grads_kernel, plan, len(own_rows)),
-        out_shape=(out, out, shape((blocks, height, lanes), bf16)),
+        functools.partial(weight_grads_kernel, plan, len(own_rows), hops),
+        out_shape=outs,
         in_specs=[smem] + [vmem] * (2 + 2 * len(own_rows)) + [untouched] * len(after),
-        out_specs=[vmem] * 3,
+        out_specs=[vmem] * len(outs),
         scratch_shapes=[pltpu.VMEM((kinds, features, 2 * slots), bf16)],
         cost_estimate=cost(microseconds),
         compiler_params=params(20),
@@ -1026,10 +1051,13 @@
     if staged:
         rows_b = (rows_early, rows_late)
         other_rows_b = (other_rows_early, send(rows_late, links.core))
-        own_b, across_b, second_b = weight_grads(
-            plan_second, place, mine_b, send(theirs_b, links.core), rows_b, other_rows_b, height, 4 * width, 4
-        )
+        grads_of = functools.partial(
+            weight_grads, plan_second, place, mine_b, send(theirs_b, links.core), rows_b, other_rows_b,
+            height, 4 * width, 2,
+        )
+        (second_b,) = grads_of(hops=2)
         got_second_b = send(second_b, links.second)
+        own_b, across_b = grads_of((second_b,), hops=1)
         after = own_b
     score_grads, mine_a, theirs_a, grad_layer_in, sums = attend_back(
         place, probs, value_win, transposed, grad_att_t, grad_values, weights,

time: 134 us -> 134 us (level)
  waiting for transfers between devices: 26.2 us -> 24.6 us
    ppermute x33, waiting for transfers between devices: 26.2 us -> 24.6 us  [send(): return lax.ppermute(values, ('dp', 'mp'), hop)]
    pallas_call x2 -> x3, Pallas kernels: 3.51 us -> 4.44 us  [weight_grads(): pl.pallas_call(functools.partial(weight_grads_kernel, plan, len(own_rows)...]
  transfers between devices with their start and end apart: 33 -> 33, of which waited for: 15 -> 15; matrix products, arithmetic and copies ran while one was open for 0% -> 0% of each run, Pallas kernels for 43% -> 45%
where the time goes in v7:
time: 134 us; the launch traced here: 133 us
  Pallas kernels  70.8 us (53%)
  starting transfers between devices  32.5 us (24%)
  waiting for transfers between devices  24.6 us (18%)
  local copies, waits for them, and re-layouts  4.1 us (3%)
    ppermute x33, starting transfers between devices, send(): return lax.ppermute(values, ('dp', 'mp'), hop)  32.5 us
    ppermute x33, waiting for transfers between devices, send(): return lax.ppermute(values, ('dp', 'mp'), hop)  24.6 us
    pallas_call x4, Pallas kernels, lookup(): pl.pallas_call(functools.partial(lookup_kernel, first, step, share), out_...  24.5 us
    pallas_call x4, Pallas kernels, table_grads(): pl.pallas_call(functools.partial(table_kernel, digit, start, stop, len(pr...  15 us
    pallas_call x1, Pallas kernels, feed(): pl.pallas_call(functools.partial(feed_kernel, len(parts)), grid=(1,), out...  5.69 us
    pallas_call x1, Pallas kernels, attend(): pl.pallas_call(functools.partial(attend_kernel, len(parts)), out_shape=(s...  5.4 us
    pallas_call x1, Pallas kernels, attend_back(): pl.pallas_call(attend_back_kernel, out_shape=(shape((groups, slots, 8, sl...  5.23 us
    pallas_call x3, Pallas kernels, weight_grads(): pl.pallas_call(functools.partial(weight_grads_kernel, plan, len(own_rows)...  4.44 us
  transfers between devices with their start and end apart: 33, of which 15 were waited for; matrix products, arithmetic and copies ran while one was open for 0% of the time, Pallas kernels for 45%

profile of v7, /device:TPU:0, one launch (start us, length us, event | category | flops | bytes accessed | tf_op | source)
XLA Modules:
  0.0 133.2 jit_solution(18009755933529592267)
XLA Ops:
  0.7 3.0 %collective-permute-start = (bf16[32,192]{1,0:T(8,128)(2,1)}, bf16[32,192]{1,0:T(8,128)(2,1)S(1)}, u32[]{:S(2)}, u32[]{:S(2)}) collective-permute-start(bf16[32,192]{1,0:T(8,128)(2,1)} %bitcast.8), channel_id=1, source_target_pairs={{0,4},{1,5},{2,6},{3,7},{4,0},{5,1},{6,2},{7,3},{8,12},{9,13},{10,... | collective-permute-start | bytes 36872 | tf_op jit(solution)/shard_map/ppermute | solution.py:835
  4.3 1.5 %pack_second.1.after.refs_0_ = bf16[96,384]{1,0:T(8,128)(2,1)} custom-call(bf16[96,192]{1,0:T(8,128)(2,1)} %wi.1, bf16[96,192]{1,0:T(8,128)(2,1)} %wu.1), custom_call_target="tpu_custom_call" | custom-call | flops 23000000 | bytes 1024 | tf_op jit(solution)/shard_map/pack_second/pallas_call | solution.py:140
  6.4 2.5 %pack_first.1 = (bf16[112,768]{1,0:T(8,128)(2,1)}, bf16[16,768]{1,0:T(8,128)(2,1)}) custom-call(s32[5]{0:T(128)} %stack.23.place, bf16[96,192]{1,0:T(8,128)(2,1)} %wq.1, bf16[96,192]{1,0:T(8,128)(2,1)} %wk.1, bf16[96,192]{1,0:T(8,128)(2,1)} %wv.1, bf16[96,192]{1,0:T(8,128)(2,1)} %wo.1, f32[192]{0:T(256)} %bq.1, f32[192]{0:T(256)} %bv.1, f32[192]{0:T(256)} %bi.1, ...), custom_call_target="tpu_custom_call" | custom-call | flops 46000000 | bytes 1024 | tf_op jit(solution)/shard_map/pack_first/pallas_call | solution.py:117
  9.0 4.0 %collective-permute-start.1 = (bf16[112,768]{1,0:T(8,128)(2,1)}, bf16[112,768]{1,0:T(8,128)(2,1)S(1)}, u32[]{:S(2)}, u32[]{:S(2)}) collective-permute-start(bf16[112,768]{1,0:T(8,128)(2,1)} %get-tuple-element.99.chunk.refs_0_), channel_id=1, source_target_pairs={{0,24},{1,25},{2,26},{3,27},{4,28},{5,29},{6,30},{7,31},{8,16},{9,... | collective-permute-start | bytes 516104 | tf_op jit(solution)/shard_map/ppermute | solution.py:835
  13.6 1.6 %collective-permute-start.4 = (bf16[96,384]{1,0:T(8,128)(2,1)}, bf16[96,384]{1,0:T(8,128)(2,1)S(1)}, u32[]{:S(2)}, u32[]{:S(2)}) collective-permute-start(bf16[96,384]{1,0:T(8,128)(2,1)} %pack_second.1.after.refs_0_), channel_id=1, source_target_pairs={{0,4},{1,3},{2,6},{3,1},{4,0},{5,7},{6,2},{7,5},{8,12},{9,11},{10,... | collective-permute-start | bytes 221192 | tf_op jit(solution)/shard_map/ppermute | solution.py:835
  15.2 3.3 %prepare.1 = (s32[5,128,128]{2,1,0:T(8,128)}, s32[128,128]{1,0:T(8,128)}, bf16[128,768]{1,0:T(8,128)(2,1)}, bf16[2,768,128]{2,1,0:T(8,128)(2,1)}) custom-call(s32[5]{0:T(128)} %stack.23.place, s32[4,128,128]{2,1,0:T(8,128)} %spatial.1, s32[4,5,128,128]{3,2,1,0:T(8,128)} %path.1, f32[128,768]{1,0:T(8,128)} %layer_in.5, f32[768]{0:T(1024)} %gain.7, f32[768]{0:T(1024)} %bias.2, ...), custom_call_target="tpu_custom_call" | custom-call | flops 23000000 | bytes 1024 | tf_op jit(solution)/shard_map/prepare/pallas_call | solution.py:171
  20.5 6.1 %lookup.4.refs_5_.refs_0_ = s32[16,128,128]{2,1,0:T(8,128)S(1)} custom-call(s32[5]{0:T(128)S(1)} %copy-done.10, bf16[112,768]{1,0:T(8,128)(2,1)S(1)} %copy-done.8, s32[5,128,128]{2,1,0:T(8,128)S(1)} %copy-done, bf16[192,384]{1,0:T(8,128)(2,1)S(1)} %join.3.refs_0_), custom_call_target="tpu_custom_call" | custom-call | flops 138000000 | bytes 1024 | tf_op jit(solution)/shard_map/lookup/pallas_call | solution.py:265
  28.2 1.9 %collective-permute-start.5 = (bf16[192,384]{1,0:T(8,128)(2,1)S(1)}, bf16[192,384]{1,0:T(8,128)(2,1)S(1)}, u32[]{:S(2)}, u32[]{:S(2)}) collective-permute-start(bf16[192,384]{1,0:T(8,128)(2,1)S(1)} %join.3.refs_0_), channel_id=1, source_target_pairs={{0,16},{1,17},{2,18},{3,19},{4,20},{5,21},{6,22},{7,23},{8,24},{9,... | collective-permute-start | bytes 442376 | tf_op jit(solution)/shard_map/ppermute | solution.py:835
  30.1 6.1 %lookup.5.refs_2_.refs_0_ = s32[16,128,128]{2,1,0:T(8,128)S(1)} custom-call(s32[5]{0:T(128)S(1)} %copy-done.10, bf16[112,768]{1,0:T(8,128)(2,1)S(1)} %collective-permute-done.3.refs_1_.chunk, s32[5,128,128]{2,1,0:T(8,128)S(1)} %copy-done.1, s32[16,128,128]{2,1,0:T(8,128)S(1)} %lookup.4.refs_5_.refs_0_, ...), custom_call_target="tpu_custom_call", output_to_operand_aliasing={{}: (3, {})} | custom-call | flops 138000000 | bytes 1024 | tf_op jit(solution)/shard_map/lookup/pallas_call | solution.py:265
  36.5 1.8 %collective-permute-start.6 = (bf16[384,384]{1,0:T(8,128)(2,1)S(1)}, bf16[384,384]{1,0:T(8,128)(2,1)S(1)}, u32[]{:S(2)}, u32[]{:S(2)}) collective-permute-start(bf16[384,384]{1,0:T(8,128)(2,1)S(1)} %join.5.refs_1_.own), channel_id=1, source_target_pairs={{0,8},{1,9},{2,10},{3,11},{4,12},{5,13},{6,14},{7,15},{8,0},{9,1},... | collective-permute-start | bytes 884744 | tf_op jit(solution)/shard_map/ppermute | solution.py:835
  38.4 1.5 %collective-permute-start.9 = (bf16[400,768]{1,0:T(8,128)(2,1)S(1)}, bf16[400,768]{1,0:T(8,128)(2,1)S(1)}, u32[]{:S(2)}, u32[]{:S(2)}) collective-permute-start(bf16[400,768]{1,0:T(8,128)(2,1)S(1)} %join.4.refs_1_.refs_0_), channel_id=1, source_target_pairs={{0,2},{1,5},{2,0},{3,7},{4,6},{5,1},{6,4},{7,3},{8,10},{9,13},{10,... | collective-permute-start | bytes 1843208 | tf_op jit(solution)/shard_map/ppermute | solution.py:835
  39.9 6.1 %lookup.6.refs_0_ = s32[16,128,128]{2,1,0:T(8,128)S(1)} custom-call(s32[5]{0:T(128)S(1)} %copy-done.10, bf16[112,768]{1,0:T(8,128)(2,1)S(1)} %collective-permute-done.2.refs_2_.chunk, s32[5,128,128]{2,1,0:T(8,128)S(1)} %copy-done.1, s32[16,128,128]{2,1,0:T(8,128)S(1)} %lookup.5.refs_2_.refs_0_, ...), custom_call_target="tpu_custom_call", output_to_operand_aliasing={{}: (3, {})} | custom-call | flops 138000000 | bytes 1024 | tf_op jit(solution)/shard_map/lookup/pallas_call | solution.py:265
  46.7 1.5 %collective-permute-start.15 = (bf16[832,384]{1,0:T(8,128)(2,1)S(1)}, bf16[832,384]{1,0:T(8,128)(2,1)S(1)}, u32[]{:S(2)}, u32[]{:S(2)}) collective-permute-start(bf16[832,384]{1,0:T(8,128)(2,1)S(1)} %join_pairs.1.refs_1_.refs_0_), channel_id=1, source_target_pairs={{0,2},{1,5},{2,0},{3,7},{4,6},{5,1},{6,4},{7,3},{8,10},{9,13},{10,... | collective-permute-start | bytes 1916936 | tf_op jit(solution)/shard_map/ppermute | solution.py:835
  48.5 6.3 %lookup.7.edge_sums = s32[16,128,128]{2,1,0:T(8,128)S(1)} custom-call(s32[5]{0:T(128)S(1)} %copy-done.10, bf16[112,768]{1,0:T(8,128)(2,1)S(1)} %collective-permute-done.1.refs_3_.chunk, s32[5,128,128]{2,1,0:T(8,128)S(1)} %copy-done.1, s32[16,128,128]{2,1,0:T(8,128)S(1)} %lookup.6.refs_0_, ...), custom_call_target="tpu_custom_call", output_to_operand_aliasing={{}: (3, {})} | custom-call | flops 138000000 | bytes 1024 | tf_op jit(solution)/shard_map/lookup/pallas_call | solution.py:265
  58.7 5.4 %attend.1 = (bf16[4,768,768]{2,1,0:T(8,128)(2,1)S(1)}, f32[4,1,768]{2,1,0:T(1,128)S(1)}, bf16[4,384,128]{2,1,0:T(8,128)(2,1)S(1)}, bf16[4,128,256]{2,1,0:T(8,128...) custom-call(s32[5]{0:T(128)S(1)} %copy-done.10, ...), custom_call_target="tpu_custom_call" | custom-call | flops 161000000 | bytes 1024 | tf_op jit(solution)/shard_map/attend/pallas_call | solution.py:381
  64.5 1.8 %collective-permute-done.17.refs_3_ = bf16[832,384]{1,0:T(8,128)(2,1)S(1)} collective-permute-done((bf16[832,384]{1,0:T(8,128)(2,1)S(1)}, bf16[832,384]{1,0:T(8,128)(2,1)S(1)}, u32[]{:S(2)}, u32[]{:S(2)}) %collective-permute-start.17) | collective-permute-done | bytes 639008 | tf_op jit(solution)/shard_map/ppermute | solution.py:835
  66.3 5.7 %feed.1 = (f32[128,768]{1,0:T(8,128)}, f32[128,768]{1,0:T(8,128)S(1)}, bf16[4,256,128]{2,1,0:T(8,128)(2,1)S(1)}, bf16[4,128,256]{2,1,0:T(8,128)(2,1)S(1)}, bf16[...) custom-call(s32[5]{0:T(128)S(1)} %copy-done.10, ...), custom_call_target="tpu_custom_call" | custom-call | flops 161000000 | bytes 1024 | tf_op jit(solution)/shard_map/feed/pallas_call | solution.py:491
  72.5 2.0 %collective-permute-done.19.refs_3_ = bf16[2,768,128]{2,1,0:T(8,128)(2,1)S(1)} collective-permute-done((bf16[2,768,128]{2,1,0:T(8,128)(2,1)S(1)}, bf16[2,768,128]{2,1,0:T(8,128)(2,1)S(1)}, u32[]{:S(2)}, u32[]{:S(2)}) %collective-permute-start.19) | collective-permute-done | bytes 393248 | tf_op jit(solution)/shard_map/ppermute | solution.py:835
  74.4 1.6 %weight_grads.3.refs_4_ = bf16[8,96,768]{2,1,0:T(8,128)(2,1)S(1)} custom-call(s32[5]{0:T(128)S(1)} %copy-done.10, bf16[2,128,1024]{2,1,0:T(8,128)(2,1)S(1)} %get-tuple-element.124.columns_own, bf16[2,128,1024]{2,1,0:T(8,128)(2,1)S(1)} %collective-permute-done.18.columns_other, bf16[2,768,128]{2,1,0:T(8,128)(2,1)S(1)} %copy-done.3, ...), custom_call_target="tpu_custom_call" | custom-call | flops 46000000 | bytes 1024 | tf_op jit(solution)/shard_map/weight_grads/pallas_call | solution.py:641
  76.0 1.6 %collective-permute-start.21 = (bf16[8,96,768]{2,1,0:T(8,128)(2,1)S(1)}, bf16[8,96,768]{2,1,0:T(8,128)(2,1)S(1)}, u32[]{:S(2)}, u32[]{:S(2)}) collective-permute-start(bf16[8,96,768]{2,1,0:T(8,128)(2,1)S(1)} %weight_grads.3.refs_4_), channel_id=1, source_target_pairs={{0,2},{1,5},{2,0},{3,7},{4,6},{5,1},{6,4},{7,3},{8,10},{9,13},{10,... | collective-permute-start | bytes 3538952 | tf_op jit(solution)/shard_map/ppermute | solution.py:835
  77.6 1.6 %weight_grads.4 = (bf16[4,96,768]{2,1,0:T(8,128)(2,1)S(1)}, bf16[4,96,768]{2,1,0:T(8,128)(2,1)S(1)}) custom-call(s32[5]{0:T(128)S(1)} %copy-done.10, bf16[2,128,1024]{2,1,0:T(8,128)(2,1)S(1)} %get-tuple-element.124.columns_own, bf16[2,128,1024]{2,1,0:T(8,128)(2,1)S(1)} %collective-permute-done.18.columns_other, bf16[2,768,128]{2,1,0:T(8,128)(2,1)S(1)} %copy-done.3, ...), custom_call_target="tpu_custom_call" | custom-call | flops 46000000 | bytes 1024 | tf_op jit(solution)/shard_map/weight_grads/pallas_call | solution.py:641
  79.2 5.2 %attend_back.1 = (f32[4,128,8,128]{3,2,1,0:T(8,128)S(1)}, bf16[2,128,384]{2,1,0:T(8,128)(2,1)S(1)}, bf16[2,128,384]{2,1,0:T(8,128)(2,1)S(1)}, f32[128,768]{1,0:T(8,128)}, f32[16,768]{1,0:T(8,128)S(1)}) custom-call(s32[5]{0:T(128)S(1)} %copy-done.10, f32[32,128,128]{2,1,0:T(8,128)S(1)} %get-tuple-element.114.probs_in, ...), custom_call_target="tpu_custom_call" | custom-call | flops 161000000 | bytes 1024 | tf_op jit(solution)/shard_map/attend_back/pallas_call | solution.py:557
  84.5 2.1 %table_grads.4 = (f32[256,192]{1,0:T(8,128)S(1)}, f32[32,32]{1,0:T(8,128)S(1)}) custom-call(s32[5]{0:T(128)S(1)} %copy-done.10, f32[4,128,8,128]{3,2,1,0:T(8,128)S(1)} %get-tuple-element.129.grads, s32[5,128,128]{2,1,0:T(8,128)S(1)} %copy-done.1, s32[128,128]{1,0:T(8,128)S(1)} %copy-done.4), custom_call_target="tpu_custom_call" | custom-call | flops 43125000 | bytes 1024 | tf_op jit(solution)/shard_map/table_grads/pallas_call | solution.py:737
  88.6 5.3 %table_grads.5 = (f32[256,192]{1,0:T(8,128)S(1)}, f32[32,32]{1,0:T(8,128)S(1)}) custom-call(s32[5]{0:T(128)S(1)} %copy-done.10, f32[4,128,8,128]{3,2,1,0:T(8,128)S(1)} %get-tuple-element.129.grads, s32[5,128,128]{2,1,0:T(8,128)S(1)} %copy-done.1, s32[128,128]{1,0:T(8,128)S(1)} %copy-done.4, f32[256,192]{1,0:T(8,128)S(1)} %get-tuple-element.130.refs_2_.refs_0_, ...), custom_call_target="tpu_custom_call" | custom-call | flops 129375000 | bytes 1024 | tf_op jit(solution)/shard_map/table_grads/pallas_call | solution.py:737
  95.4 5.3 %table_grads.6 = (f32[256,192]{1,0:T(8,128)S(1)}, f32[32,32]{1,0:T(8,128)S(1)}) custom-call(s32[5]{0:T(128)S(1)} %copy-done.10, f32[4,128,8,128]{3,2,1,0:T(8,128)S(1)} %get-tuple-element.129.grads, s32[5,128,128]{2,1,0:T(8,128)S(1)} %copy-done.1, s32[128,128]{1,0:T(8,128)S(1)} %copy-done.4, f32[256,192]{1,0:T(8,128)S(1)} %get-tuple-element.135.refs_2_.refs_0_, ...), custom_call_target="tpu_custom_call" | custom-call | flops 129375000 | bytes 1024 | tf_op jit(solution)/shard_map/table_grads/pallas_call | solution.py:737
  100.7 2.2 %table_grads.7 = (f32[64,384]{1,0:T(8,128)S(1)}, f32[96,384]{1,0:T(8,128)S(1)}, f32[32,384]{1,0:T(8,128)S(1)}) custom-call(s32[5]{0:T(128)S(1)} %copy-done.10, f32[4,128,8,128]{3,2,1,0:T(8,128)S(1)} %get-tuple-element.129.grads, s32[5,128,128]{2,1,0:T(8,128)S(1)} %copy-done.1, s32[128,128]{1,0:T(8,128)S(1)} %copy-done.4, ...), custom_call_target="tpu_custom_call" | custom-call | flops 43125000 | bytes 1024 | tf_op jit(solution)/shard_map/table_grads/pallas_call | solution.py:737
  103.0 1.4 %collective-permute-done.22.got = f32[96,384]{1,0:T(8,128)S(1)} collective-permute-done((f32[96,384]{1,0:T(8,128)S(1)}, f32[96,384]{1,0:T(8,128)S(1)}, u32[]{:S(2)}, u32[]{:S(2)}) %collective-permute-start.22) | collective-permute-done | bytes 147488 | tf_op jit(solution)/shard_map/ppermute | solution.py:835
  107.8 4.4 %collective-permute-done.23.got = f32[64,384]{1,0:T(8,128)S(1)} collective-permute-done((f32[64,384]{1,0:T(8,128)S(1)}, f32[64,384]{1,0:T(8,128)S(1)}, u32[]{:S(2)}, u32[]{:S(2)}) %collective-permute-start.23) | collective-permute-done | bytes 98336 | tf_op jit(solution)/shard_map/ppermute | solution.py:835
  116.7 2.0 %collective-permute-start.28 = (bf16[128,384]{1,0:T(8,128)(2,1)S(1)}, bf16[128,384]{1,0:T(8,128)(2,1)S(1)}, u32[]{:S(2)}, u32[]{:S(2)}) collective-permute-start(bf16[128,384]{1,0:T(8,128)(2,1)S(1)} %get-tuple-element.152), channel_id=1, source_target_pairs={{0,8},{1,9},{2,10},{3,11},{4,12},{5,13},{6,14},{7,15},{8,0},{9,1},... | collective-permute-start | bytes 294920 | tf_op jit(solution)/shard_map/ppermute | solution.py:835
  119.8 1.4 %collective-permute-start.30 = (bf16[128,384]{1,0:T(8,128)(2,1)S(1)}, bf16[128,384]{1,0:T(8,128)(2,1)S(1)}, u32[]{:S(2)}, u32[]{:S(2)}) collective-permute-start(bf16[128,384]{1,0:T(8,128)(2,1)S(1)} %get-tuple-element.154), channel_id=1, source_target_pairs={{0,24},{1,25},{2,26},{3,27},{4,28},{5,29},{6,30},{7,31},{8,16},{9,... | collective-permute-start | bytes 294920 | tf_op jit(solution)/shard_map/ppermute | solution.py:835
  121.2 7.4 %collective-permute-done.32.refs_1_ = bf16[96,768]{1,0:T(8,128)(2,1)S(1)} collective-permute-done((bf16[96,768]{1,0:T(8,128)(2,1)S(1)}, bf16[96,768]{1,0:T(8,128)(2,1)S(1)}, u32[]{:S(2)}, u32[]{:S(2)}) %collective-permute-start.32) | collective-permute-done | bytes 147488 | tf_op jit(solution)/shard_map/ppermute | solution.py:835
  131.5 1.5 %finish.1 = (f32[96,192]{1,0:T(8,128)}, f32[96,192]{1,0:T(8,128)}, f32[8,192]{1,0:T(8,128)}, f32[8,22]{1,0:T(8,128)}, f32[768]{0:T(1024)}, /*index=5*/f32[768]{0...) custom-call(s32[5]{0:T(128)S(1)} %copy-done.10, ...), custom_call_target="tpu_custom_call" | custom-call | flops 23000000 | bytes 1024 | tf_op jit(solution)/shard_map/finish/pallas_call | solution.py:807
  (109 shorter events, 26.8 us)
Async XLA Ops:
  0.7 5.2 %collective-permute-start = (bf16[32,192]{1,0:T(8,128)(2,1)}, bf16[32,192]{1,0:T(8,128)(2,1)S(1)}, u32[]{:S(2)}, u32[]{:S(2)}) collective-permute-start(bf16[32,192]{1,0:T(8,128)(2,1)} %bitcast.8), channel_id=1, source_target_pairs={{0,4},{1,5},{2,6},{3,7},{4,0},{5,1},{6,2},{7,3},{8,12},{9,13},{10,... | collective-permute-start | bytes 36872 | tf_op jit(solution)/shard_map/ppermute | solution.py:835
  9.0 17.6 %collective-permute-start.1 = (bf16[112,768]{1,0:T(8,128)(2,1)}, bf16[112,768]{1,0:T(8,128)(2,1)S(1)}, u32[]{:S(2)}, u32[]{:S(2)}) collective-permute-start(bf16[112,768]{1,0:T(8,128)(2,1)} %get-tuple-element.99.chunk.refs_0_), channel_id=1, source_target_pairs={{0,24},{1,25},{2,26},{3,27},{4,28},{5,29},{6,30},{7,31},{8,16},{9,... | collective-permute-start | bytes 516104 | tf_op jit(solution)/shard_map/ppermute | solution.py:835
  12.9 14.2 %collective-permute-start.2 = (bf16[112,768]{1,0:T(8,128)(2,1)}, bf16[112,768]{1,0:T(8,128)(2,1)S(1)}, u32[]{:S(2)}, u32[]{:S(2)}) collective-permute-start(bf16[112,768]{1,0:T(8,128)(2,1)} %get-tuple-element.99.chunk.refs_0_), channel_id=1, source_target_pairs={{0,16},{1,17},{2,18},{3,19},{4,20},{5,21},{6,22},{7,23},{8,24},{9,... | collective-permute-start | bytes 516104 | tf_op jit(solution)/shard_map/ppermute | solution.py:835
  12.9 14.2 %collective-permute-start.3 = (bf16[112,768]{1,0:T(8,128)(2,1)}, bf16[112,768]{1,0:T(8,128)(2,1)S(1)}, u32[]{:S(2)}, u32[]{:S(2)}) collective-permute-start(bf16[112,768]{1,0:T(8,128)(2,1)} %get-tuple-element.99.chunk.refs_0_), channel_id=1, source_target_pairs={{0,8},{1,9},{2,10},{3,11},{4,12},{5,13},{6,14},{7,15},{8,0},{9,1},... | collective-permute-start | bytes 516104 | tf_op jit(solution)/shard_map/ppermute | solution.py:835
  13.6 5.0 %collective-permute-start.4 = (bf16[96,384]{1,0:T(8,128)(2,1)}, bf16[96,384]{1,0:T(8,128)(2,1)S(1)}, u32[]{:S(2)}, u32[]{:S(2)}) collective-permute-start(bf16[96,384]{1,0:T(8,128)(2,1)} %pack_second.1.after.refs_0_), channel_id=1, source_target_pairs={{0,4},{1,3},{2,6},{3,1},{4,0},{5,7},{6,2},{7,5},{8,12},{9,11},{10,... | collective-permute-start | bytes 221192 | tf_op jit(solution)/shard_map/ppermute | solution.py:835
  27.2 19.0 %collective-permute-start.8 = (bf16[400,768]{1,0:T(8,128)(2,1)S(1)}, bf16[400,768]{1,0:T(8,128)(2,1)S(1)}, u32[]{:S(2)}, u32[]{:S(2)}) collective-permute-start(bf16[400,768]{1,0:T(8,128)(2,1)S(1)} %join.4.refs_1_.refs_0_), channel_id=1, source_target_pairs={{0,4},{1,3},{2,6},{3,1},{4,0},{5,7},{6,2},{7,5},{8,12},{9,11},{10,... | collective-permute-start | bytes 1843208 | tf_op jit(solution)/shard_map/ppermute | solution.py:835
  28.2 8.3 %collective-permute-start.5 = (bf16[192,384]{1,0:T(8,128)(2,1)S(1)}, bf16[192,384]{1,0:T(8,128)(2,1)S(1)}, u32[]{:S(2)}, u32[]{:S(2)}) collective-permute-start(bf16[192,384]{1,0:T(8,128)(2,1)S(1)} %join.3.refs_0_), channel_id=1, source_target_pairs={{0,16},{1,17},{2,18},{3,19},{4,20},{5,21},{6,22},{7,23},{8,24},{9,... | collective-permute-start | bytes 442376 | tf_op jit(solution)/shard_map/ppermute | solution.py:835
  36.5 9.4 %collective-permute-start.6 = (bf16[384,384]{1,0:T(8,128)(2,1)S(1)}, bf16[384,384]{1,0:T(8,128)(2,1)S(1)}, u32[]{:S(2)}, u32[]{:S(2)}) collective-permute-start(bf16[384,384]{1,0:T(8,128)(2,1)S(1)} %join.5.refs_1_.own), channel_id=1, source_target_pairs={{0,8},{1,9},{2,10},{3,11},{4,12},{5,13},{6,14},{7,15},{8,0},{9,1},... | collective-permute-start | bytes 884744 | tf_op jit(solution)/shard_map/ppermute | solution.py:835
  38.4 16.8 %collective-permute-start.9 = (bf16[400,768]{1,0:T(8,128)(2,1)S(1)}, bf16[400,768]{1,0:T(8,128)(2,1)S(1)}, u32[]{:S(2)}, u32[]{:S(2)}) collective-permute-start(bf16[400,768]{1,0:T(8,128)(2,1)S(1)} %join.4.refs_1_.refs_0_), channel_id=1, source_target_pairs={{0,2},{1,5},{2,0},{3,7},{4,6},{5,1},{6,4},{7,3},{8,10},{9,13},{10,... | collective-permute-start | bytes 1843208 | tf_op jit(solution)/shard_map/ppermute | solution.py:835
  46.2 10.2 %collective-permute-start.10 = (bf16[400,768]{1,0:T(8,128)(2,1)S(1)}, bf16[400,768]{1,0:T(8,128)(2,1)S(1)}, u32[]{:S(2)}, u32[]{:S(2)}) collective-permute-start(bf16[400,768]{1,0:T(8,128)(2,1)S(1)} %collective-permute-done.8.refs_1_), channel_id=1, source_target_pairs={{0,2},{1,5},{2,0},{3,7},{4,6},{5,1},{6,4},{7,3},{8,10},{9,13},{10,... | collective-permute-start | bytes 1843208 | tf_op jit(solution)/shard_map/ppermute | solution.py:835
  46.7 1.7 %collective-permute-start.7 = (bf16[2,768,128]{2,1,0:T(8,128)(2,1)S(1)}, bf16[2,768,128]{2,1,0:T(8,128)(2,1)S(1)}, u32[]{:S(2)}, u32[]{:S(2)}) collective-permute-start(bf16[2,768,128]{2,1,0:T(8,128)(2,1)S(1)} %copy-done.3), channel_id=1, source_target_pairs={{0,1},{1,0},{2,3},{3,2},{4,5},{5,4},{6,7},{7,6},{8,9},{9,8},{10,11... | collective-permute-start | bytes 1179656 | tf_op jit(solution)/shard_map/ppermute | solution.py:835
  46.7 17.4 %collective-permute-start.15 = (bf16[832,384]{1,0:T(8,128)(2,1)S(1)}, bf16[832,384]{1,0:T(8,128)(2,1)S(1)}, u32[]{:S(2)}, u32[]{:S(2)}) collective-permute-start(bf16[832,384]{1,0:T(8,128)(2,1)S(1)} %join_pairs.1.refs_1_.refs_0_), channel_id=1, source_target_pairs={{0,2},{1,5},{2,0},{3,7},{4,6},{5,1},{6,4},{7,3},{8,10},{9,13},{10,... | collective-permute-start | bytes 1916936 | tf_op jit(solution)/shard_map/ppermute | solution.py:835
  48.3 8.1 %collective-permute-start.11 = (bf16[400,768]{1,0:T(8,128)(2,1)S(1)}, bf16[400,768]{1,0:T(8,128)(2,1)S(1)}, u32[]{:S(2)}, u32[]{:S(2)}) collective-permute-start(bf16[400,768]{1,0:T(8,128)(2,1)S(1)} %join.4.refs_1_.refs_0_), channel_id=1, source_target_pairs={{0,1},{1,0},{2,3},{3,2},{4,5},{5,4},{6,7},{7,6},{8,9},{9,8},{10,11... | collective-permute-start | bytes 1843208 | tf_op jit(solution)/shard_map/ppermute | solution.py:835
  54.7 3.0 %collective-permute-start.12 = (bf16[400,768]{1,0:T(8,128)(2,1)S(1)}, bf16[400,768]{1,0:T(8,128)(2,1)S(1)}, u32[]{:S(2)}, u32[]{:S(2)}) collective-permute-start(bf16[400,768]{1,0:T(8,128)(2,1)S(1)} %collective-permute-done.8.refs_1_), channel_id=1, source_target_pairs={{0,1},{1,0},{2,3},{3,2},{4,5},{5,4},{6,7},{7,6},{8,9},{9,8},{10,11... | collective-permute-start | bytes 1843208 | tf_op jit(solution)/shard_map/ppermute | solution.py:835
  55.1 2.6 %collective-permute-start.13 = (bf16[400,768]{1,0:T(8,128)(2,1)S(1)}, bf16[400,768]{1,0:T(8,128)(2,1)S(1)}, u32[]{:S(2)}, u32[]{:S(2)}) collective-permute-start(bf16[400,768]{1,0:T(8,128)(2,1)S(1)} %collective-permute-done.9.refs_2_), channel_id=1, source_target_pairs={{0,1},{1,0},{2,3},{3,2},{4,5},{5,4},{6,7},{7,6},{8,9},{9,8},{10,11... | collective-permute-start | bytes 1843208 | tf_op jit(solution)/shard_map/ppermute | solution.py:835
  56.4 2.2 %collective-permute-start.14 = (bf16[400,768]{1,0:T(8,128)(2,1)S(1)}, bf16[400,768]{1,0:T(8,128)(2,1)S(1)}, u32[]{:S(2)}, u32[]{:S(2)}) collective-permute-start(bf16[400,768]{1,0:T(8,128)(2,1)S(1)} %collective-permute-done.10.refs_3_), channel_id=1, source_target_pairs={{0,1},{1,0},{2,3},{3,2},{4,5},{5,4},{6,7},{7,6},{8,9},{9,8},{10,11... | collective-permute-start | bytes 1843208 | tf_op jit(solution)/shard_map/ppermute | solution.py:835
  56.4 8.1 %collective-permute-start.16 = (bf16[832,384]{1,0:T(8,128)(2,1)S(1)}, bf16[832,384]{1,0:T(8,128)(2,1)S(1)}, u32[]{:S(2)}, u32[]{:S(2)}) collective-permute-start(bf16[832,384]{1,0:T(8,128)(2,1)S(1)} %join_pairs.1.refs_1_.refs_0_), channel_id=1, source_target_pairs={{0,1},{1,0},{2,3},{3,2},{4,5},{5,4},{6,7},{7,6},{8,9},{9,8},{10,11... | collective-permute-start | bytes 1916936 | tf_op jit(solution)/shard_map/ppermute | solution.py:835
  64.1 2.1 %collective-permute-start.17 = (bf16[832,384]{1,0:T(8,128)(2,1)S(1)}, bf16[832,384]{1,0:T(8,128)(2,1)S(1)}, u32[]{:S(2)}, u32[]{:S(2)}) collective-permute-start(bf16[832,384]{1,0:T(8,128)(2,1)S(1)} %collective-permute-done.15.refs_1_), channel_id=1, source_target_pairs={{0,1},{1,0},{2,3},{3,2},{4,5},{5,4},{6,7},{7,6},{8,9},{9,8},{10,11... | collective-permute-start | bytes 1916936 | tf_op jit(solution)/shard_map/ppermute | solution.py:835
  71.9 2.5 %collective-permute-start.18 = (bf16[2,128,1024]{2,1,0:T(8,128)(2,1)S(1)}, bf16[2,128,1024]{2,1,0:T(8,128)(2,1)S(1)}, u32[]{:S(2)}, u32[]{:S(2)}) collective-permute-start(bf16[2,128,1024]{2,1,0:T(8,128)(2,1)S(1)} %get-tuple-element.125), channel_id=1, source_target_pairs={{0,1},{1,0},{2,3},{3,2},{4,5},{5,4},{6,7},{7,6},{8,9},{9,8},{10,11... | collective-permute-start | bytes 1572872 | tf_op jit(solution)/shard_map/ppermute | solution.py:835
  72.3 2.2 %collective-permute-start.19 = (bf16[2,768,128]{2,1,0:T(8,128)(2,1)S(1)}, bf16[2,768,128]{2,1,0:T(8,128)(2,1)S(1)}, u32[]{:S(2)}, u32[]{:S(2)}) collective-permute-start(bf16[2,768,128]{2,1,0:T(8,128)(2,1)S(1)} %get-tuple-element.126.refs_1_), channel_id=1, source_target_pairs={{0,1},{1,0},{2,3},{3,2},{4,5},{5,4},{6,7},{7,6},{8,9},{9,8},{10,11... | collective-permute-start | bytes 1179656 | tf_op jit(solution)/shard_map/ppermute | solution.py:835
  76.0 17.9 %collective-permute-start.21 = (bf16[8,96,768]{2,1,0:T(8,128)(2,1)S(1)}, bf16[8,96,768]{2,1,0:T(8,128)(2,1)S(1)}, u32[]{:S(2)}, u32[]{:S(2)}) collective-permute-start(bf16[8,96,768]{2,1,0:T(8,128)(2,1)S(1)} %weight_grads.3.refs_4_), channel_id=1, source_target_pairs={{0,2},{1,5},{2,0},{3,7},{4,6},{5,1},{6,4},{7,3},{8,10},{9,13},{10,... | collective-permute-start | bytes 3538952 | tf_op jit(solution)/shard_map/ppermute | solution.py:835
  84.5 2.2 %collective-permute-start.20 = (bf16[2,128,384]{2,1,0:T(8,128)(2,1)S(1)}, bf16[2,128,384]{2,1,0:T(8,128)(2,1)S(1)}, u32[]{:S(2)}, u32[]{:S(2)}) collective-permute-start(bf16[2,128,384]{2,1,0:T(8,128)(2,1)S(1)} %get-tuple-element.133), channel_id=1, source_target_pairs={{0,1},{1,0},{2,3},{3,2},{4,5},{5,4},{6,7},{7,6},{8,9},{9,8},{10,11... | collective-permute-start | bytes 589832 | tf_op jit(solution)/shard_map/ppermute | solution.py:835
  87.9 17.6 %collective-permute-start.24 = (bf16[9,96,384]{2,1,0:T(8,128)(2,1)S(1)}, bf16[9,96,384]{2,1,0:T(8,128)(2,1)S(1)}, u32[]{:S(2)}, u32[]{:S(2)}) collective-permute-start(bf16[9,96,384]{2,1,0:T(8,128)(2,1)S(1)} %get-tuple-element.147), channel_id=1, source_target_pairs={{0,2},{1,5},{2,0},{3,7},{4,6},{5,1},{6,4},{7,3},{8,10},{9,13},{10,... | collective-permute-start | bytes 1990664 | tf_op jit(solution)/shard_map/ppermute | solution.py:835
  94.1 11.0 %collective-permute-start.25 = (bf16[4,96,768]{2,1,0:T(8,128)(2,1)S(1)}, bf16[4,96,768]{2,1,0:T(8,128)(2,1)S(1)}, u32[]{:S(2)}, u32[]{:S(2)}) collective-permute-start(bf16[4,96,768]{2,1,0:T(8,128)(2,1)S(1)} %add.13.refs_2_), channel_id=1, source_target_pairs={{0,4},{1,3},{2,6},{3,1},{4,0},{5,7},{6,2},{7,5},{8,12},{9,11},{10,... | collective-permute-start | bytes 1769480 | tf_op jit(solution)/shard_map/ppermute | solution.py:835
  105.3 9.5 %collective-permute-start.31 = (bf16[2,96,768]{2,1,0:T(8,128)(2,1)S(1)}, bf16[2,96,768]{2,1,0:T(8,128)(2,1)S(1)}, u32[]{:S(2)}, u32[]{:S(2)}) collective-permute-start(bf16[2,96,768]{2,1,0:T(8,128)(2,1)S(1)} %get-tuple-element.155), channel_id=1, source_target_pairs={{0,8},{1,9},{2,10},{3,11},{4,12},{5,13},{6,14},{7,15},{8,0},{9,1},... | collective-permute-start | bytes 884744 | tf_op jit(solution)/shard_map/ppermute | solution.py:835
  105.5 11.0 %collective-permute-start.27 = (bf16[4,96,384]{2,1,0:T(8,128)(2,1)S(1)}, bf16[4,96,384]{2,1,0:T(8,128)(2,1)S(1)}, u32[]{:S(2)}, u32[]{:S(2)}) collective-permute-start(bf16[4,96,384]{2,1,0:T(8,128)(2,1)S(1)} %add.14.after), channel_id=1, source_target_pairs={{0,4},{1,3},{2,6},{3,1},{4,0},{5,7},{6,2},{7,5},{8,12},{9,11},{10,... | collective-permute-start | bytes 884744 | tf_op jit(solution)/shard_map/ppermute | solution.py:835
  106.4 5.7 %collective-permute-start.23 = (f32[64,384]{1,0:T(8,128)S(1)}, f32[64,384]{1,0:T(8,128)S(1)}, u32[]{:S(2)}, u32[]{:S(2)}) collective-permute-start(f32[64,384]{1,0:T(8,128)S(1)} %get-tuple-element.145.refs_3_.sent), channel_id=1, source_target_pairs={{0,2},{1,5},{2,0},{3,7},{4,6},{5,1},{6,4},{7,3},{8,10},{9,13},{10,... | collective-permute-start | bytes 294920 | tf_op jit(solution)/shard_map/ppermute | solution.py:835
  112.1 4.4 %collective-permute-start.26 = (f32[48,384]{1,0:T(8,128)S(1)}, f32[48,384]{1,0:T(8,128)S(1)}, u32[]{:S(2)}, u32[]{:S(2)}) collective-permute-start(f32[48,384]{1,0:T(8,128)S(1)} %get-tuple-element.150.sent.refs_0_), channel_id=1, source_target_pairs={{0,4},{1,3},{2,6},{3,1},{4,0},{5,7},{6,2},{7,5},{8,12},{9,11},{10,... | collective-permute-start | bytes 221192 | tf_op jit(solution)/shard_map/ppermute | solution.py:835
  114.8 13.7 %collective-permute-start.32 = (bf16[96,768]{1,0:T(8,128)(2,1)S(1)}, bf16[96,768]{1,0:T(8,128)(2,1)S(1)}, u32[]{:S(2)}, u32[]{:S(2)}) collective-permute-start(bf16[96,768]{1,0:T(8,128)(2,1)S(1)} %get-tuple-element.157), channel_id=1, source_target_pairs={{0,16},{1,17},{2,18},{3,19},{4,20},{5,21},{6,22},{7,23},{8,24},{9,... | collective-permute-start | bytes 442376 | tf_op jit(solution)/shard_map/ppermute | solution.py:835
  116.7 12.6 %collective-permute-start.28 = (bf16[128,384]{1,0:T(8,128)(2,1)S(1)}, bf16[128,384]{1,0:T(8,128)(2,1)S(1)}, u32[]{:S(2)}, u32[]{:S(2)}) collective-permute-start(bf16[128,384]{1,0:T(8,128)(2,1)S(1)} %get-tuple-element.152), channel_id=1, source_target_pairs={{0,8},{1,9},{2,10},{3,11},{4,12},{5,13},{6,14},{7,15},{8,0},{9,1},... | collective-permute-start | bytes 294920 | tf_op jit(solution)/shard_map/ppermute | solution.py:835
  118.7 11.9 %collective-permute-start.29 = (bf16[128,384]{1,0:T(8,128)(2,1)S(1)}, bf16[128,384]{1,0:T(8,128)(2,1)S(1)}, u32[]{:S(2)}, u32[]{:S(2)}) collective-permute-start(bf16[128,384]{1,0:T(8,128)(2,1)S(1)} %get-tuple-element.153), channel_id=1, source_target_pairs={{0,16},{1,17},{2,18},{3,19},{4,20},{5,21},{6,22},{7,23},{8,24},{9,... | collective-permute-start | bytes 294920 | tf_op jit(solution)/shard_map/ppermute | solution.py:835
  119.8 10.9 %collective-permute-start.30 = (bf16[128,384]{1,0:T(8,128)(2,1)S(1)}, bf16[128,384]{1,0:T(8,128)(2,1)S(1)}, u32[]{:S(2)}, u32[]{:S(2)}) collective-permute-start(bf16[128,384]{1,0:T(8,128)(2,1)S(1)} %get-tuple-element.154), channel_id=1, source_target_pairs={{0,24},{1,25},{2,26},{3,27},{4,28},{5,29},{6,30},{7,31},{8,16},{9,... | collective-permute-start | bytes 294920 | tf_op jit(solution)/shard_map/ppermute | solution.py:835
  (22 other events, 193.8 us)
